TPU v7x, 32 devices: a whole 2x2x4 slice. The times are simulated.
32 devices in a mesh: struct: 2 (over y), sample: 16 (over z, x, core).
Axes of the slice: x: 2, y: 2, z: 4, core: 2. Of those that a mesh axis runs over, the one named last changes fastest.
Arguments:
- acts: bfloat16 [2, 32, 768, 768], P('struct', 'sample'), may hold values from -6 to 6
- cond: bfloat16 [2, 768, 384], P('struct'), may hold values from -6 to 6
- pair: bfloat16 [2, 768, 768, 128], P('struct', 'sample'), may hold values from -6 to 6
- lengths: int32 [2], P('struct'), may hold values from 384 to 768, as said below
- token_mask: int32 [2, 768], P('struct'), may hold values 0 or 1
- cond_gains: bfloat16 [768], replicated, may hold values from 0.099609375 to 1.8984375
- cond_w: bfloat16 [384, 3072], replicated, may hold values from -0.3125 to 0.3125
- cond_bias: bfloat16 [1536], replicated, may hold values from -4 to 4
- output_gate_weights: bfloat16 [384, 1536], replicated, may hold values from -0.3125 to 0.3125
- zero_bias: bfloat16 [1536], replicated, may hold values from -4 to 4
- qkvg_w: bfloat16 [768, 3072], replicated, may hold values from -0.21875 to 0.21875
- q_bias: bfloat16 [768], replicated, may hold values from -3 to 3
- out_w: bfloat16 [768, 768], replicated, may hold values from -3 to 3
- swiglu_w: bfloat16 [768, 3072], replicated, may hold values from -0.21875 to 0.21875
- down_w: bfloat16 [1536, 768], replicated, may hold values from -0.4375 to 0.4375
- pair_gain: bfloat16 [128], replicated, may hold values from 0.099609375 to 1.8984375
- pair_w: bfloat16 [128, 16], replicated, may hold values from -0.5 to 0.5
- cotangent: bfloat16 [2, 32, 768, 768], P('struct', 'sample'), may hold values from -6 to 6
Outputs:
- block_out: bfloat16 [2, 32, 768, 768], P('struct', 'sample')
- acts_grad: bfloat16 [2, 32, 768, 768], P('struct', 'sample')
- cond_grad: float32 [2, 768, 384], P('struct', 'sample')
- pair_grad: float32 [2, 768, 768, 128], P('struct', 'sample')
- cond_gains_grad: float32 [768], P('sample')
- cond_w_grad: float32 [384, 3072], P('sample')
- cond_bias_grad: float32 [1536], P('sample')
- zero_w_grad: float32 [384, 1536], P('sample')
- zero_bias_grad: float32 [1536], P('sample')
- qkvg_w_grad: float32 [768, 3072], P('sample')
- q_bias_grad: float32 [768], P('sample')
- out_w_grad: float32 [768, 768], P('sample')
- swiglu_w_grad: float32 [768, 3072], P('sample')
- down_w_grad: float32 [1536, 768], P('sample')
- pair_gain_grad: float32 [128], P('sample')
- pair_w_grad: float32 [128, 16], P('sample')
Inputs may be any that keep to these rules, and one draw needn't show every extreme that they name: `lengths`: each structure has 384 to 768 tokens; in every draw some structure has 768.
All inputs are finite; a program needn't handle non-finite values. No bound on the sum of `token_mask` on one device may be relied on, other than what follows from the above.
Results may differ from a plain program's by a relative error of at most 0.013.
The roundings to bfloat16 on the way count: a program that leaves them out, or rounds other values in their place, can miss the bound.
Values may be sent and summed in bfloat16 or wider, within the bound.
No kernel may reach another device: no remote copies, remote signals or barrier semaphores. Data moves between devices by JAX's collectives and lax.ppermute only.
A program may use at most 384 MiB of HBM per device.

v0:
```python
import jax
import jax.numpy as jnp
from jax import lax
from jax.sharding import PartitionSpec as P

EPS = 1e-05
MASKED = -1000000000.0


def matmul(left_side, right_side):
    return jnp.dot(left_side, right_side, preferred_element_type=jnp.float32)


def layer_norm(values):
    center = values - jnp.mean(values, axis=-1, keepdims=True)
    inverse = lax.rsqrt(jnp.mean(center * center, axis=-1, keepdims=True) + EPS)
    return (center * inverse, inverse)


def norm_back(grad_in, normed, inverse):
    mean_grad = jnp.mean(grad_in, axis=-1, keepdims=True)
    mean_proj = jnp.mean(grad_in * normed, axis=-1, keepdims=True)
    return inverse * (grad_in - mean_grad - normed * mean_proj)


def sigmoid_slope(gate_value):
    return gate_value * (1.0 - gate_value)


def body(
    acts,
    cond,
    pair,
    lengths,
    token_mask,
    cond_gains,
    cond_w,
    cond_bias,
    output_gate_weights,
    zero_bias,
    qkvg_w,
    q_bias,
    out_w,
    swiglu_w,
    down_w,
    pair_gain,
    pair_w,
    cotangent,
):
    sample_count = acts.shape[1]
    length_max = acts.shape[2]
    model_width = acts.shape[3]
    cond_width = cond.shape[2]
    head_count = pair_w.shape[1]
    head_dim = model_width // head_count
    half_heads = head_count // 2
    hidden_width = down_w.shape[0]
    flat_rows = sample_count * length_max
    scale_qk = head_dim ** (-0.5)
    single_conditioning = cond[0]
    position = lax.iota(jnp.int32, length_max)
    key_valid = (position < lengths[0]) & ((token_mask[0] == 1) | (position == 0))
    group_ids = jnp.arange(2, dtype=jnp.int32)
    pair_normed, pair_inverse = layer_norm(pair[0].astype(jnp.float32))
    pair_gain_full = pair_gain.astype(jnp.float32)
    pair_affine = (pair_normed * pair_gain_full).astype(jnp.bfloat16)
    bias_local = jnp.einsum(
        "ijc,ch->ihj", pair_affine, pair_w, preferred_element_type=jnp.float32
    ).astype(jnp.bfloat16)
    bias_full = lax.all_gather(bias_local, "sample", axis=0, tiled=True)
    zero_gates = jax.nn.sigmoid(
        matmul(single_conditioning, output_gate_weights) + zero_bias.astype(jnp.float32)
    )
    cond_normed, cond_inverse = layer_norm(single_conditioning.astype(jnp.float32))
    gains_full = cond_gains.astype(jnp.float32)
    scale_bias = cond_bias.astype(jnp.float32)

    def conditioning(branch):
        scaled_rows = (
            cond_normed * gains_full[branch * cond_width : (branch + 1) * cond_width]
        ).astype(jnp.bfloat16)
        projected = matmul(
            scaled_rows, cond_w[:, 2 * branch * model_width : 2 * (branch + 1) * model_width]
        )
        factor = jax.nn.sigmoid(
            projected[:, :model_width]
            + scale_bias[branch * model_width : (branch + 1) * model_width]
        )
        return (scaled_rows, factor, projected[:, model_width:])

    scaled_one, factor_one, shift_one = conditioning(0)
    scaled_two, factor_two, shift_two = conditioning(1)
    acts_all = acts[0].astype(jnp.float32)
    acts_normed, acts_inverse = layer_norm(acts_all)
    input_one = (factor_one * acts_normed + shift_one).astype(jnp.bfloat16)
    joined = matmul(input_one.reshape(flat_rows, model_width), qkvg_w).reshape(
        sample_count, length_max, 4 * model_width
    )
    queries = (
        (joined[..., :model_width] + q_bias.astype(jnp.float32))
        .astype(jnp.bfloat16)
        .reshape(sample_count, length_max, head_count, head_dim)
    )
    key_rows = (
        joined[..., model_width : 2 * model_width]
        .astype(jnp.bfloat16)
        .reshape(sample_count, length_max, head_count, head_dim)
    )
    value_rows = (
        joined[..., 2 * model_width : 3 * model_width]
        .astype(jnp.bfloat16)
        .reshape(sample_count, length_max, head_count, head_dim)
    )
    gate_heads = jax.nn.sigmoid(joined[..., 3 * model_width :])

    def head_slice(tensor, group):
        return lax.dynamic_slice_in_dim(tensor, group * half_heads, half_heads, 2)

    def group_scores(group, pair_term):
        raw_scores = jnp.einsum(
            "sqhd,skhd->sqhk",
            head_slice(queries, group),
            head_slice(key_rows, group),
            preferred_element_type=jnp.float32,
        )
        bias_part = lax.dynamic_slice_in_dim(pair_term, group * half_heads, half_heads, 1).astype(
            jnp.float32
        )
        return jnp.where(
            key_valid[None, None, None, :], raw_scores * scale_qk + bias_part[None], MASKED
        )

    def attend_group(group):
        scores = group_scores(group, bias_full)
        highest = jnp.max(scores, axis=-1, keepdims=True)
        shifted = jnp.exp(scores - highest)
        row_totals = jnp.sum(shifted, axis=-1, keepdims=True)
        probs_low = (shifted / row_totals).astype(jnp.bfloat16)
        mixed = jnp.einsum(
            "sqhk,skhd->sqhd",
            probs_low,
            head_slice(value_rows, group),
            preferred_element_type=jnp.float32,
        )
        return (mixed, highest + jnp.log(row_totals))

    mixed_groups, log_totals = lax.map(attend_group, group_ids)

    def join_heads(stacked):
        return jnp.moveaxis(stacked, 0, 2).reshape(sample_count, length_max, model_width)

    mixed_heads = join_heads(mixed_groups)
    gated = (gate_heads * mixed_heads).astype(jnp.bfloat16)
    attended = matmul(gated.reshape(flat_rows, model_width), out_w).reshape(
        sample_count, length_max, model_width
    )
    input_two = (factor_two * acts_normed + shift_two).astype(jnp.bfloat16)
    hidden = matmul(input_two.reshape(flat_rows, model_width), swiglu_w).reshape(
        sample_count, length_max, 2 * hidden_width
    )
    gate_part = hidden[..., :hidden_width]
    up_part = hidden[..., hidden_width:]
    gate_sig = jax.nn.sigmoid(gate_part)
    product = (gate_part * gate_sig * up_part).astype(jnp.bfloat16)
    transition = matmul(product.reshape(flat_rows, hidden_width), down_w).reshape(
        sample_count, length_max, model_width
    )
    block_out = (
        acts_all + zero_gates[:, :model_width] * attended + zero_gates[:, model_width:] * transition
    )
    grad_out = cotangent[0].astype(jnp.float32)
    grad_att = (grad_out * zero_gates[:, :model_width]).astype(jnp.bfloat16)
    grad_tr = (grad_out * zero_gates[:, model_width:]).astype(jnp.bfloat16)
    grad_zero = jnp.concatenate(
        [grad_out * attended, grad_out * transition], axis=-1
    ) * sigmoid_slope(zero_gates)
    reduced_zero_gradient = grad_zero.astype(jnp.bfloat16)
    zero_w_grad = jnp.einsum(
        "ou,hoi->ui", single_conditioning, reduced_zero_gradient, preferred_element_type=jnp.float32
    )
    zero_bias_grad = jnp.sum(grad_zero, axis=(0, 1))
    conditioning_gradient = jnp.einsum(
        "opv,hv->ph", reduced_zero_gradient, output_gate_weights, preferred_element_type=jnp.float32
    )
    grad_tr_flat = grad_tr.reshape(flat_rows, model_width)
    grad_product = matmul(grad_tr_flat, down_w.T).reshape(sample_count, length_max, hidden_width)
    down_w_grad = matmul(product.reshape(flat_rows, hidden_width).T, grad_tr_flat)
    grad_up = grad_product * gate_part * gate_sig
    grad_gate = grad_product * up_part * gate_sig * (1.0 + gate_part * (1.0 - gate_sig))
    grad_hidden = (
        jnp.concatenate([grad_gate, grad_up], axis=-1)
        .astype(jnp.bfloat16)
        .reshape(flat_rows, 2 * hidden_width)
    )
    swiglu_w_grad = matmul(input_two.reshape(flat_rows, model_width).T, grad_hidden)
    grad_input_two = matmul(grad_hidden, swiglu_w.T).reshape(sample_count, length_max, model_width)
    grad_att_flat = grad_att.reshape(flat_rows, model_width)
    grad_gated = matmul(grad_att_flat, out_w.T).reshape(sample_count, length_max, model_width)
    out_w_grad = matmul(gated.reshape(flat_rows, model_width).T, grad_att_flat)
    grad_gate_heads = grad_gated * mixed_heads * sigmoid_slope(gate_heads)
    grad_mixed = (
        (grad_gated * gate_heads)
        .astype(jnp.bfloat16)
        .reshape(sample_count, length_max, head_count, head_dim)
    )

    def attend_back(item):
        group, log_total = item
        scores = group_scores(group, bias_full)
        probs_full = jnp.exp(scores - log_total)
        probs_low = probs_full.astype(jnp.bfloat16)
        grad_mixed_group = head_slice(grad_mixed, group)
        grad_probs = jnp.einsum(
            "sqhd,skhd->sqhk",
            grad_mixed_group,
            head_slice(value_rows, group),
            preferred_element_type=jnp.float32,
        )
        grad_values = jnp.einsum(
            "sqhk,sqhd->skhd", probs_low, grad_mixed_group, preferred_element_type=jnp.float32
        )
        grad_scores = probs_full * (
            grad_probs - jnp.sum(probs_full * grad_probs, axis=-1, keepdims=True)
        )
        grad_raw = (grad_scores * scale_qk).astype(jnp.bfloat16)
        grad_queries = jnp.einsum(
            "sqhk,skhd->sqhd",
            grad_raw,
            head_slice(key_rows, group),
            preferred_element_type=jnp.float32,
        )
        grad_keys = jnp.einsum(
            "sqhk,sqhd->skhd",
            grad_raw,
            head_slice(queries, group),
            preferred_element_type=jnp.float32,
        )
        group_total = jnp.sum(grad_scores, axis=0)
        return (grad_queries, grad_keys, grad_values, group_total)

    query_groups, key_groups, value_groups, total_groups = lax.map(
        attend_back, (group_ids, log_totals)
    )
    bias_grad_stack = jnp.moveaxis(total_groups, 0, 1)
    bias_grad_rows = bias_grad_stack.reshape(bias_grad_stack.shape[0], head_count, length_max)
    bias_grad_rows = lax.psum_scatter(bias_grad_rows, "sample", scatter_dimension=0, tiled=True)
    grad_queries = join_heads(query_groups)
    grad_keys = join_heads(key_groups)
    grad_values = join_heads(value_groups)
    q_bias_grad = jnp.sum(grad_queries, axis=(0, 1))
    grad_joined = jnp.concatenate(
        [grad_queries, grad_keys, grad_values, grad_gate_heads], axis=-1
    ).astype(jnp.bfloat16)
    grad_joined_flat = grad_joined.reshape(flat_rows, 4 * model_width)
    qkvg_w_grad = matmul(input_one.reshape(flat_rows, model_width).T, grad_joined_flat)
    grad_input_one = matmul(grad_joined_flat, qkvg_w.T).reshape(
        sample_count, length_max, model_width
    )

    def adaptive_back(branch, grad_input, scaled_rows, factor):
        grad_factor = grad_input * acts_normed * sigmoid_slope(factor)
        projection_gradient = jnp.concatenate([grad_factor, grad_input], axis=-1).astype(
            jnp.bfloat16
        )
        column_count = cond_w[:, 2 * branch * model_width : 2 * (branch + 1) * model_width]
        weight_grad = jnp.einsum(
            "ou,hoi->ui", scaled_rows, projection_gradient, preferred_element_type=jnp.float32
        )
        grad_scaled = jnp.einsum(
            "opv,hv->ph", projection_gradient, column_count, preferred_element_type=jnp.float32
        )
        gain_grad = jnp.sum(grad_scaled * cond_normed, axis=0)
        normed_grad = grad_scaled * gains_full[branch * cond_width : (branch + 1) * cond_width]
        return (
            weight_grad,
            jnp.sum(grad_factor, axis=(0, 1)),
            gain_grad,
            normed_grad,
            grad_input * factor,
        )

    weight_one, bias_one, gain_one, normgrad_one, actsgrad_one = adaptive_back(
        0, grad_input_one, scaled_one, factor_one
    )
    weight_two, bias_two, gain_two, normgrad_two, actsgrad_two = adaptive_back(
        1, grad_input_two, scaled_two, factor_two
    )
    cond_w_grad = jnp.concatenate([weight_one, weight_two], axis=1)
    cond_bias_grad = jnp.concatenate([bias_one, bias_two])
    cond_gains_grad = jnp.concatenate([gain_one, gain_two])
    conditioning_gradient = conditioning_gradient + norm_back(
        normgrad_one + normgrad_two, cond_normed, cond_inverse
    )
    acts_grad = grad_out + norm_back(actsgrad_one + actsgrad_two, acts_normed, acts_inverse)
    bias_grad_low = bias_grad_rows.astype(jnp.bfloat16)
    pair_w_grad = jnp.einsum(
        "ijc,ihj->ch", pair_affine, bias_grad_low, preferred_element_type=jnp.float32
    )
    grad_affine = jnp.einsum(
        "ihj,ch->ijc", bias_grad_low, pair_w, preferred_element_type=jnp.float32
    )
    pair_gain_grad = jnp.sum(grad_affine * pair_normed, axis=(0, 1))
    grad_pair = norm_back(grad_affine * pair_gain_full, pair_normed, pair_inverse)
    shares = (
        lax.psum_scatter(cond_gains_grad, "sample", scatter_dimension=0, tiled=True),
        lax.psum_scatter(cond_w_grad, "sample", scatter_dimension=0, tiled=True),
        lax.psum_scatter(cond_bias_grad, "sample", scatter_dimension=0, tiled=True),
        lax.psum_scatter(zero_w_grad, "sample", scatter_dimension=0, tiled=True),
        lax.psum_scatter(zero_bias_grad, "sample", scatter_dimension=0, tiled=True),
        lax.psum_scatter(qkvg_w_grad, "sample", scatter_dimension=0, tiled=True),
        lax.psum_scatter(q_bias_grad, "sample", scatter_dimension=0, tiled=True),
        lax.psum_scatter(out_w_grad, "sample", scatter_dimension=0, tiled=True),
        lax.psum_scatter(swiglu_w_grad, "sample", scatter_dimension=0, tiled=True),
        lax.psum_scatter(down_w_grad, "sample", scatter_dimension=0, tiled=True),
        lax.psum_scatter(pair_gain_grad, "sample", scatter_dimension=0, tiled=True),
        lax.psum_scatter(pair_w_grad, "sample", scatter_dimension=0, tiled=True),
        lax.psum_scatter(conditioning_gradient, "sample", scatter_dimension=0, tiled=True),
    )
    summed = (
        lax.psum(shares[0].astype(jnp.bfloat16), "struct").astype(jnp.float32),
        lax.psum(shares[1].astype(jnp.bfloat16), "struct").astype(jnp.float32),
        lax.psum(shares[2].astype(jnp.bfloat16), "struct").astype(jnp.float32),
        lax.psum(shares[3].astype(jnp.bfloat16), "struct").astype(jnp.float32),
        lax.psum(shares[4].astype(jnp.bfloat16), "struct").astype(jnp.float32),
        lax.psum(shares[5].astype(jnp.bfloat16), "struct").astype(jnp.float32),
        lax.psum(shares[6].astype(jnp.bfloat16), "struct").astype(jnp.float32),
        lax.psum(shares[7].astype(jnp.bfloat16), "struct").astype(jnp.float32),
        lax.psum(shares[8].astype(jnp.bfloat16), "struct").astype(jnp.float32),
        lax.psum(shares[9].astype(jnp.bfloat16), "struct").astype(jnp.float32),
        lax.psum(shares[10].astype(jnp.bfloat16), "struct").astype(jnp.float32),
        lax.psum(shares[11].astype(jnp.bfloat16), "struct").astype(jnp.float32),
    )
    return (
        block_out.astype(jnp.bfloat16)[None],
        acts_grad.astype(jnp.bfloat16)[None],
        shares[12][None],
        grad_pair[None],
        summed[0],
        summed[1],
        summed[2],
        summed[3],
        summed[4],
        summed[5],
        summed[6],
        summed[7],
        summed[8],
        summed[9],
        summed[10],
        summed[11],
    )


def solution(mesh):
    in_specs = (
        P("struct", "sample", None, None),
        P("struct", None, None),
        P("struct", "sample", None, None),
        P("struct"),
        P("struct", None),
        P(),
        P(),
        P(),
        P(),
        P(),
        P(),
        P(),
        P(),
        P(),
        P(),
        P(),
        P(),
        P("struct", "sample", None, None),
    )
    out_specs = (
        P("struct", "sample", None, None),
        P("struct", "sample", None, None),
        P("struct", "sample", None),
        P("struct", "sample", None, None),
        P("sample"),
        P("sample", None),
        P("sample"),
        P("sample", None),
        P("sample"),
        P("sample", None),
        P("sample"),
        P("sample", None),
        P("sample", None),
        P("sample", None),
        P("sample"),
        P("sample", None),
    )
    return jax.shard_map(body, mesh=mesh, in_specs=in_specs, out_specs=out_specs, check_vma=False)
```

profile of v0, /device:TPU:0, one launch (start us, length us, event | category | flops | bytes accessed | tf_op | source)
XLA Modules:
  0.0 1709.5 jit_solution(10442800875744858769)
XLA Ops:
  100.8 18.3 %multiply_convert_fusion.8 = (bf16[2,768,1536]{2,1,0:T(8,128)(2,1)}, bf16[2,768,1536]{2,1,0:T(8,128)(2,1)}, bf16[2,768,1536]{2,1,0:T(8,128)(2,1)}) fusion(f32[2,768,3072]{2,1,0:T(8,128)} %fusion.139, bf16[1536,768]{1,0:T(8,128)(2,1)S(1)} %copy-done, bf16[1,2,768,768]{2,3,1,0:T(8,128)(2,1)} %copy.160, f32[768,768]{0,1:T(8,128)S(1)} %copy-done.6), kind=kOutput, calls=%fused_computation.92 | convolution fusion | flops 3665166336 | bytes 40108032 | tf_op jit(solution)/shard_map/dot_general | solution.py:11
  208.0 24.9 %copy.151 = bf16[768,16,768]{0,2,1:T(8,128)(2,1)} copy(bf16[768,16,768]{2,1,0:T(8,128)(2,1)} %all-gather.2.cloned.1.call-done) | data formatting | bytes 37748736 | tf_op jit(solution)/shard_map/while | solution.py:147
  235.6 158.3 %while.28 = (s32[]{:T(128)}, f32[2,2,768,8,48]{2,4,3,0,1:T(8,128)}, f32[2,2,768,8,1]{2,3,1,4,0:T(8,128)S(1)}, s32[2]{0:T(128)S(1)}, bf16[2,768,16,48]{1,3,2,0:T(...) while((s32[]{:T(128)}, f32[2,2,768,8,48]{2,4,3,0,1:T(8,128)}, ...), condition=%wide.region_9.10_spmd, body=%wide.region_6.9_spmd.sunk | while | flops 1958203392 | bytes 204476112 | solution.py:147
  249.7 22.3 %fusion.286 = (f32[2,768,8]{1,2,0:T(8,128)S(1)}, f32[2,8,768,768]{3,2,1,0:T(8,128)}) fusion(f32[768,8,768]{0,2,1:T(8,128)} %dynamic-slice_convert_fusion.10, pred[768]{0:T(1024)(128)(4,1)S(1)} %get-tuple-element.543, bf16[2,768,16,48]{1,3,2,0:T(8,128)(2,1)} %get-tuple-element.545, s32[]{:T(128)S(6)} %select_n.46, ...), kind=kOutput, calls=%fused_computation.5.clone.1 | convolution fusion | flops 943706112 | bytes 59033344 | tf_op jit(solution)/shard_map/while/body/eval_jaxpr/sqhd,skhd->sqhk/dot_general | solution.py:120
  271.9 21.2 %fusion.287 = f32[2,768,8]{1,2,0:T(8,128)S(1)} fusion(f32[2,8,768,768]{3,2,1,0:T(8,128)} %get-tuple-element.497, f32[2,768,8]{1,2,0:T(8,128)S(1)} %get-tuple-element.498, f32[768,8,768]{0,2,1:T(8,128)} %dynamic-slice_convert_fusion.10, pred[768]{0:T(1024)(128)(4,1)S(1)} %get-tuple-element.543), kind=kLoop, calls=%fused_computation.4.clone.1 | loop fusion | flops 47173632 | bytes 56722176 | tf_op jit(solution)/shard_map/while/body/eval_jaxpr/reduce_sum | solution.py:137
  293.2 22.7 %bitcast_dynamic-update-slice_fusion.10 = f32[2,2,768,8,48]{2,4,3,0,1:T(8,128)} fusion(f32[2,2,768,8,48]{2,4,3,0,1:T(8,128)} %get-tuple-element.526, s32[]{:T(128)S(6)} %copy.255, f32[2,8,768,768]{3,2,1,0:T(8,128)} %get-tuple-element.497, f32[2,768,8]{1,2,0:T(8,128)S(1)} %fusion.287, f32[2,768,8]{1,2,0:T(8,128)S(1)} %get-tuple-element.498, ...), kind=kOutput, calls=%fused_computation.8.clone.1 | convolution fusion | flops 962592768 | bytes 60261384 | tf_op jit(solution)/shard_map/while/body/eval_jaxpr/sqhk,skhd->sqhd/dot_general | solution.py:139
  329.0 22.0 %fusion.286 = (f32[2,768,8]{1,2,0:T(8,128)S(1)}, f32[2,8,768,768]{3,2,1,0:T(8,128)}) fusion(f32[768,8,768]{0,2,1:T(8,128)} %dynamic-slice_convert_fusion.10, pred[768]{0:T(1024)(128)(4,1)S(1)} %get-tuple-element.543, bf16[2,768,16,48]{1,3,2,0:T(8,128)(2,1)} %get-tuple-element.545, s32[]{:T(128)S(6)} %select_n.46, ...), kind=kOutput, calls=%fused_computation.5.clone.1 | convolution fusion | flops 943706112 | bytes 59033344 | tf_op jit(solution)/shard_map/while/body/eval_jaxpr/sqhd,skhd->sqhk/dot_general | solution.py:120
  351.0 20.8 %fusion.287 = f32[2,768,8]{1,2,0:T(8,128)S(1)} fusion(f32[2,8,768,768]{3,2,1,0:T(8,128)} %get-tuple-element.497, f32[2,768,8]{1,2,0:T(8,128)S(1)} %get-tuple-element.498, f32[768,8,768]{0,2,1:T(8,128)} %dynamic-slice_convert_fusion.10, pred[768]{0:T(1024)(128)(4,1)S(1)} %get-tuple-element.543), kind=kLoop, calls=%fused_computation.4.clone.1 | loop fusion | flops 47173632 | bytes 56722176 | tf_op jit(solution)/shard_map/while/body/eval_jaxpr/reduce_sum | solution.py:137
  371.8 22.1 %bitcast_dynamic-update-slice_fusion.10 = f32[2,2,768,8,48]{2,4,3,0,1:T(8,128)} fusion(f32[2,2,768,8,48]{2,4,3,0,1:T(8,128)} %get-tuple-element.526, s32[]{:T(128)S(6)} %copy.255, f32[2,8,768,768]{3,2,1,0:T(8,128)} %get-tuple-element.497, f32[2,768,8]{1,2,0:T(8,128)S(1)} %fusion.287, f32[2,768,8]{1,2,0:T(8,128)S(1)} %get-tuple-element.498, ...), kind=kOutput, calls=%fused_computation.8.clone.1 | convolution fusion | flops 962592768 | bytes 60261384 | tf_op jit(solution)/shard_map/while/body/eval_jaxpr/sqhk,skhd->sqhd/dot_general | solution.py:139
  418.5 385.4 %while.29 = (s32[]{:T(128)}, f32[2,2,768,8,48]{2,4,3,0,1:T(8,128)}, bf16[2,2,768,8,48]{2,4,3,0,1:T(8,128)(2,1)}, bf16[2,2,768,8,48]{2,4,3,0,1:T(8,128)(2,1)}, f3...) while((s32[]{:T(128)}, f32[2,2,768,8,48]{2,4,3,0,1:T(8,128)}, ...), condition=%wide.region_13.14_spmd, body=%wide.region_10.13_spmd.sunk | while | flops 9239042048 | bytes 470837216 | solution.py:241
  432.1 23.5 %fusion.308 = f32[2,768,8,768]{1,3,2,0:T(8,128)} fusion(f32[2,768,8]{1,2,0:T(8,128)S(1)} %dynamic-slice_bitcast_fusion.2, f32[768,8,768]{0,2,1:T(8,128)} %dynamic-slice_convert_fusion.11, pred[768]{0:T(1024)(128)(4,1)S(1)} %get-tuple-element.592, bf16[2,768,16,48]{1,3,2,0:T(8,128)(2,1)} %get-tuple-element.593, s32[]{:T(128)S(6)} %select_n.48, ...), kind=kOutput, calls=%fused_computation.25.clone.1 | convolution fusion | flops 943718400 | bytes 59033344 | tf_op jit(solution)/shard_map/while/body/eval_jaxpr/sqhd,skhd->sqhk/dot_general | solution.py:120
  455.6 16.0 bitcast_dynamic-update-slice_fusion.14
  471.7 38.0 %bitcast_dynamic-update-slice_fusion.13 = bf16[2,2,768,8,48]{2,4,3,0,1:T(8,128)(2,1)} fusion(bf16[2,2,768,8,48]{2,4,3,0,1:T(8,128)(2,1)} %get-tuple-element.570, s32[]{:T(128)S(6)} %copy.266, f32[2,768,8,768]{1,3,2,0:T(8,128)} %fusion.308, bf16[2,768,16,48]{1,3,2,0:T(8,128)(2,1)} %get-tuple-element.593, s32[]{:T(128)S(6)} %select_n.48, ...), kind=kOutput, calls=%fused_computation.35.clone.1 | convolution fusion | flops 2765107968 | bytes 83758080 | tf_op jit(solution)/shard_map/while/body/eval_jaxpr/sqhk,sqhd->skhd/dot_general | solution.py:232
  509.7 34.1 %bitcast_dynamic-update-slice_fusion.12 = f32[2,2,768,8,48]{2,4,3,0,1:T(8,128)} fusion(f32[2,2,768,8,48]{2,4,3,0,1:T(8,128)} %get-tuple-element.569, s32[]{:T(128)S(6)} %copy.266, f32[2,768,8,768]{1,3,2,0:T(8,128)} %fusion.308, bf16[2,768,16,48]{1,3,2,0:T(8,128)(2,1)} %get-tuple-element.591, s32[]{:T(128)S(6)} %select_n.48, ...), kind=kOutput, calls=%fused_computation.36.clone.1 | convolution fusion | flops 2765107968 | bytes 83758080 | tf_op jit(solution)/shard_map/while/body/eval_jaxpr/sqhk,skhd->sqhd/dot_general | solution.py:226
  543.9 33.5 %fusion.309 = f32[768,8,768]{0,2,1:T(8,128)} fusion(f32[2,768,8,768]{1,3,2,0:T(8,128)} %fusion.308, bf16[2,768,16,48]{1,3,2,0:T(8,128)(2,1)} %get-tuple-element.596, s32[]{:T(128)S(6)} %select_n.48, bf16[2,768,16,48]{1,3,2,0:T(8,128)(2,1)S(1)} %get-tuple-element.597), kind=kOutput, calls=%fused_computation.253.clone.1 | convolution fusion | flops 1844982528 | bytes 99092480 | tf_op jit(solution)/shard_map/while/body/eval_jaxpr/sub | solution.py:223
  577.4 19.1 %copy.245 = f32[1,768,8,768]{3,2,0,1:T(8,128)} copy(f32[1,768,8,768]{1,3,2,0:T(8,128)} %bitcast.356) | data formatting | bytes 37748736 | tf_op jit(solution)/shard_map/while/body/jit(dynamic_update_index_in_dim)/dynamic_update_slice | solution.py:241
  624.6 23.6 %fusion.308 = f32[2,768,8,768]{1,3,2,0:T(8,128)} fusion(f32[2,768,8]{1,2,0:T(8,128)S(1)} %dynamic-slice_bitcast_fusion.2, f32[768,8,768]{0,2,1:T(8,128)} %dynamic-slice_convert_fusion.11, pred[768]{0:T(1024)(128)(4,1)S(1)} %get-tuple-element.592, bf16[2,768,16,48]{1,3,2,0:T(8,128)(2,1)} %get-tuple-element.593, s32[]{:T(128)S(6)} %select_n.48, ...), kind=kOutput, calls=%fused_computation.25.clone.1 | convolution fusion | flops 943718400 | bytes 59033344 | tf_op jit(solution)/shard_map/while/body/eval_jaxpr/sqhd,skhd->sqhk/dot_general | solution.py:120
  648.2 16.0 bitcast_dynamic-update-slice_fusion.14
  664.2 38.0 %bitcast_dynamic-update-slice_fusion.13 = bf16[2,2,768,8,48]{2,4,3,0,1:T(8,128)(2,1)} fusion(bf16[2,2,768,8,48]{2,4,3,0,1:T(8,128)(2,1)} %get-tuple-element.570, s32[]{:T(128)S(6)} %copy.266, f32[2,768,8,768]{1,3,2,0:T(8,128)} %fusion.308, bf16[2,768,16,48]{1,3,2,0:T(8,128)(2,1)} %get-tuple-element.593, s32[]{:T(128)S(6)} %select_n.48, ...), kind=kOutput, calls=%fused_computation.35.clone.1 | convolution fusion | flops 2765107968 | bytes 83758080 | tf_op jit(solution)/shard_map/while/body/eval_jaxpr/sqhk,sqhd->skhd/dot_general | solution.py:232
  702.2 34.2 %bitcast_dynamic-update-slice_fusion.12 = f32[2,2,768,8,48]{2,4,3,0,1:T(8,128)} fusion(f32[2,2,768,8,48]{2,4,3,0,1:T(8,128)} %get-tuple-element.569, s32[]{:T(128)S(6)} %copy.266, f32[2,768,8,768]{1,3,2,0:T(8,128)} %fusion.308, bf16[2,768,16,48]{1,3,2,0:T(8,128)(2,1)} %get-tuple-element.591, s32[]{:T(128)S(6)} %select_n.48, ...), kind=kOutput, calls=%fused_computation.36.clone.1 | convolution fusion | flops 2765107968 | bytes 83758080 | tf_op jit(solution)/shard_map/while/body/eval_jaxpr/sqhk,skhd->sqhd/dot_general | solution.py:226
  736.4 33.5 %fusion.309 = f32[768,8,768]{0,2,1:T(8,128)} fusion(f32[2,768,8,768]{1,3,2,0:T(8,128)} %fusion.308, bf16[2,768,16,48]{1,3,2,0:T(8,128)(2,1)} %get-tuple-element.596, s32[]{:T(128)S(6)} %select_n.48, bf16[2,768,16,48]{1,3,2,0:T(8,128)(2,1)S(1)} %get-tuple-element.597), kind=kOutput, calls=%fused_computation.253.clone.1 | convolution fusion | flops 1844982528 | bytes 99092480 | tf_op jit(solution)/shard_map/while/body/eval_jaxpr/sub | solution.py:223
  769.9 19.1 %copy.245 = f32[1,768,8,768]{3,2,0,1:T(8,128)} copy(f32[1,768,8,768]{1,3,2,0:T(8,128)} %bitcast.356) | data formatting | bytes 37748736 | tf_op jit(solution)/shard_map/while/body/jit(dynamic_update_index_in_dim)/dynamic_update_slice | solution.py:241
  789.0 14.6 constant_dynamic-update-slice_fusion.2
  824.2 21.4 %fusion.223 = (f32[2,768]{1,0:T(2,128)S(1)}, f32[2,768]{1,0:T(2,128)S(1)}, f32[768]{0:T(1024)S(1)}, f32[768]{0:T(1024)S(1)}, f32[2,768,768]{1,2,0:T(8,128)}, /*i...) fusion(f32[2,768]{1,0:T(2,128)S(1)} %copy-done.33, ...), kind=kOutput, calls=%fused_computation.251 | convolution fusion | flops 7307914240 | bytes 44857344 | tf_op jit(solution)/shard_map/dot_general | solution.py:11
  902.4 54.1 %reduce-scatter.25.cloned.1.call-done = f32[24,1536]{1,0:T(8,128)} async-done(((f32[384,1536]{1,0:T(8,128)}), f32[24,1536]{1,0:T(8,128)}) %reduce-scatter.25.cloned.1.call-update) | async-done | bytes 147472
  958.4 76.5 %reduce-scatter.15.cloned.1.call-done = f32[24,3072]{1,0:T(8,128)} async-done(((f32[384,3072]{1,0:T(8,128)}), f32[24,3072]{1,0:T(8,128)}) %reduce-scatter.15.cloned.1.call-update) | async-done | bytes 294928 | tf_op jit(solution)/shard_map/reduce_scatter | solution.py:306
  1036.5 114.0 %reduce-scatter.17.cloned.1.call-done = f32[48,3072]{1,0:T(8,128)} async-done(((f32[768,3072]{1,0:T(8,128)}), f32[48,3072]{1,0:T(8,128)}) %reduce-scatter.17.cloned.1.call-update) | async-done | bytes 589840 | tf_op jit(solution)/shard_map/reduce_scatter | solution.py:310
  1175.8 25.9 %all-reduce.11.cloned.1.call-done = (bf16[24,1536]{0,1:T(8,128)(2,1)}, bf16[24,3072]{1,0:T(8,128)(2,1)}, bf16[48,3072]{1,0:T(8,128)(2,1)}, bf16[48,768]{1,0:T(8,...) async-done(((bf16[24,1536]{0,1:T(8,128)(2,1)}, bf16[24,3072]{1,0:T(8,128)(2,1)}, bf16[48,3072]{1,0:T(8,128)(2,1)}, bf16[48,768]{1,0:T(8,128)(2,1)}, ...) | async-done | bytes 1032208 | tf_op jit(solution)/shard_map/psum | solution.py:323
  1212.0 362.7 %reduce-scatter.13.cloned.1.call-done = f32[48,16,768]{2,1,0:T(8,128)} async-done(((f32[768,16,768]{2,1,0:T(8,128)}), f32[48,16,768]{2,1,0:T(8,128)}) %reduce-scatter.13.cloned.1.call-update) | async-done | bytes 2359312 | tf_op jit(solution)/shard_map/reduce_scatter | solution.py:246
  1595.3 60.8 %all-reduce.6 = (bf16[768]{0:T(1024)(128)(2,1)S(1)}, bf16[1536]{0:T(1024)(128)(2,1)S(1)}, bf16[1536]{0:T(1024)(128)(2,1)S(1)}, bf16[768]{0:T(1024)(128)(2,1)S(1)...) all-reduce(f32[768]{0:T(1024)S(1)} %pad_maximum_fusion.10, ...), channel_id=4, replica_groups=mesh['struct'=2,'sample'=16] {'sample'}, use_global_device_ids=true, to_apply=%region_27.28.clone | all-reduce | flops 6784 | bytes 40704
  1664.6 19.1 %fusion.99 = f32[1,48,768,128]{2,3,1,0:T(8,128)} fusion(bf16[1,48,768,128]{2,3,1,0:T(8,128)(2,1)} %copy.149, f32[48,768,128]{1,2,0:T(8,128)} %get-tuple-element.370, f32[48,768]{1,0:T(8,128)S(1)} %broadcast_multiply_fusion, f32[48,768]{1,0:T(8,128)S(1)} %broadcast_multiply_fusion.1, f32[128]{0:T(128)S(1)} %copy-done.44, f32[48,768]{1,0:T(8,128)S(1)} %copy-done.25, ...), kind=kLoop, calls=%fused_computation.76 | loop fusion | flops 37748736 | bytes 47776256 | tf_op jit(solution)/shard_map/broadcast_in_dim | solution.py:337
  1683.8 18.8 %copy.188 = f32[1,48,768,128]{3,2,1,0:T(8,128)} copy(f32[1,48,768,128]{2,3,1,0:T(8,128)} %fusion.99) | data formatting | bytes 37748736
  (266 shorter events, 417.5 us)
Async XLA Ops:
  7.2 93.6 %copy-start = (bf16[1536,768]{1,0:T(8,128)(2,1)S(1)}, bf16[1536,768]{1,0:T(8,128)(2,1)}, u32[]{:S(2)}) copy-start(bf16[1536,768]{1,0:T(8,128)(2,1)} %param.36) | copy-start | bytes 7077892
  7.2 200.8 %all-gather.2.cloned.1.call-start = ((), (), s32[]{:S(2)}) async-start(), calls=%async_computation.8 | async-start | bytes 20054016 | tf_op jit(solution)/shard_map/all_gather | solution.py:70
  8.1 22.8 %copy-start.43 = (f32[128]{0:T(128)}, f32[128]{0:T(128)S(1)}, u32[]{:S(2)}) copy-start(f32[128]{0:T(128)S(1)} %convert_element_type.224) | copy-start | bytes 1540
  35.5 861.9 %reduce-scatter.23.cloned.1.call-start = ((), (), s32[]{:S(2)}) async-start(), calls=%async_computation.15 | async-start | bytes 5013504 | tf_op jit(solution)/shard_map/reduce_scatter | solution.py:314
  36.0 8.6 copy-start.8
  36.0 9.2 copy-start.39
  36.1 9.2 copy-start.38
  81.0 7.6 copy-start.30
  81.0 9.0 slice-start
  90.0 10.8 copy-start.6
  128.6 770.5 %reduce-scatter.21.cloned.1.call-start = ((), (), s32[]{:S(2)}) async-start(), calls=%async_computation.14 | async-start | bytes 10027008 | tf_op jit(solution)/shard_map/reduce_scatter | solution.py:313
  142.7 758.1 %reduce-scatter.19.cloned.1.call-start = ((), (), s32[]{:S(2)}) async-start(), calls=%async_computation.13 | async-start | bytes 2506752 | tf_op jit(solution)/shard_map/reduce_scatter | solution.py:312
  142.8 15.5 slice-start.2
  144.4 13.9 slice-start.3
  394.0 6.9 copy-start.3
  817.4 6.8 copy-start.5
  817.4 6.8 copy-start.31
  817.4 6.8 copy-start.33
  824.1 132.4 %reduce-scatter.25.cloned.1.call-start = ((), (), s32[]{:S(2)}) async-start(), calls=%async_computation.16 | async-start | bytes 2506752
  824.2 21.5 %copy-start.7 = (f32[768,768]{0,1:T(8,128)S(1)}, f32[768,768]{0,1:T(8,128)}, u32[]{:S(2)}) copy-start(f32[768,768]{0,1:T(8,128)} %copy.155) | copy-start | bytes 7077892
  824.2 21.5 %copy-start.23 = (bf16[768,768]{1,0:T(8,128)(2,1)S(1)}, bf16[768,768]{1,0:T(8,128)(2,1)}, u32[]{:S(2)}) copy-start(bf16[768,768]{1,0:T(8,128)(2,1)} %param.34) | copy-start | bytes 3538948
  856.9 7.7 copy-start.9
  870.6 164.3 %reduce-scatter.15.cloned.1.call-start = ((), (), s32[]{:S(2)}) async-start(), calls=%async_computation.11 | async-start | bytes 5013504 | tf_op jit(solution)/shard_map/reduce_scatter | solution.py:306
  883.9 266.7 %reduce-scatter.17.cloned.1.call-start = ((), (), s32[]{:S(2)}) async-start(), calls=%async_computation.12 | async-start | bytes 10027008 | tf_op jit(solution)/shard_map/reduce_scatter | solution.py:310
  897.3 304.4 %all-reduce.11.cloned.1.call-start = ((), (), s32[]{:S(2)}) async-start(), calls=%async_computation.17 | async-start | bytes 2703360 | tf_op jit(solution)/shard_map/psum | solution.py:323
  1152.4 422.3 %reduce-scatter.13.cloned.1.call-start = ((), (), s32[]{:S(2)}) async-start(), calls=%async_computation.10 | async-start | bytes 40108032 | tf_op jit(solution)/shard_map/reduce_scatter | solution.py:246
  1153.1 549.4 %reduce-scatter.11.cloned.1.call-start = ((), (), s32[]{:S(2)}) async-start(), calls=%async_computation.9 | async-start | bytes 1253376 | tf_op jit(solution)/shard_map/reduce_scatter | solution.py:317
  1172.8 401.8 %copy-start.22 = (f32[48,768]{1,0:T(8,128)S(1)}, f32[48,768]{1,0:T(8,128)}, u32[]{:S(2)}) copy-start(f32[48,768]{1,0:T(8,128)} %copy-done.21) | copy-start | bytes 442372
  1172.8 401.8 %copy-start.25 = (f32[48,768]{1,0:T(8,128)S(1)}, f32[48,768]{1,0:T(8,128)}, u32[]{:S(2)}) copy-start(f32[48,768]{1,0:T(8,128)} %copy-done.24) | copy-start | bytes 442372
  1172.9 401.8 %copy-start.44 = (f32[128]{0:T(128)S(1)}, f32[128]{0:T(128)}, u32[]{:S(2)}) copy-start(f32[128]{0:T(128)} %copy-done.43) | copy-start | bytes 1540
  1212.0 369.1 %copy-start.48 = (bf16[128,16]{0,1:T(8,128)(2,1)S(1)}, bf16[128,16]{0,1:T(8,128)(2,1)}, u32[]{:S(2)}) copy-start(bf16[128,16]{0,1:T(8,128)(2,1)} %param.38) | copy-start | bytes 12292
  1683.7 18.8 %copy-start.1 = (bf16[1536,768]{1,0:T(8,128)(2,1)S(1)}, bf16[1536,768]{1,0:T(8,128)(2,1)}, u32[]{:S(2)}) copy-start(bf16[1536,768]{1,0:T(8,128)(2,1)} %param.36) | copy-start | bytes 7077892
  (32 other events, 125.4 us)
Sparse Core Ops, SparseCore 0:
  35.6 101.6 all-gather.1
  141.2 75.5 reduce-scatter.22
  221.4 110.4 reduce-scatter.20
  824.3 66.1 reduce-scatter.18
  894.6 61.9 reduce-scatter.24
  960.3 74.5 reduce-scatter.14
  1040.1 110.3 reduce-scatter.16
  1154.4 47.2 all-reduce.10
  1206.5 368.0 reduce-scatter.12
  1579.1 57.3 reduce-scatter.10
where the time goes:
time: 1720 us; the launch traced here: 1710 us
  waiting for transfers between devices  634 us (37%)
  matrix products  579 us (34%)
  local copies, waits for them, and re-layouts  226 us (13%)
  other arithmetic  182 us (11%)
  blocking collectives  65.7 us (4%)
  between operations  17.9 us (1%)
    reduce_scatter x1, waiting for transfers between devices, body(): lax.psum_scatter(bias_grad_rows, 'sample', scatter_dimension=0, tiled=True)  363 us
    dot_general x15, matrix products, matmul(): return jnp.dot(left_side, right_side, preferred_element_type=jnp.float32)  160 us
    reduce_scatter x1, waiting for transfers between devices, body(): lax.psum_scatter(qkvg_w_grad, 'sample', scatter_dimension=0, tiled=True)  114 us
    dot_general x4, matrix products, group_scores(): jnp.einsum('sqhd,skhd->sqhk', head_slice(queries, group), head_slice(key_...  91.4 us
    reduce_scatter x1, waiting for transfers between devices, body(): lax.psum_scatter(cond_w_grad, 'sample', scatter_dimension=0, tiled=True)  76.5 us
    dot_general x2, matrix products, attend_back(): jnp.einsum('sqhk,sqhd->skhd', grad_raw, head_slice(queries, group), prefe...  76 us
    dot_general x2, matrix products, attend_back(): jnp.einsum('sqhk,skhd->sqhd', grad_raw, head_slice(key_rows, group), pref...  68.3 us
    dynamic_update_slice x4, local copies, waits for them, and re-layouts, body(): lax.map(attend_back, (group_ids, log_totals))  67.4 us
  transfers between devices with their start and end apart: 10, of which 5 were waited for; matrix products, arithmetic and copies ran while one was open for 56% of the time, Pallas kernels for 0%

commit v1 on v0

v1 whole, which is shorter than its diff:
```python
import functools

import jax
import jax.numpy as jnp
from jax import lax
from jax.experimental import pallas as pl
from jax.experimental.pallas import tpu as pltpu
from jax.sharding import PartitionSpec as P

EPS = 1e-05
MASKED = -1000000000.0
F32 = jnp.float32
BF16 = jnp.bfloat16
CHUNK_HEADS = 4
WINDOW = 256
LANES = 128
TOKENS = 128
PAIR_ROWS = 8
VMEM_LIMIT = 60 * 2**20


def dot(left, right, left_dim=1, right_dim=0):
    return lax.dot_general(
        left, right, (((left_dim,), (right_dim,)), ((), ())), preferred_element_type=F32
    )


def layer_norm(values):
    center = values - jnp.mean(values, axis=-1, keepdims=True)
    inverse = lax.rsqrt(jnp.mean(center * center, axis=-1, keepdims=True) + EPS)
    return (center * inverse, inverse)


def norm_back(grad_in, normed, inverse):
    mean_grad = jnp.mean(grad_in, axis=-1, keepdims=True)
    mean_proj = jnp.mean(grad_in * normed, axis=-1, keepdims=True)
    return inverse * (grad_in - mean_grad - normed * mean_proj)


def slope(gate):
    return gate * (1.0 - gate)


def column_sum(values):
    return jnp.sum(values.reshape(-1, values.shape[-1]), axis=0, keepdims=True)


def params(flops_limit=VMEM_LIMIT):
    return pltpu.CompilerParams(
        vmem_limit_bytes=flops_limit, dimension_semantics=("arbitrary",)
    )


def cost(flops, nbytes, exps=0):
    return pl.CostEstimate(flops=int(flops), bytes_accessed=int(nbytes), transcendentals=int(exps))


def whole(array):
    rank = len(array.shape)
    return pl.BlockSpec(array.shape, lambda t: (0,) * rank, pipeline_mode=pl.Buffered(1))


def fixed_out(shape):
    rank = len(shape)
    return pl.BlockSpec(shape, lambda t: (0,) * rank, pipeline_mode=pl.Buffered(1))


def rows_of(block, axis, rank, squeeze=None):
    return pl.BlockSpec(block, lambda t: tuple(t if a == axis else 0 for a in range(rank)))


def pair_forward_kernel(pair_ref, gain_ref, weight_ref, valid_ref, out_ref):
    gain = gain_ref[...].astype(F32)
    valid = valid_ref[...] > 0

    def row(i, carry):
        normed, _ = layer_norm(pair_ref[i].astype(F32))
        affine = (normed * gain).astype(BF16)
        term = dot(weight_ref[...], affine, 1, 1)
        out_ref[i] = jnp.where(valid, term, MASKED).astype(BF16)
        return carry

    lax.fori_loop(0, pair_ref.shape[0], row, 0, unroll=2)


def pair_forward(pair, gain, weight_t, valid):
    rows, length, channels = pair.shape
    heads = weight_t.shape[0]
    return pl.pallas_call(
        pair_forward_kernel,
        grid=(rows // PAIR_ROWS,),
        in_specs=[
            rows_of((PAIR_ROWS, length, channels), 0, 3),
            whole(gain),
            whole(weight_t),
            whole(valid),
        ],
        out_specs=rows_of((PAIR_ROWS, heads, length), 0, 3),
        out_shape=jax.ShapeDtypeStruct((rows, heads, length), BF16),
        compiler_params=params(),
        cost_estimate=cost(2 * pair.size * heads, pair.size * 2.3),
        name="pair_forward",
    )(pair, gain, weight_t, valid)


def pair_backward_kernel(pair_ref, grad_ref, gain_ref, weight_ref, out_ref, weight_grad_ref, gain_grad_ref):
    gain = gain_ref[...].astype(F32)

    @pl.when(pl.program_id(0) == 0)
    def _():
        weight_grad_ref[...] = jnp.zeros_like(weight_grad_ref)
        gain_grad_ref[...] = jnp.zeros_like(gain_grad_ref)

    def row(i, carry):
        normed, inverse = layer_norm(pair_ref[i].astype(F32))
        affine = (normed * gain).astype(BF16)
        grad = grad_ref[i]
        weight_grad_ref[...] += dot(grad, affine)
        grad_affine = dot(grad, weight_ref[...], 0, 0)
        gain_grad_ref[...] += column_sum(grad_affine * normed)
        out_ref[i] = norm_back(grad_affine * gain, normed, inverse)
        return carry

    lax.fori_loop(0, pair_ref.shape[0], row, 0, unroll=2)


def pair_backward(pair, grad, gain, weight_t):
    rows, length, channels = pair.shape
    heads = weight_t.shape[0]
    return pl.pallas_call(
        pair_backward_kernel,
        grid=(rows // PAIR_ROWS,),
        in_specs=[
            rows_of((PAIR_ROWS, length, channels), 0, 3),
            rows_of((PAIR_ROWS, heads, length), 0, 3),
            whole(gain),
            whole(weight_t),
        ],
        out_specs=[
            rows_of((PAIR_ROWS, length, channels), 0, 3),
            fixed_out((heads, channels)),
            fixed_out((1, channels)),
        ],
        out_shape=[
            jax.ShapeDtypeStruct((rows, length, channels), F32),
            jax.ShapeDtypeStruct((heads, channels), F32),
            jax.ShapeDtypeStruct((1, channels), F32),
        ],
        compiler_params=params(),
        cost_estimate=cost(4 * pair.size * heads, pair.size * 6.3),
        name="pair_backward",
    )(pair, grad, gain, weight_t)


def conditioned(cond_normed, gain, weight, bias):
    width = bias.shape[-1]
    scaled = (cond_normed * gain.astype(F32)).astype(BF16)
    projected = dot(scaled, weight)
    factor = jax.nn.sigmoid(projected[:, :width] + bias.astype(F32))
    return scaled, factor, projected[:, width:]


def window_start(chunk, head_dim):
    return chunk * CHUNK_HEADS * head_dim // LANES * LANES


def inputs_kernel(
    head_dim, acts_ref, cot_ref, cond_ref, gain_ref, cond_w_ref, cond_b_ref, zero_w_ref, zero_b_ref,
    qkvg_ref, q_bias_ref, out_wt_ref,
    input_ref, gate_ref, gated_grad_ref, q_ref, k_ref, v_ref, g_ref, qt_ref, kt_ref, vt_ref, gt_ref,
):
    samples, tokens, width = acts_ref.shape
    cond = cond_ref[...]
    cond_normed, _ = layer_norm(cond.astype(F32))
    zero_gate = jax.nn.sigmoid(dot(cond, zero_w_ref[...]) + zero_b_ref[...].astype(F32))
    _, factor, shift = conditioned(cond_normed, gain_ref[...], cond_w_ref[...], cond_b_ref[...])
    normed, _ = layer_norm(acts_ref[...].astype(F32))
    first = (factor[None] * normed + shift[None]).astype(BF16)
    input_ref[...] = first
    first = first.reshape(samples * tokens, width)
    grad_att = (cot_ref[...].astype(F32) * zero_gate[None]).astype(BF16)
    grad_gated = dot(grad_att.reshape(samples * tokens, width), out_wt_ref[...])
    gated_grad_ref[...] = grad_gated.reshape(samples, tokens, width)
    gate = jax.nn.sigmoid(dot(first, qkvg_ref[:, 3 * width :]))
    gate_ref[...] = gate.reshape(samples, tokens, width)

    def put(values, nat_ref, t_ref):
        low = values.astype(BF16).reshape(samples, tokens, width)
        for chunk in range(nat_ref.shape[0]):
            start = window_start(chunk, head_dim)
            nat_ref[chunk] = low[:, :, start : start + WINDOW]
        for s in range(samples):
            t_ref[s] = low[s].T

    put(grad_gated * gate, g_ref, gt_ref)
    put(dot(first, qkvg_ref[:, :width]) + q_bias_ref[...].astype(F32), q_ref, qt_ref)
    put(dot(first, qkvg_ref[:, width : 2 * width]), k_ref, kt_ref)
    put(dot(first, qkvg_ref[:, 2 * width : 3 * width]), v_ref, vt_ref)


def inputs_call(acts, cot, cond, gain, cond_w, cond_b, zero_w, zero_b, qkvg_w, q_bias, out_wt, heads):
    samples, length, width = acts.shape
    chunks = heads // CHUNK_HEADS
    block = rows_of((samples, TOKENS, width), 1, 3)
    nat = rows_of((chunks, samples, TOKENS, WINDOW), 2, 4)
    turned = rows_of((samples, width, TOKENS), 2, 3)
    rows = samples * length
    fixed = (gain, cond_w, cond_b, zero_w, zero_b, qkvg_w, q_bias, out_wt)
    return pl.pallas_call(
        functools.partial(inputs_kernel, width // heads),
        grid=(length // TOKENS,),
        in_specs=[block, block, rows_of((TOKENS, cond.shape[1]), 0, 2)] + [whole(a) for a in fixed],
        out_specs=[block] * 3 + [nat] * 4 + [turned] * 4,
        out_shape=[
            jax.ShapeDtypeStruct(acts.shape, BF16),
            jax.ShapeDtypeStruct(acts.shape, F32),
            jax.ShapeDtypeStruct(acts.shape, F32),
        ]
        + [jax.ShapeDtypeStruct((chunks, samples, length, WINDOW), BF16)] * 4
        + [jax.ShapeDtypeStruct((samples, width, length), BF16)] * 4,
        compiler_params=params(),
        cost_estimate=cost(2 * rows * width * width * 6, rows * width * 40),
        name="inputs",
    )(acts, cot, cond, *fixed)


def add_to(step, ref, value):
    @pl.when(step == 0)
    def _():
        ref[...] = value

    @pl.when(step > 0)
    def _():
        ref[...] += value


def zero_back(grad_zero, cond, zero_w_ref):
    total = jnp.sum(grad_zero, axis=0)
    low = total.astype(BF16)
    return dot(cond, low, 0, 0), column_sum(total), dot(low, zero_w_ref[...], 1, 1)


def adaptive_back(grad_input, normed, factor, scaled, gain, cond_normed, cond_w_ref):
    grad_factor = jnp.sum(grad_input * normed * slope(factor)[None], axis=0)
    projected = jnp.concatenate([grad_factor, jnp.sum(grad_input, axis=0)], axis=-1).astype(BF16)
    weight_grad = dot(scaled, projected, 0, 0)
    grad_scaled = dot(projected, cond_w_ref[...], 1, 1)
    return (
        weight_grad,
        column_sum(grad_factor),
        column_sum(grad_scaled * cond_normed),
        grad_scaled * gain.astype(F32),
        grad_input * factor[None],
    )


def transition_kernel(
    acts_ref, cot_ref, cond_ref, gain_ref, cond_w_ref, cond_b_ref, zero_w_ref, zero_b_ref,
    swiglu_ref, down_ref,
    partial_ref, acts_grad_ref, cond_gate_ref, cond_norm_ref,
    swiglu_out, down_out, cond_w_out, zero_w_out, cond_b_out, zero_b_out, gain_out,
    swiglu_acc, down_acc, cond_w_acc, zero_w_acc,
):
    step = pl.program_id(0)
    samples, tokens, width = acts_ref.shape
    rows = samples * tokens
    hidden_width = down_ref.shape[0]
    cond = cond_ref[...]
    cond_normed, _ = layer_norm(cond.astype(F32))
    zero_gate = jax.nn.sigmoid(dot(cond, zero_w_ref[...]) + zero_b_ref[...].astype(F32))
    scaled, factor, shift = conditioned(cond_normed, gain_ref[...], cond_w_ref[...], cond_b_ref[...])
    acts = acts_ref[...].astype(F32)
    normed, _ = layer_norm(acts)
    second = (factor[None] * normed + shift[None]).astype(BF16).reshape(rows, width)
    grad_out = cot_ref[...].astype(F32)
    grad_tr = (grad_out * zero_gate[None]).astype(BF16).reshape(rows, width)
    hidden = dot(second, swiglu_ref[...])
    gate_part = hidden[:, :hidden_width]
    up_part = hidden[:, hidden_width:]
    gate_sig = jax.nn.sigmoid(gate_part)
    silu = gate_part * gate_sig
    product = (silu * up_part).astype(BF16)
    transition = dot(product, down_ref[...]).reshape(samples, tokens, width)
    partial_ref[...] = acts + zero_gate[None] * transition
    grad_product = dot(grad_tr, down_ref[...], 1, 1)
    add_to(step, down_acc, dot(product, grad_tr, 0, 0))
    grad_up = grad_product * silu
    grad_gate = grad_product * up_part * gate_sig * (1.0 + gate_part * (1.0 - gate_sig))
    grad_hidden = jnp.concatenate([grad_gate, grad_up], axis=-1).astype(BF16)
    add_to(step, swiglu_acc, dot(second, grad_hidden, 0, 0))
    grad_input = dot(grad_hidden, swiglu_ref[...], 1, 1).reshape(samples, tokens, width)
    zero_grad, zero_sum, cond_gate = zero_back(
        grad_out * transition * slope(zero_gate)[None], cond, zero_w_ref
    )
    cond_gate_ref[...] = cond_gate
    add_to(step, zero_w_acc, zero_grad)
    add_to(step, zero_b_out, zero_sum)
    weight_grad, bias_sum, gain_sum, cond_norm, acts_grad = adaptive_back(
        grad_input, normed, factor, scaled, gain_ref[...], cond_normed, cond_w_ref
    )
    add_to(step, cond_w_acc, weight_grad)
    add_to(step, cond_b_out, bias_sum)
    add_to(step, gain_out, gain_sum)
    cond_norm_ref[...] = cond_norm
    acts_grad_ref[...] = acts_grad

    @pl.when(step == pl.num_programs(0) - 1)
    def _():
        swiglu_out[...] = swiglu_acc[...].astype(BF16)
        down_out[...] = down_acc[...].astype(BF16)
        cond_w_out[...] = cond_w_acc[...].astype(BF16)
        zero_w_out[...] = zero_w_acc[...].astype(BF16)


def transition_call(acts, cot, cond, gain, cond_w, cond_b, zero_w, zero_b, swiglu, down):
    samples, length, width = acts.shape
    cond_width = cond.shape[1]
    hidden = down.shape[0]
    rows = samples * length
    block = rows_of((samples, TOKENS, width), 1, 3)
    cond_block = rows_of((TOKENS, cond_width), 0, 2)
    fixed = (gain, cond_w, cond_b, zero_w, zero_b, swiglu, down)
    weights = [(width, 2 * hidden), (hidden, width), (cond_width, 2 * width), (cond_width, width)]
    vectors = [(1, width), (1, width), (1, cond_width)]
    return pl.pallas_call(
        transition_kernel,
        grid=(length // TOKENS,),
        in_specs=[block, block, cond_block] + [whole(a) for a in fixed],
        out_specs=[block, block, cond_block, cond_block] + [fixed_out(s) for s in weights + vectors],
        out_shape=[jax.ShapeDtypeStruct(acts.shape, F32)] * 2
        + [jax.ShapeDtypeStruct(cond.shape, F32)] * 2
        + [jax.ShapeDtypeStruct(s, BF16) for s in weights]
        + [jax.ShapeDtypeStruct(s, F32) for s in vectors],
        scratch_shapes=[pltpu.VMEM(s, F32) for s in weights],
        compiler_params=params(),
        cost_estimate=cost(2 * rows * width * hidden * 9, rows * width * 40),
        name="transition",
    )(acts, cot, cond, *fixed)


def attention_kernel(
    head_dim, first_lane, q_ref, k_ref, v_ref, g_ref, qt_ref, kt_ref, vt_ref, gt_ref, bias_ref,
    mixed_ref, dq_ref, dkt_ref, dvt_ref, db_ref, kz, vz, plow, dslow, dsum,
):
    h = pl.program_id(0)
    samples, length, wide = q_ref.shape
    scale = head_dim ** (-0.5)
    off = pl.multiple_of(first_lane + h * head_dim, 16)
    lane = lax.broadcasted_iota(jnp.int32, (1, wide), 1)
    mask = ((lane >= off) & (lane < off + head_dim)).astype(BF16)

    @pl.when(h == 0)
    def _():
        mixed_ref[...] = jnp.zeros_like(mixed_ref)
        dq_ref[...] = jnp.zeros_like(dq_ref)

    kz[...] = jnp.zeros_like(kz)
    vz[...] = jnp.zeros_like(vz)
    for s in range(samples):
        kz[s, pl.ds(off, head_dim), :] = kt_ref[s]
        vz[s, pl.ds(off, head_dim), :] = vt_ref[s]
    bias = bias_ref[:, 0].reshape(length, length).astype(F32)
    for s in range(samples):
        x = dot(q_ref[s], kz[s]) * scale + bias
        x = jnp.exp(x - jnp.max(x, axis=-1, keepdims=True))
        probs = x * (1.0 / jnp.sum(x, axis=-1, keepdims=True))
        low = probs.astype(BF16)
        plow[...] = low
        mixed = dot(low, v_ref[s] * mask)
        mixed_ref[s] += mixed
        grad = g_ref[s]
        delta = jnp.sum(grad.astype(F32) * mixed, axis=-1, keepdims=True)
        grad_scores = probs * (dot(grad, vz[s]) - delta)
        grad_low = (grad_scores * scale).astype(BF16)
        dslow[...] = grad_low
        total = grad_scores if s == 0 else dsum[...] + grad_scores
        if s < samples - 1:
            dsum[...] = total
        else:
            db_ref[:, 0] = total.astype(BF16).reshape(db_ref.shape[0], db_ref.shape[2], length)
        dq_ref[s] += dot(grad_low, k_ref[s] * mask)
        dvt_ref[s] = dot(gt_ref[s], plow[...]).astype(BF16)
        dkt_ref[s] = dot(qt_ref[s], dslow[...]).astype(BF16)


def attention_call(chunk, nats, turned, bias, head_dim):
    _, samples, length, wide = nats[0].shape
    parts, _, part_rows, _ = bias.shape
    nat = pl.BlockSpec((None, samples, length, wide), lambda h: (chunk, 0, 0, 0))
    turn = pl.BlockSpec((samples, head_dim, length), lambda h: (0, chunk * CHUNK_HEADS + h, 0))
    turn_out = pl.BlockSpec((samples, head_dim, length), lambda h: (0, h, 0))
    bias_in = pl.BlockSpec((parts, 1, part_rows, length), lambda h: (0, chunk * CHUNK_HEADS + h, 0, 0))
    bias_out = pl.BlockSpec((parts, 1, part_rows, length), lambda h: (0, h, 0, 0))
    held = pl.BlockSpec((samples, length, wide), lambda h: (0, 0, 0))
    pairs = samples * CHUNK_HEADS
    return pl.pallas_call(
        functools.partial(
            attention_kernel, head_dim, chunk * CHUNK_HEADS * head_dim - window_start(chunk, head_dim)
        ),
        grid=(CHUNK_HEADS,),
        in_specs=[nat] * 4 + [turn] * 4 + [bias_in],
        out_specs=[held, held, turn_out, turn_out, bias_out],
        out_shape=[
            jax.ShapeDtypeStruct((samples, length, wide), F32),
            jax.ShapeDtypeStruct((samples, length, wide), F32),
            jax.ShapeDtypeStruct((samples, CHUNK_HEADS * head_dim, length), BF16),
            jax.ShapeDtypeStruct((samples, CHUNK_HEADS * head_dim, length), BF16),
            jax.ShapeDtypeStruct((parts, CHUNK_HEADS, part_rows, length), BF16),
        ],
        scratch_shapes=[
            pltpu.VMEM((samples, wide, length), BF16),
            pltpu.VMEM((samples, wide, length), BF16),
            pltpu.VMEM((length, length), BF16),
            pltpu.VMEM((length, length), BF16),
            pltpu.VMEM((length, length), F32),
        ],
        compiler_params=params(),
        cost_estimate=cost(
            12 * pairs * length * length * wide, 8 * CHUNK_HEADS * length * length, pairs * length * length
        ),
        name="attention",
    )(*nats, *turned, bias)


def outputs_kernel(
    head_dim, chunks, *refs
):
    (acts_ref, cot_ref, cond_ref, input_ref, gate_ref, gated_grad_ref, partial_ref, acts_part_ref,
     cond_gate_in, cond_norm_in), refs = refs[:10], refs[10:]
    mixed_refs, refs = refs[:chunks], refs[chunks:]
    dq_refs, refs = refs[:chunks], refs[chunks:]
    dkt_refs, refs = refs[:chunks], refs[chunks:]
    dvt_refs, refs = refs[:chunks], refs[chunks:]
    (gain_ref, cond_w_ref, cond_b_ref, zero_w_ref, zero_b_ref, qkvg_t_ref, out_w_ref), refs = refs[:7], refs[7:]
    (block_ref, acts_grad_ref, cond_grad_ref, qkvg_out, out_out, cond_w_out, zero_w_out,
     cond_b_out, zero_b_out, gain_out, q_bias_out), refs = refs[:11], refs[11:]
    qkvg_acc, out_acc, cond_w_acc, zero_w_acc = refs
    step = pl.program_id(0)
    samples, tokens, width = acts_ref.shape
    rows = samples * tokens
    cond = cond_ref[...]
    cond_normed, cond_inverse = layer_norm(cond.astype(F32))
    zero_gate = jax.nn.sigmoid(dot(cond, zero_w_ref[...]) + zero_b_ref[...].astype(F32))
    scaled, factor, _ = conditioned(cond_normed, gain_ref[...], cond_w_ref[...], cond_b_ref[...])
    normed, inverse = layer_norm(acts_ref[...].astype(F32))
    first = input_ref[...].reshape(rows, width)
    grad_out = cot_ref[...].astype(F32)
    grad_att = (grad_out * zero_gate[None]).astype(BF16).reshape(rows, width)

    def join(window_refs):
        pieces = []
        for tile in range(width // LANES):
            held = [
                ref[:, :, tile * LANES - start : (tile + 1) * LANES - start]
                for chunk, ref in enumerate(window_refs)
                for start in [window_start(chunk, head_dim)]
                if start <= tile * LANES < start + WINDOW
            ]
            pieces.append(functools.reduce(jnp.add, held))
        return jnp.concatenate(pieces, axis=-1).reshape(rows, width)

    def turn(turned_refs):
        joined = jnp.concatenate([ref[...] for ref in turned_refs], axis=1)
        return jnp.concatenate([joined[s].T for s in range(samples)], axis=0)

    mixed = join(mixed_refs)
    gate = gate_ref[...].reshape(rows, width)
    gated = (gate * mixed).astype(BF16)
    attended = dot(gated, out_w_ref[...]).reshape(samples, tokens, width)
    block_ref[...] = (partial_ref[...] + zero_gate[None] * attended).astype(BF16)
    add_to(step, out_acc, dot(gated, grad_att, 0, 0))
    zero_grad, zero_sum, cond_gate = zero_back(
        grad_out * attended * slope(zero_gate)[None], cond, zero_w_ref
    )
    add_to(step, zero_w_acc, zero_grad)
    add_to(step, zero_b_out, zero_sum)
    grad_queries = join(dq_refs)
    add_to(step, q_bias_out, column_sum(grad_queries))
    grad_gate = gated_grad_ref[...].reshape(rows, width) * mixed * slope(gate)
    grad_joined = jnp.concatenate(
        [grad_queries.astype(BF16), turn(dkt_refs), turn(dvt_refs), grad_gate.astype(BF16)], axis=-1
    )
    add_to(step, qkvg_acc, dot(first, grad_joined, 0, 0))
    grad_input = dot(grad_joined, qkvg_t_ref[...]).reshape(samples, tokens, width)
    weight_grad, bias_sum, gain_sum, cond_norm, acts_part = adaptive_back(
        grad_input, normed, factor, scaled, gain_ref[...], cond_normed, cond_w_ref
    )
    add_to(step, cond_w_acc, weight_grad)
    add_to(step, cond_b_out, bias_sum)
    add_to(step, gain_out, gain_sum)
    acts_grad_ref[...] = (
        grad_out + norm_back(acts_part + acts_part_ref[...], normed, inverse)
    ).astype(BF16)
    cond_grad_ref[...] = (
        cond_gate
        + cond_gate_in[...]
        + norm_back(cond_norm + cond_norm_in[...], cond_normed, cond_inverse)
    )

    @pl.when(step == pl.num_programs(0) - 1)
    def _():
        qkvg_out[...] = qkvg_acc[...].astype(BF16)
        out_out[...] = out_acc[...].astype(BF16)
        cond_w_out[...] = cond_w_acc[...].astype(BF16)
        zero_w_out[...] = zero_w_acc[...].astype(BF16)


def outputs_call(acts, cot, cond, first, gate, gated_grad, partial, acts_part, cond_gate, cond_norm,
                 mixeds, dqs, dkts, dvts, fixed, heads):
    samples, length, width = acts.shape
    cond_width = cond.shape[1]
    rows = samples * length
    chunks = len(mixeds)
    block = rows_of((samples, TOKENS, width), 1, 3)
    cond_block = rows_of((TOKENS, cond_width), 0, 2)
    window = rows_of((samples, TOKENS, WINDOW), 1, 3)
    turned = rows_of((samples, width // chunks, TOKENS), 2, 3)
    weights = [(width, 4 * width), (width, width), (cond_width, 2 * width), (cond_width, width)]
    vectors = [(1, width), (1, width), (1, cond_width), (1, width)]
    return pl.pallas_call(
        functools.partial(outputs_kernel, width // heads, chunks),
        grid=(length // TOKENS,),
        in_specs=[block, block, cond_block] + [block] * 5 + [cond_block] * 2
        + [window] * (2 * chunks) + [turned] * (2 * chunks) + [whole(a) for a in fixed],
        out_specs=[block, block, cond_block] + [fixed_out(s) for s in weights + vectors],
        out_shape=[jax.ShapeDtypeStruct(acts.shape, BF16)] * 2
        + [jax.ShapeDtypeStruct(cond.shape, F32)]
        + [jax.ShapeDtypeStruct(s, BF16) for s in weights]
        + [jax.ShapeDtypeStruct(s, F32) for s in vectors],
        scratch_shapes=[pltpu.VMEM(s, F32) for s in weights],
        compiler_params=params(),
        cost_estimate=cost(2 * rows * width * width * 12, rows * width * 50),
        name="outputs",
    )(acts, cot, cond, first, gate, gated_grad, partial, acts_part, cond_gate, cond_norm,
      *mixeds, *dqs, *dkts, *dvts, *fixed)


def scatter_sum(parts, axis, count, order):
    bits = count.bit_length() - 1
    index = lax.axis_index(axis)
    held = [part.reshape((2,) * bits + part.shape[1:]) for part in parts]
    left = list(range(bits - 1, -1, -1))
    for bit in order:
        place = left.index(bit)
        left.remove(bit)
        mine = (index >> bit) & 1
        pairs = [(i, i ^ (1 << bit)) for i in range(count)]
        sent = [
            lax.ppermute(lax.dynamic_index_in_dim(part, 1 - mine, place, keepdims=False), axis, pairs)
            for part in held
        ]
        kept = [lax.dynamic_index_in_dim(part, mine, place, keepdims=False) for part in held]
        held = [(k.astype(F32) + s.astype(F32)).astype(k.dtype) for k, s in zip(kept, sent)]
    return held


def all_sum(parts, axis, count):
    for bit in range(count.bit_length() - 1):
        pairs = [(i, i ^ (1 << bit)) for i in range(count)]
        sent = [lax.ppermute(part, axis, pairs) for part in parts]
        parts = [(p.astype(F32) + s.astype(F32)).astype(p.dtype) for p, s in zip(parts, sent)]
    return parts


def body(
    struct_count, sample_devices,
    acts, cond, pair, lengths, token_mask, cond_gains, cond_w, cond_bias, output_gate_weights, zero_bias,
    qkvg_w, q_bias, out_w, swiglu_w, down_w, pair_gain, pair_w, cotangent,
):
    acts, cond, pair, cotangent = acts[0], cond[0], pair[0], cotangent[0]
    samples, length, width = acts.shape
    cond_width = cond.shape[1]
    heads = pair_w.shape[1]
    head_dim = width // heads
    chunks = heads // CHUNK_HEADS
    count = sample_devices
    share = length // count
    low_first = range(count.bit_length() - 1)
    position = lax.iota(jnp.int32, length)
    key_valid = (position < lengths[0]) & ((token_mask[0] == 1) | (position == 0))
    valid = key_valid.astype(F32)[None]
    gain_row = pair_gain[None]
    pair_wt = pair_w.T

    bias_rows = pair_forward(pair, gain_row, pair_wt, valid)
    bias = lax.all_gather(jnp.swapaxes(bias_rows, 0, 1), "sample", axis=0, tiled=False)
    split = share % 16 != 0
    if split:
        bias = jnp.swapaxes(bias, 0, 1).reshape(1, heads, length, length)

    gains = [cond_gains[None, b * cond_width : (b + 1) * cond_width] for b in range(2)]
    cond_ws = [cond_w[:, 2 * b * width : 2 * (b + 1) * width] for b in range(2)]
    cond_bs = [cond_bias[None, b * width : (b + 1) * width] for b in range(2)]
    zero_ws = [output_gate_weights[:, b * width : (b + 1) * width] for b in range(2)]
    zero_bs = [zero_bias[None, b * width : (b + 1) * width] for b in range(2)]

    first, gate, gated_grad, *rest = inputs_call(
        acts, cotangent, cond, gains[0], cond_ws[0], cond_bs[0], zero_ws[0], zero_bs[0],
        qkvg_w, q_bias[None], out_w.T, heads,
    )
    nats, turned = rest[:4], rest[4:]
    (partial, acts_part, cond_gate, cond_norm, swiglu_grad, down_grad, cond_w_one, zero_w_one,
     cond_b_one, zero_b_one, gain_one) = transition_call(
        acts, cotangent, cond, gains[1], cond_ws[1], cond_bs[1], zero_ws[1], zero_bs[1],
        swiglu_w, down_w,
    )

    def slabs(array):
        return array.reshape((count, array.shape[0] // count) + array.shape[1:])

    early = scatter_sum(
        [slabs(a) for a in (swiglu_grad, down_grad, cond_w_one, zero_w_one)], "sample", count, low_first
    )
    early = all_sum(early, "struct", struct_count)

    mixeds, dqs, dkts, dvts, bias_grads = [], [], [], [], []
    for chunk in range(chunks):
        mixed, dq, dkt, dvt, db = attention_call(chunk, nats, turned, bias, head_dim)
        mixeds.append(mixed)
        dqs.append(dq)
        dkts.append(dkt)
        dvts.append(dvt)
        if split:
            db = jnp.swapaxes(db.reshape(CHUNK_HEADS, count, share, length), 0, 1)
        bias_grads += scatter_sum([db], "sample", count, low_first)

    (block_out, acts_grad, cond_grad, qkvg_grad, out_grad, cond_w_zero, zero_w_zero,
     cond_b_zero, zero_b_zero, gain_zero, q_bias_grad) = outputs_call(
        acts, cotangent, cond, first, gate, gated_grad, partial, acts_part, cond_gate, cond_norm,
        mixeds, dqs, dkts, dvts,
        (gains[0], cond_ws[0], cond_bs[0], zero_ws[0], zero_bs[0], qkvg_w.T, out_w), heads,
    )
    late = scatter_sum(
        [slabs(a) for a in (qkvg_grad, out_grad, cond_w_zero, zero_w_zero)], "sample", count, low_first
    )
    late = all_sum(late, "struct", struct_count)
    (cond_grad,) = scatter_sum([slabs(cond_grad)], "sample", count, low_first)

    bias_grad = jnp.swapaxes(jnp.concatenate(bias_grads, axis=0), 0, 1)
    grad_pair, pair_w_grad, pair_gain_grad = pair_backward(pair, bias_grad, gain_row, pair_wt)
    vectors = [
        jnp.concatenate([gain_zero[0], gain_one[0]]),
        jnp.concatenate([cond_b_zero[0], cond_b_one[0]]),
        jnp.concatenate([zero_b_zero[0], zero_b_one[0]]),
        q_bias_grad[0],
        pair_gain_grad[0],
        pair_w_grad.T.reshape(-1),
    ]
    sizes = [v.shape[0] // count for v in vectors]
    packed = jnp.concatenate([v.reshape(count, -1) for v in vectors], axis=1)
    (packed,) = scatter_sum([packed], "sample", count, low_first)
    (packed,) = all_sum([packed], "struct", struct_count)
    small = []
    at = 0
    for size in sizes:
        small.append(packed[at : at + size])
        at += size
    wide = lambda array: array.astype(F32)
    return (
        block_out[None],
        acts_grad[None],
        cond_grad[None],
        grad_pair[None],
        small[0],
        wide(jnp.concatenate([late[2], early[2]], axis=1)),
        small[1],
        wide(jnp.concatenate([late[3], early[3]], axis=1)),
        small[2],
        wide(late[0]),
        small[3],
        wide(late[1]),
        wide(early[0]),
        wide(early[1]),
        small[4],
        small[5].reshape(-1, heads),
    )


def solution(mesh):
    per_struct = P("struct", "sample", None, None)
    in_specs = (
        (per_struct, P("struct", None, None), per_struct, P("struct"), P("struct", None))
        + (P(),) * 12
        + (per_struct,)
    )
    one, two = P("sample"), P("sample", None)
    out_specs = (
        per_struct, per_struct, P("struct", "sample", None), per_struct,
        one, two, one, two, one, two, one, two, two, two, one, two,
    )
    local = functools.partial(body, mesh.shape["struct"], mesh.shape["sample"])
    return jax.shard_map(local, mesh=mesh, in_specs=in_specs, out_specs=out_specs, check_vma=False)
```

time: 1720 us -> 861 us (0.50)
  matrix products: 579 us -> 0 us
  Pallas kernels: 0 us -> 297 us
  waiting for transfers between devices: 634 us -> 348 us
  other arithmetic: 182 us -> 37.3 us
  local copies, waits for them, and re-layouts: 226 us -> 89.6 us
  blocking collectives: 65.7 us -> 0 us
  starting transfers between devices: 1.45 us -> 63.3 us
    reduce_scatter x7 -> x0, waiting for transfers between devices: 553 us -> none  [the longest x1 363 us: body(): lax.psum_scatter(bias_grad_rows, 'sample', scatter_dimension=0, tiled=True)]
    dot_general x36 -> x0, matrix products: 512 us -> none  [the longest x15 160 us: matmul(): return jnp.dot(left_side, right_side, preferred_element_type=jnp.float32)]
    ppermute x0 -> x65, waiting for transfers between devices: none -> 348 us  [the longest x56 330 us: scatter_sum(): lax.ppermute(lax.dynamic_index_in_dim(part, 1 - mine, place, keepdims=Fal...]
    pallas_call x0 -> x9, Pallas kernels: none -> 297 us  [the longest x4 95.1 us: attention_call(): pl.pallas_call(functools.partial(attention_kernel, head_dim, chunk * CHUN...]
    reduce_sum x12 -> x0, other arithmetic: 73 us -> none  [the longest x2 42 us: attend_group(): row_totals = jnp.sum(shifted, axis=-1, keepdims=True)]
    dynamic_update_slice x4 -> x0, local copies, waits for them, and re-layouts: 67.4 us -> none  [body(): lax.map(attend_back, (group_ids, log_totals))]
    sub x2 -> x0, matrix products: 67 us -> none  [attend_back(): grad_probs - jnp.sum(probs_full * grad_probs, axis=-1, keepdims=True)]
    ppermute x0 -> x65, starting transfers between devices: none -> 63.3 us  [the longest x56 53 us: scatter_sum(): lax.ppermute(lax.dynamic_index_in_dim(part, 1 - mine, place, keepdims=Fal...]
  transfers between devices with their start and end apart: 10 -> 66, of which waited for: 5 -> 45; matrix products, arithmetic and copies ran while one was open for 56% -> 11% of each run, Pallas kernels for 0% -> 22%
where the time goes in v1:
time: 861 us; the launch traced here: 851 us
  waiting for transfers between devices  348 us (40%)
  Pallas kernels  297 us (34%)
  local copies, waits for them, and re-layouts  89.6 us (10%)
  starting transfers between devices  63.3 us (7%)
  other arithmetic  37.3 us (4%)
  between operations  16.3 us (2%)
    ppermute x56, waiting for transfers between devices, scatter_sum(): lax.ppermute(lax.dynamic_index_in_dim(part, 1 - mine, place, keepdims=Fal...  330 us
    pallas_call x4, Pallas kernels, attention_call(): pl.pallas_call(functools.partial(attention_kernel, head_dim, chunk * CHUN...  95.1 us
    pallas_call x1, Pallas kernels, transition_call(): pl.pallas_call(transition_kernel, grid=(length // TOKENS,), in_specs=[blo...  70.5 us
    pallas_call x1, Pallas kernels, outputs_call(): pl.pallas_call(functools.partial(outputs_kernel, width // heads, chunks),...  58 us
    ppermute x56, starting transfers between devices, scatter_sum(): lax.ppermute(lax.dynamic_index_in_dim(part, 1 - mine, place, keepdims=Fal...  53 us
    pallas_call x1, Pallas kernels, pair_backward(): pl.pallas_call(pair_backward_kernel, grid=(rows // PAIR_ROWS,), in_specs=...  36 us
    convert_element_type x48, other arithmetic, scatter_sum(): (k.astype(F32) + s.astype(F32)).astype(k.dtype)  23.3 us
    dynamic_slice x11, local copies, waits for them, and re-layouts, scatter_sum(): lax.dynamic_index_in_dim(part, mine, place, keepdims=False)  22.2 us
  transfers between devices with their start and end apart: 66, of which 45 were waited for; matrix products, arithmetic and copies ran while one was open for 11% of the time, Pallas kernels for 22%

profile of v1, /device:TPU:0, one launch (start us, length us, event | category | flops | bytes accessed | tf_op | source)
XLA Modules:
  0.0 851.4 jit_solution(10722134877691712825)
XLA Ops:
  9.1 16.9 %pair_forward.1 = bf16[48,16,768]{2,1,0:T(8,128)(2,1)} custom-call(bf16[48,768,128]{2,1,0:T(8,128)(2,1)} %bitcast.348, bf16[1,128]{1,0:T(2,128)(2,1)} %bitcast.386, bf16[16,128]{1,0:T(8,128)(2,1)} %bitcast.379, f32[1,768]{1,0:T(1,128)} %and_convert_fusion.valid_ref), custom_call_target="tpu_custom_call" | custom-call | flops 150994944 | bytes 10852761 | tf_op jit(solution)/shard_map/pair_forward/pallas_call | solution.py:89
  31.4 70.5 %transition.1 = (f32[2,768,768]{2,1,0:T(8,128)}, f32[2,768,768]{2,1,0:T(8,128)}, f32[768,384]{1,0:T(8,128)}, f32[768,384]{1,0:T(8,128)}, bf16[768,3072]{1,0:T(8,...) custom-call(bf16[2,768,768]{2,1,0:T(8,128)(2,1)} %bitcast.390, ...), custom_call_target="tpu_custom_call" | custom-call | flops 32614907904 | bytes 47185920 | tf_op jit(solution)/shard_map/transition/pallas_call | solution.py:325
  111.0 26.7 %collective-permute-done.61 = bf16[2,2,96,768]{3,2,0,1:T(8,128)(2,1)S(1)} collective-permute-done((bf16[2,2,96,768]{3,2,0,1:T(8,128)(2,1)S(1)}, bf16[2,2,96,768]{3,2,0,1:T(8,128)(2,1)S(1)}, u32[]{:S(2)}, u32[]{:S(2)}) %collective-permute-start.61) | collective-permute-done | bytes 589856 | tf_op jit(solution)/shard_map/ppermute | solution.py:549
  137.9 8.8 %collective-permute-done.62 = bf16[2,96,768]{2,1,0:T(8,128)(2,1)S(1)} collective-permute-done((bf16[2,96,768]{2,1,0:T(8,128)(2,1)S(1)}, bf16[2,96,768]{2,1,0:T(8,128)(2,1)S(1)}, u32[]{:S(2)}, u32[]{:S(2)}) %collective-permute-start.62) | collective-permute-done | bytes 294944 | tf_op jit(solution)/shard_map/ppermute | solution.py:549
  157.1 20.4 %inputs.1 = (bf16[2,768,768]{2,1,0:T(8,128)(2,1)}, f32[2,768,768]{2,1,0:T(8,128)}, f32[2,768,768]{2,1,0:T(8,128)}, bf16[4,2,768,256]{3,2,1,0:T(8,128)(2,1)}, bf1...) custom-call(bf16[2,768,768]{2,1,0:T(8,128)(2,1)} %bitcast.391, ...), custom_call_target="tpu_custom_call" | custom-call | flops 10871635968 | bytes 47185920 | tf_op jit(solution)/shard_map/inputs/pallas_call | solution.py:209
  177.6 6.6 copy.55
  187.0 19.8 %copy.54 = bf16[256,48,768]{2,1,0:T(8,128)(2,1)} copy(bf16[256,48,768]{2,0,1:T(8,128)(2,1)} %all-gather.3.cloned.1.call-done) | data formatting | bytes 37748736 | tf_op jit(solution)/shard_map/all_gather | solution.py:586
  206.9 23.6 %attention.7 = (f32[2,768,256]{2,1,0:T(8,128)}, f32[2,768,256]{2,1,0:T(8,128)}, bf16[2,192,768]{2,1,0:T(8,128)(2,1)}, bf16[2,192,768]{2,1,0:T(8,128)(2,1)}, bf16[16,4,48,768]{3,2,1,0:T(8,128)(2,1)}) custom-call(bf16[4,2,768,256]{3,2,1,0:T(8,128)(2,1)} %get-tuple-element.79.q_ref, bf16[4,2,768,256]{3,2,1,0:T(8,128)(2,1)} %get-tuple-element.80.k_ref, ...), custom_call_target="tpu_custom_call" | custom-call | flops 14495514624 | bytes 18874368 | tf_op jit(solution)/shard_map/attention/pallas_call | solution.py:396
  230.5 23.9 %attention.6 = (f32[2,768,256]{2,1,0:T(8,128)}, f32[2,768,256]{2,1,0:T(8,128)}, bf16[2,192,768]{2,1,0:T(8,128)(2,1)}, bf16[2,192,768]{2,1,0:T(8,128)(2,1)}, bf16[16,4,48,768]{3,2,1,0:T(8,128)(2,1)}) custom-call(bf16[4,2,768,256]{3,2,1,0:T(8,128)(2,1)} %get-tuple-element.79.q_ref, bf16[4,2,768,256]{3,2,1,0:T(8,128)(2,1)} %get-tuple-element.80.k_ref, ...), custom_call_target="tpu_custom_call" | custom-call | flops 14495514624 | bytes 18874368 | tf_op jit(solution)/shard_map/attention/pallas_call | solution.py:396
  254.4 23.7 %attention.5 = (f32[2,768,256]{2,1,0:T(8,128)}, f32[2,768,256]{2,1,0:T(8,128)}, bf16[2,192,768]{2,1,0:T(8,128)(2,1)}, bf16[2,192,768]{2,1,0:T(8,128)(2,1)}, bf16[16,4,48,768]{3,2,1,0:T(8,128)(2,1)}) custom-call(bf16[4,2,768,256]{3,2,1,0:T(8,128)(2,1)} %get-tuple-element.79.q_ref, bf16[4,2,768,256]{3,2,1,0:T(8,128)(2,1)} %get-tuple-element.80.k_ref, ...), custom_call_target="tpu_custom_call" | custom-call | flops 14495514624 | bytes 18874368 | tf_op jit(solution)/shard_map/attention/pallas_call | solution.py:396
  278.0 23.9 %attention.4 = (f32[2,768,256]{2,1,0:T(8,128)}, f32[2,768,256]{2,1,0:T(8,128)}, bf16[2,192,768]{2,1,0:T(8,128)(2,1)}, bf16[2,192,768]{2,1,0:T(8,128)(2,1)}, bf16[16,4,48,768]{3,2,1,0:T(8,128)(2,1)}) custom-call(bf16[4,2,768,256]{3,2,1,0:T(8,128)(2,1)} %get-tuple-element.79.q_ref, bf16[4,2,768,256]{3,2,1,0:T(8,128)(2,1)} %get-tuple-element.80.k_ref, ...), custom_call_target="tpu_custom_call" | custom-call | flops 14495514624 | bytes 18874368 | tf_op jit(solution)/shard_map/attention/pallas_call | solution.py:396
  301.9 6.0 constant_dynamic-slice_fusion.25
  313.8 58.0 %outputs.1 = (bf16[2,768,768]{2,1,0:T(8,128)(2,1)}, bf16[2,768,768]{2,1,0:T(8,128)(2,1)}, f32[768,384]{1,0:T(8,128)}, bf16[768,3072]{1,0:T(8,128)(2,1)}, bf16[76...) custom-call(bf16[2,768,768]{2,1,0:T(8,128)(2,1)} %bitcast.392, ...), custom_call_target="tpu_custom_call" | custom-call | flops 21743271936 | bytes 58982400 | tf_op jit(solution)/shard_map/outputs/pallas_call | solution.py:520
  384.8 4.9 constant_dynamic-slice_fusion.3
  393.1 6.9 constant_dynamic-slice_fusion.29
  452.1 6.9 collective-permute-done.26
  460.5 4.8 collective-permute-done.31
  506.2 5.6 collective-permute-done.33
  511.8 5.6 collective-permute-done.3
  556.7 13.2 %collective-permute-done.13 = bf16[2,2,4,48,768]{4,2,3,0,1:T(4,128)(2,1)S(1)} collective-permute-done((bf16[2,2,4,48,768]{4,2,3,0,1:T(4,128)(2,1)S(1)}, bf16[2,2,4,48,768]{4,2,3,0,1:T(4,128)(2,1)S(1)}, u32[]{:S(2)}, u32[]{:S(2)}) %collective-permute-start.13) | collective-permute-done | bytes 1179680 | tf_op jit(solution)/shard_map/ppermute | solution.py:549
  572.2 23.0 %collective-permute-done.17 = bf16[2,2,4,48,768]{4,2,3,0,1:T(4,128)(2,1)S(1)} collective-permute-done((bf16[2,2,4,48,768]{4,2,3,0,1:T(4,128)(2,1)S(1)}, bf16[2,2,4,48,768]{4,2,3,0,1:T(4,128)(2,1)S(1)}, u32[]{:S(2)}, u32[]{:S(2)}) %collective-permute-start.17) | collective-permute-done | bytes 1179680 | tf_op jit(solution)/shard_map/ppermute | solution.py:549
  596.1 24.5 %collective-permute-done.46 = bf16[2,2,48,3072]{3,2,0,1:T(8,128)(2,1)} collective-permute-done((bf16[2,2,48,3072]{3,2,0,1:T(8,128)(2,1)S(1)}, bf16[2,2,48,3072]{3,2,0,1:T(8,128)(2,1)}, u32[]{:S(2)}, u32[]{:S(2)}) %collective-permute-start.46) | collective-permute-done | bytes 1179680 | tf_op jit(solution)/shard_map/ppermute | solution.py:549
  622.4 23.4 %collective-permute-done.56 = bf16[2,2,48,3072]{3,2,0,1:T(8,128)(2,1)S(1)} collective-permute-done((bf16[2,2,48,3072]{3,2,0,1:T(8,128)(2,1)S(1)}, bf16[2,2,48,3072]{3,2,0,1:T(8,128)(2,1)S(1)}, u32[]{:S(2)}, u32[]{:S(2)}) %collective-permute-start.56) | collective-permute-done | bytes 1179680 | tf_op jit(solution)/shard_map/ppermute | solution.py:549
  646.3 24.8 %collective-permute-done.5 = bf16[2,2,4,48,768]{4,2,3,0,1:T(4,128)(2,1)S(1)} collective-permute-done((bf16[2,2,4,48,768]{4,2,3,0,1:T(4,128)(2,1)S(1)}, bf16[2,2,4,48,768]{4,2,3,0,1:T(4,128)(2,1)S(1)}, u32[]{:S(2)}, u32[]{:S(2)}) %collective-permute-start.5) | collective-permute-done | bytes 1179680 | tf_op jit(solution)/shard_map/ppermute | solution.py:549
  672.2 23.2 %collective-permute-done.9 = bf16[2,2,4,48,768]{4,2,3,0,1:T(4,128)(2,1)S(1)} collective-permute-done((bf16[2,2,4,48,768]{4,2,3,0,1:T(4,128)(2,1)S(1)}, bf16[2,2,4,48,768]{4,2,3,0,1:T(4,128)(2,1)S(1)}, u32[]{:S(2)}, u32[]{:S(2)}) %collective-permute-start.9) | collective-permute-done | bytes 1179680 | tf_op jit(solution)/shard_map/ppermute | solution.py:549
  699.6 21.5 %collective-permute-done.6 = bf16[2,4,48,768]{3,1,2,0:T(4,128)(2,1)S(1)} collective-permute-done((bf16[2,4,48,768]{3,1,2,0:T(4,128)(2,1)S(1)}, bf16[2,4,48,768]{3,1,2,0:T(4,128)(2,1)S(1)}, u32[]{:S(2)}, u32[]{:S(2)}) %collective-permute-start.6) | collective-permute-done | bytes 589856 | tf_op jit(solution)/shard_map/ppermute | solution.py:549
  721.5 10.5 %collective-permute-done.10 = bf16[2,4,48,768]{3,1,2,0:T(4,128)(2,1)S(1)} collective-permute-done((bf16[2,4,48,768]{3,1,2,0:T(4,128)(2,1)S(1)}, bf16[2,4,48,768]{3,1,2,0:T(4,128)(2,1)S(1)}, u32[]{:S(2)}, u32[]{:S(2)}) %collective-permute-start.10) | collective-permute-done | bytes 589856 | tf_op jit(solution)/shard_map/ppermute | solution.py:549
  735.8 18.2 %collective-permute-done.19 = bf16[4,48,768]{2,0,1:T(4,128)(2,1)S(1)} collective-permute-done((bf16[4,48,768]{2,0,1:T(4,128)(2,1)S(1)}, bf16[4,48,768]{2,0,1:T(4,128)(2,1)S(1)}, u32[]{:S(2)}, u32[]{:S(2)}) %collective-permute-start.19) | collective-permute-done | bytes 294944 | tf_op jit(solution)/shard_map/ppermute | solution.py:549
  754.1 6.2 collective-permute-done.7
  765.5 36.0 %pair_backward.1 = (f32[48,768,128]{2,1,0:T(8,128)}, f32[16,128]{1,0:T(8,128)}, f32[1,128]{1,0:T(1,128)}) custom-call(bf16[48,768,128]{2,1,0:T(8,128)(2,1)} %bitcast.349, bf16[48,16,768]{2,1,0:T(8,128)(2,1)} %maximum_bitcast_fusion.grad_ref, bf16[1,128]{1,0:T(2,128)(2,1)} %bitcast.387, bf16[16,128]{1,0:T(8,128)(2,1)} %bitcast.380), custom_call_target="tpu_custom_call" | custom-call | flops 301989888 | bytes 29727128 | tf_op jit(solution)/shard_map/pair_backward/pallas_call | solution.py:130
  815.4 11.7 %collective-permute-done.48 = bf16[48,3072]{1,0:T(8,128)(2,1)S(1)} collective-permute-done((bf16[48,3072]{1,0:T(8,128)(2,1)S(1)}, bf16[48,3072]{1,0:T(8,128)(2,1)S(1)}, u32[]{:S(2)}, u32[]{:S(2)}) %collective-permute-start.48) | collective-permute-done | bytes 294944 | tf_op jit(solution)/shard_map/ppermute | solution.py:549
  828.2 5.3 collective-permute-done.23
  (349 shorter events, 230.0 us)
Async XLA Ops:
  7.2 179.8 %all-gather.3.cloned.1.call-start = ((), (), s32[]{:S(2)}) async-start(), calls=%async_computation | async-start | bytes 20054016 | tf_op jit(solution)/shard_map/all_gather | solution.py:586
  107.6 30.1 %collective-permute-start.61 = (bf16[2,2,96,768]{3,2,0,1:T(8,128)(2,1)S(1)}, bf16[2,2,96,768]{3,2,0,1:T(8,128)(2,1)S(1)}, u32[]{:S(2)}, u32[]{:S(2)}) collective-permute-start(bf16[2,2,96,768]{3,2,0,1:T(8,128)(2,1)S(1)} %dynamic-slice_bitcast_fusion.6), channel_id=1, source_target_pairs={{0,2},{1,3},{2,0},{3,1},{4,6},{5,7},{6,4},{7,5},{8,10},{9,11},{10,... | collective-permute-start | bytes 1769480 | tf_op jit(solution)/shard_map/ppermute | solution.py:549
  155.8 30.5 %collective-permute-start.64 = (bf16[96,768]{1,0:T(8,128)(2,1)S(1)}, bf16[96,768]{1,0:T(8,128)(2,1)S(1)}, u32[]{:S(2)}, u32[]{:S(2)}) collective-permute-start(bf16[96,768]{1,0:T(8,128)(2,1)S(1)} %fusion.37), channel_id=1, source_target_pairs={{0,16},{16,0},{1,17},{17,1},{2,18},{18,2},{3,19},{19,3},{4,20},{20... | collective-permute-start | bytes 442376 | tf_op jit(solution)/shard_map/ppermute | solution.py:560
  313.3 223.3 %collective-permute-start.12 = (bf16[2,2,2,4,48,768]{5,3,4,0,1,2:T(4,128)(2,1)}, bf16[2,2,2,4,48,768]{5,3,4,0,1,2:T(4,128)(2,1)}, u32[]{:S(2)}, u32[]{:S(2)}) collective-permute-start(bf16[2,2,2,4,48,768]{5,3,4,0,1,2:T(4,128)(2,1)} %bitcast.334), channel_id=1, source_target_pairs={{0,1},{1,0},{2,3},{3,2},{4,5},{5,4},{6,7},{7,6},{8,9},{9,8},{10,11... | collective-permute-start | bytes 7077896 | tf_op jit(solution)/shard_map/ppermute | solution.py:549
  313.3 227.8 %collective-permute-start.16 = (bf16[2,2,2,4,48,768]{5,3,4,0,1,2:T(4,128)(2,1)}, bf16[2,2,2,4,48,768]{5,3,4,0,1,2:T(4,128)(2,1)}, u32[]{:S(2)}, u32[]{:S(2)}) collective-permute-start(bf16[2,2,2,4,48,768]{5,3,4,0,1,2:T(4,128)(2,1)} %bitcast.333), channel_id=1, source_target_pairs={{0,1},{1,0},{2,3},{3,2},{4,5},{5,4},{6,7},{7,6},{8,9},{9,8},{10,11... | collective-permute-start | bytes 7077896 | tf_op jit(solution)/shard_map/ppermute | solution.py:549
  380.5 26.5 %collective-permute-start.35 = (bf16[2,2,2,24,768]{4,3,0,1,2:T(8,128)(2,1)}, bf16[2,2,2,24,768]{4,3,0,1,2:T(8,128)(2,1)S(1)}, u32[]{:S(2)}, u32[]{:S(2)}) collective-permute-start(bf16[2,2,2,24,768]{4,3,0,1,2:T(8,128)(2,1)} %bitcast.343), channel_id=1, source_target_pairs={{0,1},{1,0},{2,3},{3,2},{4,5},{5,4},{6,7},{7,6},{8,9},{9,8},{10,11... | collective-permute-start | bytes 884744 | tf_op jit(solution)/shard_map/ppermute | solution.py:549
  380.5 28.3 %collective-permute-start.40 = (bf16[2,2,2,24,768]{4,3,0,1,2:T(8,128)(2,1)}, bf16[2,2,2,24,768]{4,3,0,1,2:T(8,128)(2,1)}, u32[]{:S(2)}, u32[]{:S(2)}) collective-permute-start(bf16[2,2,2,24,768]{4,3,0,1,2:T(8,128)(2,1)} %bitcast.342), channel_id=1, source_target_pairs={{0,1},{1,0},{2,3},{3,2},{4,5},{5,4},{6,7},{7,6},{8,9},{9,8},{10,11... | collective-permute-start | bytes 884744 | tf_op jit(solution)/shard_map/ppermute | solution.py:549
  382.9 56.1 %collective-permute-start.25 = (bf16[2,2,2,24,1536]{4,3,0,1,2:T(8,128)(2,1)}, bf16[2,2,2,24,1536]{4,3,0,1,2:T(8,128)(2,1)}, u32[]{:S(2)}, u32[]{:S(2)}) collective-permute-start(bf16[2,2,2,24,1536]{4,3,0,1,2:T(8,128)(2,1)} %bitcast.340), channel_id=1, source_target_pairs={{0,1},{1,0},{2,3},{3,2},{4,5},{5,4},{6,7},{7,6},{8,9},{9,8},{10,11... | collective-permute-start | bytes 1769480 | tf_op jit(solution)/shard_map/ppermute | solution.py:549
  407.0 33.8 %collective-permute-start.30 = (bf16[2,2,2,24,1536]{4,3,0,1,2:T(8,128)(2,1)S(1)}, bf16[2,2,2,24,1536]{4,3,0,1,2:T(8,128)(2,1)S(1)}, u32[]{:S(2)}, u32[]{:S(2)}) collective-permute-start(bf16[2,2,2,24,1536]{4,3,0,1,2:T(8,128)(2,1)S(1)} %bitcast.372), channel_id=1, source_target_pairs={{0,1},{1,0},{2,3},{3,2},{4,5},{5,4},{6,7},{7,6},{8,9},{9,8},{10,11... | collective-permute-start | bytes 1769480 | tf_op jit(solution)/shard_map/ppermute | solution.py:549
  440.8 105.5 %collective-permute-start.45 = (bf16[2,2,2,48,3072]{4,3,0,1,2:T(8,128)(2,1)S(1)}, bf16[2,2,2,48,3072]{4,3,0,1,2:T(8,128)(2,1)S(1)}, u32[]{:S(2)}, u32[]{:S(2)}) collective-permute-start(bf16[2,2,2,48,3072]{4,3,0,1,2:T(8,128)(2,1)S(1)} %bitcast.364), channel_id=1, source_target_pairs={{0,1},{1,0},{2,3},{3,2},{4,5},{5,4},{6,7},{7,6},{8,9},{9,8},{10,11... | collective-permute-start | bytes 7077896 | tf_op jit(solution)/shard_map/ppermute | solution.py:549
  450.5 14.8 %collective-permute-start.31 = (bf16[2,2,24,1536]{3,2,0,1:T(8,128)(2,1)S(1)}, bf16[2,2,24,1536]{3,2,0,1:T(8,128)(2,1)S(1)}, u32[]{:S(2)}, u32[]{:S(2)}) collective-permute-start(bf16[2,2,24,1536]{3,2,0,1:T(8,128)(2,1)S(1)} %dynamic-slice_bitcast_fusion.17), channel_id=1, source_target_pairs={{0,2},{1,3},{2,0},{3,1},{4,6},{5,7},{6,4},{7,5},{8,10},{9,11},{10,... | collective-permute-start | bytes 884744 | tf_op jit(solution)/shard_map/ppermute | solution.py:549
  471.7 76.3 %collective-permute-start.55 = (bf16[2,2,2,48,3072]{4,3,0,1,2:T(8,128)(2,1)}, bf16[2,2,2,48,3072]{4,3,0,1,2:T(8,128)(2,1)S(1)}, u32[]{:S(2)}, u32[]{:S(2)}) collective-permute-start(bf16[2,2,2,48,3072]{4,3,0,1,2:T(8,128)(2,1)} %bitcast.331), channel_id=1, source_target_pairs={{0,1},{1,0},{2,3},{3,2},{4,5},{5,4},{6,7},{7,6},{8,9},{9,8},{10,11... | collective-permute-start | bytes 7077896 | tf_op jit(solution)/shard_map/ppermute | solution.py:549
  536.6 16.6 %collective-permute-start.8 = (bf16[2,2,2,4,48,768]{5,3,4,0,1,2:T(4,128)(2,1)S(1)}, bf16[2,2,2,4,48,768]{5,3,4,0,1,2:T(4,128)(2,1)S(1)}, u32[]{:S(2)}, u32[]{:S(2)}) collective-permute-start(bf16[2,2,2,4,48,768]{5,3,4,0,1,2:T(4,128)(2,1)S(1)} %bitcast.363), channel_id=1, source_target_pairs={{0,1},{1,0},{2,3},{3,2},{4,5},{5,4},{6,7},{7,6},{8,9},{9,8},{10,11... | collective-permute-start | bytes 7077896 | tf_op jit(solution)/shard_map/ppermute | solution.py:549
  541.1 28.9 %collective-permute-start.13 = (bf16[2,2,4,48,768]{4,2,3,0,1:T(4,128)(2,1)S(1)}, bf16[2,2,4,48,768]{4,2,3,0,1:T(4,128)(2,1)S(1)}, u32[]{:S(2)}, u32[]{:S(2)}) collective-permute-start(bf16[2,2,4,48,768]{4,2,3,0,1:T(4,128)(2,1)S(1)} %dynamic-slice_bitcast_fusion.3), channel_id=1, source_target_pairs={{0,2},{1,3},{2,0},{3,1},{4,6},{5,7},{6,4},{7,5},{8,10},{9,11},{10,... | collective-permute-start | bytes 3538952 | tf_op jit(solution)/shard_map/ppermute | solution.py:549
  546.3 49.0 %collective-permute-start.17 = (bf16[2,2,4,48,768]{4,2,3,0,1:T(4,128)(2,1)S(1)}, bf16[2,2,4,48,768]{4,2,3,0,1:T(4,128)(2,1)S(1)}, u32[]{:S(2)}, u32[]{:S(2)}) collective-permute-start(bf16[2,2,4,48,768]{4,2,3,0,1:T(4,128)(2,1)S(1)} %dynamic-slice_bitcast_fusion.2), channel_id=1, source_target_pairs={{0,2},{1,3},{2,0},{3,1},{4,6},{5,7},{6,4},{7,5},{8,10},{9,11},{10,... | collective-permute-start | bytes 3538952 | tf_op jit(solution)/shard_map/ppermute | solution.py:549
  548.0 72.7 %collective-permute-start.46 = (bf16[2,2,48,3072]{3,2,0,1:T(8,128)(2,1)S(1)}, bf16[2,2,48,3072]{3,2,0,1:T(8,128)(2,1)}, u32[]{:S(2)}, u32[]{:S(2)}) collective-permute-start(bf16[2,2,48,3072]{3,2,0,1:T(8,128)(2,1)S(1)} %dynamic-slice_bitcast_fusion.1), channel_id=1, source_target_pairs={{0,2},{1,3},{2,0},{3,1},{4,6},{5,7},{6,4},{7,5},{8,10},{9,11},{10,... | collective-permute-start | bytes 3538952 | tf_op jit(solution)/shard_map/ppermute | solution.py:549
  550.4 95.4 %collective-permute-start.56 = (bf16[2,2,48,3072]{3,2,0,1:T(8,128)(2,1)S(1)}, bf16[2,2,48,3072]{3,2,0,1:T(8,128)(2,1)S(1)}, u32[]{:S(2)}, u32[]{:S(2)}) collective-permute-start(bf16[2,2,48,3072]{3,2,0,1:T(8,128)(2,1)S(1)} %dynamic-slice_bitcast_fusion), channel_id=1, source_target_pairs={{0,2},{1,3},{2,0},{3,1},{4,6},{5,7},{6,4},{7,5},{8,10},{9,11},{10,... | collective-permute-start | bytes 3538952 | tf_op jit(solution)/shard_map/ppermute | solution.py:549
  553.2 117.9 %collective-permute-start.5 = (bf16[2,2,4,48,768]{4,2,3,0,1:T(4,128)(2,1)S(1)}, bf16[2,2,4,48,768]{4,2,3,0,1:T(4,128)(2,1)S(1)}, u32[]{:S(2)}, u32[]{:S(2)}) collective-permute-start(bf16[2,2,4,48,768]{4,2,3,0,1:T(4,128)(2,1)S(1)} %dynamic-slice_bitcast_fusion.5), channel_id=1, source_target_pairs={{0,2},{1,3},{2,0},{3,1},{4,6},{5,7},{6,4},{7,5},{8,10},{9,11},{10,... | collective-permute-start | bytes 3538952 | tf_op jit(solution)/shard_map/ppermute | solution.py:549
  570.0 125.4 %collective-permute-start.9 = (bf16[2,2,4,48,768]{4,2,3,0,1:T(4,128)(2,1)S(1)}, bf16[2,2,4,48,768]{4,2,3,0,1:T(4,128)(2,1)S(1)}, u32[]{:S(2)}, u32[]{:S(2)}) collective-permute-start(bf16[2,2,4,48,768]{4,2,3,0,1:T(4,128)(2,1)S(1)} %dynamic-slice_bitcast_fusion.4), channel_id=1, source_target_pairs={{0,2},{1,3},{2,0},{3,1},{4,6},{5,7},{6,4},{7,5},{8,10},{9,11},{10,... | collective-permute-start | bytes 3538952 | tf_op jit(solution)/shard_map/ppermute | solution.py:549
  595.2 101.0 %collective-permute-start.14 = (bf16[2,4,48,768]{3,1,2,0:T(4,128)(2,1)S(1)}, bf16[2,4,48,768]{3,1,2,0:T(4,128)(2,1)S(1)}, u32[]{:S(2)}, u32[]{:S(2)}) collective-permute-start(bf16[2,4,48,768]{3,1,2,0:T(4,128)(2,1)S(1)} %dynamic-slice_bitcast_fusion.10), channel_id=1, source_target_pairs={{0,4},{1,5},{2,6},{3,7},{4,0},{5,1},{6,2},{7,3},{8,12},{9,13},{10,... | collective-permute-start | bytes 1769480 | tf_op jit(solution)/shard_map/ppermute | solution.py:549
  620.6 78.2 %collective-permute-start.18 = (bf16[2,4,48,768]{3,1,2,0:T(4,128)(2,1)S(1)}, bf16[2,4,48,768]{3,1,2,0:T(4,128)(2,1)S(1)}, u32[]{:S(2)}, u32[]{:S(2)}) collective-permute-start(bf16[2,4,48,768]{3,1,2,0:T(4,128)(2,1)S(1)} %dynamic-slice_bitcast_fusion.9), channel_id=1, source_target_pairs={{0,4},{1,5},{2,6},{3,7},{4,0},{5,1},{6,2},{7,3},{8,12},{9,13},{10,... | collective-permute-start | bytes 1769480 | tf_op jit(solution)/shard_map/ppermute | solution.py:549
  645.8 86.7 %collective-permute-start.47 = (bf16[2,48,3072]{2,1,0:T(8,128)(2,1)S(1)}, bf16[2,48,3072]{2,1,0:T(8,128)(2,1)S(1)}, u32[]{:S(2)}, u32[]{:S(2)}) collective-permute-start(bf16[2,48,3072]{2,1,0:T(8,128)(2,1)S(1)} %dynamic-slice_bitcast_fusion.8), channel_id=1, source_target_pairs={{0,4},{1,5},{2,6},{3,7},{4,0},{5,1},{6,2},{7,3},{8,12},{9,13},{10,... | collective-permute-start | bytes 1769480 | tf_op jit(solution)/shard_map/ppermute | solution.py:549
  671.1 136.3 %collective-permute-start.57 = (bf16[2,48,3072]{2,1,0:T(8,128)(2,1)S(1)}, bf16[2,48,3072]{2,1,0:T(8,128)(2,1)S(1)}, u32[]{:S(2)}, u32[]{:S(2)}) collective-permute-start(bf16[2,48,3072]{2,1,0:T(8,128)(2,1)S(1)} %dynamic-slice_bitcast_fusion.7), channel_id=1, source_target_pairs={{0,4},{1,5},{2,6},{3,7},{4,0},{5,1},{6,2},{7,3},{8,12},{9,13},{10,... | collective-permute-start | bytes 1769480 | tf_op jit(solution)/shard_map/ppermute | solution.py:549
  695.4 25.7 %collective-permute-start.6 = (bf16[2,4,48,768]{3,1,2,0:T(4,128)(2,1)S(1)}, bf16[2,4,48,768]{3,1,2,0:T(4,128)(2,1)S(1)}, u32[]{:S(2)}, u32[]{:S(2)}) collective-permute-start(bf16[2,4,48,768]{3,1,2,0:T(4,128)(2,1)S(1)} %dynamic-slice_bitcast_fusion.12), channel_id=1, source_target_pairs={{0,4},{1,5},{2,6},{3,7},{4,0},{5,1},{6,2},{7,3},{8,12},{9,13},{10,... | collective-permute-start | bytes 1769480 | tf_op jit(solution)/shard_map/ppermute | solution.py:549
  696.3 35.8 %collective-permute-start.10 = (bf16[2,4,48,768]{3,1,2,0:T(4,128)(2,1)S(1)}, bf16[2,4,48,768]{3,1,2,0:T(4,128)(2,1)S(1)}, u32[]{:S(2)}, u32[]{:S(2)}) collective-permute-start(bf16[2,4,48,768]{3,1,2,0:T(4,128)(2,1)S(1)} %dynamic-slice_bitcast_fusion.11), channel_id=1, source_target_pairs={{0,4},{1,5},{2,6},{3,7},{4,0},{5,1},{6,2},{7,3},{8,12},{9,13},{10,... | collective-permute-start | bytes 1769480 | tf_op jit(solution)/shard_map/ppermute | solution.py:549
  698.8 36.8 %collective-permute-start.15 = (bf16[4,48,768]{2,0,1:T(4,128)(2,1)S(1)}, bf16[4,48,768]{2,0,1:T(4,128)(2,1)S(1)}, u32[]{:S(2)}, u32[]{:S(2)}) collective-permute-start(bf16[4,48,768]{2,0,1:T(4,128)(2,1)S(1)} %dynamic-slice_bitcast_fusion.20), channel_id=1, source_target_pairs={{0,8},{1,9},{2,10},{3,11},{4,12},{5,13},{6,14},{7,15},{8,0},{9,1},... | collective-permute-start | bytes 884744 | tf_op jit(solution)/shard_map/ppermute | solution.py:549
  721.1 32.9 %collective-permute-start.19 = (bf16[4,48,768]{2,0,1:T(4,128)(2,1)S(1)}, bf16[4,48,768]{2,0,1:T(4,128)(2,1)S(1)}, u32[]{:S(2)}, u32[]{:S(2)}) collective-permute-start(bf16[4,48,768]{2,0,1:T(4,128)(2,1)S(1)} %dynamic-slice_bitcast_fusion.19), channel_id=1, source_target_pairs={{0,8},{1,9},{2,10},{3,11},{4,12},{5,13},{6,14},{7,15},{8,0},{9,1},... | collective-permute-start | bytes 884744 | tf_op jit(solution)/shard_map/ppermute | solution.py:549
  732.0 28.3 %collective-permute-start.7 = (bf16[4,48,768]{2,0,1:T(4,128)(2,1)S(1)}, bf16[4,48,768]{2,0,1:T(4,128)(2,1)S(1)}, u32[]{:S(2)}, u32[]{:S(2)}) collective-permute-start(bf16[4,48,768]{2,0,1:T(4,128)(2,1)S(1)} %dynamic-slice_bitcast_fusion.22), channel_id=1, source_target_pairs={{0,8},{1,9},{2,10},{3,11},{4,12},{5,13},{6,14},{7,15},{8,0},{9,1},... | collective-permute-start | bytes 884744 | tf_op jit(solution)/shard_map/ppermute | solution.py:549
  732.5 31.1 %collective-permute-start.11 = (bf16[4,48,768]{2,0,1:T(4,128)(2,1)S(1)}, bf16[4,48,768]{2,0,1:T(4,128)(2,1)S(1)}, u32[]{:S(2)}, u32[]{:S(2)}) collective-permute-start(bf16[4,48,768]{2,0,1:T(4,128)(2,1)S(1)} %dynamic-slice_bitcast_fusion.21), channel_id=1, source_target_pairs={{0,8},{1,9},{2,10},{3,11},{4,12},{5,13},{6,14},{7,15},{8,0},{9,1},... | collective-permute-start | bytes 884744 | tf_op jit(solution)/shard_map/ppermute | solution.py:549
  804.7 22.5 %collective-permute-start.48 = (bf16[48,3072]{1,0:T(8,128)(2,1)S(1)}, bf16[48,3072]{1,0:T(8,128)(2,1)S(1)}, u32[]{:S(2)}, u32[]{:S(2)}) collective-permute-start(bf16[48,3072]{1,0:T(8,128)(2,1)S(1)} %dynamic-slice_bitcast_fusion.16), channel_id=1, source_target_pairs={{0,8},{1,9},{2,10},{3,11},{4,12},{5,13},{6,14},{7,15},{8,0},{9,1},... | collective-permute-start | bytes 884744 | tf_op jit(solution)/shard_map/ppermute | solution.py:549
  811.3 23.1 %collective-permute-start.58 = (bf16[48,3072]{1,0:T(8,128)(2,1)S(1)}, bf16[48,3072]{1,0:T(8,128)(2,1)S(1)}, u32[]{:S(2)}, u32[]{:S(2)}) collective-permute-start(bf16[48,3072]{1,0:T(8,128)(2,1)S(1)} %dynamic-slice_bitcast_fusion.14), channel_id=1, source_target_pairs={{0,8},{1,9},{2,10},{3,11},{4,12},{5,13},{6,14},{7,15},{8,0},{9,1},... | collective-permute-start | bytes 884744 | tf_op jit(solution)/shard_map/ppermute | solution.py:549
  813.3 20.2 %collective-permute-start.23 = (f32[424]{0:T(512)S(1)}, f32[424]{0:T(512)S(1)}, u32[]{:S(2)}, u32[]{:S(2)}) collective-permute-start(f32[424]{0:T(512)S(1)} %bitcast.388), channel_id=1, source_target_pairs={{0,8},{1,9},{2,10},{3,11},{4,12},{5,13},{6,14},{7,15},{8,0},{9,1},... | collective-permute-start | bytes 5096 | tf_op jit(solution)/shard_map/ppermute | solution.py:549
  (64 other events, 672.2 us)
Sparse Core Ops, SparseCore 0:
  26.2 114.0 all-gather.2

commit v2 on v1

v2 whole, which is shorter than its diff:
```python
import functools

import jax
import jax.numpy as jnp
from jax import lax
from jax.experimental import pallas as pl
from jax.experimental.pallas import tpu as pltpu
from jax.sharding import PartitionSpec as P

EPS = 1e-05
MASKED = -1000000000.0
F32 = jnp.float32
BF16 = jnp.bfloat16
CHUNK_HEADS = 4
WINDOW = 256
LANES = 128
PIECE = 384
TOKENS = 128
HIDDEN = 768
VMEM_LIMIT = 60 * 2**20


def dot(left, right, left_dim=1, right_dim=0):
    return lax.dot_general(
        left, right, (((left_dim,), (right_dim,)), ((), ())), preferred_element_type=F32
    )


def layer_norm(values):
    center = values - jnp.mean(values, axis=-1, keepdims=True)
    inverse = lax.rsqrt(jnp.mean(center * center, axis=-1, keepdims=True) + EPS)
    return (center * inverse, inverse)


def norm_back(grad_in, normed, inverse):
    mean_grad = jnp.mean(grad_in, axis=-1, keepdims=True)
    mean_proj = jnp.mean(grad_in * normed, axis=-1, keepdims=True)
    return inverse * (grad_in - mean_grad - normed * mean_proj)


def slope(gate):
    return gate * (1.0 - gate)


def column_sum(values):
    return jnp.sum(values.reshape(-1, values.shape[-1]), axis=0, keepdims=True)


def clear(step, *refs):
    @pl.when(step == 0)
    def _():
        for ref in refs:
            ref[...] = jnp.zeros_like(ref)


def spec(block, along=None, at=None):
    rank = len(block)
    if along is not None:
        return pl.BlockSpec(block, lambda t: tuple(t if a == along else 0 for a in range(rank)))
    index = (0,) * rank if at is None else at
    return pl.BlockSpec(block, lambda t: index, pipeline_mode=pl.Buffered(1))


class Order:
    def __init__(self):
        self.zero = 0


def call(name, kernel, grid, ins, outs, scratch, deps, order):
    inputs = len(ins)
    results = len(outs)

    def run(*refs):
        given, rest = refs[:inputs], refs[inputs + len(deps) :]
        rest[results][0] = 0
        kernel(*given, *rest[:results], *rest[results + 1 :])

    *found, zero = pl.pallas_call(
        run,
        grid=(grid,),
        in_specs=[s for _, s in ins] + [pl.BlockSpec(memory_space=pl.ANY)] * len(deps),
        out_specs=[s for _, _, s in outs] + [pl.BlockSpec(memory_space=pltpu.SMEM)],
        out_shape=[jax.ShapeDtypeStruct(shape, dtype) for shape, dtype, _ in outs]
        + [jax.ShapeDtypeStruct((1,), jnp.int32)],
        scratch_shapes=scratch,
        compiler_params=pltpu.CompilerParams(
            vmem_limit_bytes=VMEM_LIMIT, dimension_semantics=("arbitrary",)
        ),
        cost_estimate=pl.CostEstimate(flops=10**11, bytes_accessed=10**6, transcendentals=0),
        name=name,
    )(*[a for a, _ in ins], *deps)
    order.zero = zero[0]
    return found


def tick(deps, order):
    def kernel(out_ref):
        out_ref[0] = 1

    call("tick", kernel, 1, [], [((1,), jnp.int32, pl.BlockSpec(memory_space=pltpu.SMEM))], [], deps, order)


class Halving:
    def __init__(self, order, counts):
        self.order = order
        self.counts = counts

    def places(self):
        found = []
        for p in range(2 ** len(self.order)):
            dest, half = 0, 0
            for i, (axis, bit) in enumerate(self.order):
                value = (p >> (len(self.order) - 1 - i)) & 1
                if axis == "sample":
                    dest |= value << bit
                else:
                    half = value
            found.append((dest, half))
        return found

    def halves(self):
        return 2 if any(axis == "struct" for axis, _ in self.order) else 1

    def pieces(self, shape):
        rows, columns = shape
        return rows // self.counts["sample"], columns // self.halves() // PIECE

    def slabs(self, shapes):
        return (2 ** len(self.order), sum(r * c for r, c in map(self.pieces, shapes)), PIECE)

    def pack(self, out_ref, arrays):
        for p, (dest, half) in enumerate(self.places()):
            held = []
            for array in arrays:
                rows, count = self.pieces(array.shape)
                for c in range(count):
                    at = (half * count + c) * PIECE
                    held.append(array[dest * rows : (dest + 1) * rows, at : at + PIECE])
            out_ref[p] = jnp.concatenate(held, axis=0).astype(out_ref.dtype)

    def unpack(self, slab, shapes):
        found, at = [], 0
        for shape in shapes:
            rows, count = self.pieces(shape)
            part = slab[at : at + rows * count].reshape(count, rows, PIECE)
            found.append(jnp.swapaxes(part, 0, 1).reshape(rows, count * PIECE))
            at += rows * count
        return found

    def arrange(self, array):
        bits = len(self.order)
        split = array.reshape((2,) * bits + array.shape[1:])
        turn = [bits - 1 - bit for _, bit in self.order] + list(range(bits, split.ndim))
        return jnp.transpose(split, turn).reshape(array.shape)

    def run(self, array, order, over_struct=True):
        def exchange(array, axis, bit):
            return lax.ppermute(array, axis, [(i, i ^ (1 << bit)) for i in range(self.counts[axis])])

        def take(pair, start, size):
            left, right = [lax.dynamic_slice_in_dim(a, start, size, 0) for a in pair]
            zero = order.zero.astype(F32) if size == 1 else 0.0
            return (left.astype(F32) + right.astype(F32) + zero).astype(left.dtype)

        pair, start, size = None, 0, array.shape[0]
        for axis, bit in self.order:
            mine = (lax.axis_index(axis) >> bit) & 1
            size = size // 2
            if pair is None:
                sent = kept = array
                after = mine * size
            else:
                start = start + order.zero
                sent = take(pair, start + (1 - mine) * size, size)
                kept = take(pair, start + mine * size, size)
                after = 0
            received = exchange(sent, axis, bit)
            yield [sent]
            pair, start = (kept, received), after
        held = take(pair, start + order.zero, 1)[0]
        if not over_struct:
            return held
        if self.halves() == 2:
            received = exchange(held, "struct", 0)
            yield [held]
            first = lax.axis_index("struct") == 0
            return jnp.where(first, held, received), jnp.where(first, received, held)
        for bit in range(self.counts["struct"].bit_length() - 1):
            received = exchange(held, "struct", bit)
            yield [held]
            held = (held.astype(F32) + received.astype(F32)).astype(held.dtype)
        return held

    def unpack_sum(self, result, shapes):
        if self.halves() == 1:
            return self.unpack(result, shapes)
        parts = [self.unpack(half, shapes) for half in result]
        return [jnp.concatenate(pair, axis=1) for pair in zip(*parts)]


def doubling(array, exchanges, counts, order):
    for axis, bit in exchanges:
        received = lax.ppermute(array, axis, [(i, i ^ (1 << bit)) for i in range(counts[axis])])
        yield [array]
        array = array + received + order.zero.astype(F32)
    return array


class Running:
    def __init__(self, steps):
        self.steps = steps
        self.result = None

    def step(self):
        if self.result is None:
            try:
                return list(next(self.steps))
            except StopIteration as stop:
                self.result = stop.value
                return list(self.result) if isinstance(self.result, tuple) else [self.result]
        return []

    def finish(self):
        while self.result is None:
            self.step()
        return self.result


def advance(*running):
    return [array for r in running for array in r.step()]


def finish(*running):
    while any(r.result is None for r in running):
        advance(*running)
    return [r.result for r in running]


def pair_forward_kernel(pair_ref, gain_ref, weight_ref, mask_ref, lengths_ref, out_ref, terms):
    gain = gain_ref[...].astype(F32)
    rows, length, channels = pair_ref.shape
    average = jnp.full((channels, channels), 1.0 / channels, BF16)
    position = lax.broadcasted_iota(jnp.int32, (1, length), 1)
    valid = (position < lengths_ref[0]) & ((mask_ref[...] == 1) | (position == 0))
    for i in range(rows):
        values = pair_ref[i]
        center = values.astype(F32) - dot(values, average)
        inverse = lax.rsqrt(jnp.mean(center * center, axis=-1, keepdims=True) + EPS)
        affine = (center * inverse * gain).astype(BF16)
        terms[i] = jnp.where(valid, dot(weight_ref[...], affine, 0, 1), MASKED)
    for h in range(terms.shape[1]):
        out_ref[h] = terms[:, h, :].astype(BF16)


def pair_forward(pair, gain, weight, mask, lengths, order):
    rows, length, channels = pair.shape
    heads = weight.shape[1]
    block = 16 if rows % 16 == 0 else rows
    return call(
        "pair_forward",
        pair_forward_kernel,
        rows // block,
        [
            (pair, spec((block, length, channels), 0)),
            (gain, spec(gain.shape)),
            (weight, spec(weight.shape)),
            (mask, spec(mask.shape)),
            (lengths, pl.BlockSpec(memory_space=pltpu.SMEM)),
        ],
        [((heads, rows, length), BF16, spec((heads, block, length), 1))],
        [pltpu.VMEM((block, heads, length), F32)],
        [],
        order,
    )[0]


def pair_backward_kernel(chunks, pair_ref, gain_ref, weight_ref, *refs):
    grad_refs, (out_ref, weight_grad_ref, grads) = refs[:chunks], refs[chunks:]
    gain = gain_ref[...]
    channels = pair_ref.shape[2]
    average = jnp.full((channels, channels), 1.0 / channels, BF16)
    clear(pl.program_id(0), weight_grad_ref)
    for chunk, ref in enumerate(grad_refs):
        for h in range(ref.shape[0]):
            grads[:, chunk * ref.shape[0] + h, :] = ref[h].astype(F32)
    scaled = weight_ref[...].astype(F32) * gain
    means = jnp.broadcast_to(jnp.mean(scaled, axis=-1, keepdims=True), scaled.shape)
    full = jnp.concatenate([scaled, means], axis=1)
    high = full.astype(BF16)
    parts = jnp.concatenate([high, (full - high.astype(F32)).astype(BF16)], axis=0)

    def row(i, carry):
        values = pair_ref[i]
        center = values.astype(F32) - dot(values, average)
        inverse = lax.rsqrt(jnp.mean(center * center, axis=-1, keepdims=True) + EPS)
        normed = center * inverse
        grad = grads[i].astype(BF16)
        weight_grad_ref[...] += dot(grad, (normed * gain).astype(BF16))
        both = dot(jnp.concatenate([grad, grad], axis=0), parts, 0, 0)
        grad_normed = both[:, :channels]
        mean_proj = jnp.mean(grad_normed * normed, axis=-1, keepdims=True)
        out_ref[i] = inverse * (grad_normed - both[:, channels:] - normed * mean_proj)
        return carry

    lax.fori_loop(0, pair_ref.shape[0], row, 0, unroll=8)


def pair_backward(block, pair, grads, gain, weight_t, deps, order):
    rows, length, channels = pair.shape
    heads = weight_t.shape[0]
    return call(
        "pair_backward",
        functools.partial(pair_backward_kernel, len(grads)),
        rows // block,
        [
            (pair, spec((block, length, channels), 0)),
            (gain, spec(gain.shape)),
            (weight_t, spec(weight_t.shape)),
        ]
        + [(g, spec((g.shape[0], block, length), 1)) for g in grads],
        [
            (pair.shape, F32, spec((block, length, channels), 0)),
            ((heads, channels), F32, spec((heads, channels))),
        ],
        [pltpu.VMEM((block, heads, length), F32)],
        deps,
        order,
    )


def conditions(cond_ref, gain_ref, cond_w_ref, cond_b_ref, zero_w_ref, zero_b_ref, zero_gate_ref, factor_ref, shift_ref):
    cond = cond_ref[...]
    width = zero_gate_ref.shape[1]
    zero_gate_ref[...] = jax.nn.sigmoid(dot(cond, zero_w_ref[...]) + zero_b_ref[...])
    cond_normed, _ = layer_norm(cond.astype(F32))
    projected = dot((cond_normed * gain_ref[...]).astype(BF16), cond_w_ref[...])
    factor_ref[...] = jax.nn.sigmoid(projected[:, :width] + cond_b_ref[...])
    shift_ref[...] = projected[:, width:]


def conditions_back(cond_ref, gain_ref, cond_w_ref, zero_w_ref, zero_grad, projected):
    cond = cond_ref[...]
    cond_normed, cond_inverse = layer_norm(cond.astype(F32))
    scaled = (cond_normed * gain_ref[...]).astype(BF16)
    grad_scaled = dot(projected, cond_w_ref[...], 1, 1)
    return (
        dot(scaled, projected, 0, 0),
        dot(cond, zero_grad, 0, 0),
        column_sum(grad_scaled * cond_normed),
        dot(zero_grad, zero_w_ref[...], 1, 1),
        grad_scaled * gain_ref[...],
        cond_normed,
        cond_inverse,
    )


def step_rows(step, tokens):
    return pl.ds(pl.multiple_of(step * tokens, tokens), tokens)


def window_start(chunk, head_dim):
    return chunk * CHUNK_HEADS * head_dim // LANES * LANES


def inputs_kernel(
    head_dim, acts_ref, cot_ref, cond_ref, gain_ref, cond_w_ref, cond_b_ref, zero_w_ref, zero_b_ref,
    qkvg_ref, q_bias_ref, out_w_ref,
    input_ref, gate_ref, gated_grad_ref, q_ref, k_ref, v_ref, g_ref, qt_ref, kt_ref, vt_ref, gt_ref,
    zero_gate_ref, factor_ref, shift_ref,
):
    step = pl.program_id(0)
    samples, tokens, width = acts_ref.shape

    @pl.when(step == 0)
    def _():
        conditions(
            cond_ref, gain_ref, cond_w_ref, cond_b_ref, zero_w_ref, zero_b_ref, zero_gate_ref, factor_ref, shift_ref
        )

    here = step_rows(step, tokens)
    normed, _ = layer_norm(acts_ref[...].astype(F32))
    first = (factor_ref[here, :][None] * normed + shift_ref[here, :][None]).astype(BF16)
    input_ref[...] = first
    first = first.reshape(samples * tokens, width)
    grad_att = (cot_ref[...].astype(F32) * zero_gate_ref[here, :][None]).astype(BF16)
    grad_gated = dot(grad_att.reshape(samples * tokens, width), out_w_ref[...], 1, 1)
    gated_grad_ref[...] = grad_gated.reshape(samples, tokens, width)
    gate = jax.nn.sigmoid(dot(first, qkvg_ref[:, 3 * width :]))
    gate_ref[...] = gate.reshape(samples, tokens, width)

    def put(values, nat_ref, t_ref):
        low = values.astype(BF16).reshape(samples, tokens, width)
        for chunk in range(nat_ref.shape[0]):
            start = window_start(chunk, head_dim)
            nat_ref[chunk] = low[:, :, start : start + WINDOW]
        for s in range(samples):
            t_ref[s] = low[s].T

    put(grad_gated * gate, g_ref, gt_ref)
    put(dot(first, qkvg_ref[:, :width]) + q_bias_ref[...], q_ref, qt_ref)
    put(dot(first, qkvg_ref[:, width : 2 * width]), k_ref, kt_ref)
    put(dot(first, qkvg_ref[:, 2 * width : 3 * width]), v_ref, vt_ref)


def inputs_call(acts, cot, cond, branch, qkvg_w, q_bias, out_w, heads, deps, order):
    samples, length, width = acts.shape
    chunks = heads // CHUNK_HEADS
    block = spec((samples, TOKENS, width), 1)
    nat = spec((chunks, samples, TOKENS, WINDOW), 2)
    turned = spec((samples, width, TOKENS), 2)
    rows = samples * length
    return call(
        "inputs",
        functools.partial(inputs_kernel, width // heads),
        length // TOKENS,
        [(acts, block), (cot, block), (cond, spec(cond.shape))]
        + branch
        + [(a, spec(a.shape)) for a in (qkvg_w, q_bias, out_w)],
        [(acts.shape, BF16, block), (acts.shape, F32, block), (acts.shape, F32, block)]
        + [((chunks, samples, length, WINDOW), BF16, nat)] * 4
        + [((samples, width, length), BF16, turned)] * 4
        + [((length, width), F32, spec((length, width)))] * 2,
        [pltpu.VMEM((length, width), F32)],
        deps,
        order,
    )


def transition_kernel(
    halving, acts_ref, cot_ref, cond_ref, gain_ref, cond_w_ref, cond_b_ref, zero_w_ref, zero_b_ref,
    swiglu_ref, down_ref,
    partial_ref, acts_grad_ref, cond_gate_ref, cond_norm_ref, packed_out, cond_b_out, zero_b_out, gain_out,
    swiglu_acc, down_acc, zero_gate_ref, factor_ref, shift_ref, zero_low, projected,
):
    step = pl.program_id(0)
    clear(step, swiglu_acc, down_acc, cond_b_out, zero_b_out)
    samples, tokens, width = acts_ref.shape
    rows = samples * tokens
    hidden_width = down_ref.shape[0]

    @pl.when(step == 0)
    def _():
        conditions(
            cond_ref, gain_ref, cond_w_ref, cond_b_ref, zero_w_ref, zero_b_ref, zero_gate_ref, factor_ref, shift_ref
        )

    here = step_rows(step, tokens)
    zero_gate = zero_gate_ref[here, :]
    factor = factor_ref[here, :]
    acts = acts_ref[...].astype(F32)
    normed, _ = layer_norm(acts)
    second = (factor[None] * normed + shift_ref[here, :][None]).astype(BF16).reshape(rows, width)
    grad_out = cot_ref[...].astype(F32)
    grad_tr = (grad_out * zero_gate[None]).astype(BF16).reshape(rows, width)
    transition = grad_input = 0.0
    second_t = second.T
    for at in range(0, hidden_width, HIDDEN):
        gate_at, up_at = slice(at, at + HIDDEN), slice(hidden_width + at, hidden_width + at + HIDDEN)
        gate_part = dot(second, swiglu_ref[:, gate_at])
        up_part = dot(second, swiglu_ref[:, up_at])
        gate_sig = jax.nn.sigmoid(gate_part)
        silu = gate_part * gate_sig
        product = (silu * up_part).astype(BF16)
        transition += dot(product, down_ref[gate_at, :])
        grad_product = dot(grad_tr, down_ref[gate_at, :], 1, 1)
        down_acc[gate_at, :] += dot(product, grad_tr, 0, 0)
        grad_up = (grad_product * silu).astype(BF16)
        grad_gate = (grad_product * up_part * gate_sig * (1.0 + gate_part * (1.0 - gate_sig))).astype(BF16)
        swiglu_acc[:, gate_at] += dot(second_t, grad_gate)
        swiglu_acc[:, up_at] += dot(second_t, grad_up)
        grad_input += dot(grad_gate, swiglu_ref[:, gate_at], 1, 1)
        grad_input += dot(grad_up, swiglu_ref[:, up_at], 1, 1)
    transition = transition.reshape(samples, tokens, width)
    grad_input = grad_input.reshape(samples, tokens, width)
    partial_ref[...] = acts + zero_gate[None] * transition
    grad_zero = jnp.sum(grad_out * transition, axis=0) * slope(zero_gate)
    zero_b_out[...] += column_sum(grad_zero)
    zero_low[here, :] = grad_zero.astype(BF16)
    grad_factor = jnp.sum(grad_input * normed, axis=0) * slope(factor)
    cond_b_out[...] += column_sum(grad_factor)
    projected[here, :width] = grad_factor.astype(BF16)
    projected[here, width:] = jnp.sum(grad_input, axis=0).astype(BF16)
    acts_grad_ref[...] = grad_input * factor[None]

    @pl.when(step == pl.num_programs(0) - 1)
    def _():
        cond_w_grad, zero_w_grad, gain_grad, cond_gate, cond_norm, _, _ = conditions_back(
            cond_ref, gain_ref, cond_w_ref, zero_w_ref, zero_low[...], projected[...]
        )
        gain_out[...] = gain_grad
        cond_gate_ref[...] = cond_gate
        cond_norm_ref[...] = cond_norm
        halving.pack(packed_out, [swiglu_acc, down_acc, cond_w_grad, zero_w_grad])


def transition_call(acts, cot, cond, branch, swiglu, down, halving, deps, order):
    samples, length, width = acts.shape
    cond_width = cond.shape[1]
    hidden = down.shape[0]
    rows = samples * length
    block = spec((samples, TOKENS, width), 1)
    weights = [(width, 2 * hidden), (hidden, width), (cond_width, 2 * width), (cond_width, width)]
    vectors = [(1, width), (1, width), (1, cond_width)]
    results = call(
        "transition",
        functools.partial(transition_kernel, halving),
        length // TOKENS,
        [(acts, block), (cot, block), (cond, spec(cond.shape))]
        + branch
        + [(swiglu, spec(swiglu.shape)), (down, spec(down.shape))],
        [(acts.shape, F32, block)] * 2
        + [(cond.shape, F32, spec(cond.shape))] * 2
        + [(halving.slabs(weights), BF16, spec(halving.slabs(weights)))]
        + [(s, F32, spec(s)) for s in vectors],
        [pltpu.VMEM(s, F32) for s in weights[:2]]
        + [pltpu.VMEM((length, width), F32)] * 3
        + [pltpu.VMEM((length, width), BF16), pltpu.VMEM((length, 2 * width), BF16)],
        deps,
        order,
    )
    return results, weights


def attention_kernel(
    halving, head_dim, first_lane, q_ref, k_ref, v_ref, g_ref, qt_ref, kt_ref, vt_ref, gt_ref, bias_ref,
    mixed_ref, dq_ref, dkt_ref, dvt_ref, db_ref, kz, vz, plow, dslow, dsum,
):
    h = pl.program_id(0)
    samples, length, wide = q_ref.shape
    scale = head_dim ** (-0.5)
    off = pl.multiple_of(first_lane + h * head_dim, 16)
    lane = lax.broadcasted_iota(jnp.int32, (1, wide), 1)
    mask = ((lane >= off) & (lane < off + head_dim)).astype(BF16)

    @pl.when(h == 0)
    def _():
        mixed_ref[...] = jnp.zeros_like(mixed_ref)
        dq_ref[...] = jnp.zeros_like(dq_ref)

    kz[...] = jnp.zeros_like(kz)
    vz[...] = jnp.zeros_like(vz)
    for s in range(samples):
        kz[s, pl.ds(off, head_dim), :] = kt_ref[s]
        vz[s, pl.ds(off, head_dim), :] = vt_ref[s]
    parts, _, share, _ = bias_ref.shape
    if share % 16 == 0:
        bias = bias_ref[:, 0].reshape(length, length).astype(F32)
    else:
        bias = jnp.concatenate([bias_ref[p, 0].astype(F32) for p in range(parts)], axis=0)
    for s in range(samples):
        x = dot(q_ref[s], kz[s]) * scale + bias
        x = jnp.exp(x - jnp.max(x, axis=-1, keepdims=True))
        probs = x * (1.0 / jnp.sum(x, axis=-1, keepdims=True))
        low = probs.astype(BF16)
        plow[...] = low
        mixed = dot(low, v_ref[s] * mask)
        mixed_ref[s] += mixed
        grad = g_ref[s]
        delta = jnp.sum(grad.astype(F32) * mixed, axis=-1, keepdims=True)
        grad_scores = probs * (dot(grad, vz[s]) - delta)
        grad_low = (grad_scores * scale).astype(BF16)
        dslow[...] = grad_low
        total = grad_scores if s == 0 else dsum[...] + grad_scores
        if s < samples - 1:
            dsum[...] = total
        else:
            for p, (dest, _) in enumerate(halving.places()):
                db_ref[p, 0] = total[dest * share : (dest + 1) * share].astype(BF16)
        dq_ref[s] += dot(grad_low, k_ref[s] * mask)
        dvt_ref[s] = dot(gt_ref[s], plow[...]).astype(BF16)
        dkt_ref[s] = dot(qt_ref[s], dslow[...]).astype(BF16)


def attention_call(chunk, nats, turned, bias, first_head, head_dim, halving, deps, order):
    _, samples, length, wide = nats[0].shape
    parts, _, share, _ = bias.shape
    local = chunk * CHUNK_HEADS - first_head
    nat = pl.BlockSpec((None, samples, length, wide), lambda h: (chunk, 0, 0, 0))
    turn = pl.BlockSpec((samples, head_dim, length), lambda h: (0, chunk * CHUNK_HEADS + h, 0))
    turn_out = pl.BlockSpec((samples, head_dim, length), lambda h: (0, h, 0))
    bias_in = pl.BlockSpec((parts, 1, share, length), lambda h: (0, local + h, 0, 0))
    bias_out = pl.BlockSpec((parts, 1, share, length), lambda h: (0, h, 0, 0))
    held = pl.BlockSpec((samples, length, wide), lambda h: (0, 0, 0))
    return call(
        "attention",
        functools.partial(
            attention_kernel,
            halving,
            head_dim,
            chunk * CHUNK_HEADS * head_dim - window_start(chunk, head_dim),
        ),
        CHUNK_HEADS,
        [(a, nat) for a in nats] + [(a, turn) for a in turned] + [(bias, bias_in)],
        [((samples, length, wide), F32, held)] * 2
        + [((samples, CHUNK_HEADS * head_dim, length), BF16, turn_out)] * 2
        + [((parts, CHUNK_HEADS, share, length), BF16, bias_out)],
        [
            pltpu.VMEM((samples, wide, length), BF16),
            pltpu.VMEM((samples, wide, length), BF16),
            pltpu.VMEM((length, length), BF16),
            pltpu.VMEM((length, length), BF16),
            pltpu.VMEM((length, length), F32),
        ],
        deps,
        order,
    )


def mixed_kernel(head_dim, chunks, *refs):
    (cot_ref, gate_ref, gated_grad_ref, partial_ref, zero_gate_ref, out_w_ref), refs = refs[:6], refs[6:]
    mixed_refs, refs = refs[:chunks], refs[chunks:]
    dq_refs, refs = refs[:chunks], refs[chunks:]
    dkt_refs, refs = refs[:chunks], refs[chunks:]
    dvt_refs, refs = refs[:chunks], refs[chunks:]
    block_ref, joined_ref, zero_low_ref, out_out, zero_b_out, q_bias_out = refs
    clear(pl.program_id(0), out_out, zero_b_out, q_bias_out)
    samples, tokens, width = cot_ref.shape
    rows = samples * tokens
    zero_gate = zero_gate_ref[...]
    grad_out = cot_ref[...].astype(F32)
    grad_att = (grad_out * zero_gate[None]).astype(BF16).reshape(rows, width)

    def join(window_refs):
        pieces = []
        for tile in range(width // LANES):
            held = [
                ref[:, :, tile * LANES - start : (tile + 1) * LANES - start]
                for chunk, ref in enumerate(window_refs)
                for start in [window_start(chunk, head_dim)]
                if start <= tile * LANES < start + WINDOW
            ]
            pieces.append(functools.reduce(jnp.add, held))
        return jnp.concatenate(pieces, axis=-1).reshape(rows, width)

    def turn(turned_refs):
        joined = jnp.concatenate([ref[...] for ref in turned_refs], axis=1)
        return jnp.concatenate([joined[s].T for s in range(samples)], axis=0)

    mixed = join(mixed_refs)
    gate = gate_ref[...].reshape(rows, width)
    gated = (gate * mixed).astype(BF16)
    attended = dot(gated, out_w_ref[...]).reshape(samples, tokens, width)
    block_ref[...] = (partial_ref[...] + zero_gate[None] * attended).astype(BF16)
    out_out[...] += dot(gated, grad_att, 0, 0)
    grad_zero = jnp.sum(grad_out * attended, axis=0) * slope(zero_gate)
    zero_b_out[...] += column_sum(grad_zero)
    zero_low_ref[...] = grad_zero.astype(BF16)
    grad_queries = join(dq_refs)
    q_bias_out[...] += column_sum(grad_queries)
    grad_gate = gated_grad_ref[...].reshape(rows, width) * mixed * slope(gate)
    parts = [grad_queries.astype(BF16), turn(dkt_refs), turn(dvt_refs), grad_gate.astype(BF16)]
    for i, part in enumerate(parts):
        joined_ref[:, :, i * width : (i + 1) * width] = part.reshape(samples, tokens, width)


def mixed_call(cot, gate, gated_grad, partial, zero_gate, out_w, mixeds, dqs, dkts, dvts, heads, deps, order):
    samples, length, width = cot.shape
    chunks = len(mixeds)
    block = spec((samples, TOKENS, width), 1)
    window = spec((samples, TOKENS, WINDOW), 1)
    turned = spec((samples, width // chunks, TOKENS), 2)
    tokens = spec((TOKENS, width), 0)
    return call(
        "mixed",
        functools.partial(mixed_kernel, width // heads, chunks),
        length // TOKENS,
        [(a, block) for a in (cot, gate, gated_grad, partial)]
        + [(zero_gate, tokens), (out_w, spec(out_w.shape))]
        + [(a, window) for a in mixeds + dqs]
        + [(a, turned) for a in dkts + dvts],
        [
            (cot.shape, BF16, block),
            ((samples, length, 4 * width), BF16, spec((samples, TOKENS, 4 * width), 1)),
            ((length, width), BF16, tokens),
        ]
        + [(s, F32, spec(s)) for s in ((width, width), (1, width), (1, width))],
        [],
        deps,
        order,
    )


def qkvg_kernel(halving, first_ref, joined_ref, packed_out):
    step = pl.program_id(0)
    samples, length, width = first_ref.shape
    rows = samples * length
    grad = dot(first_ref[...].reshape(rows, width), joined_ref[...].reshape(rows, width), 0, 0)
    blocks = 4
    share, count = halving.pieces((width, blocks * width))
    wide = width // PIECE

    for block in range(blocks):

        @pl.when(step == block)
        def _():
            for p, (dest, half) in enumerate(halving.places()):
                for c in range(wide):
                    piece = block * wide + c - half * count
                    if 0 <= piece < count:
                        packed_out[p, piece * share : (piece + 1) * share] = grad[
                            dest * share : (dest + 1) * share, c * PIECE : (c + 1) * PIECE
                        ].astype(BF16)


def qkvg_call(first, grad_joined, halving, deps, order):
    samples, length, width = first.shape
    slabs = halving.slabs([(width, 4 * width)])
    (packed,) = call(
        "qkvg_grad",
        functools.partial(qkvg_kernel, halving),
        4,
        [(first, spec(first.shape)), (grad_joined, spec((samples, length, width), 2))],
        [(slabs, BF16, spec(slabs))],
        [],
        deps,
        order,
    )
    return packed


def outputs_kernel(
    acts_ref, cot_ref, joined_ref, acts_part_ref, factor_ref, qkvg_ref, acts_grad_ref, projected_ref, cond_b_out
):
    clear(pl.program_id(0), cond_b_out)
    samples, tokens, width = acts_ref.shape
    rows = samples * tokens
    factor = factor_ref[...]
    normed, inverse = layer_norm(acts_ref[...].astype(F32))
    grad_input = dot(joined_ref[...].reshape(rows, 4 * width), qkvg_ref[...], 1, 1).reshape(
        samples, tokens, width
    )
    grad_factor = jnp.sum(grad_input * normed, axis=0) * slope(factor)
    cond_b_out[...] += column_sum(grad_factor)
    projected_ref[:, :width] = grad_factor.astype(BF16)
    projected_ref[:, width:] = jnp.sum(grad_input, axis=0).astype(BF16)
    acts_grad_ref[...] = (
        cot_ref[...].astype(F32) + norm_back(grad_input * factor[None] + acts_part_ref[...], normed, inverse)
    ).astype(BF16)


def outputs_call(acts, cot, joined, acts_part, factor, qkvg_w, deps, order):
    samples, length, width = acts.shape
    block = spec((samples, TOKENS, width), 1)
    return call(
        "outputs",
        outputs_kernel,
        length // TOKENS,
        [(acts, block), (cot, block), (joined, spec((samples, TOKENS, 4 * width), 1)), (acts_part, block)]
        + [(factor, spec((TOKENS, width), 0)), (qkvg_w, spec(qkvg_w.shape))],
        [
            (acts.shape, BF16, block),
            ((length, 2 * width), BF16, spec((TOKENS, 2 * width), 0)),
            ((1, width), F32, spec((1, width))),
        ],
        [],
        deps,
        order,
    )


def conditions_kernel(
    rest, small, vector_parts, cond_ref, gain_ref, cond_w_ref, zero_w_ref, zero_low_ref, projected_ref,
    cond_gate_in, cond_norm_in, out_w_grad_ref, *refs
):
    vector_refs, (packed_out, small_out) = refs[:vector_parts], refs[vector_parts:]
    cond_w_grad, zero_w_grad, gain_grad, cond_gate, cond_norm, cond_normed, cond_inverse = conditions_back(
        cond_ref, gain_ref, cond_w_ref, zero_w_ref, zero_low_ref[...], projected_ref[...]
    )
    cond_grad = (
        cond_gate + cond_gate_in[...] + norm_back(cond_norm + cond_norm_in[...], cond_normed, cond_inverse)
    )
    rest.pack(packed_out, [out_w_grad_ref, cond_w_grad, zero_w_grad])
    vectors = [gain_grad] + [ref[...] for ref in vector_refs]
    pieces = [v[:, at : at + PIECE] for v in vectors for at in range(0, v.shape[1], PIECE)]
    share = cond_grad.shape[0] // rest.counts["sample"]
    for p, (dest, _) in enumerate(small.places()):
        small_out[p] = jnp.concatenate([cond_grad[dest * share : (dest + 1) * share]] + pieces, axis=0)


def conditions_call(cond, branch, zero_w, zero_low, projected, cond_gate, cond_norm, out_w_grad, vectors, rest, small, deps, order):
    length, cond_width = cond.shape
    width = zero_low.shape[1]
    weights = [out_w_grad.shape, (cond_width, 2 * width), (cond_width, width)]
    slabs = rest.slabs(weights)
    sent = length // rest.counts["sample"] + (sum(v.shape[1] for v in vectors) + cond_width) // PIECE
    small_slabs = (rest.counts["sample"], sent, PIECE)
    fixed = (zero_low, projected, cond_gate, cond_norm, out_w_grad, *vectors)
    results = call(
        "conditions",
        functools.partial(conditions_kernel, rest, small, len(vectors)),
        1,
        [(cond, spec(cond.shape))] + branch[:2] + [zero_w] + [(a, spec(a.shape)) for a in fixed],
        [(slabs, BF16, spec(slabs)), (small_slabs, F32, spec(small_slabs))],
        [],
        deps,
        order,
    )
    return results, weights


def body(
    struct_count, sample_devices,
    acts, cond, pair, lengths, token_mask, cond_gains, cond_w, cond_bias, output_gate_weights, zero_bias,
    qkvg_w, q_bias, out_w, swiglu_w, down_w, pair_gain, pair_w, cotangent,
):
    acts, cond, pair, cotangent = acts[0], cond[0], pair[0], cotangent[0]
    samples, length, width = acts.shape
    cond_width = cond.shape[1]
    heads = pair_w.shape[1]
    head_dim = width // heads
    chunks = heads // CHUNK_HEADS
    counts = {"struct": struct_count, "sample": sample_devices}
    bits = sample_devices.bit_length() - 1
    pair_wt = pair_w.T
    order = Order()

    bias_rows = pair_forward(pair, pair_gain[None], pair_w, token_mask, lengths, order)
    bias = lax.all_gather(bias_rows, "sample", axis=0, tiled=False)

    rows = {}
    at = 0
    packed = [
        ("gain", cond_gains), ("cond_b", cond_bias), ("zero_b", zero_bias), ("q_bias", q_bias), ("pair", pair_gain)
    ]
    vector = jnp.concatenate([v for _, v in packed]).astype(F32)[None]
    for name, v in packed:
        rows[name] = vector[:, at : at + v.shape[0]]
        at += v.shape[0]

    def conditioning(b):
        return [
            (rows["gain"], spec((1, cond_width), at=(0, b))),
            (cond_w, spec((cond_width, 2 * width), at=(0, b))),
            (rows["cond_b"], spec((1, width), at=(0, b))),
        ]

    def zero(b):
        return [
            (output_gate_weights, spec((cond_width, width), at=(0, b))),
            (rows["zero_b"], spec((1, width), at=(0, b))),
        ]

    def path(*order):
        steps = [("struct", 0) if o == "y" else ("sample", o) for o in order]
        steps = [s for s in steps if s[0] == "sample" or struct_count == 2]
        return Halving(steps + [("sample", b) for b in range(4, bits)], counts)

    along_x = path(0, 1, 2, 3)
    along_y = path(0, "y", 2, 3, 1)
    results, early_shapes = transition_call(
        acts, cotangent, cond, conditioning(1) + zero(1), swiglu_w, down_w, along_y, [], order
    )
    partial, acts_part, cond_gate, cond_norm, early, cond_b_one, zero_b_one, gain_one = results
    early = Running(along_y.run(early, order))
    first, gate, gated_grad, *rest = inputs_call(
        acts, cotangent, cond, conditioning(0) + zero(0), qkvg_w, rows["q_bias"], out_w, heads, advance(early), order
    )
    nats, turned, (zero_gate, factor) = rest[:4], rest[4:8], rest[8:]

    mixeds, dqs, dkts, dvts, bias_sums = [], [], [], [], []
    deps = advance(early)
    for chunk in range(chunks):
        mixed, dq, dkt, dvt, db = attention_call(chunk, nats, turned, bias, 0, head_dim, along_x, deps, order)
        mixeds.append(mixed)
        dqs.append(dq)
        dkts.append(dkt)
        dvts.append(dvt)
        bias_sums.append(Running(along_x.run(db, order, over_struct=False)))
        deps = advance(*bias_sums)
        deps += advance(early)

    block_out, grad_joined, zero_low, out_grad, zero_b_zero, q_bias_grad = mixed_call(
        cotangent, gate, gated_grad, partial, zero_gate, out_w, mixeds, dqs, dkts, dvts, heads, deps, order
    )
    deps = advance(*bias_sums, early)
    qkvg_sum = Running(along_y.run(qkvg_call(first, grad_joined, along_y, deps, order), order))
    deps = advance(*bias_sums[:-1], qkvg_sum)
    acts_grad, projected, cond_b_zero = outputs_call(
        acts, cotangent, grad_joined, acts_part, factor, qkvg_w, deps, order
    )
    deps = advance(*bias_sums, qkvg_sum, early)
    (rest, small), rest_shapes = conditions_call(
        cond, conditioning(0), zero(0)[0], zero_low, projected, cond_gate, cond_norm, out_grad,
        [gain_one, cond_b_zero, cond_b_one, zero_b_zero, zero_b_one, q_bias_grad], along_y, along_x, deps, order,
    )
    rest = Running(along_y.run(rest, order))
    small = Running(along_x.run(small, order, over_struct=False))
    deps = advance(*bias_sums, rest, small)
    while any(b.result is None for b in bias_sums):
        tick(deps, order)
        deps = advance(*bias_sums)
    share = length // sample_devices
    block = 16 if share % 16 == 0 else share
    grads = [b.result.reshape(CHUNK_HEADS, -1, length) for b in bias_sums]
    deps += advance(qkvg_sum, rest, small)
    grad_pair, pair_w_grad = pair_backward(block, pair, grads, rows["pair"], pair_wt, deps, order)
    exchanges = [("sample", bit) for bit in range(bits)]
    over_struct = [("struct", bit) for bit in range(struct_count.bit_length() - 1)]
    pair_sum = Running(doubling(pair_w_grad, over_struct + exchanges, counts, order))
    while small.result is None:
        tick(advance(pair_sum, rest, small, qkvg_sum, early), order)
    cond_sum = small.result[:share]
    small = Running(doubling(small.result[share:], over_struct, counts, order))
    finish(pair_sum, rest, small, qkvg_sum, early)

    swiglu_sum, down_sum, cond_w_one, zero_w_one = along_y.unpack_sum(early.result, early_shapes)
    (qkvg_sum,) = along_y.unpack_sum(qkvg_sum.result, [qkvg_w.shape])
    out_sum, cond_w_zero, zero_w_zero = along_y.unpack_sum(rest.result, rest_shapes)

    device = lax.axis_index("sample")

    def mine(array, axis=0):
        size = array.shape[axis] // sample_devices
        return lax.dynamic_slice_in_dim(array, device * size, size, axis)

    vector = small.result.reshape(-1)
    at, found = 0, []
    for size in (2 * cond_width, 2 * width, 2 * width, width):
        found.append(mine(vector[at : at + size]))
        at += size
    gains, cond_b, zero_b, q_b = found
    pair_w_sum = mine(pair_sum.result, 1).T
    pair_g = jnp.sum(pair_w_sum * mine(pair_w).astype(F32), axis=-1) / mine(pair_gain).astype(F32)

    def wide(*parts):
        return jnp.concatenate([p.astype(F32) for p in parts], axis=-1)

    return (
        block_out[None],
        acts_grad[None],
        cond_sum[None],
        grad_pair[None],
        gains,
        wide(cond_w_zero, cond_w_one),
        cond_b,
        wide(zero_w_zero, zero_w_one),
        zero_b,
        wide(qkvg_sum),
        q_b,
        wide(out_sum),
        wide(swiglu_sum),
        wide(down_sum),
        pair_g,
        pair_w_sum,
    )


def solution(mesh):
    per_struct = P("struct", "sample", None, None)
    in_specs = (
        (per_struct, P("struct", None, None), per_struct, P("struct"), P("struct", None))
        + (P(),) * 12
        + (per_struct,)
    )
    one, two = P("sample"), P("sample", None)
    out_specs = (
        per_struct, per_struct, P("struct", "sample", None), per_struct,
        one, two, one, two, one, two, one, two, two, two, one, two,
    )
    local = functools.partial(body, mesh.shape["struct"], mesh.shape["sample"])
    return jax.shard_map(local, mesh=mesh, in_specs=in_specs, out_specs=out_specs, check_vma=False)
```

time: 861 us -> 525 us (0.61)
  waiting for transfers between devices: 348 us -> 59.4 us
  local copies, waits for them, and re-layouts: 89.6 us -> 15.6 us
  other arithmetic: 37.3 us -> 74.2 us
  between operations: 16.3 us -> 52.4 us
  Pallas kernels: 297 us -> 273 us
  starting transfers between devices: 63.3 us -> 46.2 us
    ppermute x65 -> x44, waiting for transfers between devices: 348 us -> 48.7 us  [the longest x38 47.8 us: exchange(): lax.ppermute(array, axis, [(i, i ^ 1 << bit) for i in range(self.counts[a...]
    dynamic_slice x25 -> x5, local copies, waits for them, and re-layouts: 41.6 us -> 4.54 us  [the longest x4 2.34 us: mine(): return lax.dynamic_slice_in_dim(array, device * size, size, axis)]
    convert_element_type x59 -> x28, other arithmetic: 29.2 us -> 55.8 us  [the longest x24 52.6 us: take(): return (left.astype(F32) + right.astype(F32) + zero).astype(left.dtype)]
    pallas_call x9 -> x16, Pallas kernels: 297 us -> 273 us  [call(): pl.pallas_call(run, grid=(grid,), in_specs=[s for _, s in ins] + [pl.Bloc...]
    all_gather x1 -> x0, local copies, waits for them, and re-layouts: 19.8 us -> none  [body(): lax.all_gather(jnp.swapaxes(bias_rows, 0, 1), 'sample', axis=0, tiled=False)]
    ppermute x65 -> x44, starting transfers between devices: 63.3 us -> 46.2 us  [the longest x38 37.3 us: exchange(): lax.ppermute(array, axis, [(i, i ^ 1 << bit) for i in range(self.counts[a...]
    all_gather x1, waiting for transfers between devices: 0.01 us -> 10.7 us  [body(): bias = lax.all_gather(bias_rows, 'sample', axis=0, tiled=False)]
    squeeze x0 -> x7, other arithmetic: none -> 9.66 us  [run(): held = take(pair, start + order.zero, 1)[0]]
  transfers between devices with their start and end apart: 66 -> 45, of which waited for: 45 -> 11; matrix products, arithmetic and copies ran while one was open for 11% -> 16% of each run, Pallas kernels for 22% -> 50%
where the time goes in v2:
time: 525 us; the launch traced here: 521 us
  Pallas kernels  273 us (52%)
  other arithmetic  74.2 us (14%)
  waiting for transfers between devices  59.4 us (11%)
  between operations  52.4 us (10%)
  starting transfers between devices  46.2 us (9%)
  local copies, waits for them, and re-layouts  15.6 us (3%)
    pallas_call x16, Pallas kernels, call(): pl.pallas_call(run, grid=(grid,), in_specs=[s for _, s in ins] + [pl.Bloc...  273 us
    convert_element_type x24, other arithmetic, take(): return (left.astype(F32) + right.astype(F32) + zero).astype(left.dtype)  52.6 us
    ppermute x38, waiting for transfers between devices, exchange(): lax.ppermute(array, axis, [(i, i ^ 1 << bit) for i in range(self.counts[a...  47.8 us
    ppermute x38, starting transfers between devices, exchange(): lax.ppermute(array, axis, [(i, i ^ 1 << bit) for i in range(self.counts[a...  37.3 us
    all_gather x1, waiting for transfers between devices, body(): bias = lax.all_gather(bias_rows, 'sample', axis=0, tiled=False)  10.7 us
  transfers between devices with their start and end apart: 45, of which 11 were waited for; matrix products, arithmetic and copies ran while one was open for 16% of the time, Pallas kernels for 50%

profile of v2, /device:TPU:0, one launch (start us, length us, event | category | flops | bytes accessed | tf_op | source)
XLA Modules:
  0.0 520.8 jit_solution(17392811938037895103)
XLA Ops:
  9.3 12.8 %pair_forward.1 = (bf16[16,48,768]{2,1,0:T(8,128)(2,1)}, s32[1]{0:T(128)}) custom-call(bf16[48,768,128]{2,1,0:T(8,128)(2,1)} %bitcast.110, bf16[1,128]{1,0:T(2,128)(2,1)} %bitcast.105, bf16[128,16]{1,0:T(8,128)(2,1)} %copy.44.refs_2_, s32[1,768]{1,0:T(1,128)} %refs_3_.2, s32[1]{0:T(128)S(6)} %copy.73.refs_4_), custom_call_target="tpu_custom_call" | custom-call | flops 99999997952 | bytes 1000000 | tf_op jit(solution)/shard_map/pair_forward/pallas_call | solution.py:78
  23.5 56.9 %transition.1 = (f32[2,768,768]{2,1,0:T(8,128)}, f32[2,768,768]{2,1,0:T(8,128)}, f32[768,384]{1,0:T(8,128)}, f32[768,384]{1,0:T(8,128)}, bf16[32,360,384]{2,1,0:...) custom-call(bf16[2,768,768]{2,1,0:T(8,128)(2,1)} %bitcast.116, ...), custom_call_target="tpu_custom_call" | custom-call | flops 99999997952 | bytes 1000000 | tf_op jit(solution)/shard_map/transition/pallas_call | solution.py:78
  80.9 22.9 %inputs.1 = (bf16[2,768,768]{2,1,0:T(8,128)(2,1)}, f32[2,768,768]{2,1,0:T(8,128)}, f32[2,768,768]{2,1,0:T(8,128)}, bf16[4,2,768,256]{3,2,1,0:T(8,128)(2,1)}, bf1...) custom-call(bf16[2,768,768]{2,1,0:T(8,128)(2,1)} %bitcast.117, ...), custom_call_target="tpu_custom_call" | custom-call | flops 99999997952 | bytes 1000000 | tf_op jit(solution)/shard_map/inputs/pallas_call | solution.py:78
  104.5 6.2 %add_convert_fusion = (bf16[8,360,384]{2,1,0:T(8,128)(2,1)S(1)}, bf16[8,360,384]{2,1,0:T(8,128)(2,1)}) fusion(bf16[32,360,384]{2,1,0:T(8,128)(2,1)} %collective-permute-done, s32[]{:T(128)S(6)} %select_n.282, bf16[32,360,384]{2,1,0:T(8,128)(2,1)} %get-tuple-element.86.refs_11_, s32[]{:T(128)S(6)} %select_n.281), kind=kLoop, calls=%fused_computation | loop fusion | flops 8847360 | bytes 13271048 | tf_op jit(solution)/shard_map/convert_element_type | solution.py:163
  110.7 2.5 collective-permute-start.1
  113.3 10.7 %all-gather.3.cloned.1.call-done = bf16[256,48,768]{2,1,0:T(8,128)(2,1)} async-done(((bf16[16,48,768]{2,1,0:T(8,128)(2,1)}), bf16[256,48,768]{2,1,0:T(8,128)(2,1)}) %all-gather.3.cloned.1.call-update) | async-done | bytes 18874384 | tf_op jit(solution)/shard_map/all_gather | solution.py:818
  124.0 23.7 %attention.4 = (f32[2,768,256]{2,1,0:T(8,128)}, f32[2,768,256]{2,1,0:T(8,128)}, bf16[2,192,768]{2,1,0:T(8,128)(2,1)}, bf16[2,192,768]{2,1,0:T(8,128)(2,1)}, bf16[16,4,48,768]{3,2,1,0:T(8,128)(2,1)}, /*index=5*/s32[1]{0:T(128)}) custom-call(bf16[4,2,768,256]{3,2,1,0:T(8,128)(2,1)} %get-tuple-element.91.refs_0_, ...), custom_call_target="tpu_custom_call" | custom-call | flops 99999997952 | bytes 1000000 | tf_op jit(solution)/shard_map/attention/pallas_call | solution.py:78
  149.3 13.1 %collective-permute-done.1 = bf16[8,360,384]{2,1,0:T(8,128)(2,1)} collective-permute-done((bf16[8,360,384]{2,1,0:T(8,128)(2,1)}, bf16[8,360,384]{2,1,0:T(8,128)(2,1)}, u32[]{:S(2)}, u32[]{:S(2)}) %collective-permute-start.1) | collective-permute-done | bytes 2211872 | tf_op jit(solution)/shard_map/ppermute | solution.py:158
  162.4 3.3 add_convert_fusion.12
  167.3 23.8 %attention.5 = (f32[2,768,256]{2,1,0:T(8,128)}, f32[2,768,256]{2,1,0:T(8,128)}, bf16[2,192,768]{2,1,0:T(8,128)(2,1)}, bf16[2,192,768]{2,1,0:T(8,128)(2,1)}, bf16[16,4,48,768]{3,2,1,0:T(8,128)(2,1)}, /*index=5*/s32[1]{0:T(128)}) custom-call(bf16[4,2,768,256]{3,2,1,0:T(8,128)(2,1)} %get-tuple-element.91.refs_0_, ...), custom_call_target="tpu_custom_call" | custom-call | flops 99999997952 | bytes 1000000 | tf_op jit(solution)/shard_map/attention/pallas_call | solution.py:78
  194.5 2.6 collective-permute-start.6
  197.1 4.0 add_convert_fusion.10
  202.6 23.9 %attention.6 = (f32[2,768,256]{2,1,0:T(8,128)}, f32[2,768,256]{2,1,0:T(8,128)}, bf16[2,192,768]{2,1,0:T(8,128)(2,1)}, bf16[2,192,768]{2,1,0:T(8,128)(2,1)}, bf16[16,4,48,768]{3,2,1,0:T(8,128)(2,1)}, /*index=5*/s32[1]{0:T(128)}) custom-call(bf16[4,2,768,256]{3,2,1,0:T(8,128)(2,1)} %get-tuple-element.91.refs_0_, ...), custom_call_target="tpu_custom_call" | custom-call | flops 99999997952 | bytes 1000000 | tf_op jit(solution)/shard_map/attention/pallas_call | solution.py:78
  230.4 4.1 add_convert_fusion.8
  239.8 23.7 %attention.7 = (f32[2,768,256]{2,1,0:T(8,128)}, f32[2,768,256]{2,1,0:T(8,128)}, bf16[2,192,768]{2,1,0:T(8,128)(2,1)}, bf16[2,192,768]{2,1,0:T(8,128)(2,1)}, bf16[16,4,48,768]{3,2,1,0:T(8,128)(2,1)}, /*index=5*/s32[1]{0:T(128)}) custom-call(bf16[4,2,768,256]{3,2,1,0:T(8,128)(2,1)} %get-tuple-element.91.refs_0_, ...), custom_call_target="tpu_custom_call" | custom-call | flops 99999997952 | bytes 1000000 | tf_op jit(solution)/shard_map/attention/pallas_call | solution.py:78
  264.1 4.4 collective-permute-done.10
  284.5 4.4 collective-permute-done.7
  290.2 4.0 add_convert_fusion.6
  294.7 18.9 %mixed.1 = (bf16[2,768,768]{2,1,0:T(8,128)(2,1)}, bf16[2,768,3072]{2,1,0:T(8,128)(2,1)}, bf16[768,768]{1,0:T(8,128)(2,1)}, f32[768,768]{1,0:T(8,128)}, f32[1,768...) custom-call(bf16[2,768,768]{2,1,0:T(8,128)(2,1)} %bitcast.114, f32[2,768,768]{2,1,0:T(8,128)} %get-tuple-element.87.refs_1_, ...), custom_call_target="tpu_custom_call" | custom-call | flops 99999997952 | bytes 1000000 | tf_op jit(solution)/shard_map/mixed/pallas_call | solution.py:78
  319.4 2.6 collective-permute-start.12
  325.4 4.3 add_convert_fusion.4
  329.8 13.8 %qkvg_grad.1 = (bf16[32,192,384]{2,1,0:T(8,128)(2,1)}, s32[1]{0:T(128)}) custom-call(bf16[2,768,768]{2,1,0:T(8,128)(2,1)} %get-tuple-element.130.refs_0_, bf16[2,768,3072]{2,1,0:T(8,128)(2,1)} %get-tuple-element.126.refs_1_.refs_2_, bf16[4,48,768]{2,1,0:T(8,128)(2,1)} %fusion.refs_2_.refs_3_, bf16[1,4,48,768]{3,2,1,0:T(8,128)(2,1)} %add_convert_fusion.41.refs_3_, ...), custom_call_target="tpu_custom_call" | custom-call | flops 99999997952 | bytes 1000000 | tf_op jit(solution)/shard_map/qkvg_grad/pallas_call | solution.py:78
  350.1 16.3 %outputs.1 = (bf16[2,768,768]{2,1,0:T(8,128)(2,1)}, bf16[768,1536]{1,0:T(8,128)(2,1)}, f32[1,768]{1,0:T(1,128)}, s32[1]{0:T(128)}) custom-call(bf16[2,768,768]{2,1,0:T(8,128)(2,1)} %bitcast.118, bf16[2,768,768]{2,1,0:T(8,128)(2,1)} %bitcast.115, bf16[2,768,3072]{2,1,0:T(8,128)(2,1)} %get-tuple-element.126.refs_1_.refs_2_, ...), custom_call_target="tpu_custom_call" | custom-call | flops 99999997952 | bytes 1000000 | tf_op jit(solution)/shard_map/outputs/pallas_call | solution.py:78
  373.7 4.4 add_convert_fusion.2
  378.1 9.8 %conditions.1 = (bf16[32,120,384]{2,1,0:T(8,128)(2,1)}, f32[16,60,384]{2,1,0:T(8,128)}, s32[1]{0:T(128)}) custom-call(bf16[768,384]{1,0:T(8,128)(2,1)} %bitcast.121, f32[1,768]{1,0:T(1,128)} %get-tuple-element.245.refs_3_.refs_1_, bf16[384,3072]{1,0:T(8,128)(2,1)} %refs_2_.2, bf16[384,1536]{1,0:T(8,128)(2,1)} %refs_3_.3, ...), custom_call_target="tpu_custom_call" | custom-call | flops 99999997952 | bytes 1000000 | tf_op jit(solution)/shard_map/conditions/pallas_call | solution.py:78
  393.1 2.5 collective-permute-start.23
  400.4 9.4 %collective-permute-done.23 = bf16[1,4,48,768]{3,2,1,0:T(8,128)(2,1)S(1)} collective-permute-done((bf16[1,4,48,768]{3,2,1,0:T(8,128)(2,1)}, bf16[1,4,48,768]{3,2,1,0:T(8,128)(2,1)S(1)}, u32[]{:S(2)}, u32[]{:S(2)}) %collective-permute-start.23) | collective-permute-done | bytes 294944 | tf_op jit(solution)/shard_map/ppermute | solution.py:158
  411.6 5.8 %collective-permute-done.24 = bf16[8,192,384]{2,1,0:T(8,128)(2,1)} collective-permute-done((bf16[8,192,384]{2,1,0:T(8,128)(2,1)}, bf16[8,192,384]{2,1,0:T(8,128)(2,1)}, u32[]{:S(2)}, u32[]{:S(2)}) %collective-permute-start.24) | collective-permute-done | bytes 1179680 | tf_op jit(solution)/shard_map/ppermute | solution.py:158
  426.6 24.4 %pair_backward.1 = (f32[48,768,128]{2,1,0:T(8,128)}, f32[16,128]{1,0:T(8,128)}, s32[1]{0:T(128)}) custom-call(bf16[48,768,128]{2,1,0:T(8,128)(2,1)} %bitcast.111, f32[1,128]{1,0:T(1,128)} %slice.125.refs_1_, bf16[16,128]{1,0:T(8,128)(2,1)} %bitcast.104, bf16[4,48,768]{2,1,0:T(8,128)(2,1)} %fusion.refs_2_.refs_3_, bf16[4,48,768]{2,1,0:T(8,128)(2,1)} %fusion.1.refs_6_.refs_4_, ...), custom_call_target="tpu_custom_call" | custom-call | flops 99999997952 | bytes 1000000 | tf_op jit(solution)/shard_map/pair_backward/pallas_call | solution.py:78
  461.1 2.6 collective-permute-start.33
  472.0 4.0 collective-permute-done.33
  501.7 2.7 collective-permute-start.43
  (239 shorter events, 99.8 us)
Async XLA Ops:
  7.2 116.8 %all-gather.3.cloned.1.call-start = ((), (), s32[]{:S(2)}) async-start(), calls=%async_computation | async-start | bytes 20054016 | tf_op jit(solution)/shard_map/all_gather | solution.py:818
  80.4 24.1 %collective-permute-start = (bf16[32,360,384]{2,1,0:T(8,128)(2,1)}, bf16[32,360,384]{2,1,0:T(8,128)(2,1)}, u32[]{:S(2)}, u32[]{:S(2)}) collective-permute-start(bf16[32,360,384]{2,1,0:T(8,128)(2,1)} %get-tuple-element.86.refs_11_), channel_id=1, source_target_pairs={{0,1},{1,0},{2,3},{3,2},{4,5},{5,4},{6,7},{7,6},{8,9},{9,8},{10,11... | collective-permute-start | bytes 26542088 | tf_op jit(solution)/shard_map/ppermute | solution.py:158
  110.7 51.6 %collective-permute-start.1 = (bf16[8,360,384]{2,1,0:T(8,128)(2,1)}, bf16[8,360,384]{2,1,0:T(8,128)(2,1)}, u32[]{:S(2)}, u32[]{:S(2)}) collective-permute-start(bf16[8,360,384]{2,1,0:T(8,128)(2,1)} %get-tuple-element.191.refs_9_), channel_id=1, source_target_pairs={{0,16},{16,0},{1,17},{17,1},{2,18},{18,2},{3,19},{19,3},{4,20},{20... | collective-permute-start | bytes 6635528 | tf_op jit(solution)/shard_map/ppermute | solution.py:158
  148.9 48.2 %collective-permute-start.2 = (bf16[16,4,48,768]{3,2,1,0:T(8,128)(2,1)}, bf16[16,4,48,768]{3,2,1,0:T(8,128)(2,1)}, u32[]{:S(2)}, u32[]{:S(2)}) collective-permute-start(bf16[16,4,48,768]{3,2,1,0:T(8,128)(2,1)} %get-tuple-element.102.refs_9_), channel_id=1, source_target_pairs={{0,1},{1,0},{2,3},{3,2},{4,5},{5,4},{6,7},{7,6},{8,9},{9,8},{10,11... | collective-permute-start | bytes 14155784 | tf_op jit(solution)/shard_map/ppermute | solution.py:158
  165.6 27.6 %collective-permute-start.3 = (bf16[4,360,384]{2,1,0:T(8,128)(2,1)}, bf16[4,360,384]{2,1,0:T(8,128)(2,1)S(1)}, u32[]{:S(2)}, u32[]{:S(2)}) collective-permute-start(bf16[4,360,384]{2,1,0:T(8,128)(2,1)} %get-tuple-element.205.refs_10_), channel_id=1, source_target_pairs={{0,4},{1,5},{2,6},{3,7},{4,0},{5,1},{6,2},{7,3},{8,12},{9,13},{10,... | collective-permute-start | bytes 3317768 | tf_op jit(solution)/shard_map/ppermute | solution.py:158
  193.1 37.3 %collective-permute-start.5 = (bf16[16,4,48,768]{3,2,1,0:T(8,128)(2,1)}, bf16[16,4,48,768]{3,2,1,0:T(8,128)(2,1)}, u32[]{:S(2)}, u32[]{:S(2)}) collective-permute-start(bf16[16,4,48,768]{3,2,1,0:T(8,128)(2,1)} %get-tuple-element.106.refs_10_), channel_id=1, source_target_pairs={{0,1},{1,0},{2,3},{3,2},{4,5},{5,4},{6,7},{7,6},{8,9},{9,8},{10,11... | collective-permute-start | bytes 14155784 | tf_op jit(solution)/shard_map/ppermute | solution.py:158
  194.5 40.5 %collective-permute-start.6 = (bf16[2,360,384]{2,1,0:T(8,128)(2,1)}, bf16[2,360,384]{2,1,0:T(8,128)(2,1)S(1)}, u32[]{:S(2)}, u32[]{:S(2)}) collective-permute-start(bf16[2,360,384]{2,1,0:T(8,128)(2,1)} %get-tuple-element.217.refs_11_), channel_id=1, source_target_pairs={{0,8},{1,9},{2,10},{3,11},{4,12},{5,13},{6,14},{7,15},{8,0},{9,1},... | collective-permute-start | bytes 1658888 | tf_op jit(solution)/shard_map/ppermute | solution.py:158
  201.1 36.3 %collective-permute-start.4 = (bf16[4,4,48,768]{3,2,1,0:T(8,128)(2,1)}, bf16[4,4,48,768]{3,2,1,0:T(8,128)(2,1)}, u32[]{:S(2)}, u32[]{:S(2)}) collective-permute-start(bf16[4,4,48,768]{3,2,1,0:T(8,128)(2,1)} %get-tuple-element.201.refs_9_), channel_id=1, source_target_pairs={{0,2},{1,3},{2,0},{3,1},{4,6},{5,7},{6,4},{7,5},{8,10},{9,11},{10,... | collective-permute-start | bytes 3538952 | tf_op jit(solution)/shard_map/ppermute | solution.py:158
  234.5 41.7 %collective-permute-start.8 = (bf16[4,4,48,768]{3,2,1,0:T(8,128)(2,1)}, bf16[4,4,48,768]{3,2,1,0:T(8,128)(2,1)}, u32[]{:S(2)}, u32[]{:S(2)}) collective-permute-start(bf16[4,4,48,768]{3,2,1,0:T(8,128)(2,1)} %get-tuple-element.199.refs_10_), channel_id=1, source_target_pairs={{0,2},{1,3},{2,0},{3,1},{4,6},{5,7},{6,4},{7,5},{8,10},{9,11},{10,... | collective-permute-start | bytes 3538952 | tf_op jit(solution)/shard_map/ppermute | solution.py:158
  235.0 55.1 %collective-permute-start.9 = (bf16[16,4,48,768]{3,2,1,0:T(8,128)(2,1)}, bf16[16,4,48,768]{3,2,1,0:T(8,128)(2,1)}, u32[]{:S(2)}, u32[]{:S(2)}) collective-permute-start(bf16[16,4,48,768]{3,2,1,0:T(8,128)(2,1)} %get-tuple-element.109.refs_11_), channel_id=1, source_target_pairs={{0,1},{1,0},{2,3},{3,2},{4,5},{5,4},{6,7},{7,6},{8,9},{9,8},{10,11... | collective-permute-start | bytes 14155784 | tf_op jit(solution)/shard_map/ppermute | solution.py:158
  235.9 32.6 %collective-permute-start.10 = (bf16[1,360,384]{2,1,0:T(8,128)(2,1)}, bf16[1,360,384]{2,1,0:T(8,128)(2,1)}, u32[]{:S(2)}, u32[]{:S(2)}) collective-permute-start(bf16[1,360,384]{2,1,0:T(8,128)(2,1)} %add_convert_fusion.46.refs_12_), channel_id=1, source_target_pairs={{0,2},{1,3},{2,0},{3,1},{4,6},{5,7},{6,4},{7,5},{8,10},{9,11},{10,... | collective-permute-start | bytes 829448 | tf_op jit(solution)/shard_map/ppermute | solution.py:158
  272.4 16.5 %collective-permute-start.7 = (bf16[2,4,48,768]{3,2,1,0:T(8,128)(2,1)}, bf16[2,4,48,768]{3,2,1,0:T(8,128)(2,1)S(1)}, u32[]{:S(2)}, u32[]{:S(2)}) collective-permute-start(bf16[2,4,48,768]{3,2,1,0:T(8,128)(2,1)} %get-tuple-element.215.refs_9_), channel_id=1, source_target_pairs={{0,4},{1,5},{2,6},{3,7},{4,0},{5,1},{6,2},{7,3},{8,12},{9,13},{10,... | collective-permute-start | bytes 1769480 | tf_op jit(solution)/shard_map/ppermute | solution.py:158
  278.6 38.9 %collective-permute-start.11 = (bf16[2,4,48,768]{3,2,1,0:T(8,128)(2,1)}, bf16[2,4,48,768]{3,2,1,0:T(8,128)(2,1)}, u32[]{:S(2)}, u32[]{:S(2)}) collective-permute-start(bf16[2,4,48,768]{3,2,1,0:T(8,128)(2,1)} %get-tuple-element.213.refs_23_), channel_id=1, source_target_pairs={{0,4},{1,5},{2,6},{3,7},{4,0},{5,1},{6,2},{7,3},{8,12},{9,13},{10,... | collective-permute-start | bytes 1769480 | tf_op jit(solution)/shard_map/ppermute | solution.py:158
  280.1 45.3 %collective-permute-start.15 = (bf16[16,4,48,768]{3,2,1,0:T(8,128)(2,1)}, bf16[16,4,48,768]{3,2,1,0:T(8,128)(2,1)}, u32[]{:S(2)}, u32[]{:S(2)}) collective-permute-start(bf16[16,4,48,768]{3,2,1,0:T(8,128)(2,1)} %get-tuple-element.124.refs_25_), channel_id=1, source_target_pairs={{0,1},{1,0},{2,3},{3,2},{4,5},{5,4},{6,7},{7,6},{8,9},{9,8},{10,11... | collective-permute-start | bytes 14155784 | tf_op jit(solution)/shard_map/ppermute | solution.py:158
  289.8 32.1 %collective-permute-start.13 = (bf16[1,4,48,768]{3,2,1,0:T(8,128)(2,1)}, bf16[1,4,48,768]{3,2,1,0:T(8,128)(2,1)}, u32[]{:S(2)}, u32[]{:S(2)}) collective-permute-start(bf16[1,4,48,768]{3,2,1,0:T(8,128)(2,1)} %add_convert_fusion.43.refs_22_), channel_id=1, source_target_pairs={{0,8},{1,9},{2,10},{3,11},{4,12},{5,13},{6,14},{7,15},{8,0},{9,1},... | collective-permute-start | bytes 884744 | tf_op jit(solution)/shard_map/ppermute | solution.py:158
  294.2 29.6 %collective-permute-start.14 = (bf16[4,4,48,768]{3,2,1,0:T(8,128)(2,1)}, bf16[4,4,48,768]{3,2,1,0:T(8,128)(2,1)S(1)}, u32[]{:S(2)}, u32[]{:S(2)}) collective-permute-start(bf16[4,4,48,768]{3,2,1,0:T(8,128)(2,1)} %get-tuple-element.197.refs_24_), channel_id=1, source_target_pairs={{0,2},{1,3},{2,0},{3,1},{4,6},{5,7},{6,4},{7,5},{8,10},{9,11},{10,... | collective-permute-start | bytes 3538952 | tf_op jit(solution)/shard_map/ppermute | solution.py:158
  319.4 27.7 %collective-permute-start.12 = (bf16[1,4,48,768]{3,2,1,0:T(8,128)(2,1)}, bf16[1,4,48,768]{3,2,1,0:T(8,128)(2,1)}, u32[]{:S(2)}, u32[]{:S(2)}) collective-permute-start(bf16[1,4,48,768]{3,2,1,0:T(8,128)(2,1)} %add_convert_fusion.41.refs_3_), channel_id=1, source_target_pairs={{0,8},{1,9},{2,10},{3,11},{4,12},{5,13},{6,14},{7,15},{8,0},{9,1},... | collective-permute-start | bytes 884744 | tf_op jit(solution)/shard_map/ppermute | solution.py:158
  324.9 24.1 %collective-permute-start.17 = (bf16[2,4,48,768]{3,2,1,0:T(8,128)(2,1)}, bf16[2,4,48,768]{3,2,1,0:T(8,128)(2,1)S(1)}, u32[]{:S(2)}, u32[]{:S(2)}) collective-permute-start(bf16[2,4,48,768]{3,2,1,0:T(8,128)(2,1)} %get-tuple-element.211.refs_4_), channel_id=1, source_target_pairs={{0,4},{1,5},{2,6},{3,7},{4,0},{5,1},{6,2},{7,3},{8,12},{9,13},{10,... | collective-permute-start | bytes 1769480 | tf_op jit(solution)/shard_map/ppermute | solution.py:158
  345.5 25.5 %collective-permute-start.19 = (bf16[4,4,48,768]{3,2,1,0:T(8,128)(2,1)}, bf16[4,4,48,768]{3,2,1,0:T(8,128)(2,1)S(1)}, u32[]{:S(2)}, u32[]{:S(2)}) collective-permute-start(bf16[4,4,48,768]{3,2,1,0:T(8,128)(2,1)} %get-tuple-element.195.refs_5_), channel_id=1, source_target_pairs={{0,2},{1,3},{2,0},{3,1},{4,6},{5,7},{6,4},{7,5},{8,10},{9,11},{10,... | collective-permute-start | bytes 3538952 | tf_op jit(solution)/shard_map/ppermute | solution.py:158
  347.1 26.6 %collective-permute-start.20 = (bf16[32,192,384]{2,1,0:T(8,128)(2,1)}, bf16[32,192,384]{2,1,0:T(8,128)(2,1)}, u32[]{:S(2)}, u32[]{:S(2)}) collective-permute-start(bf16[32,192,384]{2,1,0:T(8,128)(2,1)} %get-tuple-element.132.refs_8_), channel_id=1, source_target_pairs={{0,1},{1,0},{2,3},{3,2},{4,5},{5,4},{6,7},{7,6},{8,9},{9,8},{10,11... | collective-permute-start | bytes 14155784 | tf_op jit(solution)/shard_map/ppermute | solution.py:158
  349.8 19.3 %collective-permute-start.18 = (bf16[1,4,48,768]{3,2,1,0:T(8,128)(2,1)}, bf16[1,4,48,768]{3,2,1,0:T(8,128)(2,1)}, u32[]{:S(2)}, u32[]{:S(2)}) collective-permute-start(bf16[1,4,48,768]{3,2,1,0:T(8,128)(2,1)} %add_convert_fusion.37.refs_7_), channel_id=1, source_target_pairs={{0,8},{1,9},{2,10},{3,11},{4,12},{5,13},{6,14},{7,15},{8,0},{9,1},... | collective-permute-start | bytes 884744 | tf_op jit(solution)/shard_map/ppermute | solution.py:158
  372.1 20.0 %collective-permute-start.21 = (bf16[2,4,48,768]{3,2,1,0:T(8,128)(2,1)}, bf16[2,4,48,768]{3,2,1,0:T(8,128)(2,1)S(1)}, u32[]{:S(2)}, u32[]{:S(2)}) collective-permute-start(bf16[2,4,48,768]{3,2,1,0:T(8,128)(2,1)} %get-tuple-element.209.refs_16_), channel_id=1, source_target_pairs={{0,4},{1,5},{2,6},{3,7},{4,0},{5,1},{6,2},{7,3},{8,12},{9,13},{10,... | collective-permute-start | bytes 1769480 | tf_op jit(solution)/shard_map/ppermute | solution.py:158
  389.2 28.2 %collective-permute-start.24 = (bf16[8,192,384]{2,1,0:T(8,128)(2,1)}, bf16[8,192,384]{2,1,0:T(8,128)(2,1)}, u32[]{:S(2)}, u32[]{:S(2)}) collective-permute-start(bf16[8,192,384]{2,1,0:T(8,128)(2,1)} %get-tuple-element.193.refs_17_), channel_id=1, source_target_pairs={{0,16},{16,0},{1,17},{17,1},{2,18},{18,2},{3,19},{19,3},{4,20},{20... | collective-permute-start | bytes 3538952 | tf_op jit(solution)/shard_map/ppermute | solution.py:158
  392.0 28.3 %collective-permute-start.22 = (f32[16,60,384]{2,0,1:T(8,128)S(1)}, f32[16,60,384]{2,0,1:T(8,128)}, u32[]{:S(2)}, u32[]{:S(2)}) collective-permute-start(f32[16,60,384]{2,0,1:T(8,128)S(1)} %copy.45), channel_id=1, source_target_pairs={{0,1},{1,0},{2,3},{3,2},{4,5},{5,4},{6,7},{7,6},{8,9},{9,8},{10,11... | collective-permute-start | bytes 4423688 | tf_op jit(solution)/shard_map/ppermute | solution.py:158
  393.1 16.7 %collective-permute-start.23 = (bf16[1,4,48,768]{3,2,1,0:T(8,128)(2,1)}, bf16[1,4,48,768]{3,2,1,0:T(8,128)(2,1)S(1)}, u32[]{:S(2)}, u32[]{:S(2)}) collective-permute-start(bf16[1,4,48,768]{3,2,1,0:T(8,128)(2,1)} %add_convert_fusion.34.refs_0_), channel_id=1, source_target_pairs={{0,8},{1,9},{2,10},{3,11},{4,12},{5,13},{6,14},{7,15},{8,0},{9,1},... | collective-permute-start | bytes 884744 | tf_op jit(solution)/shard_map/ppermute | solution.py:158
  395.6 28.4 %collective-permute-start.25 = (bf16[32,120,384]{2,1,0:T(8,128)(2,1)}, bf16[32,120,384]{2,1,0:T(8,128)(2,1)}, u32[]{:S(2)}, u32[]{:S(2)}) collective-permute-start(bf16[32,120,384]{2,1,0:T(8,128)(2,1)} %get-tuple-element.148.refs_1_), channel_id=1, source_target_pairs={{0,1},{1,0},{2,3},{3,2},{4,5},{5,4},{6,7},{7,6},{8,9},{9,8},{10,11... | collective-permute-start | bytes 8847368 | tf_op jit(solution)/shard_map/ppermute | solution.py:158
  419.9 39.3 %collective-permute-start.28 = (bf16[4,192,384]{2,1,0:T(8,128)(2,1)}, bf16[4,192,384]{2,1,0:T(8,128)(2,1)}, u32[]{:S(2)}, u32[]{:S(2)}) collective-permute-start(bf16[4,192,384]{2,1,0:T(8,128)(2,1)} %get-tuple-element.207.refs_8_), channel_id=1, source_target_pairs={{0,4},{1,5},{2,6},{3,7},{4,0},{5,1},{6,2},{7,3},{8,12},{9,13},{10,... | collective-permute-start | bytes 1769480 | tf_op jit(solution)/shard_map/ppermute | solution.py:158
  423.5 31.4 %collective-permute-start.26 = (f32[4,60,384]{2,1,0:T(8,128)}, f32[4,60,384]{2,1,0:T(8,128)}, u32[]{:S(2)}, u32[]{:S(2)}) collective-permute-start(f32[4,60,384]{2,1,0:T(8,128)} %get-tuple-element.219.refs_10_), channel_id=1, source_target_pairs={{0,2},{1,3},{2,0},{3,1},{4,6},{5,7},{6,4},{7,5},{8,10},{9,11},{10,... | collective-permute-start | bytes 1105928 | tf_op jit(solution)/shard_map/ppermute | solution.py:158
  425.8 37.9 %collective-permute-start.27 = (bf16[8,120,384]{2,1,0:T(8,128)(2,1)S(1)}, bf16[8,120,384]{2,1,0:T(8,128)(2,1)S(1)}, u32[]{:S(2)}, u32[]{:S(2)}) collective-permute-start(bf16[8,120,384]{2,1,0:T(8,128)(2,1)S(1)} %get-tuple-element.203.refs_9_), channel_id=1, source_target_pairs={{0,16},{16,0},{1,17},{17,1},{2,18},{18,2},{3,19},{19,3},{4,20},{20... | collective-permute-start | bytes 2211848 | tf_op jit(solution)/shard_map/ppermute | solution.py:158
  461.1 14.9 %collective-permute-start.33 = (bf16[2,192,384]{2,1,0:T(8,128)(2,1)}, bf16[2,192,384]{2,1,0:T(8,128)(2,1)}, u32[]{:S(2)}, u32[]{:S(2)}) collective-permute-start(bf16[2,192,384]{2,1,0:T(8,128)(2,1)} %get-tuple-element.225.refs_3_), channel_id=1, source_target_pairs={{0,8},{1,9},{2,10},{3,11},{4,12},{5,13},{6,14},{7,15},{8,0},{9,1},... | collective-permute-start | bytes 884744 | tf_op jit(solution)/shard_map/ppermute | solution.py:158
  471.9 17.1 %collective-permute-start.35 = (f32[16,128]{1,0:T(8,128)S(1)}, f32[16,128]{1,0:T(8,128)S(1)}, u32[]{:S(2)}, u32[]{:S(2)}) collective-permute-start(f32[16,128]{1,0:T(8,128)S(1)} %add_add_fusion.6.refs_0_), channel_id=1, source_target_pairs={{0,1},{1,0},{2,3},{3,2},{4,5},{5,4},{6,7},{7,6},{8,9},{9,8},{10,11... | collective-permute-start | bytes 24584 | tf_op jit(solution)/shard_map/ppermute | solution.py:203
  485.9 14.2 %collective-permute-start.34 = (f32[12,384]{1,0:T(8,128)S(1)}, f32[12,384]{1,0:T(8,128)S(1)}, u32[]{:S(2)}, u32[]{:S(2)}) collective-permute-start(f32[12,384]{1,0:T(8,128)S(1)} %slice_bitcast_fusion), channel_id=1, source_target_pairs={{0,16},{16,0},{1,17},{17,1},{2,18},{18,2},{3,19},{19,3},{4,20},{20... | collective-permute-start | bytes 55304 | tf_op jit(solution)/shard_map/ppermute | solution.py:203
  (48 other events, 437.5 us)
Sparse Core Ops, SparseCore 0:
  22.3 101.6 all-gather.2

commit v3 on v2

v3 whole, which is shorter than its diff:
```python
import functools

import jax
import jax.numpy as jnp
from jax import lax
from jax.experimental import pallas as pl
from jax.experimental.pallas import tpu as pltpu
from jax.sharding import PartitionSpec as P

EPS = 1e-05
MASKED = -1000000000.0
F32 = jnp.float32
BF16 = jnp.bfloat16
CHUNK_HEADS = 2
WINDOW = 256
LANES = 128
PIECE = 384
LONG, SHORT = 10**11, 17 * 10**9
TOKENS = 128
HIDDEN = 768
VMEM_LIMIT = 60 * 2**20


def dot(left, right, left_dim=1, right_dim=0):
    return lax.dot_general(
        left, right, (((left_dim,), (right_dim,)), ((), ())), preferred_element_type=F32
    )


def layer_norm(values):
    center = values - jnp.mean(values, axis=-1, keepdims=True)
    inverse = lax.rsqrt(jnp.mean(center * center, axis=-1, keepdims=True) + EPS)
    return (center * inverse, inverse)


def norm_back(grad_in, normed, inverse):
    mean_grad = jnp.mean(grad_in, axis=-1, keepdims=True)
    mean_proj = jnp.mean(grad_in * normed, axis=-1, keepdims=True)
    return inverse * (grad_in - mean_grad - normed * mean_proj)


def slope(gate):
    return gate * (1.0 - gate)


def column_sum(values):
    return jnp.sum(values.reshape(-1, values.shape[-1]), axis=0, keepdims=True)


def clear(step, *refs):
    @pl.when(step == 0)
    def _():
        for ref in refs:
            ref[...] = jnp.zeros_like(ref)


def spec(block, along=None, at=None):
    rank = len(block)
    if along is not None:
        return pl.BlockSpec(block, lambda t, core: tuple(t if a == along else 0 for a in range(rank)))
    index = (0,) * rank if at is None else at
    return pl.BlockSpec(
        block,
        lambda t, core: tuple(i(core[0]) if callable(i) else i for i in index),
        pipeline_mode=pl.Buffered(1),
    )


class Order:
    def __init__(self, place):
        self.place = place
        self.last = []


def call(name, kernel, grid, ins, outs, scratch, deps, order, flops=LONG, aliases={}):
    inputs = len(ins)
    deps = list(deps) + order.last

    def run(place_ref, *refs):
        kernel(place_ref, *refs[:inputs], *refs[inputs + len(deps) :])

    found = pl.pallas_call(
        run,
        grid_spec=pltpu.PrefetchScalarGridSpec(
            num_scalar_prefetch=1,
            grid=(grid,),
            in_specs=[s for _, s in ins] + [pl.BlockSpec(memory_space=pl.ANY)] * len(deps),
            out_specs=[s for _, _, s in outs],
            scratch_shapes=scratch,
        ),
        out_shape=[jax.ShapeDtypeStruct(shape, dtype) for shape, dtype, _ in outs],
        compiler_params=pltpu.CompilerParams(
            vmem_limit_bytes=VMEM_LIMIT, dimension_semantics=("arbitrary",)
        ),
        cost_estimate=pl.CostEstimate(flops=flops, bytes_accessed=10**6, transcendentals=0),
        name=name,
        input_output_aliases=aliases,
    )(order.place, *[a for a, _ in ins], *deps)
    order.last = [max(found, key=lambda array: array.size)]
    return found


def combine(outputs, order):
    ins, outs, plan = [], [], []
    for terms in outputs:
        if isinstance(terms, tuple):
            bit, *arrays = terms
            terms = [(array, array.shape[0], lambda place: 0) for array in arrays]
        else:
            bit = None
        array, slabs, _ = terms[0]
        shape = (slabs,) + array.shape[1:]
        rest = (0,) * (len(shape) - 1)
        plan.append((bit, list(range(len(ins), len(ins) + len(terms)))))
        for term, _, index in terms:
            ins.append(
                (term, pl.BlockSpec(shape, lambda t, place, index=index, rest=rest: (index(place),) + rest))
            )
        outs.append((shape, array.dtype, pl.BlockSpec(shape, lambda t, place, rest=rest: (0,) + rest)))

    def kernel(place, *refs):
        for (bit, sources), out_ref in zip(plan, refs[len(ins) :]):
            values = [refs[i][...] for i in sources]
            if bit is not None:
                out_ref[...] = jnp.where(place[bit] == 0, values[0], values[1])
            elif len(values) == 1:
                out_ref[...] = values[0]
            else:
                total = sum((v.astype(F32) for v in values[1:]), values[0].astype(F32))
                out_ref[...] = total.astype(out_ref.dtype)

    return call("combine", kernel, 1, ins, outs, [], [], order)


class Halving:
    def __init__(self, order, counts):
        self.order = order
        self.counts = counts

    def places(self):
        found = []
        for p in range(2 ** len(self.order)):
            dest, half = 0, 0
            for i, (axis, bit) in enumerate(self.order):
                value = (p >> (len(self.order) - 1 - i)) & 1
                if axis == "sample":
                    dest |= value << bit
                else:
                    half = value
            found.append((dest, half))
        return found

    def halves(self):
        return 2 if any(axis == "struct" for axis, _ in self.order) else 1

    def pieces(self, shape):
        rows, columns = shape
        return rows // self.counts["sample"], columns // self.halves() // PIECE

    def slabs(self, shapes):
        return (2 ** len(self.order), sum(r * c for r, c in map(self.pieces, shapes)), PIECE)

    def pack(self, out_ref, arrays, everywhere=()):
        for p, (dest, half) in enumerate(self.places()):
            held = []
            for array in arrays:
                rows, count = self.pieces(array.shape)
                for c in range(count):
                    at = (half * count + c) * PIECE
                    held.append(array[dest * rows : (dest + 1) * rows, at : at + PIECE])
            slab = jnp.concatenate(held + list(everywhere), axis=0)
            out_ref[p, : slab.shape[0]] = slab.astype(out_ref.dtype)
            if slab.shape[0] < out_ref.shape[1]:
                out_ref[p, slab.shape[0] :] = jnp.zeros(
                    (out_ref.shape[1] - slab.shape[0], PIECE), out_ref.dtype
                )

    def unpack(self, slab, shapes):
        found, at = [], 0
        for shape in shapes:
            rows, count = self.pieces(shape)
            found.append([slab[at + c * rows : at + (c + 1) * rows] for c in range(count)])
            at += rows * count
        return found

    def run(self, array, after="sum"):
        last = self.counts["sample"].bit_length() - 1

        def exchange(array, axis, bit):
            return lax.ppermute(array, axis, [(i, i ^ (1 << bit)) for i in range(self.counts[axis])])

        def halves(at, size):
            return [
                [
                    (p, size, lambda place, base=base, at=at, flip=flip: 2 * base(place) + (place[at] ^ flip))
                    for p, base in parts
                ]
                for flip in (1, 0)
            ]

        zero = lambda place: 0
        parts, size = [(array, zero)], array.shape[0]
        for axis, bit in self.order:
            at = bit if axis == "sample" else last
            size = size // 2
            if len(parts) == 1 and (axis, bit) == ("sample", 0):
                parts = [(array, lambda place: place[0]), (exchange(array, axis, bit), lambda place: place[0])]
                continue
            if len(parts) == 1:
                (sent,) = yield halves(at, size)[:1]
                parts = [(array, lambda place, at=at: place[at]), (exchange(sent, axis, bit), zero)]
            else:
                sent, kept = yield halves(at, size)
                parts = [(kept, zero), (exchange(sent, axis, bit), zero)]
        if after in ("swap", "cores"):
            sent, kept = yield halves(0, size // 2)
            return kept[0], exchange(sent, "sample", 0)[0] if after == "swap" else sent[0]
        (held,) = yield [[(p, 1, base) for p, base in parts]]
        if not after:
            return held[0]
        if self.halves() == 2:
            received = exchange(held, "struct", 0)
            first, second = yield [(last, held, received), (last, received, held)]
            return first[0], second[0]
        for bit in range(self.counts["struct"].bit_length() - 1):
            received = exchange(held, "struct", bit)
            (held,) = yield [[(p, 1, zero) for p in (held, received)]]
        return held[0]

class Running:
    def __init__(self, steps):
        self.steps = steps
        self.result = None
        self.send(None)

    def send(self, found):
        try:
            self.asked = self.steps.send(found)
        except StopIteration as stop:
            self.asked = []
            self.result = stop.value


def advance(order, *running):
    running = [r for r in running if r.result is None]
    asked = [output for r in running for output in r.asked]
    if not asked:
        return []
    made = combine(asked, order)
    at = 0
    for r in running:
        count = len(r.asked)
        r.send(made[at : at + count])
        at += count
    return made


def pair_forward_kernel(place, pair_ref, gain_ref, weight_ref, mask_ref, lengths_ref, out_ref, terms):
    gain = gain_ref[...].astype(F32)
    rows, length, channels = pair_ref.shape
    average = jnp.full((channels, channels), 1.0 / channels, BF16)
    position = lax.broadcasted_iota(jnp.int32, (1, length), 1)
    valid = (position < lengths_ref[0]) & ((mask_ref[...] == 1) | (position == 0))
    for i in range(rows):
        values = pair_ref[i]
        center = values.astype(F32) - dot(values, average)
        inverse = lax.rsqrt(jnp.mean(center * center, axis=-1, keepdims=True) + EPS)
        affine = (center * inverse * gain).astype(BF16)
        terms[i] = jnp.where(valid, dot(weight_ref[...], affine, 1, 1), MASKED)
    for h in range(terms.shape[1]):
        out_ref[h] = terms[:, h, :].astype(BF16)


def pair_forward(pair, gain, weight_t, mask, lengths, order):
    rows, length, channels = pair.shape
    heads = weight_t.shape[0]
    block = 16 if rows % 16 == 0 else rows
    return call(
        "pair_forward",
        pair_forward_kernel,
        rows // block,
        [
            (pair, spec((block, length, channels), 0)),
            (gain, spec(gain.shape)),
            (weight_t, spec(weight_t.shape)),
            (mask, spec(mask.shape)),
            (lengths, pl.BlockSpec(memory_space=pltpu.SMEM)),
        ],
        [((heads, rows, length), BF16, spec((heads, block, length), 1))],
        [pltpu.VMEM((block, heads, length), F32)],
        [],
        order,
    )[0]


def pair_backward_kernel(chunks, place, pair_ref, gain_ref, weight_ref, *refs):
    grad_refs, (out_ref, weight_grad_ref, grads) = refs[:chunks], refs[-3:]
    gain = gain_ref[...]
    channels = pair_ref.shape[2]
    average = jnp.full((channels, channels), 1.0 / channels, BF16)
    clear(pl.program_id(0), weight_grad_ref)
    head = 0
    for ref in grad_refs:
        for h in range(ref.shape[0]):
            grads[:, head, :] = ref[h].astype(F32)
            head += 1
    scaled = weight_ref[...].astype(F32) * gain
    means = jnp.broadcast_to(jnp.mean(scaled, axis=-1, keepdims=True), scaled.shape)
    full = jnp.concatenate([scaled, means], axis=1)
    high = full.astype(BF16)
    parts = jnp.concatenate([high, (full - high.astype(F32)).astype(BF16)], axis=0)

    def row(i, carry):
        values = pair_ref[i]
        center = values.astype(F32) - dot(values, average)
        inverse = lax.rsqrt(jnp.mean(center * center, axis=-1, keepdims=True) + EPS)
        normed = center * inverse
        grad = grads[i].astype(BF16)
        weight_grad_ref[...] += dot(grad, (normed * gain).astype(BF16))
        both = dot(jnp.concatenate([grad, grad], axis=0), parts, 0, 0)
        grad_normed = both[:, :channels]
        mean_proj = jnp.mean(grad_normed * normed, axis=-1, keepdims=True)
        out_ref[i] = inverse * (grad_normed - both[:, channels:] - normed * mean_proj)
        return carry

    lax.fori_loop(0, pair_ref.shape[0], row, 0, unroll=8)


def pair_backward(first, count, block, out, pair, grads, gain, weight_t, deps, order):
    rows, length, channels = pair.shape
    heads = weight_t.shape[0]
    blocked = pl.BlockSpec((block, length, channels), lambda t, place: (first + t, 0, 0))
    ins = [(pair, blocked), (gain, spec(gain.shape)), (weight_t, spec(weight_t.shape))] + [
        (g, pl.BlockSpec((g.shape[0], block, length), lambda t, place: (0, first + t, 0))) for g in grads
    ]
    aliases = {}
    if out is not None:
        aliases = {1 + len(ins): 0}
        ins.append((out, pl.BlockSpec(memory_space=pl.ANY)))
    return call(
        "pair_backward",
        functools.partial(pair_backward_kernel, len(grads)),
        count,
        ins,
        [(pair.shape, F32, blocked), ((heads, channels), F32, spec((heads, channels)))],
        [pltpu.VMEM((block, heads, length), F32)],
        deps,
        order,
        LONG,
        aliases,
    )


def conditions(cond_ref, gain_ref, cond_w_ref, cond_b_ref, zero_w_ref, zero_b_ref, zero_gate_ref, factor_ref, shift_ref):
    cond = cond_ref[...]
    width = zero_gate_ref.shape[1]
    zero_gate_ref[...] = jax.nn.sigmoid(dot(cond, zero_w_ref[...]) + zero_b_ref[...])
    cond_normed, _ = layer_norm(cond.astype(F32))
    projected = dot((cond_normed * gain_ref[...]).astype(BF16), cond_w_ref[...])
    factor_ref[...] = jax.nn.sigmoid(projected[:, :width] + cond_b_ref[...])
    shift_ref[...] = projected[:, width:]


def conditions_back(cond_ref, gain_ref, cond_w_ref, zero_w_ref, zero_grad, projected):
    cond = cond_ref[...]
    cond_normed, cond_inverse = layer_norm(cond.astype(F32))
    scaled = (cond_normed * gain_ref[...]).astype(BF16)
    grad_scaled = dot(projected, cond_w_ref[...], 1, 1)
    return (
        dot(scaled, projected, 0, 0),
        dot(cond, zero_grad, 0, 0),
        column_sum(grad_scaled * cond_normed),
        dot(zero_grad, zero_w_ref[...], 1, 1),
        grad_scaled * gain_ref[...],
        cond_normed,
        cond_inverse,
    )


def step_rows(step, tokens):
    return pl.ds(pl.multiple_of(step * tokens, tokens), tokens)


def window_start(chunk, head_dim, width):
    return min(chunk * CHUNK_HEADS * head_dim // LANES * LANES, width - WINDOW)


def inputs_kernel(
    place, acts_ref, acts_other_ref, cot_ref, cot_other_ref,
    cond_ref, gain_ref, cond_w_ref, cond_b_ref, zero_w_ref, zero_b_ref,
    query_ref, key_ref, value_ref, gate_w_ref, q_bias_ref, out_w_ref,
    input_ref, gate_ref, gated_grad_ref, q_ref, k_ref, v_ref, g_ref, qt_ref, kt_ref, vt_ref, gt_ref,
    zero_gate_ref, factor_ref, shift_ref,
):
    step = pl.program_id(0)
    samples, tokens, half = gate_ref.shape
    width = acts_ref.shape[2]
    rows = samples * tokens

    @pl.when(step == 0)
    def _():
        conditions(
            cond_ref, gain_ref, cond_w_ref, cond_b_ref, zero_w_ref, zero_b_ref, zero_gate_ref, factor_ref, shift_ref
        )

    here = step_rows(step, tokens)
    acts = jnp.concatenate([acts_ref[...], acts_other_ref[...]], axis=0)
    normed, _ = layer_norm(acts.astype(F32))
    first = (factor_ref[here, :][None] * normed + shift_ref[here, :][None]).astype(BF16)
    input_ref[...] = first
    first = first.reshape(rows, width)
    cot = jnp.concatenate([cot_ref[...], cot_other_ref[...]], axis=0)
    grad_att = (cot.astype(F32) * zero_gate_ref[here, :][None]).astype(BF16)
    grad_gated = dot(grad_att.reshape(rows, width), out_w_ref[...], 1, 1)
    gated_grad_ref[...] = grad_gated.reshape(samples, tokens, half)
    gate = jax.nn.sigmoid(dot(first, gate_w_ref[...]))
    gate_ref[...] = gate.reshape(samples, tokens, half)

    def put(values, nat_ref, t_ref):
        low = values.astype(BF16).reshape(samples, tokens, half)
        for window in range(nat_ref.shape[0]):
            nat_ref[window] = low[:, :, window * LANES : window * LANES + WINDOW]
        for s in range(samples):
            t_ref[s] = low[s].T

    put(grad_gated * gate, g_ref, gt_ref)
    put(dot(first, query_ref[...]) + q_bias_ref[...], q_ref, qt_ref)
    put(dot(first, key_ref[...]), k_ref, kt_ref)
    put(dot(first, value_ref[...]), v_ref, vt_ref)


def own(core):
    return core


def other(core):
    return 1 - core


def quarters(weight, whose):
    rows, columns = weight.shape
    return [
        (weight, spec((rows, columns // 8), at=(0, functools.partial(lambda j, core: 2 * j + whose(core), j))))
        for j in range(4)
    ]


def inputs_call(acts, acts_other, cot, cot_other, cond, branch, qkvg_w, q_bias, out_w, deps, order):
    own_samples, length, width = acts.shape
    samples, half = 2 * own_samples, width // 2
    windows = (half - WINDOW) // LANES + 1
    block = spec((own_samples, TOKENS, width), 1)
    wide = spec((samples, TOKENS, width), 1)
    narrow = spec((samples, TOKENS, half), 1)
    nat = spec((windows, samples, TOKENS, WINDOW), 2)
    turned = spec((samples, half, TOKENS), 2)
    return call(
        "inputs",
        inputs_kernel,
        length // TOKENS,
        [(a, block) for a in (acts, acts_other, cot, cot_other)]
        + [(cond, spec(cond.shape))]
        + branch
        + quarters(qkvg_w, own)
        + [(q_bias, spec((1, half), at=(0, own))), (out_w, spec((half, width), at=(own, 0)))],
        [
            ((samples, length, width), BF16, wide),
            ((samples, length, half), F32, narrow),
            ((samples, length, half), F32, narrow),
        ]
        + [((windows, samples, length, WINDOW), BF16, nat)] * 4
        + [((samples, half, length), BF16, turned)] * 4
        + [((length, width), F32, spec((length, width)))] * 2,
        [pltpu.VMEM((length, width), F32)],
        deps,
        order,
    )


def transition_kernel(
    halving, place, acts_ref, cot_ref, cond_ref, gain_ref, cond_w_ref, cond_b_ref, zero_w_ref, zero_b_ref,
    swiglu_ref, down_ref,
    partial_ref, acts_grad_ref, cond_gate_ref, cond_norm_ref, packed_out, cond_b_out, zero_b_out, gain_out,
    swiglu_acc, down_acc, zero_gate_ref, factor_ref, shift_ref, zero_low, projected,
):
    step = pl.program_id(0)
    clear(step, swiglu_acc, down_acc, cond_b_out, zero_b_out)
    samples, tokens, width = acts_ref.shape
    rows = samples * tokens
    hidden_width = down_ref.shape[0]

    @pl.when(step == 0)
    def _():
        conditions(
            cond_ref, gain_ref, cond_w_ref, cond_b_ref, zero_w_ref, zero_b_ref, zero_gate_ref, factor_ref, shift_ref
        )

    here = step_rows(step, tokens)
    zero_gate = zero_gate_ref[here, :]
    factor = factor_ref[here, :]
    acts = acts_ref[...].astype(F32)
    normed, _ = layer_norm(acts)
    second = (factor[None] * normed + shift_ref[here, :][None]).astype(BF16).reshape(rows, width)
    grad_out = cot_ref[...].astype(F32)
    grad_tr = (grad_out * zero_gate[None]).astype(BF16).reshape(rows, width)
    transition = grad_input = 0.0
    second_t = second.T
    for at in range(0, hidden_width, HIDDEN):
        gate_at, up_at = slice(at, at + HIDDEN), slice(hidden_width + at, hidden_width + at + HIDDEN)
        gate_part = dot(second, swiglu_ref[:, gate_at])
        up_part = dot(second, swiglu_ref[:, up_at])
        gate_sig = jax.nn.sigmoid(gate_part)
        silu = gate_part * gate_sig
        product = (silu * up_part).astype(BF16)
        transition += dot(product, down_ref[gate_at, :])
        grad_product = dot(grad_tr, down_ref[gate_at, :], 1, 1)
        down_acc[gate_at, :] += dot(product, grad_tr, 0, 0)
        grad_up = (grad_product * silu).astype(BF16)
        grad_gate = (grad_product * up_part * gate_sig * (1.0 + gate_part * (1.0 - gate_sig))).astype(BF16)
        swiglu_acc[:, gate_at] += dot(second_t, grad_gate)
        swiglu_acc[:, up_at] += dot(second_t, grad_up)
        grad_input += dot(grad_gate, swiglu_ref[:, gate_at], 1, 1)
        grad_input += dot(grad_up, swiglu_ref[:, up_at], 1, 1)
    transition = transition.reshape(samples, tokens, width)
    grad_input = grad_input.reshape(samples, tokens, width)
    partial_ref[...] = acts + zero_gate[None] * transition
    grad_zero = jnp.sum(grad_out * transition, axis=0) * slope(zero_gate)
    zero_b_out[...] += column_sum(grad_zero)
    zero_low[here, :] = grad_zero.astype(BF16)
    grad_factor = jnp.sum(grad_input * normed, axis=0) * slope(factor)
    cond_b_out[...] += column_sum(grad_factor)
    projected[here, :width] = grad_factor.astype(BF16)
    projected[here, width:] = jnp.sum(grad_input, axis=0).astype(BF16)
    acts_grad_ref[...] = grad_input * factor[None]

    @pl.when(step == pl.num_programs(0) - 1)
    def _():
        cond_w_grad, zero_w_grad, gain_grad, cond_gate, cond_norm, _, _ = conditions_back(
            cond_ref, gain_ref, cond_w_ref, zero_w_ref, zero_low[...], projected[...]
        )
        gain_out[...] = gain_grad
        cond_gate_ref[...] = cond_gate
        cond_norm_ref[...] = cond_norm
        halving.pack(packed_out, [swiglu_acc, down_acc, cond_w_grad, zero_w_grad])


def transition_call(acts, cot, cond, branch, swiglu, down, halving, deps, order):
    samples, length, width = acts.shape
    cond_width = cond.shape[1]
    hidden = down.shape[0]
    rows = samples * length
    block = spec((samples, TOKENS, width), 1)
    weights = [(width, 2 * hidden), (hidden, width), (cond_width, 2 * width), (cond_width, width)]
    vectors = [(1, width), (1, width), (1, cond_width)]
    results = call(
        "transition",
        functools.partial(transition_kernel, halving),
        length // TOKENS,
        [(acts, block), (cot, block), (cond, spec(cond.shape))]
        + branch
        + [(swiglu, spec(swiglu.shape)), (down, spec(down.shape))],
        [(acts.shape, F32, block)] * 2
        + [(cond.shape, F32, spec(cond.shape))] * 2
        + [(halving.slabs(weights), BF16, spec(halving.slabs(weights)))]
        + [(s, F32, spec(s)) for s in vectors],
        [pltpu.VMEM(s, F32) for s in weights[:2]]
        + [pltpu.VMEM((length, width), F32)] * 3
        + [pltpu.VMEM((length, width), BF16), pltpu.VMEM((length, 2 * width), BF16)],
        deps,
        order,
    )
    return results, weights


def attention_kernel(
    halving, head_dim, first_lane, place, q_ref, k_ref, v_ref, g_ref, qt_ref, kt_ref, vt_ref, gt_ref, bias_ref,
    mixed_ref, dq_ref, dkt_ref, dvt_ref, db_ref, kz, vz, plow, dslow, dsum,
):
    h = pl.program_id(0)
    samples, length, wide = q_ref.shape
    scale = head_dim ** (-0.5)
    off = pl.multiple_of(first_lane + h * head_dim, 16)
    lane = lax.broadcasted_iota(jnp.int32, (1, wide), 1)
    mask = ((lane >= off) & (lane < off + head_dim)).astype(BF16)

    @pl.when(h == 0)
    def _():
        mixed_ref[...] = jnp.zeros_like(mixed_ref)
        dq_ref[...] = jnp.zeros_like(dq_ref)

    kz[...] = jnp.zeros_like(kz)
    vz[...] = jnp.zeros_like(vz)
    for s in range(samples):
        kz[s, pl.ds(off, head_dim), :] = kt_ref[s]
        vz[s, pl.ds(off, head_dim), :] = vt_ref[s]
    parts, _, share, _ = bias_ref.shape
    if share % 16 == 0:
        bias = bias_ref[:, 0].reshape(length, length).astype(F32)
    else:
        bias = jnp.concatenate([bias_ref[p, 0].astype(F32) for p in range(parts)], axis=0)
    for s in range(samples):
        x = dot(q_ref[s], kz[s]) * scale + bias
        x = jnp.exp(x - jnp.max(x, axis=-1, keepdims=True))
        probs = x * (1.0 / jnp.sum(x, axis=-1, keepdims=True))
        low = probs.astype(BF16)
        plow[...] = low
        mixed = dot(low, v_ref[s] * mask)
        mixed_ref[s] += mixed
        grad = g_ref[s]
        delta = jnp.sum(grad.astype(F32) * mixed, axis=-1, keepdims=True)
        grad_scores = probs * (dot(grad, vz[s]) - delta)
        grad_low = (grad_scores * scale).astype(BF16)
        dslow[...] = grad_low
        total = grad_scores if s == 0 else dsum[...] + grad_scores
        if s < samples - 1:
            dsum[...] = total
        else:
            for p, (dest, _) in enumerate(halving.places()):
                for c in range(2):
                    at = (dest + c) * share
                    db_ref[2 * p + c, 0] = total[at : at + share].astype(BF16)
        dq_ref[s] += dot(grad_low, k_ref[s] * mask)
        dvt_ref[s] = dot(gt_ref[s], plow[...]).astype(BF16)
        dkt_ref[s] = dot(qt_ref[s], dslow[...]).astype(BF16)


def attention_call(chunk, nats, turned, bias, head_dim, halving, deps, order):
    _, samples, length, wide = nats[0].shape
    half = turned[0].shape[1]
    parts, heads, share, _ = bias.shape
    start = window_start(chunk, head_dim, half)
    nat = pl.BlockSpec((None, samples, length, wide), lambda h, core: (start // LANES, 0, 0, 0))
    turn = pl.BlockSpec((samples, head_dim, length), lambda h, core: (0, chunk * CHUNK_HEADS + h, 0))
    turn_out = pl.BlockSpec((samples, head_dim, length), lambda h, core: (0, h, 0))
    bias_in = pl.BlockSpec(
        (parts, 1, share, length), lambda h, core: (0, core[0] * (heads // 2) + chunk * CHUNK_HEADS + h, 0, 0)
    )
    bias_out = pl.BlockSpec((parts, 1, share, length), lambda h, core: (0, h, 0, 0))
    held = pl.BlockSpec((samples, length, wide), lambda h, core: (0, 0, 0))
    return call(
        "attention",
        functools.partial(attention_kernel, halving, head_dim, chunk * CHUNK_HEADS * head_dim - start),
        CHUNK_HEADS,
        [(a, nat) for a in nats] + [(a, turn) for a in turned] + [(bias, bias_in)],
        [((samples, length, wide), F32, held)] * 2
        + [((samples, CHUNK_HEADS * head_dim, length), BF16, turn_out)] * 2
        + [((parts, CHUNK_HEADS, share, length), BF16, bias_out)],
        [
            pltpu.VMEM((samples, wide, length), BF16),
            pltpu.VMEM((samples, wide, length), BF16),
            pltpu.VMEM((length, length), BF16),
            pltpu.VMEM((length, length), BF16),
            pltpu.VMEM((length, length), F32),
        ],
        deps,
        order,
        SHORT,
    )


def mixed_kernel(head_dim, chunks, place, *refs):
    (gate_ref, gated_grad_ref), refs = refs[:2], refs[2:]
    mixed_refs, refs = refs[:chunks], refs[chunks:]
    dq_refs, refs = refs[:chunks], refs[chunks:]
    dkt_refs, refs = refs[:chunks], refs[chunks:]
    dvt_refs, refs = refs[:chunks], refs[chunks:]
    gated_refs, joined_refs, q_bias_out = refs[:2], refs[2:4], refs[4]
    clear(pl.program_id(0), q_bias_out)
    samples, tokens, half = gate_ref.shape
    own_samples = samples // 2

    def join(window_refs):
        pieces = []
        for tile in range(half // LANES):
            held = [
                ref[:, :, tile * LANES - start : (tile + 1) * LANES - start]
                for chunk, ref in enumerate(window_refs)
                for start in [window_start(chunk, head_dim, half)]
                if start <= tile * LANES < start + WINDOW
            ]
            pieces.append(functools.reduce(jnp.add, held))
        return jnp.concatenate(pieces, axis=-1)

    def turn(turned_refs):
        joined = jnp.concatenate([ref[...] for ref in turned_refs], axis=1)
        return jnp.stack([joined[s].T for s in range(samples)], axis=0)

    mixed = join(mixed_refs)
    gate = gate_ref[...]
    gated = (gate * mixed).astype(BF16)
    grad_queries = join(dq_refs)
    q_bias_out[...] += column_sum(grad_queries)
    grad_gate = gated_grad_ref[...] * mixed * slope(gate)
    parts = [grad_queries.astype(BF16), turn(dkt_refs), turn(dvt_refs), grad_gate.astype(BF16)]
    for i in range(2):
        here = slice(i * own_samples, (i + 1) * own_samples)
        gated_refs[i][...] = gated[here]
        for j, part in enumerate(parts):
            joined_refs[i][:, :, j * half : (j + 1) * half] = part[here]


def mixed_call(gate, gated_grad, mixeds, dqs, dkts, dvts, head_dim, deps, order):
    samples, length, half = gate.shape
    chunks = len(mixeds)
    own_samples = samples // 2
    block = spec((samples, TOKENS, half), 1)
    window = spec((samples, TOKENS, WINDOW), 1)
    turned = spec((samples, half // chunks, TOKENS), 2)
    return call(
        "mixed",
        functools.partial(mixed_kernel, head_dim, chunks),
        length // TOKENS,
        [(a, block) for a in (gate, gated_grad)]
        + [(a, window) for a in mixeds + dqs]
        + [(a, turned) for a in dkts + dvts],
        [((own_samples, length, half), BF16, spec((own_samples, TOKENS, half), 1))] * 2
        + [((own_samples, length, 4 * half), BF16, spec((own_samples, TOKENS, 4 * half), 1))] * 2
        + [((1, half), F32, spec((1, half)))],
        [],
        deps,
        order,
    )


def qkvg_kernel(halving, place, first_ref, joined_ref, joined_other_ref, packed_out):
    step = pl.program_id(0)
    samples, length, width = first_ref.shape
    rows = samples * length // 2
    half = joined_ref.shape[2]
    grad = dot(first_ref[: samples // 2].reshape(rows, width), joined_ref[...].reshape(rows, half), 0, 0)
    grad += dot(first_ref[samples // 2 :].reshape(rows, width), joined_other_ref[...].reshape(rows, half), 0, 0)
    share = packed_out.shape[1] * halving.halves() // 4

    for block in range(4):

        @pl.when(step == block)
        def _():
            for p, (dest, part) in enumerate(halving.places()):
                piece = block - part * (4 // halving.halves())
                if 0 <= piece < 4 // halving.halves():
                    for c in range(2):
                        at = (dest + c) * share
                        packed_out[2 * p + c, piece * share : (piece + 1) * share] = grad[at : at + share].astype(BF16)


def qkvg_call(first, joined, joined_other, halving, deps, order):
    samples, length, width = first.shape
    half = joined.shape[2] // 4
    share = width // halving.counts["sample"]
    slabs = (2 * 2 ** len(halving.order), 4 // halving.halves() * share, half)
    block = spec((samples // 2, length, half), 2)
    (packed,) = call(
        "qkvg_grad",
        functools.partial(qkvg_kernel, halving),
        4,
        [(first, spec(first.shape)), (joined, block), (joined_other, block)],
        [(slabs, BF16, spec(slabs))],
        [],
        deps,
        order,
    )
    return packed


def outputs_kernel(place, acts_ref, cot_ref, partial_ref, acts_part_ref, zero_gate_ref, factor_ref, *refs):
    gated_refs, joined_refs, refs = refs[:2], refs[2:4], refs[4:]
    out_w_refs, qkvg_refs, refs = refs[:2], (refs[2:6], refs[6:10]), refs[10:]
    block_ref, acts_grad_ref, projected_ref, zero_low_ref, cond_b_out, zero_b_out, out_out = refs
    clear(pl.program_id(0), cond_b_out, zero_b_out, out_out)
    samples, tokens, width = acts_ref.shape
    rows = samples * tokens
    half = width // 2
    zero_gate = zero_gate_ref[...]
    factor = factor_ref[...]
    normed, inverse = layer_norm(acts_ref[...].astype(F32))
    grad_out = cot_ref[...].astype(F32)
    grad_att = (grad_out * zero_gate[None]).astype(BF16).reshape(rows, width)
    attended = grad_input = 0.0
    for i, half_at in enumerate((place[0], 1 - place[0])):
        gated = gated_refs[i][...].reshape(rows, half)
        attended += dot(gated, out_w_refs[i][...])
        out_out[pl.ds(pl.multiple_of(half_at * half, half), half), :] += dot(gated, grad_att, 0, 0)
        for j in range(4):
            grad_input += dot(
                joined_refs[i][:, :, j * half : (j + 1) * half].reshape(rows, half), qkvg_refs[i][j][...], 1, 1
            )
    attended = attended.reshape(samples, tokens, width)
    grad_input = grad_input.reshape(samples, tokens, width)
    block_ref[...] = (partial_ref[...] + zero_gate[None] * attended).astype(BF16)
    grad_zero = jnp.sum(grad_out * attended, axis=0) * slope(zero_gate)
    zero_b_out[...] += column_sum(grad_zero)
    zero_low_ref[...] = grad_zero.astype(BF16)
    grad_factor = jnp.sum(grad_input * normed, axis=0) * slope(factor)
    cond_b_out[...] += column_sum(grad_factor)
    projected_ref[:, :width] = grad_factor.astype(BF16)
    projected_ref[:, width:] = jnp.sum(grad_input, axis=0).astype(BF16)
    acts_grad_ref[...] = (
        grad_out + norm_back(grad_input * factor[None] + acts_part_ref[...], normed, inverse)
    ).astype(BF16)


def outputs_call(acts, cot, partial, acts_part, zero_gate, factor, gateds, joineds, out_w, qkvg_w, deps, order):
    samples, length, width = acts.shape
    half = width // 2
    block = spec((samples, TOKENS, width), 1)
    tokens = spec((TOKENS, width), 0)
    return call(
        "outputs",
        outputs_kernel,
        length // TOKENS,
        [(a, block) for a in (acts, cot, partial, acts_part)]
        + [(zero_gate, tokens), (factor, tokens)]
        + [(a, spec((samples, TOKENS, half), 1)) for a in gateds]
        + [(a, spec((samples, TOKENS, 4 * half), 1)) for a in joineds]
        + [(out_w, spec((half, width), at=(whose, 0))) for whose in (own, other)]
        + quarters(qkvg_w, own)
        + quarters(qkvg_w, other),
        [
            (acts.shape, BF16, block),
            (acts.shape, BF16, block),
            ((length, 2 * width), BF16, spec((TOKENS, 2 * width), 0)),
            ((length, width), BF16, tokens),
        ]
        + [(s, F32, spec(s)) for s in ((1, width), (1, width), (width, width))],
        [],
        deps,
        order,
    )


def conditions_kernel(
    rest, vector_parts, place, cond_ref, gain_ref, cond_w_ref, zero_w_ref, zero_low_ref, projected_ref,
    cond_gate_in, cond_norm_in, out_w_grad_ref, *refs
):
    vector_refs, (packed_out,) = refs[:vector_parts], refs[vector_parts:]
    cond_w_grad, zero_w_grad, gain_grad, cond_gate, cond_norm, cond_normed, cond_inverse = conditions_back(
        cond_ref, gain_ref, cond_w_ref, zero_w_ref, zero_low_ref[...], projected_ref[...]
    )
    cond_grad = (
        cond_gate + cond_gate_in[...] + norm_back(cond_norm + cond_norm_in[...], cond_normed, cond_inverse)
    )
    vectors = [gain_grad] + [ref[...] for ref in vector_refs[:-1]]
    q_bias = vector_refs[-1][...]
    vectors += [jnp.where(place[0] == 0, q_bias, 0.0), jnp.where(place[0] == 1, q_bias, 0.0)]
    pieces = [v[:, at : at + PIECE] for v in vectors for at in range(0, v.shape[1], PIECE)]
    rest.pack(packed_out, [out_w_grad_ref[...], cond_w_grad, zero_w_grad, cond_grad], pieces)


def conditions_call(cond, branch, zero_w, zero_low, projected, cond_gate, cond_norm, out_w_grad, vectors, rest, deps, order):
    cond_width = cond.shape[1]
    width = zero_low.shape[1]
    weights = [out_w_grad.shape, (cond_width, 2 * width), (cond_width, width), cond.shape]
    count, rows, columns = rest.slabs(weights)
    rows += (sum(v.shape[1] for v in vectors) + cond_width + width // 2) // PIECE
    rows += -rows % 16
    fixed = (zero_low, projected, cond_gate, cond_norm, out_w_grad, *vectors)
    (packed,) = call(
        "conditions",
        functools.partial(conditions_kernel, rest, len(vectors)),
        1,
        [(cond, spec(cond.shape))] + branch[:2] + [zero_w] + [(a, spec(a.shape)) for a in fixed],
        [((count, rows, columns), BF16, spec((count, rows, columns)))],
        [],
        deps,
        order,
    )
    return packed, weights


def results_kernel(
    early_halving, rest_halving, early_shapes, rest_shapes, halves, place, *refs
):
    early_refs, refs = refs[:halves], refs[halves:]
    qkvg_refs, refs = refs[: 2 * halves], refs[2 * halves :]
    (rest_ref, rest_got_ref, pair_sum_ref, pair_wt_ref, pair_gain_ref), refs = refs[:5], refs[5:]
    (cond_ref, cond_w_ref, zero_w_ref, qkvg_ref, out_w_ref, swiglu_ref, down_ref), refs = refs[:7], refs[7:]
    gains_ref, cond_b_ref, zero_b_ref, q_bias_ref, pair_gain_out, pair_w_out = refs
    bits = place.shape[0] - 1
    device = sum(place[bit] << bit for bit in range(bits))

    def columns(ref, pieces):
        for c, piece in enumerate(pieces):
            ref[:, c * PIECE : (c + 1) * PIECE] = piece.astype(F32)

    early = [early_halving.unpack(ref[...].astype(F32), early_shapes) for ref in early_refs]
    swiglu, down, cond_w_one, zero_w_one = [sum(parts, []) for parts in zip(*early)]
    before = rest_ref[...].astype(F32)
    total = before + rest_got_ref[...].astype(F32)
    out_w, cond_w_zero, zero_w_zero, _ = rest_halving.unpack(total, rest_shapes)
    columns(swiglu_ref, swiglu)
    columns(down_ref, down)
    columns(cond_w_ref, cond_w_zero + cond_w_one)
    columns(zero_w_ref, zero_w_zero + zero_w_one)
    columns(out_w_ref, out_w)
    columns(cond_ref, rest_halving.unpack(before, rest_shapes)[3])
    parts = []
    for i in range(2):
        held = [ref[...].astype(F32) for ref in qkvg_refs[i * halves : (i + 1) * halves]]
        if halves == 2:
            first = place[bits] == 0
            held = [jnp.where(first, held[0], held[1]), jnp.where(first, held[1], held[0])]
        parts.append(jnp.concatenate(held, axis=0))
    first = place[0] == 0
    parts = [jnp.where(first, parts[0], parts[1]), jnp.where(first, parts[1], parts[0])]
    rows = parts[0].shape[0] // 4
    columns(qkvg_ref, [part[j * rows : (j + 1) * rows] for j in range(4) for part in parts])
    at = sum(r * c for r, c in map(rest_halving.pieces, rest_shapes))
    for ref in (gains_ref, cond_b_ref, zero_b_ref, q_bias_ref):
        size = ref.shape[1]
        count = size * rest_halving.counts["sample"] // PIECE
        value = 0.0
        for c in range(count):
            source = lax.broadcasted_iota(jnp.int32, (PIECE, size), 0) + c * PIECE
            target = lax.broadcasted_iota(jnp.int32, (PIECE, size), 1) + device * size
            chosen = (source == target).astype(F32)
            value += lax.dot_general(
                total[at + c : at + c + 1],
                chosen,
                (((1,), (0,)), ((), ())),
                precision=lax.Precision.HIGHEST,
                preferred_element_type=F32,
            )
        ref[...] = value
        at += count
    size, heads = pair_w_out.shape
    channels = pair_sum_ref.shape[1]
    source = lax.broadcasted_iota(jnp.int32, (channels, size), 0)
    target = lax.broadcasted_iota(jnp.int32, (channels, size), 1) + device * size
    chosen = (source == target).astype(F32)

    def choose(array):
        return lax.dot_general(
            chosen,
            array,
            (((0,), (1,)), ((), ())),
            precision=lax.Precision.HIGHEST,
            preferred_element_type=F32,
        )

    grad = choose(pair_sum_ref[...])
    pair_w_out[...] = grad
    weighted = jnp.sum(grad * choose(pair_wt_ref[...].astype(F32)), axis=1, keepdims=True)
    pair_gain_out[...] = weighted / choose(pair_gain_ref[...])


def results_call(
    early, early_halving, early_shapes, qkvg, rest, rest_got, rest_halving, rest_shapes, pair_sum, pair_wt, pair_gain, order
):
    count = rest_halving.counts["sample"]
    heads, channels = pair_wt.shape
    swiglu, down, cond_w, zero_w = early_shapes
    out_w, _, _, cond = rest_shapes
    width = out_w[1]
    arrays = [cond, (cond_w[0], 2 * cond_w[1]), (zero_w[0], 2 * zero_w[1]), (width, 4 * width), out_w, swiglu, down]
    shapes = [(rows // count, columns) for rows, columns in arrays]
    shapes += [(1, size // count) for size in (2 * cond[1], 2 * width, 2 * width, width)]
    shapes += [(channels // count, 1), (channels // count, heads)]
    ins = [*early, *qkvg, rest, rest_got, pair_sum, pair_wt, pair_gain]
    return call(
        "results",
        functools.partial(
            results_kernel, early_halving, rest_halving, early_shapes, rest_shapes, early_halving.halves()
        ),
        1,
        [(a, spec(a.shape)) for a in ins],
        [(shape, F32, spec(shape)) for shape in shapes],
        [],
        [],
        order,
    )


def body(
    struct_count, sample_devices,
    acts, cond, pair, lengths, token_mask, cond_gains, cond_w, cond_bias, output_gate_weights, zero_bias,
    qkvg_w, q_bias, out_w, swiglu_w, down_w, pair_gain, pair_w, cotangent,
):
    acts, cond, pair, cotangent = acts[0], cond[0], pair[0], cotangent[0]
    samples, length, width = acts.shape
    cond_width = cond.shape[1]
    heads = pair_w.shape[1]
    head_dim = width // heads
    chunks = heads // 2 // CHUNK_HEADS
    counts = {"struct": struct_count, "sample": sample_devices}
    bits = sample_devices.bit_length() - 1
    pair_wt = pair_w.T
    device = lax.axis_index("sample")
    core = device & 1
    place = [(device >> bit) & 1 for bit in range(bits)] + [lax.axis_index("struct")]
    order = Order(jnp.stack(place).astype(jnp.int32))

    def swap(array):
        return lax.ppermute(array, "sample", [(i, i ^ 1) for i in range(sample_devices)])

    acts_other, cotangent_other = swap(acts), swap(cotangent)

    bias_rows = pair_forward(pair, pair_gain[None], pair_wt, token_mask, lengths, Order(jnp.zeros(bits + 1, jnp.int32)))
    bias = lax.all_gather(bias_rows, "sample", axis=0, tiled=False)

    rows = {}
    at = 0
    packed = [
        ("gain", cond_gains), ("cond_b", cond_bias), ("zero_b", zero_bias), ("q_bias", q_bias), ("pair", pair_gain)
    ]
    vector = jnp.concatenate([v for _, v in packed]).astype(F32)[None]
    for name, v in packed:
        rows[name] = vector[:, at : at + v.shape[0]]
        at += v.shape[0]

    def conditioning(b):
        return [
            (rows["gain"], spec((1, cond_width), at=(0, b))),
            (cond_w, spec((cond_width, 2 * width), at=(0, b))),
            (rows["cond_b"], spec((1, width), at=(0, b))),
        ]

    def zero(b):
        return [
            (output_gate_weights, spec((cond_width, width), at=(0, b))),
            (rows["zero_b"], spec((1, width), at=(0, b))),
        ]

    def path(*order):
        steps = [("struct", 0) if o == "y" else ("sample", o) for o in order]
        steps = [s for s in steps if s[0] == "sample" or struct_count == 2]
        return Halving(steps + [("sample", b) for b in range(4, bits)], counts)

    along_x = path(0, 1, 2, 3)
    along_y = path(0, "y", 2, 3, 1)
    chip_x = path(1, 2, 3)
    chip_y = path("y", 2, 3, 1)
    results, early_shapes = transition_call(
        acts, cotangent, cond, conditioning(1) + zero(1), swiglu_w, down_w, along_y, [], order
    )
    partial, acts_part, cond_gate, cond_norm, early, cond_b_one, zero_b_one, gain_one = results
    early = Running(along_y.run(early))
    first, gate, gated_grad, *rest = inputs_call(
        acts, acts_other, cotangent, cotangent_other, cond, conditioning(0) + zero(0), qkvg_w, rows["q_bias"], out_w,
        [], order,
    )
    nats, turned, (zero_gate, factor) = rest[:4], rest[4:8], rest[8:]

    mixeds, dqs, dkts, dvts, bias_sums = [], [], [], [], []
    deps = advance(order, early)
    for chunk in range(chunks):
        mixed, dq, dkt, dvt, db = attention_call(chunk, nats, turned, bias, head_dim, chip_x, deps, order)
        mixeds.append(mixed)
        dqs.append(dq)
        dkts.append(dkt)
        dvts.append(dvt)
        bias_sums.append(Running(chip_x.run(db, "swap")))
        deps = advance(order, *bias_sums, *([early] if chunk % 2 else []))

    gated, gated_sent, joined, joined_sent, q_bias_grad = mixed_call(
        gate, gated_grad, mixeds, dqs, dkts, dvts, head_dim, deps, order
    )
    gated_got, joined_got = swap(gated_sent), swap(joined_sent)
    deps = advance(order, *bias_sums)
    qkvg_sum = Running(
        chip_y.run(qkvg_call(first, joined, joined_sent, chip_y, deps, order), "cores")
    )
    deps = advance(order, *bias_sums, qkvg_sum, early)
    block_out, acts_grad, projected, zero_low, cond_b_zero, zero_b_zero, out_grad = outputs_call(
        acts, cotangent, partial, acts_part, zero_gate, factor, [gated, gated_got], [joined, joined_got],
        out_w, qkvg_w, deps, order,
    )
    deps = advance(order, *bias_sums, qkvg_sum)
    while any(b.result is None for b in bias_sums):
        deps += advance(order, *bias_sums)
    rest, rest_shapes = conditions_call(
        cond, conditioning(0), zero(0)[0], zero_low, projected, cond_gate, cond_norm, out_grad,
        [gain_one, cond_b_zero, cond_b_one, zero_b_zero, zero_b_one, q_bias_grad], along_x, deps, order,
    )
    rest = Running(along_x.run(rest, ""))
    share = length // sample_devices
    block = 16 if share % 16 == 0 else share
    turned_wt = jnp.where(core == 0, pair_wt, jnp.roll(pair_wt, heads // 2, axis=0))
    grads = [b.result[0] for b in bias_sums] + [b.result[1] for b in bias_sums]
    grad_pair, part = pair_backward(0, 1, block, None, pair, grads, rows["pair"], turned_wt, [], order)
    pair_parts = [part]
    if share > block:
        deps = advance(order, qkvg_sum, rest, early)
        grad_pair, part = pair_backward(
            1, share // block - 1, block, grad_pair, pair, grads, rows["pair"], turned_wt, deps, order
        )
        pair_parts.append(part)
    struct_bits = struct_count.bit_length() - 1

    def summed(array, *masks):
        found = [
            lax.ppermute(array, ("struct", "sample"), [(i, i ^ mask) for i in range(struct_count * sample_devices)])
            for mask in masks
        ]
        if len(found) == 1:
            return array + found[0]
        return (array + found[0]) + (found[1] + found[2])

    class Pair:
        asked = [[(p, p.shape[0], lambda place: 0) for p in pair_parts]]
        result = None

        def send(self, found):
            self.result = found[0]

    pair_grad = Pair()
    advance(order, pair_grad, qkvg_sum, rest, early)
    left = [bits + struct_bits - 1] + list(range(bits + struct_bits - 1)) if struct_bits else list(range(bits))
    pair_sum = pair_grad.result
    pair_sum = jnp.where(core == 0, pair_sum, jnp.roll(pair_sum, heads // 2, axis=0))
    while left:
        one = 1 << left.pop(0)
        two = 1 << left.pop(0) if left else 0
        pair_sum = summed(pair_sum, one, two, one | two) if two else summed(pair_sum, one)
    chains = (qkvg_sum, rest, early)
    while any(r.result is None for r in chains):
        advance(order, *chains)
    mine_qkvg, sent = qkvg_sum.result
    if chip_y.halves() == 2:
        across = [
            (s * sample_devices + i, (1 - s) * sample_devices + (i ^ 1))
            for s in range(2)
            for i in range(sample_devices)
        ]
        from_y = lax.ppermute(mine_qkvg, "struct", [(0, 1), (1, 0)])
        from_both = lax.ppermute(sent, ("struct", "sample"), across)
        qkvg = [mine_qkvg, from_y, swap(sent), from_both]
    else:
        for bit in range(struct_bits):
            mine_qkvg, sent = [summed(part, 1 << (bits + bit)) for part in (mine_qkvg, sent)]
        qkvg = [mine_qkvg, swap(sent)]
    early = list(early.result) if along_y.halves() == 2 else [early.result]
    rest_sum, rest_got = rest.result, jnp.zeros_like(rest.result)
    for bit in range(struct_bits):
        if bit:
            rest_sum = rest_sum + rest_got
        rest_got = lax.ppermute(
            rest_sum, "struct", [(i, i ^ (1 << bit)) for i in range(struct_count)]
        )
    (cond_sum, cond_w_sum, zero_w_sum, qkvg_total, out_sum, swiglu_sum, down_sum,
     gains, cond_b, zero_b, q_b, pair_g, pair_w_sum) = results_call(
        early, along_y, early_shapes, qkvg, rest_sum, rest_got, along_x, rest_shapes, pair_sum, pair_wt, rows["pair"], order
    )
    if struct_bits > 1:
        cond_sum = along_x.unpack(rest.result, rest_shapes)[3][0].astype(F32)
    return (
        block_out[None], acts_grad[None], cond_sum[None], grad_pair[None], gains[0], cond_w_sum, cond_b[0], zero_w_sum,
        zero_b[0], qkvg_total, q_b[0], out_sum, swiglu_sum, down_sum, pair_g[:, 0], pair_w_sum,
    )


def solution(mesh):
    per_struct = P("struct", "sample", None, None)
    in_specs = (
        (per_struct, P("struct", None, None), per_struct, P("struct"), P("struct", None))
        + (P(),) * 12
        + (per_struct,)
    )
    one, two = P("sample"), P("sample", None)
    out_specs = (
        per_struct, per_struct, P("struct", "sample", None), per_struct,
        one, two, one, two, one, two, one, two, two, two, one, two,
    )
    local = functools.partial(body, mesh.shape["struct"], mesh.shape["sample"])
    return jax.shard_map(local, mesh=mesh, in_specs=in_specs, out_specs=out_specs, check_vma=False)
```

time: 525 us -> 483 us (0.920)
  Pallas kernels: 273 us -> 362 us
  other arithmetic: 74.2 us -> 3.22 us
  between operations: 52.4 us -> 15.4 us
  waiting for transfers between devices: 59.4 us -> 39.7 us
    pallas_call x16 -> x26, Pallas kernels: 273 us -> 362 us  [call(): pl.pallas_call(run, grid_spec=pltpu.PrefetchScalarGridSpec(num_scalar_pre...]
    convert_element_type x28 -> x0, other arithmetic: 55.8 us -> none  [the longest x24 52.6 us: take(): return (left.astype(F32) + right.astype(F32) + zero).astype(left.dtype)]
    ppermute x38 -> x30, waiting for transfers between devices: 47.8 us -> 28.7 us  [exchange(): lax.ppermute(array, axis, [(i, i ^ 1 << bit) for i in range(self.counts[a...]
    squeeze x7 -> x0, other arithmetic: 9.66 us -> none  [run(): held = take(pair, start + order.zero, 1)[0]]
    unnamed x76 -> x78, local copies, waits for them, and re-layouts: 3.04 us -> 12.7 us
    all_gather x1, waiting for transfers between devices: 10.7 us -> 4.69 us  [body(): bias = lax.all_gather(bias_rows, 'sample', axis=0, tiled=False)]
    add x9 -> x3, other arithmetic: 6.59 us -> 0.61 us  [the longest x1 0.6 us: summed(): return array + found[0]]
    ppermute x6 -> x15, waiting for transfers between devices: 0.89 us -> 6.28 us  [the longest x7 4.55 us: summed(): lax.ppermute(array, ('struct', 'sample'), [(i, i ^ mask) for i in range(s...]
  transfers between devices with their start and end apart: 45 -> 46, of which waited for: 11 -> 12; matrix products, arithmetic and copies ran while one was open for 16% -> 1% of each run, Pallas kernels for 50% -> 67%
where the time goes in v3:
time: 483 us; the launch traced here: 479 us
  Pallas kernels  362 us (75%)
  starting transfers between devices  42.6 us (9%)
  waiting for transfers between devices  39.7 us (8%)
  local copies, waits for them, and re-layouts  16.2 us (3%)
  between operations  15.4 us (3%)
    pallas_call x26, Pallas kernels, call(): pl.pallas_call(run, grid_spec=pltpu.PrefetchScalarGridSpec(num_scalar_pre...  362 us
    ppermute x30, starting transfers between devices, exchange(): lax.ppermute(array, axis, [(i, i ^ 1 << bit) for i in range(self.counts[a...  34.1 us
    ppermute x30, waiting for transfers between devices, exchange(): lax.ppermute(array, axis, [(i, i ^ 1 << bit) for i in range(self.counts[a...  28.7 us
    unnamed x78, local copies, waits for them, and re-layouts  12.7 us
  transfers between devices with their start and end apart: 46, of which 12 were waited for; matrix products, arithmetic and copies ran while one was open for 1% of the time, Pallas kernels for 67%

profile of v3, /device:TPU:0, one launch (start us, length us, event | category | flops | bytes accessed | tf_op | source)
XLA Modules:
  0.0 478.8 jit_solution(5941724327790947282)
XLA Ops:
  8.4 13.1 %pair_forward.1 = bf16[16,48,768]{2,1,0:T(8,128)(2,1)} custom-call(s32[5]{0:T(128)} %broadcast_1_place_ref.2.place_ref, bf16[48,768,128]{2,1,0:T(8,128)(2,1)} %bitcast.42, bf16[1,128]{1,0:T(2,128)(2,1)} %bitcast.64, bf16[16,128]{1,0:T(8,128)(2,1)} %bitcast.35, s32[1,768]{1,0:T(1,128)} %refs_3_.2, s32[1]{0:T(128)S(6)} %copy.40.refs_4_), custom_call_target="tpu_custom_call" | custom-call | flops 99999997952 | bytes 1000000 | tf_op jit(solution)/shard_map/pair_forward/pallas_call | solution.py:82
  24.1 57.3 %transition.1 = (f32[2,768,768]{2,1,0:T(8,128)}, f32[2,768,768]{2,1,0:T(8,128)}, f32[768,384]{1,0:T(8,128)}, f32[768,384]{1,0:T(8,128)}, bf16[32,360,384]{2,1,0:...) custom-call(s32[5]{0:T(128)} %stack.23.place_ref, bf16[2,768,768]{2,1,0:T(8,128)(2,1)} %bitcast.45, ...), custom_call_target="tpu_custom_call" | custom-call | flops 99999997952 | bytes 1000000 | tf_op jit(solution)/shard_map/transition/pallas_call | solution.py:82
  83.1 26.2 %inputs.1 = (bf16[4,768,768]{2,1,0:T(8,128)(2,1)}, f32[4,768,384]{2,1,0:T(8,128)}, f32[4,768,384]{2,1,0:T(8,128)}, bf16[2,4,768,256]{3,2,1,0:T(8,128)(2,1)}, bf1...) custom-call(s32[5]{0:T(128)} %stack.23.place_ref, ...), custom_call_target="tpu_custom_call" | custom-call | flops 99999997952 | bytes 1000000 | tf_op jit(solution)/shard_map/inputs/pallas_call | solution.py:82
  109.3 6.9 %combine.12 = (bf16[8,360,384]{2,1,0:T(8,128)(2,1)}, bf16[8,360,384]{2,1,0:T(8,128)(2,1)}) custom-call(s32[5]{0:T(128)} %stack.23.place_ref, bf16[32,360,384]{2,1,0:T(8,128)(2,1)} %get-tuple-element.142.refs_16_.refs_0_.refs_2_, bf16[32,360,384]{2,1,0:T(8,128)(2,1)} %collective-permute-done.2.refs_1_.refs_3_, ...), custom_call_target="tpu_custom_call" | custom-call | flops 99999997952 | bytes 1000000 | tf_op jit(solution)/shard_map/combine/pallas_call | solution.py:82
  118.7 4.7 all-gather.3.cloned.1.call-done
  123.4 26.1 %attention.4 = (f32[4,768,256]{2,1,0:T(8,128)}, f32[4,768,256]{2,1,0:T(8,128)}, bf16[4,96,768]{2,1,0:T(8,128)(2,1)}, bf16[4,96,768]{2,1,0:T(8,128)(2,1)}, bf16[16,2,48,768]{3,2,1,0:T(8,128)(2,1)}) custom-call(s32[5]{0:T(128)} %stack.23.place_ref, bf16[2,4,768,256]{3,2,1,0:T(8,128)(2,1)} %get-tuple-element.147.refs_0_, ...), custom_call_target="tpu_custom_call" | custom-call | flops 16999999488 | bytes 1000000 | tf_op jit(solution)/shard_map/attention/pallas_call | solution.py:82
  149.5 3.1 combine.13.refs_9_.refs_10_
  153.9 26.3 %attention.5 = (f32[4,768,256]{2,1,0:T(8,128)}, f32[4,768,256]{2,1,0:T(8,128)}, bf16[4,96,768]{2,1,0:T(8,128)(2,1)}, bf16[4,96,768]{2,1,0:T(8,128)(2,1)}, bf16[16,2,48,768]{3,2,1,0:T(8,128)(2,1)}) custom-call(s32[5]{0:T(128)} %stack.23.place_ref, bf16[2,4,768,256]{3,2,1,0:T(8,128)(2,1)} %get-tuple-element.147.refs_0_, ...), custom_call_target="tpu_custom_call" | custom-call | flops 16999999488 | bytes 1000000 | tf_op jit(solution)/shard_map/attention/pallas_call | solution.py:82
  182.1 6.2 %combine.14 = (bf16[4,2,48,768]{3,2,1,0:T(8,128)(2,1)}, bf16[4,2,48,768]{3,2,1,0:T(8,128)(2,1)}, bf16[8,2,48,768]{3,2,1,0:T(8,128)(2,1)}, bf16[4,360,384]{2,1,0:T(8,128)(2,1)}, bf16[4,360,384]{2,1,0:T(8,128)(2,1)}) custom-call(s32[5]{0:T(128)} %stack.23.place_ref, bf16[16,2,48,768]{3,2,1,0:T(8,128)(2,1)} %get-tuple-element.159.refs_0_.refs_1_.refs_2_, ...), custom_call_target="tpu_custom_call" | custom-call | flops 99999997952 | bytes 1000000 | tf_op jit(solution)/shard_map/combine/pallas_call | solution.py:82
  191.5 26.4 %attention.6 = (f32[4,768,256]{2,1,0:T(8,128)}, f32[4,768,256]{2,1,0:T(8,128)}, bf16[4,96,768]{2,1,0:T(8,128)(2,1)}, bf16[4,96,768]{2,1,0:T(8,128)(2,1)}, bf16[16,2,48,768]{3,2,1,0:T(8,128)(2,1)}) custom-call(s32[5]{0:T(128)} %stack.23.place_ref, bf16[2,4,768,256]{3,2,1,0:T(8,128)(2,1)} %get-tuple-element.147.refs_0_, ...), custom_call_target="tpu_custom_call" | custom-call | flops 16999999488 | bytes 1000000 | tf_op jit(solution)/shard_map/attention/pallas_call | solution.py:82
  219.1 4.7 combine.15
  228.4 26.6 %attention.7 = (f32[4,768,256]{2,1,0:T(8,128)}, f32[4,768,256]{2,1,0:T(8,128)}, bf16[4,96,768]{2,1,0:T(8,128)(2,1)}, bf16[4,96,768]{2,1,0:T(8,128)(2,1)}, bf16[16,2,48,768]{3,2,1,0:T(8,128)(2,1)}) custom-call(s32[5]{0:T(128)} %stack.23.place_ref, bf16[2,4,768,256]{3,2,1,0:T(8,128)(2,1)} %get-tuple-element.147.refs_0_, ...), custom_call_target="tpu_custom_call" | custom-call | flops 16999999488 | bytes 1000000 | tf_op jit(solution)/shard_map/attention/pallas_call | solution.py:82
  256.7 6.0 %combine.16 = (bf16[1,2,48,768]{3,2,1,0:T(8,128)(2,1)}, bf16[1,2,48,768]{3,2,1,0:T(8,128)(2,1)}, bf16[2,2,48,768]{3,2,1,0:T(8,128)(2,1)}, bf16[2,2,48,768]{3,2,1...) custom-call(s32[5]{0:T(128)} %stack.23.place_ref, ...), custom_call_target="tpu_custom_call" | custom-call | flops 99999997952 | bytes 1000000 | tf_op jit(solution)/shard_map/combine/pallas_call | solution.py:82
  267.6 18.7 %mixed.1 = (bf16[2,768,384]{2,1,0:T(8,128)(2,1)}, bf16[2,768,384]{2,1,0:T(8,128)(2,1)}, bf16[2,768,1536]{2,1,0:T(8,128)(2,1)}, bf16[2,768,1536]{2,1,0:T(8,128)(2,1)}, f32[1,384]{1,0:T(1,128)}) custom-call(s32[5]{0:T(128)} %stack.23.place_ref, f32[4,768,384]{2,1,0:T(8,128)} %get-tuple-element.145.refs_0_, f32[4,768,384]{2,1,0:T(8,128)} %get-tuple-element.146.refs_1_, ...), custom_call_target="tpu_custom_call" | custom-call | flops 99999997952 | bytes 1000000 | tf_op jit(solution)/shard_map/mixed/pallas_call | solution.py:82
  286.3 5.3 %collective-permute-done.13.refs_1_.refs_3_ = bf16[2,2,48,768]{3,2,1,0:T(8,128)(2,1)S(1)} collective-permute-done((bf16[2,2,48,768]{3,2,1,0:T(8,128)(2,1)}, bf16[2,2,48,768]{3,2,1,0:T(8,128)(2,1)S(1)}, u32[]{:S(2)}, u32[]{:S(2)}) %collective-permute-start.13) | collective-permute-done | bytes 294944 | tf_op jit(solution)/shard_map/ppermute | solution.py:190
  291.6 3.5 collective-permute-done.14.refs_5_.refs_7_
  296.4 4.2 combine.17
  300.6 3.3 collective-permute-start.16
  303.9 16.2 %qkvg_grad.1.refs_8_.refs_13_.refs_4_.refs_6_ = bf16[32,96,384]{2,1,0:T(8,128)(2,1)} custom-call(s32[5]{0:T(128)} %stack.23.place_ref, bf16[4,768,768]{2,1,0:T(8,128)(2,1)} %get-tuple-element.155.refs_4_.refs_0_, bf16[2,768,1536]{2,1,0:T(8,128)(2,1)} %get-tuple-element.199.refs_12_.refs_1_.refs_8_, bf16[2,768,1536]{2,1,0:T(8,128)(2,1)} %get-tuple-element.200.refs_2_, ...), custom_call_target="tpu_custom_call" | custom-call | flops 99999997952 | bytes 1000000 | tf_op jit(solution)/shard_map/qkvg_grad/pallas_call | solution.py:82
  320.7 3.0 collective-permute-done.17.refs_5_.refs_7_
  324.6 4.4 combine.18
  332.1 25.6 %outputs.1 = (bf16[2,768,768]{2,1,0:T(8,128)(2,1)}, bf16[2,768,768]{2,1,0:T(8,128)(2,1)}, bf16[768,1536]{1,0:T(8,128)(2,1)}, bf16[768,768]{1,0:T(8,128)(2,1)}, f...) custom-call(s32[5]{0:T(128)} %stack.23.place_ref, bf16[2,768,768]{2,1,0:T(8,128)(2,1)} %bitcast.47, ...), custom_call_target="tpu_custom_call" | custom-call | flops 99999997952 | bytes 1000000 | tf_op jit(solution)/shard_map/outputs/pallas_call | solution.py:82
  360.0 3.8 combine.19
  363.8 10.3 %conditions.1.refs_11_.refs_4_.refs_6_ = bf16[16,304,384]{2,1,0:T(8,128)(2,1)} custom-call(s32[5]{0:T(128)} %stack.23.place_ref, bf16[768,384]{1,0:T(8,128)(2,1)} %bitcast.55, f32[1,768]{1,0:T(1,128)} %get-tuple-element.265.refs_3_.refs_5_.refs_1_, bf16[384,3072]{1,0:T(8,128)(2,1)} %refs_2_.1, bf16[384,1536]{1,0:T(8,128)(2,1)} %refs_3_.3, ...), custom_call_target="tpu_custom_call" | custom-call | flops 99999997952 | bytes 1000000 | tf_op jit(solution)/shard_map/conditions/pallas_call | solution.py:82
  375.5 11.8 %pair_backward.2 = (f32[48,768,128]{2,1,0:T(8,128)}, f32[16,128]{1,0:T(8,128)}) custom-call(s32[5]{0:T(128)} %stack.23.place_ref, bf16[48,768,128]{2,1,0:T(8,128)(2,1)} %bitcast.43, f32[1,128]{1,0:T(1,128)} %slice.44.refs_1_.refs_10_, bf16[16,128]{1,0:T(8,128)(2,1)} %maximum_select_fusion.1.refs_2_, bf16[2,48,768]{2,1,0:T(8,128)(2,1)} %bitcast.70, ...), custom_call_target="tpu_custom_call" | custom-call | flops 99999997952 | bytes 1000000 | tf_op jit(solution)/shard_map/pair_backward/pallas_call | solution.py:82
  392.0 4.9 %combine.20 = (bf16[4,96,384]{2,1,0:T(8,128)(2,1)}, bf16[4,96,384]{2,1,0:T(8,128)(2,1)}, bf16[4,304,384]{2,1,0:T(8,128)(2,1)}, bf16[4,304,384]{2,1,0:T(8,128)(2,1)}, bf16[1,360,384]{2,1,0:T(8,128)(2,1)}) custom-call(s32[5]{0:T(128)} %stack.23.place_ref, bf16[8,96,384]{2,1,0:T(8,128)(2,1)} %get-tuple-element.230.refs_18_.refs_0_.refs_2_, ...), custom_call_target="tpu_custom_call" | custom-call | flops 99999997952 | bytes 1000000 | tf_op jit(solution)/shard_map/combine/pallas_call | solution.py:82
  400.8 18.5 %pair_backward.3 = (f32[48,768,128]{2,1,0:T(8,128)}, f32[16,128]{1,0:T(8,128)}) custom-call(s32[5]{0:T(128)} %stack.23.place_ref, bf16[48,768,128]{2,1,0:T(8,128)(2,1)} %bitcast.44, f32[1,128]{1,0:T(1,128)} %slice.44.refs_1_.refs_10_, bf16[16,128]{1,0:T(8,128)(2,1)} %maximum_select_fusion.1.refs_2_, ...), custom_call_target="tpu_custom_call", output_to_operand_aliasing={{0}: (12, {})} | custom-call | flops 99999997952 | bytes 1000000 | tf_op jit(solution)/shard_map/pair_backward/pallas_call | solution.py:82
  422.6 4.0 combine.21
  433.6 4.2 collective-permute-done.32.refs_5_.refs_7_
  446.6 6.0 %collective-permute-done.36.refs_1_ = bf16[1,304,384]{2,1,0:T(8,128)(2,1)S(1)} collective-permute-done((bf16[1,304,384]{2,1,0:T(8,128)(2,1)}, bf16[1,304,384]{2,1,0:T(8,128)(2,1)S(1)}, u32[]{:S(2)}, u32[]{:S(2)}) %collective-permute-start.36) | collective-permute-done | bytes 233504 | tf_op jit(solution)/shard_map/ppermute | solution.py:190
  458.0 4.5 collective-permute-done.44
  465.6 4.8 %results.1 = (f32[48,384]{1,0:T(8,128)}, f32[24,3072]{1,0:T(8,128)}, f32[24,1536]{1,0:T(8,128)}, f32[48,3072]{1,0:T(8,128)}, f32[48,768]{1,0:T(8,128)}, /*index=...) custom-call(s32[5]{0:T(128)} %stack.23.place_ref, ...), custom_call_target="tpu_custom_call" | custom-call | flops 99999997952 | bytes 1000000 | tf_op jit(solution)/shard_map/results/pallas_call | solution.py:82
  (179 shorter events, 72.5 us)
Async XLA Ops:
  7.2 116.2 %all-gather.3.cloned.1.call-start = ((), (), s32[]{:S(2)}) async-start(), calls=%async_computation | async-start | bytes 20054016 | tf_op jit(solution)/shard_map/all_gather | solution.py:998
  21.6 61.5 %collective-permute-start = (bf16[2,768,768]{2,1,0:T(8,128)(2,1)S(1)}, bf16[2,768,768]{2,1,0:T(8,128)(2,1)}, u32[]{:S(2)}, u32[]{:S(2)}) collective-permute-start(bf16[2,768,768]{2,1,0:T(8,128)(2,1)S(1)} %bitcast.48), channel_id=1, source_target_pairs={{0,1},{1,0},{2,3},{3,2},{4,5},{5,4},{6,7},{7,6},{8,9},{9,8},{10,11... | collective-permute-start | bytes 7077896 | tf_op jit(solution)/shard_map/ppermute | solution.py:993
  22.1 61.0 %collective-permute-start.1 = (bf16[2,768,768]{2,1,0:T(8,128)(2,1)}, bf16[2,768,768]{2,1,0:T(8,128)(2,1)}, u32[]{:S(2)}, u32[]{:S(2)}) collective-permute-start(bf16[2,768,768]{2,1,0:T(8,128)(2,1)} %bitcast.49), channel_id=1, source_target_pairs={{0,1},{1,0},{2,3},{3,2},{4,5},{5,4},{6,7},{7,6},{8,9},{9,8},{10,11... | collective-permute-start | bytes 7077896 | tf_op jit(solution)/shard_map/ppermute | solution.py:993
  81.4 27.8 %collective-permute-start.2 = (bf16[32,360,384]{2,1,0:T(8,128)(2,1)}, bf16[32,360,384]{2,1,0:T(8,128)(2,1)}, u32[]{:S(2)}, u32[]{:S(2)}) collective-permute-start(bf16[32,360,384]{2,1,0:T(8,128)(2,1)} %get-tuple-element.142.refs_16_.refs_0_.refs_2_), channel_id=1, source_target_pairs={{0,1},{1,0},{2,3},{3,2},{4,5},{5,4},{6,7},{7,6},{8,9},{9,8},{10,11... | collective-permute-start | bytes 26542088 | tf_op jit(solution)/shard_map/ppermute | solution.py:190
  116.2 64.0 %collective-permute-start.4 = (bf16[8,360,384]{2,1,0:T(8,128)(2,1)}, bf16[8,360,384]{2,1,0:T(8,128)(2,1)S(1)}, u32[]{:S(2)}, u32[]{:S(2)}) collective-permute-start(bf16[8,360,384]{2,1,0:T(8,128)(2,1)} %get-tuple-element.156.refs_9_.refs_11_), channel_id=1, source_target_pairs={{0,16},{16,0},{1,17},{17,1},{2,18},{18,2},{3,19},{19,3},{4,20},{20... | collective-permute-start | bytes 6635528 | tf_op jit(solution)/shard_map/ppermute | solution.py:190
  152.6 28.3 %collective-permute-start.3 = (bf16[8,2,48,768]{3,2,1,0:T(8,128)(2,1)}, bf16[8,2,48,768]{3,2,1,0:T(8,128)(2,1)S(1)}, u32[]{:S(2)}, u32[]{:S(2)}) collective-permute-start(bf16[8,2,48,768]{3,2,1,0:T(8,128)(2,1)} %combine.13.refs_9_.refs_10_), channel_id=1, source_target_pairs={{0,2},{1,3},{2,0},{3,1},{4,6},{5,7},{6,4},{7,5},{8,10},{9,11},{10,... | collective-permute-start | bytes 3538952 | tf_op jit(solution)/shard_map/ppermute | solution.py:190
  188.3 29.6 %collective-permute-start.5 = (bf16[4,2,48,768]{3,2,1,0:T(8,128)(2,1)}, bf16[4,2,48,768]{3,2,1,0:T(8,128)(2,1)S(1)}, u32[]{:S(2)}, u32[]{:S(2)}) collective-permute-start(bf16[4,2,48,768]{3,2,1,0:T(8,128)(2,1)} %get-tuple-element.162.refs_9_), channel_id=1, source_target_pairs={{0,4},{1,5},{2,6},{3,7},{4,0},{5,1},{6,2},{7,3},{8,12},{9,13},{10,... | collective-permute-start | bytes 1769480 | tf_op jit(solution)/shard_map/ppermute | solution.py:190
  189.8 65.2 %collective-permute-start.10 = (bf16[4,360,384]{2,1,0:T(8,128)(2,1)}, bf16[4,360,384]{2,1,0:T(8,128)(2,1)S(1)}, u32[]{:S(2)}, u32[]{:S(2)}) collective-permute-start(bf16[4,360,384]{2,1,0:T(8,128)(2,1)} %get-tuple-element.165.refs_12_), channel_id=1, source_target_pairs={{0,4},{1,5},{2,6},{3,7},{4,0},{5,1},{6,2},{7,3},{8,12},{9,13},{10,... | collective-permute-start | bytes 3317768 | tf_op jit(solution)/shard_map/ppermute | solution.py:190
  190.4 27.6 %collective-permute-start.6 = (bf16[8,2,48,768]{3,2,1,0:T(8,128)(2,1)}, bf16[8,2,48,768]{3,2,1,0:T(8,128)(2,1)S(1)}, u32[]{:S(2)}, u32[]{:S(2)}) collective-permute-start(bf16[8,2,48,768]{3,2,1,0:T(8,128)(2,1)} %get-tuple-element.164.refs_11_.refs_14_), channel_id=1, source_target_pairs={{0,2},{1,3},{2,0},{3,1},{4,6},{5,7},{6,4},{7,5},{8,10},{9,11},{10,... | collective-permute-start | bytes 3538952 | tf_op jit(solution)/shard_map/ppermute | solution.py:190
  223.8 31.2 %collective-permute-start.7 = (bf16[2,2,48,768]{3,2,1,0:T(8,128)(2,1)}, bf16[2,2,48,768]{3,2,1,0:T(8,128)(2,1)S(1)}, u32[]{:S(2)}, u32[]{:S(2)}) collective-permute-start(bf16[2,2,48,768]{3,2,1,0:T(8,128)(2,1)} %get-tuple-element.169.refs_9_), channel_id=1, source_target_pairs={{0,8},{1,9},{2,10},{3,11},{4,12},{5,13},{6,14},{7,15},{8,0},{9,1},... | collective-permute-start | bytes 884744 | tf_op jit(solution)/shard_map/ppermute | solution.py:190
  226.2 28.9 %collective-permute-start.8 = (bf16[4,2,48,768]{3,2,1,0:T(8,128)(2,1)}, bf16[4,2,48,768]{3,2,1,0:T(8,128)(2,1)S(1)}, u32[]{:S(2)}, u32[]{:S(2)}) collective-permute-start(bf16[4,2,48,768]{3,2,1,0:T(8,128)(2,1)} %get-tuple-element.171.refs_11_), channel_id=1, source_target_pairs={{0,4},{1,5},{2,6},{3,7},{4,0},{5,1},{6,2},{7,3},{8,12},{9,13},{10,... | collective-permute-start | bytes 1769480 | tf_op jit(solution)/shard_map/ppermute | solution.py:190
  227.3 27.8 %collective-permute-start.9 = (bf16[8,2,48,768]{3,2,1,0:T(8,128)(2,1)}, bf16[8,2,48,768]{3,2,1,0:T(8,128)(2,1)S(1)}, u32[]{:S(2)}, u32[]{:S(2)}) collective-permute-start(bf16[8,2,48,768]{3,2,1,0:T(8,128)(2,1)} %get-tuple-element.173.refs_13_.refs_14_), channel_id=1, source_target_pairs={{0,2},{1,3},{2,0},{3,1},{4,6},{5,7},{6,4},{7,5},{8,10},{9,11},{10,... | collective-permute-start | bytes 3538952 | tf_op jit(solution)/shard_map/ppermute | solution.py:190
  262.8 111.3 %collective-permute-start.21 = (bf16[1,2,48,768]{3,2,1,0:T(8,128)(2,1)}, bf16[1,2,48,768]{3,2,1,0:T(8,128)(2,1)}, u32[]{:S(2)}, u32[]{:S(2)}) collective-permute-start(bf16[1,2,48,768]{3,2,1,0:T(8,128)(2,1)} %get-tuple-element.188.refs_18_), channel_id=1, source_target_pairs={{0,1},{1,0},{2,3},{3,2},{4,5},{5,4},{6,7},{7,6},{8,9},{9,8},{10,11... | collective-permute-start | bytes 442376 | tf_op jit(solution)/shard_map/ppermute | solution.py:190
  262.8 28.9 %collective-permute-start.13 = (bf16[2,2,48,768]{3,2,1,0:T(8,128)(2,1)}, bf16[2,2,48,768]{3,2,1,0:T(8,128)(2,1)S(1)}, u32[]{:S(2)}, u32[]{:S(2)}) collective-permute-start(bf16[2,2,48,768]{3,2,1,0:T(8,128)(2,1)} %get-tuple-element.190.refs_20_), channel_id=1, source_target_pairs={{0,8},{1,9},{2,10},{3,11},{4,12},{5,13},{6,14},{7,15},{8,0},{9,1},... | collective-permute-start | bytes 884744 | tf_op jit(solution)/shard_map/ppermute | solution.py:190
  263.5 56.7 %collective-permute-start.18 = (bf16[2,360,384]{2,1,0:T(8,128)(2,1)}, bf16[2,360,384]{2,1,0:T(8,128)(2,1)}, u32[]{:S(2)}, u32[]{:S(2)}) collective-permute-start(bf16[2,360,384]{2,1,0:T(8,128)(2,1)} %get-tuple-element.195.refs_25_), channel_id=1, source_target_pairs={{0,8},{1,9},{2,10},{3,11},{4,12},{5,13},{6,14},{7,15},{8,0},{9,1},... | collective-permute-start | bytes 1658888 | tf_op jit(solution)/shard_map/ppermute | solution.py:190
  265.8 29.4 %collective-permute-start.14 = (bf16[4,2,48,768]{3,2,1,0:T(8,128)(2,1)}, bf16[4,2,48,768]{3,2,1,0:T(8,128)(2,1)S(1)}, u32[]{:S(2)}, u32[]{:S(2)}) collective-permute-start(bf16[4,2,48,768]{3,2,1,0:T(8,128)(2,1)} %get-tuple-element.192.refs_22_), channel_id=1, source_target_pairs={{0,4},{1,5},{2,6},{3,7},{4,0},{5,1},{6,2},{7,3},{8,12},{9,13},{10,... | collective-permute-start | bytes 1769480 | tf_op jit(solution)/shard_map/ppermute | solution.py:190
  266.4 28.8 %collective-permute-start.15 = (bf16[8,2,48,768]{3,2,1,0:T(8,128)(2,1)}, bf16[8,2,48,768]{3,2,1,0:T(8,128)(2,1)S(1)}, u32[]{:S(2)}, u32[]{:S(2)}) collective-permute-start(bf16[8,2,48,768]{3,2,1,0:T(8,128)(2,1)} %get-tuple-element.194.refs_24_.refs_27_), channel_id=1, source_target_pairs={{0,2},{1,3},{2,0},{3,1},{4,6},{5,7},{6,4},{7,5},{8,10},{9,11},{10,... | collective-permute-start | bytes 3538952 | tf_op jit(solution)/shard_map/ppermute | solution.py:190
  291.6 39.0 %collective-permute-start.12 = (bf16[2,768,1536]{2,1,0:T(8,128)(2,1)}, bf16[2,768,1536]{2,1,0:T(8,128)(2,1)}, u32[]{:S(2)}, u32[]{:S(2)}) collective-permute-start(bf16[2,768,1536]{2,1,0:T(8,128)(2,1)} %get-tuple-element.200.refs_2_), channel_id=1, source_target_pairs={{0,1},{1,0},{2,3},{3,2},{4,5},{5,4},{6,7},{7,6},{8,9},{9,8},{10,11... | collective-permute-start | bytes 14155784 | tf_op jit(solution)/shard_map/ppermute | solution.py:993
  300.6 19.6 %collective-permute-start.16 = (bf16[2,2,48,768]{3,2,1,0:T(8,128)(2,1)}, bf16[2,2,48,768]{3,2,1,0:T(8,128)(2,1)S(1)}, u32[]{:S(2)}, u32[]{:S(2)}) collective-permute-start(bf16[2,2,48,768]{3,2,1,0:T(8,128)(2,1)} %get-tuple-element.202.refs_5_), channel_id=1, source_target_pairs={{0,8},{1,9},{2,10},{3,11},{4,12},{5,13},{6,14},{7,15},{8,0},{9,1},... | collective-permute-start | bytes 884744 | tf_op jit(solution)/shard_map/ppermute | solution.py:190
  303.9 19.9 %collective-permute-start.17 = (bf16[4,2,48,768]{3,2,1,0:T(8,128)(2,1)}, bf16[4,2,48,768]{3,2,1,0:T(8,128)(2,1)S(1)}, u32[]{:S(2)}, u32[]{:S(2)}) collective-permute-start(bf16[4,2,48,768]{3,2,1,0:T(8,128)(2,1)} %get-tuple-element.204.refs_7_.refs_9_), channel_id=1, source_target_pairs={{0,4},{1,5},{2,6},{3,7},{4,0},{5,1},{6,2},{7,3},{8,12},{9,13},{10,... | collective-permute-start | bytes 1769480 | tf_op jit(solution)/shard_map/ppermute | solution.py:190
  320.3 54.4 %collective-permute-start.22 = (bf16[1,2,48,768]{3,2,1,0:T(8,128)(2,1)}, bf16[1,2,48,768]{3,2,1,0:T(8,128)(2,1)}, u32[]{:S(2)}, u32[]{:S(2)}) collective-permute-start(bf16[1,2,48,768]{3,2,1,0:T(8,128)(2,1)} %get-tuple-element.205.refs_3_), channel_id=1, source_target_pairs={{0,1},{1,0},{2,3},{3,2},{4,5},{5,4},{6,7},{7,6},{8,9},{9,8},{10,11... | collective-permute-start | bytes 442376 | tf_op jit(solution)/shard_map/ppermute | solution.py:190
  329.0 45.9 %collective-permute-start.23 = (bf16[1,2,48,768]{3,2,1,0:T(8,128)(2,1)}, bf16[1,2,48,768]{3,2,1,0:T(8,128)(2,1)}, u32[]{:S(2)}, u32[]{:S(2)}) collective-permute-start(bf16[1,2,48,768]{3,2,1,0:T(8,128)(2,1)} %get-tuple-element.207.refs_20_), channel_id=1, source_target_pairs={{0,1},{1,0},{2,3},{3,2},{4,5},{5,4},{6,7},{7,6},{8,9},{9,8},{10,11... | collective-permute-start | bytes 442376 | tf_op jit(solution)/shard_map/ppermute | solution.py:190
  329.0 28.8 %collective-permute-start.19 = (bf16[2,2,48,768]{3,2,1,0:T(8,128)(2,1)}, bf16[2,2,48,768]{3,2,1,0:T(8,128)(2,1)S(1)}, u32[]{:S(2)}, u32[]{:S(2)}) collective-permute-start(bf16[2,2,48,768]{3,2,1,0:T(8,128)(2,1)} %get-tuple-element.209.refs_22_), channel_id=1, source_target_pairs={{0,8},{1,9},{2,10},{3,11},{4,12},{5,13},{6,14},{7,15},{8,0},{9,1},... | collective-permute-start | bytes 884744 | tf_op jit(solution)/shard_map/ppermute | solution.py:190
  330.6 28.4 %collective-permute-start.20 = (bf16[16,96,384]{2,1,0:T(8,128)(2,1)}, bf16[16,96,384]{2,1,0:T(8,128)(2,1)S(1)}, u32[]{:S(2)}, u32[]{:S(2)}) collective-permute-start(bf16[16,96,384]{2,1,0:T(8,128)(2,1)} %get-tuple-element.211.refs_24_.refs_27_), channel_id=1, source_target_pairs={{0,16},{16,0},{1,17},{17,1},{2,18},{18,2},{3,19},{19,3},{4,20},{20... | collective-permute-start | bytes 3538952 | tf_op jit(solution)/shard_map/ppermute | solution.py:190
  357.8 29.5 %collective-permute-start.27 = (bf16[1,360,384]{2,1,0:T(8,128)(2,1)}, bf16[1,360,384]{2,1,0:T(8,128)(2,1)}, u32[]{:S(2)}, u32[]{:S(2)}) collective-permute-start(bf16[1,360,384]{2,1,0:T(8,128)(2,1)} %get-tuple-element.212.refs_25_), channel_id=1, source_target_pairs={{0,2},{1,3},{2,0},{3,1},{4,6},{5,7},{6,4},{7,5},{8,10},{9,11},{10,... | collective-permute-start | bytes 829448 | tf_op jit(solution)/shard_map/ppermute | solution.py:190
  374.1 16.0 %collective-permute-start.25 = (bf16[8,96,384]{2,1,0:T(8,128)(2,1)}, bf16[8,96,384]{2,1,0:T(8,128)(2,1)}, u32[]{:S(2)}, u32[]{:S(2)}) collective-permute-start(bf16[8,96,384]{2,1,0:T(8,128)(2,1)} %get-tuple-element.229.refs_17_.refs_19_), channel_id=1, source_target_pairs={{0,4},{1,5},{2,6},{3,7},{4,0},{5,1},{6,2},{7,3},{8,12},{9,13},{10,... | collective-permute-start | bytes 1769480 | tf_op jit(solution)/shard_map/ppermute | solution.py:190
  374.6 15.5 %collective-permute-start.26 = (bf16[16,304,384]{2,1,0:T(8,128)(2,1)}, bf16[16,304,384]{2,1,0:T(8,128)(2,1)S(1)}, u32[]{:S(2)}, u32[]{:S(2)}) collective-permute-start(bf16[16,304,384]{2,1,0:T(8,128)(2,1)} %conditions.1.refs_11_.refs_4_.refs_6_), channel_id=1, source_target_pairs={{0,1},{1,0},{2,3},{3,2},{4,5},{5,4},{6,7},{7,6},{8,9},{9,8},{10,11... | collective-permute-start | bytes 11206664 | tf_op jit(solution)/shard_map/ppermute | solution.py:190
  396.9 22.4 %collective-permute-start.30 = (bf16[1,360,384]{2,1,0:T(8,128)(2,1)}, bf16[1,360,384]{2,1,0:T(8,128)(2,1)S(1)}, u32[]{:S(2)}, u32[]{:S(2)}) collective-permute-start(bf16[1,360,384]{2,1,0:T(8,128)(2,1)} %get-tuple-element.237.refs_16_.refs_10_.refs_13_), channel_id=1, source_target_pairs={{0,16},{16,0},{1,17},{17,1},{2,18},{18,2},{3,19},{19,3},{4,20},{20... | collective-permute-start | bytes 829448 | tf_op jit(solution)/shard_map/ppermute | solution.py:190
  398.2 21.1 %collective-permute-start.28 = (bf16[4,96,384]{2,1,0:T(8,128)(2,1)}, bf16[4,96,384]{2,1,0:T(8,128)(2,1)S(1)}, u32[]{:S(2)}, u32[]{:S(2)}) collective-permute-start(bf16[4,96,384]{2,1,0:T(8,128)(2,1)} %get-tuple-element.233.refs_12_), channel_id=1, source_target_pairs={{0,8},{1,9},{2,10},{3,11},{4,12},{5,13},{6,14},{7,15},{8,0},{9,1},... | collective-permute-start | bytes 884744 | tf_op jit(solution)/shard_map/ppermute | solution.py:190
  399.6 22.1 %collective-permute-start.29 = (bf16[4,304,384]{2,1,0:T(8,128)(2,1)}, bf16[4,304,384]{2,1,0:T(8,128)(2,1)S(1)}, u32[]{:S(2)}, u32[]{:S(2)}) collective-permute-start(bf16[4,304,384]{2,1,0:T(8,128)(2,1)} %get-tuple-element.235.refs_14_.refs_17_), channel_id=1, source_target_pairs={{0,2},{1,3},{2,0},{3,1},{4,6},{5,7},{6,4},{7,5},{8,10},{9,11},{10,... | collective-permute-start | bytes 2801672 | tf_op jit(solution)/shard_map/ppermute | solution.py:190
  443.0 12.9 %collective-permute-start.43 = (f32[16,128]{1,0:T(8,128)S(1)}, f32[16,128]{1,0:T(8,128)S(1)}, u32[]{:S(2)}, u32[]{:S(2)}) collective-permute-start(f32[16,128]{1,0:T(8,128)S(1)} %add_add_fusion.1), channel_id=1, source_target_pairs={{0,6},{1,7},{2,4},{3,5},{4,2},{5,3},{6,0},{7,1},{8,14},{9,15},{10,... | collective-permute-start | bytes 24584 | tf_op jit(solution)/shard_map/ppermute | solution.py:1091
  446.6 16.6 %collective-permute-start.35 = (bf16[96,384]{1,0:T(8,128)(2,1)}, bf16[96,384]{1,0:T(8,128)(2,1)S(1)}, u32[]{:S(2)}, u32[]{:S(2)}) collective-permute-start(bf16[96,384]{1,0:T(8,128)(2,1)} %bitcast.62), channel_id=1, source_target_pairs={{0,17},{1,16},{2,19},{3,18},{4,21},{5,20},{6,23},{7,22},{8,25},{9,... | collective-permute-start | bytes 221192 | tf_op jit(solution)/shard_map/ppermute | solution.py:1125
  (51 other events, 346.1 us)
Sparse Core Ops, SparseCore 0:
  21.7 101.6 all-gather.2

commit v4 on v3

--- a/solution.py
+++ b/solution.py
@@ -12,13 +12,12 @@
 F32 = jnp.float32
 BF16 = jnp.bfloat16
 CHUNK_HEADS = 2
-WINDOW = 256
 LANES = 128
 PIECE = 384
 LONG, SHORT = 10**11, 17 * 10**9
 TOKENS = 128
 HIDDEN = 768
-VMEM_LIMIT = 60 * 2**20
+VMEM_LIMIT = 63 * 2**20
 
 
 def dot(left, right, left_dim=1, right_dim=0):
@@ -72,7 +71,7 @@
         self.last = []
 
 
-def call(name, kernel, grid, ins, outs, scratch, deps, order, flops=LONG, aliases={}):
+def call(name, kernel, grid, ins, outs, scratch, deps, order, flops=LONG, aliases={}, vmem=VMEM_LIMIT):
     inputs = len(ins)
     deps = list(deps) + order.last
 
@@ -90,7 +89,7 @@
         ),
         out_shape=[jax.ShapeDtypeStruct(shape, dtype) for shape, dtype, _ in outs],
         compiler_params=pltpu.CompilerParams(
-            vmem_limit_bytes=VMEM_LIMIT, dimension_semantics=("arbitrary",)
+            vmem_limit_bytes=vmem, dimension_semantics=("arbitrary",)
         ),
         cost_estimate=pl.CostEstimate(flops=flops, bytes_accessed=10**6, transcendentals=0),
         name=name,
@@ -100,27 +99,38 @@
     return found
 
 
-def combine(outputs, order):
+def combine(outputs, order, near=False):
+    held = pl.BlockSpec(memory_space=pltpu.VMEM)
     ins, outs, plan = [], [], []
     for terms in outputs:
         if isinstance(terms, tuple):
             bit, *arrays = terms
-            terms = [(array, array.shape[0], lambda place: 0) for array in arrays]
+            terms = [(array, array.shape[0], lambda place: 0, True) for array in arrays]
         else:
             bit = None
-        array, slabs, _ = terms[0]
+        array, slabs = terms[0][:2]
         shape = (slabs,) + array.shape[1:]
         rest = (0,) * (len(shape) - 1)
-        plan.append((bit, list(range(len(ins), len(ins) + len(terms)))))
-        for term, _, index in terms:
-            ins.append(
-                (term, pl.BlockSpec(shape, lambda t, place, index=index, rest=rest: (index(place),) + rest))
-            )
-        outs.append((shape, array.dtype, pl.BlockSpec(shape, lambda t, place, rest=rest: (0,) + rest)))
+        sources = []
+        for term, _, index, small in terms:
+            if near and small:
+                sources.append((len(ins), index, slabs))
+                ins.append((term, held))
+            else:
+                sources.append((len(ins), None, slabs))
+                ins.append(
+                    (term, pl.BlockSpec(shape, lambda t, place, index=index, rest=rest: (index(place),) + rest))
+                )
+        plan.append((bit, sources))
+        blocked = pl.BlockSpec(shape, lambda t, place, rank=len(shape): (0,) * rank)
+        outs.append((shape, array.dtype, held if near else blocked))
 
     def kernel(place, *refs):
         for (bit, sources), out_ref in zip(plan, refs[len(ins) :]):
-            values = [refs[i][...] for i in sources]
+            values = [
+                refs[i][...] if index is None else refs[i][pl.ds(index(place) * slabs, slabs)]
+                for i, index, slabs in sources
+            ]
             if bit is not None:
                 out_ref[...] = jnp.where(place[bit] == 0, values[0], values[1])
             elif len(values) == 1:
@@ -129,7 +139,7 @@
                 total = sum((v.astype(F32) for v in values[1:]), values[0].astype(F32))
                 out_ref[...] = total.astype(out_ref.dtype)
 
-    return call("combine", kernel, 1, ins, outs, [], [], order)
+    return call("combine", kernel, 1, ins, outs, [], [], order, vmem=16 * 2**20 if near else VMEM_LIMIT)
 
 
 class Halving:
@@ -192,30 +202,31 @@
         def halves(at, size):
             return [
                 [
-                    (p, size, lambda place, base=base, at=at, flip=flip: 2 * base(place) + (place[at] ^ flip))
-                    for p, base in parts
+                    (p, size, lambda place, base=base, at=at, flip=flip: 2 * base(place) + (place[at] ^ flip), held)
+                    for p, base, held in parts
                 ]
                 for flip in (1, 0)
             ]
 
         zero = lambda place: 0
-        parts, size = [(array, zero)], array.shape[0]
+        parts, size = [(array, zero, False)], array.shape[0]
         for axis, bit in self.order:
             at = bit if axis == "sample" else last
             size = size // 2
             if len(parts) == 1 and (axis, bit) == ("sample", 0):
-                parts = [(array, lambda place: place[0]), (exchange(array, axis, bit), lambda place: place[0])]
+                first = lambda place: place[0]
+                parts = [(array, first, False), (exchange(array, axis, bit), first, False)]
                 continue
             if len(parts) == 1:
                 (sent,) = yield halves(at, size)[:1]
-                parts = [(array, lambda place, at=at: place[at]), (exchange(sent, axis, bit), zero)]
+                parts = [(array, lambda place, at=at: place[at], False), (exchange(sent, axis, bit), zero, True)]
             else:
                 sent, kept = yield halves(at, size)
-                parts = [(kept, zero), (exchange(sent, axis, bit), zero)]
+                parts = [(kept, zero, True), (exchange(sent, axis, bit), zero, True)]
         if after in ("swap", "cores"):
             sent, kept = yield halves(0, size // 2)
             return kept[0], exchange(sent, "sample", 0)[0] if after == "swap" else sent[0]
-        (held,) = yield [[(p, 1, base) for p, base in parts]]
+        (held,) = yield [[(p, 1, base, near) for p, base, near in parts]]
         if not after:
             return held[0]
         if self.halves() == 2:
@@ -224,7 +235,7 @@
             return first[0], second[0]
         for bit in range(self.counts["struct"].bit_length() - 1):
             received = exchange(held, "struct", bit)
-            (held,) = yield [[(p, 1, zero) for p in (held, received)]]
+            (held,) = yield [[(p, 1, zero, True) for p in (held, received)]]
         return held[0]
 
 class Running:
@@ -241,12 +252,12 @@
             self.result = stop.value
 
 
-def advance(order, *running):
+def advance(order, *running, near=False):
     running = [r for r in running if r.result is None]
     asked = [output for r in running for output in r.asked]
     if not asked:
         return []
-    made = combine(asked, order)
+    made = combine(asked, order, near)
     at = 0
     for r in running:
         count = len(r.asked)
@@ -324,6 +335,12 @@
         return carry
 
     lax.fori_loop(0, pair_ref.shape[0], row, 0, unroll=8)
+
+    @pl.when((pl.program_id(0) == pl.num_programs(0) - 1) & (place[0] == 1))
+    def _():
+        half = weight_grad_ref.shape[0] // 2
+        total = weight_grad_ref[...]
+        weight_grad_ref[...] = jnp.concatenate([total[half:], total[:half]], axis=0)
 
 
 def pair_backward(first, count, block, out, pair, grads, gain, weight_t, deps, order):
@@ -381,10 +398,6 @@
     return pl.ds(pl.multiple_of(step * tokens, tokens), tokens)
 
 
-def window_start(chunk, head_dim, width):
-    return min(chunk * CHUNK_HEADS * head_dim // LANES * LANES, width - WINDOW)
-
-
 def inputs_kernel(
     place, acts_ref, acts_other_ref, cot_ref, cot_other_ref,
     cond_ref, gain_ref, cond_w_ref, cond_b_ref, zero_w_ref, zero_b_ref,
@@ -418,8 +431,11 @@
 
     def put(values, nat_ref, t_ref):
         low = values.astype(BF16).reshape(samples, tokens, half)
-        for window in range(nat_ref.shape[0]):
-            nat_ref[window] = low[:, :, window * LANES : window * LANES + WINDOW]
+        chunks = nat_ref.shape[0]
+        used = half // chunks
+        for chunk in range(chunks):
+            nat_ref[chunk, :, :, :used] = low[:, :, chunk * used : (chunk + 1) * used]
+            nat_ref[chunk, :, :, used:] = jnp.zeros((samples, tokens, LANES - used), BF16)
         for s in range(samples):
             t_ref[s] = low[s].T
 
@@ -445,14 +461,14 @@
     ]
 
 
-def inputs_call(acts, acts_other, cot, cot_other, cond, branch, qkvg_w, q_bias, out_w, deps, order):
+def inputs_call(acts, acts_other, cot, cot_other, cond, branch, qkvg_w, q_bias, out_w, heads, deps, order):
     own_samples, length, width = acts.shape
     samples, half = 2 * own_samples, width // 2
-    windows = (half - WINDOW) // LANES + 1
+    chunks = heads // 2 // CHUNK_HEADS
     block = spec((own_samples, TOKENS, width), 1)
     wide = spec((samples, TOKENS, width), 1)
     narrow = spec((samples, TOKENS, half), 1)
-    nat = spec((windows, samples, TOKENS, WINDOW), 2)
+    nat = spec((chunks, samples, TOKENS, LANES), 2)
     turned = spec((samples, half, TOKENS), 2)
     return call(
         "inputs",
@@ -468,7 +484,7 @@
             ((samples, length, half), F32, narrow),
             ((samples, length, half), F32, narrow),
         ]
-        + [((windows, samples, length, WINDOW), BF16, nat)] * 4
+        + [((chunks, samples, length, LANES), BF16, nat)] * 4
         + [((samples, half, length), BF16, turned)] * 4
         + [((length, width), F32, spec((length, width)))] * 2,
         [pltpu.VMEM((length, width), F32)],
@@ -573,13 +589,13 @@
 
 
 def attention_kernel(
-    halving, head_dim, first_lane, place, q_ref, k_ref, v_ref, g_ref, qt_ref, kt_ref, vt_ref, gt_ref, bias_ref,
+    halving, head_dim, place, q_ref, k_ref, v_ref, g_ref, qt_ref, kt_ref, vt_ref, gt_ref, bias_ref,
     mixed_ref, dq_ref, dkt_ref, dvt_ref, db_ref, kz, vz, plow, dslow, dsum,
 ):
     h = pl.program_id(0)
     samples, length, wide = q_ref.shape
     scale = head_dim ** (-0.5)
-    off = pl.multiple_of(first_lane + h * head_dim, 16)
+    off = pl.multiple_of(h * head_dim, 16)
     lane = lax.broadcasted_iota(jnp.int32, (1, wide), 1)
     mask = ((lane >= off) & (lane < off + head_dim)).astype(BF16)
 
@@ -603,14 +619,14 @@
         x = jnp.exp(x - jnp.max(x, axis=-1, keepdims=True))
         probs = x * (1.0 / jnp.sum(x, axis=-1, keepdims=True))
         low = probs.astype(BF16)
-        plow[...] = low
+        plow[s % 2] = low
         mixed = dot(low, v_ref[s] * mask)
         mixed_ref[s] += mixed
         grad = g_ref[s]
         delta = jnp.sum(grad.astype(F32) * mixed, axis=-1, keepdims=True)
         grad_scores = probs * (dot(grad, vz[s]) - delta)
-        grad_low = (grad_scores * scale).astype(BF16)
-        dslow[...] = grad_low
+        grad_low = grad_scores.astype(BF16)
+        dslow[s % 2] = grad_low
         total = grad_scores if s == 0 else dsum[...] + grad_scores
         if s < samples - 1:
             dsum[...] = total
@@ -619,17 +635,15 @@
                 for c in range(2):
                     at = (dest + c) * share
                     db_ref[2 * p + c, 0] = total[at : at + share].astype(BF16)
-        dq_ref[s] += dot(grad_low, k_ref[s] * mask)
-        dvt_ref[s] = dot(gt_ref[s], plow[...]).astype(BF16)
-        dkt_ref[s] = dot(qt_ref[s], dslow[...]).astype(BF16)
+        dq_ref[s] += dot(grad_low, k_ref[s] * mask) * scale
+        dvt_ref[s] = dot(gt_ref[s], plow[s % 2]).astype(BF16)
+        dkt_ref[s] = (dot(qt_ref[s], dslow[s % 2]) * scale).astype(BF16)
 
 
 def attention_call(chunk, nats, turned, bias, head_dim, halving, deps, order):
     _, samples, length, wide = nats[0].shape
-    half = turned[0].shape[1]
     parts, heads, share, _ = bias.shape
-    start = window_start(chunk, head_dim, half)
-    nat = pl.BlockSpec((None, samples, length, wide), lambda h, core: (start // LANES, 0, 0, 0))
+    nat = pl.BlockSpec((None, samples, length, wide), lambda h, core: (chunk, 0, 0, 0))
     turn = pl.BlockSpec((samples, head_dim, length), lambda h, core: (0, chunk * CHUNK_HEADS + h, 0))
     turn_out = pl.BlockSpec((samples, head_dim, length), lambda h, core: (0, h, 0))
     bias_in = pl.BlockSpec(
@@ -639,7 +653,7 @@
     held = pl.BlockSpec((samples, length, wide), lambda h, core: (0, 0, 0))
     return call(
         "attention",
-        functools.partial(attention_kernel, halving, head_dim, chunk * CHUNK_HEADS * head_dim - start),
+        functools.partial(attention_kernel, halving, head_dim),
         CHUNK_HEADS,
         [(a, nat) for a in nats] + [(a, turn) for a in turned] + [(bias, bias_in)],
         [((samples, length, wide), F32, held)] * 2
@@ -648,8 +662,8 @@
         [
             pltpu.VMEM((samples, wide, length), BF16),
             pltpu.VMEM((samples, wide, length), BF16),
-            pltpu.VMEM((length, length), BF16),
-            pltpu.VMEM((length, length), BF16),
+            pltpu.VMEM((2, length, length), BF16),
+            pltpu.VMEM((2, length, length), BF16),
             pltpu.VMEM((length, length), F32),
         ],
         deps,
@@ -658,28 +672,19 @@
     )
 
 
-def mixed_kernel(head_dim, chunks, place, *refs):
+def mixed_kernel(chunks, place, *refs):
     (gate_ref, gated_grad_ref), refs = refs[:2], refs[2:]
     mixed_refs, refs = refs[:chunks], refs[chunks:]
     dq_refs, refs = refs[:chunks], refs[chunks:]
     dkt_refs, refs = refs[:chunks], refs[chunks:]
     dvt_refs, refs = refs[:chunks], refs[chunks:]
-    gated_refs, joined_refs, q_bias_out = refs[:2], refs[2:4], refs[4]
+    joined_refs, q_bias_out = refs[:2], refs[2]
     clear(pl.program_id(0), q_bias_out)
     samples, tokens, half = gate_ref.shape
     own_samples = samples // 2
 
-    def join(window_refs):
-        pieces = []
-        for tile in range(half // LANES):
-            held = [
-                ref[:, :, tile * LANES - start : (tile + 1) * LANES - start]
-                for chunk, ref in enumerate(window_refs)
-                for start in [window_start(chunk, head_dim, half)]
-                if start <= tile * LANES < start + WINDOW
-            ]
-            pieces.append(functools.reduce(jnp.add, held))
-        return jnp.concatenate(pieces, axis=-1)
+    def join(refs):
+        return jnp.concatenate([ref[:, :, : half // chunks] for ref in refs], axis=-1)
 
     def turn(turned_refs):
         joined = jnp.concatenate([ref[...] for ref in turned_refs], axis=1)
@@ -691,30 +696,28 @@
     grad_queries = join(dq_refs)
     q_bias_out[...] += column_sum(grad_queries)
     grad_gate = gated_grad_ref[...] * mixed * slope(gate)
-    parts = [grad_queries.astype(BF16), turn(dkt_refs), turn(dvt_refs), grad_gate.astype(BF16)]
+    parts = [gated, grad_queries.astype(BF16), turn(dkt_refs), turn(dvt_refs), grad_gate.astype(BF16)]
     for i in range(2):
         here = slice(i * own_samples, (i + 1) * own_samples)
-        gated_refs[i][...] = gated[here]
         for j, part in enumerate(parts):
             joined_refs[i][:, :, j * half : (j + 1) * half] = part[here]
 
 
-def mixed_call(gate, gated_grad, mixeds, dqs, dkts, dvts, head_dim, deps, order):
+def mixed_call(gate, gated_grad, mixeds, dqs, dkts, dvts, deps, order):
     samples, length, half = gate.shape
     chunks = len(mixeds)
     own_samples = samples // 2
     block = spec((samples, TOKENS, half), 1)
-    window = spec((samples, TOKENS, WINDOW), 1)
+    window = spec((samples, TOKENS, LANES), 1)
     turned = spec((samples, half // chunks, TOKENS), 2)
     return call(
         "mixed",
-        functools.partial(mixed_kernel, head_dim, chunks),
+        functools.partial(mixed_kernel, chunks),
         length // TOKENS,
         [(a, block) for a in (gate, gated_grad)]
         + [(a, window) for a in mixeds + dqs]
         + [(a, turned) for a in dkts + dvts],
-        [((own_samples, length, half), BF16, spec((own_samples, TOKENS, half), 1))] * 2
-        + [((own_samples, length, 4 * half), BF16, spec((own_samples, TOKENS, 4 * half), 1))] * 2
+        [((own_samples, length, 5 * half), BF16, spec((own_samples, TOKENS, 5 * half), 1))] * 2
         + [((1, half), F32, spec((1, half)))],
         [],
         deps,
@@ -722,38 +725,48 @@
     )
 
 
-def qkvg_kernel(halving, place, first_ref, joined_ref, joined_other_ref, packed_out):
+def qkvg_kernel(halving, place, first_ref, *refs):
+    joined_refs, other_refs, packed_out = refs[:2], refs[2:4], refs[4]
     step = pl.program_id(0)
     samples, length, width = first_ref.shape
     rows = samples * length // 2
-    half = joined_ref.shape[2]
-    grad = dot(first_ref[: samples // 2].reshape(rows, width), joined_ref[...].reshape(rows, half), 0, 0)
-    grad += dot(first_ref[samples // 2 :].reshape(rows, width), joined_other_ref[...].reshape(rows, half), 0, 0)
+    half = joined_refs[0].shape[2]
+
+    def both(pair):
+        return jnp.concatenate([ref[...].reshape(rows, half) for ref in pair], axis=1)
+
+    grad = dot(first_ref[: samples // 2].reshape(rows, width), both(joined_refs), 0, 0)
+    grad += dot(first_ref[samples // 2 :].reshape(rows, width), both(other_refs), 0, 0)
     share = packed_out.shape[1] * halving.halves() // 4
 
     for block in range(4):
 
-        @pl.when(step == block)
+        @pl.when(step == block // 2)
         def _():
+            column = block % 2 * half
             for p, (dest, part) in enumerate(halving.places()):
                 piece = block - part * (4 // halving.halves())
                 if 0 <= piece < 4 // halving.halves():
                     for c in range(2):
                         at = (dest + c) * share
-                        packed_out[2 * p + c, piece * share : (piece + 1) * share] = grad[at : at + share].astype(BF16)
+                        packed_out[2 * p + c, piece * share : (piece + 1) * share] = grad[
+                            at : at + share, column : column + half
+                        ].astype(BF16)
 
 
 def qkvg_call(first, joined, joined_other, halving, deps, order):
     samples, length, width = first.shape
-    half = joined.shape[2] // 4
+    half = joined.shape[2] // 5
     share = width // halving.counts["sample"]
     slabs = (2 * 2 ** len(halving.order), 4 // halving.halves() * share, half)
-    block = spec((samples // 2, length, half), 2)
+    blocks = [
+        pl.BlockSpec((samples // 2, length, half), lambda t, place, i=i: (0, 0, 1 + 2 * t + i)) for i in range(2)
+    ]
     (packed,) = call(
         "qkvg_grad",
         functools.partial(qkvg_kernel, halving),
-        4,
-        [(first, spec(first.shape)), (joined, block), (joined_other, block)],
+        2,
+        [(first, spec(first.shape))] + [(a, b) for a in (joined, joined_other) for b in blocks],
         [(slabs, BF16, spec(slabs))],
         [],
         deps,
@@ -763,7 +776,7 @@
 
 
 def outputs_kernel(place, acts_ref, cot_ref, partial_ref, acts_part_ref, zero_gate_ref, factor_ref, *refs):
-    gated_refs, joined_refs, refs = refs[:2], refs[2:4], refs[4:]
+    joined_refs, refs = refs[:2], refs[2:]
     out_w_refs, qkvg_refs, refs = refs[:2], (refs[2:6], refs[6:10]), refs[10:]
     block_ref, acts_grad_ref, projected_ref, zero_low_ref, cond_b_out, zero_b_out, out_out = refs
     clear(pl.program_id(0), cond_b_out, zero_b_out, out_out)
@@ -777,12 +790,12 @@
     grad_att = (grad_out * zero_gate[None]).astype(BF16).reshape(rows, width)
     attended = grad_input = 0.0
     for i, half_at in enumerate((place[0], 1 - place[0])):
-        gated = gated_refs[i][...].reshape(rows, half)
+        gated = joined_refs[i][:, :, :half].reshape(rows, half)
         attended += dot(gated, out_w_refs[i][...])
         out_out[pl.ds(pl.multiple_of(half_at * half, half), half), :] += dot(gated, grad_att, 0, 0)
         for j in range(4):
             grad_input += dot(
-                joined_refs[i][:, :, j * half : (j + 1) * half].reshape(rows, half), qkvg_refs[i][j][...], 1, 1
+                joined_refs[i][:, :, (1 + j) * half : (2 + j) * half].reshape(rows, half), qkvg_refs[i][j][...], 1, 1
             )
     attended = attended.reshape(samples, tokens, width)
     grad_input = grad_input.reshape(samples, tokens, width)
@@ -799,7 +812,7 @@
     ).astype(BF16)
 
 
-def outputs_call(acts, cot, partial, acts_part, zero_gate, factor, gateds, joineds, out_w, qkvg_w, deps, order):
+def outputs_call(acts, cot, partial, acts_part, zero_gate, factor, joineds, out_w, qkvg_w, deps, order):
     samples, length, width = acts.shape
     half = width // 2
     block = spec((samples, TOKENS, width), 1)
@@ -810,8 +823,7 @@
         length // TOKENS,
         [(a, block) for a in (acts, cot, partial, acts_part)]
         + [(zero_gate, tokens), (factor, tokens)]
-        + [(a, spec((samples, TOKENS, half), 1)) for a in gateds]
-        + [(a, spec((samples, TOKENS, 4 * half), 1)) for a in joineds]
+        + [(a, spec((samples, TOKENS, 5 * half), 1)) for a in joineds]
         + [(out_w, spec((half, width), at=(whose, 0))) for whose in (own, other)]
         + quarters(qkvg_w, own)
         + quarters(qkvg_w, other),
@@ -939,8 +951,18 @@
 
     grad = choose(pair_sum_ref[...])
     pair_w_out[...] = grad
-    weighted = jnp.sum(grad * choose(pair_wt_ref[...].astype(F32)), axis=1, keepdims=True)
-    pair_gain_out[...] = weighted / choose(pair_gain_ref[...])
+    weighted = grad * choose(pair_wt_ref[...].astype(F32))
+
+    def across(left, right, right_dim):
+        return lax.dot_general(
+            left,
+            right,
+            (((1,), (right_dim,)), ((), ())),
+            precision=lax.Precision.HIGHEST,
+            preferred_element_type=F32,
+        )
+
+    pair_gain_out[...] = across(jnp.ones((1, heads), F32), weighted, 1) / across(pair_gain_ref[...], chosen, 0)
 
 
 def results_call(
@@ -954,7 +976,7 @@
     arrays = [cond, (cond_w[0], 2 * cond_w[1]), (zero_w[0], 2 * zero_w[1]), (width, 4 * width), out_w, swiglu, down]
     shapes = [(rows // count, columns) for rows, columns in arrays]
     shapes += [(1, size // count) for size in (2 * cond[1], 2 * width, 2 * width, width)]
-    shapes += [(channels // count, 1), (channels // count, heads)]
+    shapes += [(1, channels // count), (channels // count, heads)]
     ins = [*early, *qkvg, rest, rest_got, pair_sum, pair_wt, pair_gain]
     return call(
         "results",
@@ -1036,7 +1058,7 @@
     early = Running(along_y.run(early))
     first, gate, gated_grad, *rest = inputs_call(
         acts, acts_other, cotangent, cotangent_other, cond, conditioning(0) + zero(0), qkvg_w, rows["q_bias"], out_w,
-        [], order,
+        heads, [], order,
     )
     nats, turned, (zero_gate, factor) = rest[:4], rest[4:8], rest[8:]
 
@@ -1051,27 +1073,26 @@
         bias_sums.append(Running(chip_x.run(db, "swap")))
         deps = advance(order, *bias_sums, *([early] if chunk % 2 else []))
 
-    gated, gated_sent, joined, joined_sent, q_bias_grad = mixed_call(
-        gate, gated_grad, mixeds, dqs, dkts, dvts, head_dim, deps, order
-    )
-    gated_got, joined_got = swap(gated_sent), swap(joined_sent)
-    deps = advance(order, *bias_sums)
+    joined, joined_sent, q_bias_grad = mixed_call(
+        gate, gated_grad, mixeds, dqs, dkts, dvts, deps, order
+    )
+    joined_got = swap(joined_sent)
     qkvg_sum = Running(
-        chip_y.run(qkvg_call(first, joined, joined_sent, chip_y, deps, order), "cores")
+        chip_y.run(qkvg_call(first, joined, joined_sent, chip_y, [], order), "cores")
     )
     deps = advance(order, *bias_sums, qkvg_sum, early)
     block_out, acts_grad, projected, zero_low, cond_b_zero, zero_b_zero, out_grad = outputs_call(
-        acts, cotangent, partial, acts_part, zero_gate, factor, [gated, gated_got], [joined, joined_got],
+        acts, cotangent, partial, acts_part, zero_gate, factor, [joined, joined_got],
         out_w, qkvg_w, deps, order,
     )
     deps = advance(order, *bias_sums, qkvg_sum)
-    while any(b.result is None for b in bias_sums):
-        deps += advance(order, *bias_sums)
     rest, rest_shapes = conditions_call(
         cond, conditioning(0), zero(0)[0], zero_low, projected, cond_gate, cond_norm, out_grad,
         [gain_one, cond_b_zero, cond_b_one, zero_b_zero, zero_b_one, q_bias_grad], along_x, deps, order,
     )
     rest = Running(along_x.run(rest, ""))
+    while any(b.result is None for b in bias_sums):
+        advance(order, *bias_sums)
     share = length // sample_devices
     block = 16 if share % 16 == 0 else share
     turned_wt = jnp.where(core == 0, pair_wt, jnp.roll(pair_wt, heads // 2, axis=0))
@@ -1096,7 +1117,7 @@
         return (array + found[0]) + (found[1] + found[2])
 
     class Pair:
-        asked = [[(p, p.shape[0], lambda place: 0) for p in pair_parts]]
+        asked = [[(p, p.shape[0], lambda place: 0, True) for p in pair_parts]]
         result = None
 
         def send(self, found):
@@ -1106,14 +1127,13 @@
     advance(order, pair_grad, qkvg_sum, rest, early)
     left = [bits + struct_bits - 1] + list(range(bits + struct_bits - 1)) if struct_bits else list(range(bits))
     pair_sum = pair_grad.result
-    pair_sum = jnp.where(core == 0, pair_sum, jnp.roll(pair_sum, heads // 2, axis=0))
     while left:
         one = 1 << left.pop(0)
         two = 1 << left.pop(0) if left else 0
         pair_sum = summed(pair_sum, one, two, one | two) if two else summed(pair_sum, one)
     chains = (qkvg_sum, rest, early)
     while any(r.result is None for r in chains):
-        advance(order, *chains)
+        advance(order, *chains, near=True)
     mine_qkvg, sent = qkvg_sum.result
     if chip_y.halves() == 2:
         across = [
@@ -1144,7 +1164,7 @@
         cond_sum = along_x.unpack(rest.result, rest_shapes)[3][0].astype(F32)
     return (
         block_out[None], acts_grad[None], cond_sum[None], grad_pair[None], gains[0], cond_w_sum, cond_b[0], zero_w_sum,
-        zero_b[0], qkvg_total, q_b[0], out_sum, swiglu_sum, down_sum, pair_g[:, 0], pair_w_sum,
+        zero_b[0], qkvg_total, q_b[0], out_sum, swiglu_sum, down_sum, pair_g[0], pair_w_sum,
     )
 
 

time: 483 us -> 458 us (0.948)
  Pallas kernels: 362 us -> 342 us
  waiting for transfers between devices: 39.7 us -> 47.6 us
  local copies, waits for them, and re-layouts: 16.2 us -> 8.89 us
    pallas_call x26, Pallas kernels: 362 us -> 342 us  [call(): pl.pallas_call(run, grid_spec=pltpu.PrefetchScalarGridSpec(num_scalar_pre...]
    ppermute x30, waiting for transfers between devices: 28.7 us -> 37.8 us  [exchange(): lax.ppermute(array, axis, [(i, i ^ 1 << bit) for i in range(self.counts[a...]
    unnamed x78 -> x62, local copies, waits for them, and re-layouts: 12.7 us -> 5.4 us
  transfers between devices with their start and end apart: 46 -> 45, of which waited for: 12 -> 14; matrix products, arithmetic and copies ran while one was open for 1% -> 1% of each run, Pallas kernels for 67% -> 67%
where the time goes in v4:
time: 458 us; the launch traced here: 454 us
  Pallas kernels  342 us (75%)
  waiting for transfers between devices  47.6 us (10%)
  starting transfers between devices  39.1 us (9%)
  between operations  15.4 us (3%)
  local copies, waits for them, and re-layouts  8.89 us (2%)
    pallas_call x26, Pallas kernels, call(): pl.pallas_call(run, grid_spec=pltpu.PrefetchScalarGridSpec(num_scalar_pre...  342 us
    ppermute x30, waiting for transfers between devices, exchange(): lax.ppermute(array, axis, [(i, i ^ 1 << bit) for i in range(self.counts[a...  37.8 us
    ppermute x30, starting transfers between devices, exchange(): lax.ppermute(array, axis, [(i, i ^ 1 << bit) for i in range(self.counts[a...  30.6 us
  transfers between devices with their start and end apart: 45, of which 14 were waited for; matrix products, arithmetic and copies ran while one was open for 1% of the time, Pallas kernels for 67%

profile of v4, /device:TPU:0, one launch (start us, length us, event | category | flops | bytes accessed | tf_op | source)
XLA Modules:
  0.0 454.0 jit_solution(8768843398314302424)
XLA Ops:
  8.4 13.0 %pair_forward.1 = bf16[16,48,768]{2,1,0:T(8,128)(2,1)} custom-call(s32[5]{0:T(128)} %broadcast_1_place_ref.2.place_ref, bf16[48,768,128]{2,1,0:T(8,128)(2,1)} %bitcast.49, bf16[1,128]{1,0:T(2,128)(2,1)} %bitcast.63, bf16[16,128]{1,0:T(8,128)(2,1)} %bitcast.42, s32[1,768]{1,0:T(1,128)} %refs_3_.2, s32[1]{0:T(128)S(6)} %copy.40.refs_4_), custom_call_target="tpu_custom_call" | custom-call | flops 99999997952 | bytes 1000000 | tf_op jit(solution)/shard_map/pair_forward/pallas_call | solution.py:81
  23.9 57.3 %transition.1 = (f32[2,768,768]{2,1,0:T(8,128)}, f32[2,768,768]{2,1,0:T(8,128)}, f32[768,384]{1,0:T(8,128)}, f32[768,384]{1,0:T(8,128)}, bf16[32,360,384]{2,1,0:...) custom-call(s32[5]{0:T(128)} %stack.23.place_ref, bf16[2,768,768]{2,1,0:T(8,128)(2,1)} %bitcast.53, ...), custom_call_target="tpu_custom_call" | custom-call | flops 99999997952 | bytes 1000000 | tf_op jit(solution)/shard_map/transition/pallas_call | solution.py:81
  83.0 27.9 %inputs.1 = (bf16[4,768,768]{2,1,0:T(8,128)(2,1)}, f32[4,768,384]{2,1,0:T(8,128)}, f32[4,768,384]{2,1,0:T(8,128)}, bf16[4,4,768,128]{3,2,1,0:T(8,128)(2,1)}, bf1...) custom-call(s32[5]{0:T(128)} %stack.23.place_ref, ...), custom_call_target="tpu_custom_call" | custom-call | flops 99999997952 | bytes 1000000 | tf_op jit(solution)/shard_map/inputs/pallas_call | solution.py:81
  110.9 7.1 %combine.12 = (bf16[8,360,384]{2,1,0:T(8,128)(2,1)}, bf16[8,360,384]{2,1,0:T(8,128)(2,1)}) custom-call(s32[5]{0:T(128)} %stack.23.place_ref, bf16[32,360,384]{2,1,0:T(8,128)(2,1)} %get-tuple-element.140.refs_16_.refs_0_.refs_2_, bf16[32,360,384]{2,1,0:T(8,128)(2,1)} %collective-permute-done.2.refs_1_.refs_3_, ...), custom_call_target="tpu_custom_call" | custom-call | flops 99999997952 | bytes 1000000 | tf_op jit(solution)/shard_map/combine/pallas_call | solution.py:81
  120.4 2.8 all-gather.3.cloned.1.call-done
  123.2 23.1 %attention.4 = (f32[4,768,128]{2,1,0:T(8,128)}, f32[4,768,128]{2,1,0:T(8,128)}, bf16[4,96,768]{2,1,0:T(8,128)(2,1)}, bf16[4,96,768]{2,1,0:T(8,128)(2,1)}, bf16[16,2,48,768]{3,2,1,0:T(8,128)(2,1)}) custom-call(s32[5]{0:T(128)} %stack.23.place_ref, bf16[4,4,768,128]{3,2,1,0:T(8,128)(2,1)} %get-tuple-element.145.refs_0_, ...), custom_call_target="tpu_custom_call" | custom-call | flops 16999999488 | bytes 1000000 | tf_op jit(solution)/shard_map/attention/pallas_call | solution.py:81
  146.3 3.0 combine.13.refs_9_.refs_10_
  150.6 23.3 %attention.5 = (f32[4,768,128]{2,1,0:T(8,128)}, f32[4,768,128]{2,1,0:T(8,128)}, bf16[4,96,768]{2,1,0:T(8,128)(2,1)}, bf16[4,96,768]{2,1,0:T(8,128)(2,1)}, bf16[16,2,48,768]{3,2,1,0:T(8,128)(2,1)}) custom-call(s32[5]{0:T(128)} %stack.23.place_ref, bf16[4,4,768,128]{3,2,1,0:T(8,128)(2,1)} %get-tuple-element.145.refs_0_, ...), custom_call_target="tpu_custom_call" | custom-call | flops 16999999488 | bytes 1000000 | tf_op jit(solution)/shard_map/attention/pallas_call | solution.py:81
  173.9 3.9 collective-permute-done.3.refs_1_.refs_3_
  177.8 6.3 %combine.14 = (bf16[4,2,48,768]{3,2,1,0:T(8,128)(2,1)}, bf16[4,2,48,768]{3,2,1,0:T(8,128)(2,1)}, bf16[8,2,48,768]{3,2,1,0:T(8,128)(2,1)}, bf16[4,360,384]{2,1,0:T(8,128)(2,1)}, bf16[4,360,384]{2,1,0:T(8,128)(2,1)}) custom-call(s32[5]{0:T(128)} %stack.23.place_ref, bf16[16,2,48,768]{3,2,1,0:T(8,128)(2,1)} %get-tuple-element.157.refs_0_.refs_1_.refs_2_, ...), custom_call_target="tpu_custom_call" | custom-call | flops 99999997952 | bytes 1000000 | tf_op jit(solution)/shard_map/combine/pallas_call | solution.py:81
  187.4 23.3 %attention.6 = (f32[4,768,128]{2,1,0:T(8,128)}, f32[4,768,128]{2,1,0:T(8,128)}, bf16[4,96,768]{2,1,0:T(8,128)(2,1)}, bf16[4,96,768]{2,1,0:T(8,128)(2,1)}, bf16[16,2,48,768]{3,2,1,0:T(8,128)(2,1)}) custom-call(s32[5]{0:T(128)} %stack.23.place_ref, bf16[4,4,768,128]{3,2,1,0:T(8,128)(2,1)} %get-tuple-element.145.refs_0_, ...), custom_call_target="tpu_custom_call" | custom-call | flops 16999999488 | bytes 1000000 | tf_op jit(solution)/shard_map/attention/pallas_call | solution.py:81
  213.2 4.7 %combine.15 = (bf16[2,2,48,768]{3,2,1,0:T(8,128)(2,1)}, bf16[2,2,48,768]{3,2,1,0:T(8,128)(2,1)}, bf16[4,2,48,768]{3,2,1,0:T(8,128)(2,1)}, bf16[4,2,48,768]{3,2,1,0:T(8,128)(2,1)}, bf16[8,2,48,768]{3,2,1,0:T(8,128)(2,1)}) custom-call(s32[5]{0:T(128)} %stack.23.place_ref, bf16[4,2,48,768]{3,2,1,0:T(8,128)(2,1)} %get-tuple-element.161.refs_10_.refs_0_.refs_2_, ...), custom_call_target="tpu_custom_call" | custom-call | flops 99999997952 | bytes 1000000 | tf_op jit(solution)/shard_map/combine/pallas_call | solution.py:81
  222.3 23.5 %attention.7 = (f32[4,768,128]{2,1,0:T(8,128)}, f32[4,768,128]{2,1,0:T(8,128)}, bf16[4,96,768]{2,1,0:T(8,128)(2,1)}, bf16[4,96,768]{2,1,0:T(8,128)(2,1)}, bf16[16,2,48,768]{3,2,1,0:T(8,128)(2,1)}) custom-call(s32[5]{0:T(128)} %stack.23.place_ref, bf16[4,4,768,128]{3,2,1,0:T(8,128)(2,1)} %get-tuple-element.145.refs_0_, ...), custom_call_target="tpu_custom_call" | custom-call | flops 16999999488 | bytes 1000000 | tf_op jit(solution)/shard_map/attention/pallas_call | solution.py:81
  247.4 6.0 %combine.16 = (bf16[1,2,48,768]{3,2,1,0:T(8,128)(2,1)}, bf16[1,2,48,768]{3,2,1,0:T(8,128)(2,1)}, bf16[2,2,48,768]{3,2,1,0:T(8,128)(2,1)}, bf16[2,2,48,768]{3,2,1...) custom-call(s32[5]{0:T(128)} %stack.23.place_ref, ...), custom_call_target="tpu_custom_call" | custom-call | flops 99999997952 | bytes 1000000 | tf_op jit(solution)/shard_map/combine/pallas_call | solution.py:81
  258.2 15.3 %mixed.1 = (bf16[2,768,1920]{2,1,0:T(8,128)(2,1)}, bf16[2,768,1920]{2,1,0:T(8,128)(2,1)}, f32[1,384]{1,0:T(1,128)}) custom-call(s32[5]{0:T(128)} %stack.23.place_ref, f32[4,768,384]{2,1,0:T(8,128)} %get-tuple-element.143.refs_0_, f32[4,768,384]{2,1,0:T(8,128)} %get-tuple-element.144.refs_1_, f32[4,768,128]{2,1,0:T(8,128)} %get-tuple-element.156.refs_2_, ...), custom_call_target="tpu_custom_call" | custom-call | flops 99999997952 | bytes 1000000 | tf_op jit(solution)/shard_map/mixed/pallas_call | solution.py:81
  273.5 14.4 %qkvg_grad.1.refs_12_.refs_17_.refs_8_.refs_10_ = bf16[32,96,384]{2,1,0:T(8,128)(2,1)} custom-call(s32[5]{0:T(128)} %stack.23.place_ref, bf16[4,768,768]{2,1,0:T(8,128)(2,1)} %get-tuple-element.153.refs_4_.refs_0_, bf16[2,768,1920]{2,1,0:T(8,128)(2,1)} %get-tuple-element.195.refs_1_.refs_2_.refs_5_.refs_6_, ...), custom_call_target="tpu_custom_call" | custom-call | flops 99999997952 | bytes 1000000 | tf_op jit(solution)/shard_map/qkvg_grad/pallas_call | solution.py:81
  288.0 6.1 %collective-permute-done.15.refs_14_.refs_16_ = bf16[2,360,384]{2,1,0:T(8,128)(2,1)} collective-permute-done((bf16[2,360,384]{2,1,0:T(8,128)(2,1)}, bf16[2,360,384]{2,1,0:T(8,128)(2,1)}, u32[]{:S(2)}, u32[]{:S(2)}) %collective-permute-start.15) | collective-permute-done | bytes 552992 | tf_op jit(solution)/shard_map/ppermute | solution.py:200
  294.1 5.5 %combine.17 = (bf16[1,2,48,768]{3,2,1,0:T(8,128)(2,1)}, bf16[1,2,48,768]{3,2,1,0:T(8,128)(2,1)}, bf16[2,2,48,768]{3,2,1,0:T(8,128)(2,1)}, bf16[2,2,48,768]{3,2,1...) custom-call(s32[5]{0:T(128)} %stack.23.place_ref, ...), custom_call_target="tpu_custom_call" | custom-call | flops 99999997952 | bytes 1000000 | tf_op jit(solution)/shard_map/combine/pallas_call | solution.py:81
  302.3 25.4 %outputs.1 = (bf16[2,768,768]{2,1,0:T(8,128)(2,1)}, bf16[2,768,768]{2,1,0:T(8,128)(2,1)}, bf16[768,1536]{1,0:T(8,128)(2,1)}, bf16[768,768]{1,0:T(8,128)(2,1)}, f...) custom-call(s32[5]{0:T(128)} %stack.23.place_ref, bf16[2,768,768]{2,1,0:T(8,128)(2,1)} %bitcast.55, ...), custom_call_target="tpu_custom_call" | custom-call | flops 99999997952 | bytes 1000000 | tf_op jit(solution)/shard_map/outputs/pallas_call | solution.py:81
  328.9 4.2 combine.18
  335.3 10.2 %conditions.1.refs_4_.refs_6_ = bf16[16,304,384]{2,1,0:T(8,128)(2,1)} custom-call(s32[5]{0:T(128)} %stack.23.place_ref, bf16[768,384]{1,0:T(8,128)(2,1)} %bitcast.62, f32[1,768]{1,0:T(1,128)} %get-tuple-element.261.refs_3_.refs_5_.refs_1_, bf16[384,3072]{1,0:T(8,128)(2,1)} %refs_2_.1, bf16[384,1536]{1,0:T(8,128)(2,1)} %refs_3_.3, ...), custom_call_target="tpu_custom_call" | custom-call | flops 99999997952 | bytes 1000000 | tf_op jit(solution)/shard_map/conditions/pallas_call | solution.py:81
  345.5 4.5 collective-permute-done.19.refs_1_.refs_3_
  350.7 2.5 combine.19
  355.3 11.9 %pair_backward.2 = (f32[48,768,128]{2,1,0:T(8,128)}, f32[16,128]{1,0:T(8,128)}) custom-call(s32[5]{0:T(128)} %stack.23.place_ref, bf16[48,768,128]{2,1,0:T(8,128)(2,1)} %bitcast.50, f32[1,128]{1,0:T(1,128)} %slice.34.refs_1_.refs_10_, bf16[16,128]{1,0:T(8,128)(2,1)} %maximum_select_fusion.refs_2_, bf16[2,48,768]{2,1,0:T(8,128)(2,1)} %bitcast.69, ...), custom_call_target="tpu_custom_call" | custom-call | flops 99999997952 | bytes 1000000 | tf_op jit(solution)/shard_map/pair_backward/pallas_call | solution.py:81
  367.3 3.3 collective-permute-done.24.refs_1_.refs_3_
  370.6 4.9 %combine.20 = (bf16[4,96,384]{2,1,0:T(8,128)(2,1)}, bf16[4,96,384]{2,1,0:T(8,128)(2,1)}, bf16[4,304,384]{2,1,0:T(8,128)(2,1)}, bf16[4,304,384]{2,1,0:T(8,128)(2,1)}, bf16[1,360,384]{2,1,0:T(8,128)(2,1)}) custom-call(s32[5]{0:T(128)} %stack.23.place_ref, bf16[8,96,384]{2,1,0:T(8,128)(2,1)} %get-tuple-element.224.refs_20_.refs_0_.refs_2_, ...), custom_call_target="tpu_custom_call" | custom-call | flops 99999997952 | bytes 1000000 | tf_op jit(solution)/shard_map/combine/pallas_call | solution.py:81
  379.6 18.3 %pair_backward.3 = (f32[48,768,128]{2,1,0:T(8,128)}, f32[16,128]{1,0:T(8,128)}) custom-call(s32[5]{0:T(128)} %stack.23.place_ref, bf16[48,768,128]{2,1,0:T(8,128)(2,1)} %bitcast.51, f32[1,128]{1,0:T(1,128)} %slice.34.refs_1_.refs_10_, bf16[16,128]{1,0:T(8,128)(2,1)} %maximum_select_fusion.refs_2_, ...), custom_call_target="tpu_custom_call", output_to_operand_aliasing={{0}: (12, {})} | custom-call | flops 99999997952 | bytes 1000000 | tf_op jit(solution)/shard_map/pair_backward/pallas_call | solution.py:81
  401.3 4.2 combine.21
  412.3 4.2 collective-permute-done.31.refs_5_.refs_7_
  424.7 6.2 %collective-permute-done.35.refs_1_ = bf16[1,304,384]{2,1,0:T(8,128)(2,1)S(1)} collective-permute-done((bf16[1,304,384]{2,1,0:T(8,128)(2,1)S(1)}, bf16[1,304,384]{2,1,0:T(8,128)(2,1)S(1)}, u32[]{:S(2)}, u32[]{:S(2)}) %collective-permute-start.35) | collective-permute-done | bytes 233504 | tf_op jit(solution)/shard_map/ppermute | solution.py:200
  433.8 4.5 collective-permute-done.43
  442.1 4.9 %results.1 = (f32[48,384]{1,0:T(8,128)}, f32[24,3072]{1,0:T(8,128)}, f32[24,1536]{1,0:T(8,128)}, f32[48,3072]{1,0:T(8,128)}, f32[48,768]{1,0:T(8,128)}, /*index=...) custom-call(s32[5]{0:T(128)} %stack.23.place_ref, ...), custom_call_target="tpu_custom_call" | custom-call | flops 99999997952 | bytes 1000000 | tf_op jit(solution)/shard_map/results/pallas_call | solution.py:81
  (158 shorter events, 62.6 us)
Async XLA Ops:
  7.2 116.0 %all-gather.3.cloned.1.call-start = ((), (), s32[]{:S(2)}) async-start(), calls=%async_computation | async-start | bytes 20054016 | tf_op jit(solution)/shard_map/all_gather | solution.py:1020
  21.4 61.6 %collective-permute-start = (bf16[2,768,768]{2,1,0:T(8,128)(2,1)}, bf16[2,768,768]{2,1,0:T(8,128)(2,1)}, u32[]{:S(2)}, u32[]{:S(2)}) collective-permute-start(bf16[2,768,768]{2,1,0:T(8,128)(2,1)} %bitcast.52), channel_id=1, source_target_pairs={{0,1},{1,0},{2,3},{3,2},{4,5},{5,4},{6,7},{7,6},{8,9},{9,8},{10,11... | collective-permute-start | bytes 7077896 | tf_op jit(solution)/shard_map/ppermute | solution.py:1015
  21.9 61.0 %collective-permute-start.1 = (bf16[2,768,768]{2,1,0:T(8,128)(2,1)}, bf16[2,768,768]{2,1,0:T(8,128)(2,1)}, u32[]{:S(2)}, u32[]{:S(2)}) collective-permute-start(bf16[2,768,768]{2,1,0:T(8,128)(2,1)} %bitcast.56), channel_id=1, source_target_pairs={{0,1},{1,0},{2,3},{3,2},{4,5},{5,4},{6,7},{7,6},{8,9},{9,8},{10,11... | collective-permute-start | bytes 7077896 | tf_op jit(solution)/shard_map/ppermute | solution.py:1015
  81.2 29.6 %collective-permute-start.2 = (bf16[32,360,384]{2,1,0:T(8,128)(2,1)}, bf16[32,360,384]{2,1,0:T(8,128)(2,1)}, u32[]{:S(2)}, u32[]{:S(2)}) collective-permute-start(bf16[32,360,384]{2,1,0:T(8,128)(2,1)} %get-tuple-element.140.refs_16_.refs_0_.refs_2_), channel_id=1, source_target_pairs={{0,1},{1,0},{2,3},{3,2},{4,5},{5,4},{6,7},{7,6},{8,9},{9,8},{10,11... | collective-permute-start | bytes 26542088 | tf_op jit(solution)/shard_map/ppermute | solution.py:200
  118.0 55.9 %collective-permute-start.4 = (bf16[8,360,384]{2,1,0:T(8,128)(2,1)}, bf16[8,360,384]{2,1,0:T(8,128)(2,1)}, u32[]{:S(2)}, u32[]{:S(2)}) collective-permute-start(bf16[8,360,384]{2,1,0:T(8,128)(2,1)} %get-tuple-element.154.refs_9_.refs_11_), channel_id=1, source_target_pairs={{0,16},{16,0},{1,17},{17,1},{2,18},{18,2},{3,19},{19,3},{4,20},{20... | collective-permute-start | bytes 6635528 | tf_op jit(solution)/shard_map/ppermute | solution.py:200
  149.4 28.4 %collective-permute-start.3 = (bf16[8,2,48,768]{3,2,1,0:T(8,128)(2,1)}, bf16[8,2,48,768]{3,2,1,0:T(8,128)(2,1)}, u32[]{:S(2)}, u32[]{:S(2)}) collective-permute-start(bf16[8,2,48,768]{3,2,1,0:T(8,128)(2,1)} %combine.13.refs_9_.refs_10_), channel_id=1, source_target_pairs={{0,2},{1,3},{2,0},{3,1},{4,6},{5,7},{6,4},{7,5},{8,10},{9,11},{10,... | collective-permute-start | bytes 3538952 | tf_op jit(solution)/shard_map/ppermute | solution.py:200
  184.1 26.6 %collective-permute-start.5 = (bf16[4,2,48,768]{3,2,1,0:T(8,128)(2,1)}, bf16[4,2,48,768]{3,2,1,0:T(8,128)(2,1)S(1)}, u32[]{:S(2)}, u32[]{:S(2)}) collective-permute-start(bf16[4,2,48,768]{3,2,1,0:T(8,128)(2,1)} %get-tuple-element.160.refs_9_), channel_id=1, source_target_pairs={{0,4},{1,5},{2,6},{3,7},{4,0},{5,1},{6,2},{7,3},{8,12},{9,13},{10,... | collective-permute-start | bytes 1769480 | tf_op jit(solution)/shard_map/ppermute | solution.py:200
  185.6 60.3 %collective-permute-start.10 = (bf16[4,360,384]{2,1,0:T(8,128)(2,1)}, bf16[4,360,384]{2,1,0:T(8,128)(2,1)}, u32[]{:S(2)}, u32[]{:S(2)}) collective-permute-start(bf16[4,360,384]{2,1,0:T(8,128)(2,1)} %get-tuple-element.163.refs_12_), channel_id=1, source_target_pairs={{0,4},{1,5},{2,6},{3,7},{4,0},{5,1},{6,2},{7,3},{8,12},{9,13},{10,... | collective-permute-start | bytes 3317768 | tf_op jit(solution)/shard_map/ppermute | solution.py:200
  186.1 27.1 %collective-permute-start.6 = (bf16[8,2,48,768]{3,2,1,0:T(8,128)(2,1)}, bf16[8,2,48,768]{3,2,1,0:T(8,128)(2,1)}, u32[]{:S(2)}, u32[]{:S(2)}) collective-permute-start(bf16[8,2,48,768]{3,2,1,0:T(8,128)(2,1)} %get-tuple-element.162.refs_11_.refs_14_), channel_id=1, source_target_pairs={{0,2},{1,3},{2,0},{3,1},{4,6},{5,7},{6,4},{7,5},{8,10},{9,11},{10,... | collective-permute-start | bytes 3538952 | tf_op jit(solution)/shard_map/ppermute | solution.py:200
  217.9 27.9 %collective-permute-start.7 = (bf16[2,2,48,768]{3,2,1,0:T(8,128)(2,1)}, bf16[2,2,48,768]{3,2,1,0:T(8,128)(2,1)S(1)}, u32[]{:S(2)}, u32[]{:S(2)}) collective-permute-start(bf16[2,2,48,768]{3,2,1,0:T(8,128)(2,1)} %get-tuple-element.167.refs_9_), channel_id=1, source_target_pairs={{0,8},{1,9},{2,10},{3,11},{4,12},{5,13},{6,14},{7,15},{8,0},{9,1},... | collective-permute-start | bytes 884744 | tf_op jit(solution)/shard_map/ppermute | solution.py:200
  220.3 25.5 %collective-permute-start.8 = (bf16[4,2,48,768]{3,2,1,0:T(8,128)(2,1)}, bf16[4,2,48,768]{3,2,1,0:T(8,128)(2,1)S(1)}, u32[]{:S(2)}, u32[]{:S(2)}) collective-permute-start(bf16[4,2,48,768]{3,2,1,0:T(8,128)(2,1)} %get-tuple-element.169.refs_11_), channel_id=1, source_target_pairs={{0,4},{1,5},{2,6},{3,7},{4,0},{5,1},{6,2},{7,3},{8,12},{9,13},{10,... | collective-permute-start | bytes 1769480 | tf_op jit(solution)/shard_map/ppermute | solution.py:200
  221.8 25.6 %collective-permute-start.9 = (bf16[8,2,48,768]{3,2,1,0:T(8,128)(2,1)}, bf16[8,2,48,768]{3,2,1,0:T(8,128)(2,1)}, u32[]{:S(2)}, u32[]{:S(2)}) collective-permute-start(bf16[8,2,48,768]{3,2,1,0:T(8,128)(2,1)} %get-tuple-element.171.refs_13_.refs_14_), channel_id=1, source_target_pairs={{0,2},{1,3},{2,0},{3,1},{4,6},{5,7},{6,4},{7,5},{8,10},{9,11},{10,... | collective-permute-start | bytes 3538952 | tf_op jit(solution)/shard_map/ppermute | solution.py:200
  253.4 101.6 %collective-permute-start.20 = (bf16[1,2,48,768]{3,2,1,0:T(8,128)(2,1)}, bf16[1,2,48,768]{3,2,1,0:T(8,128)(2,1)}, u32[]{:S(2)}, u32[]{:S(2)}) collective-permute-start(bf16[1,2,48,768]{3,2,1,0:T(8,128)(2,1)} %get-tuple-element.186.refs_18_), channel_id=1, source_target_pairs={{0,1},{1,0},{2,3},{3,2},{4,5},{5,4},{6,7},{7,6},{8,9},{9,8},{10,11... | collective-permute-start | bytes 442376 | tf_op jit(solution)/shard_map/ppermute | solution.py:200
  253.4 34.5 %collective-permute-start.12 = (bf16[2,2,48,768]{3,2,1,0:T(8,128)(2,1)}, bf16[2,2,48,768]{3,2,1,0:T(8,128)(2,1)}, u32[]{:S(2)}, u32[]{:S(2)}) collective-permute-start(bf16[2,2,48,768]{3,2,1,0:T(8,128)(2,1)} %get-tuple-element.188.refs_20_), channel_id=1, source_target_pairs={{0,8},{1,9},{2,10},{3,11},{4,12},{5,13},{6,14},{7,15},{8,0},{9,1},... | collective-permute-start | bytes 884744 | tf_op jit(solution)/shard_map/ppermute | solution.py:200
  254.1 40.0 %collective-permute-start.15 = (bf16[2,360,384]{2,1,0:T(8,128)(2,1)}, bf16[2,360,384]{2,1,0:T(8,128)(2,1)}, u32[]{:S(2)}, u32[]{:S(2)}) collective-permute-start(bf16[2,360,384]{2,1,0:T(8,128)(2,1)} %get-tuple-element.193.refs_25_), channel_id=1, source_target_pairs={{0,8},{1,9},{2,10},{3,11},{4,12},{5,13},{6,14},{7,15},{8,0},{9,1},... | collective-permute-start | bytes 1658888 | tf_op jit(solution)/shard_map/ppermute | solution.py:200
  256.4 37.7 %collective-permute-start.13 = (bf16[4,2,48,768]{3,2,1,0:T(8,128)(2,1)}, bf16[4,2,48,768]{3,2,1,0:T(8,128)(2,1)}, u32[]{:S(2)}, u32[]{:S(2)}) collective-permute-start(bf16[4,2,48,768]{3,2,1,0:T(8,128)(2,1)} %get-tuple-element.190.refs_22_), channel_id=1, source_target_pairs={{0,4},{1,5},{2,6},{3,7},{4,0},{5,1},{6,2},{7,3},{8,12},{9,13},{10,... | collective-permute-start | bytes 1769480 | tf_op jit(solution)/shard_map/ppermute | solution.py:200
  257.1 37.0 %collective-permute-start.14 = (bf16[8,2,48,768]{3,2,1,0:T(8,128)(2,1)}, bf16[8,2,48,768]{3,2,1,0:T(8,128)(2,1)}, u32[]{:S(2)}, u32[]{:S(2)}) collective-permute-start(bf16[8,2,48,768]{3,2,1,0:T(8,128)(2,1)} %get-tuple-element.192.refs_24_.refs_27_), channel_id=1, source_target_pairs={{0,2},{1,3},{2,0},{3,1},{4,6},{5,7},{6,4},{7,5},{8,10},{9,11},{10,... | collective-permute-start | bytes 3538952 | tf_op jit(solution)/shard_map/ppermute | solution.py:200
  299.6 55.5 %collective-permute-start.21 = (bf16[1,2,48,768]{3,2,1,0:T(8,128)(2,1)}, bf16[1,2,48,768]{3,2,1,0:T(8,128)(2,1)}, u32[]{:S(2)}, u32[]{:S(2)}) collective-permute-start(bf16[1,2,48,768]{3,2,1,0:T(8,128)(2,1)} %get-tuple-element.197.refs_18_), channel_id=1, source_target_pairs={{0,1},{1,0},{2,3},{3,2},{4,5},{5,4},{6,7},{7,6},{8,9},{9,8},{10,11... | collective-permute-start | bytes 442376 | tf_op jit(solution)/shard_map/ppermute | solution.py:200
  299.6 28.1 %collective-permute-start.16 = (bf16[2,2,48,768]{3,2,1,0:T(8,128)(2,1)}, bf16[2,2,48,768]{3,2,1,0:T(8,128)(2,1)S(1)}, u32[]{:S(2)}, u32[]{:S(2)}) collective-permute-start(bf16[2,2,48,768]{3,2,1,0:T(8,128)(2,1)} %get-tuple-element.199.refs_20_), channel_id=1, source_target_pairs={{0,8},{1,9},{2,10},{3,11},{4,12},{5,13},{6,14},{7,15},{8,0},{9,1},... | collective-permute-start | bytes 884744 | tf_op jit(solution)/shard_map/ppermute | solution.py:200
  299.7 28.1 %collective-permute-start.17 = (bf16[4,2,48,768]{3,2,1,0:T(8,128)(2,1)}, bf16[4,2,48,768]{3,2,1,0:T(8,128)(2,1)S(1)}, u32[]{:S(2)}, u32[]{:S(2)}) collective-permute-start(bf16[4,2,48,768]{3,2,1,0:T(8,128)(2,1)} %get-tuple-element.201.refs_22_), channel_id=1, source_target_pairs={{0,4},{1,5},{2,6},{3,7},{4,0},{5,1},{6,2},{7,3},{8,12},{9,13},{10,... | collective-permute-start | bytes 1769480 | tf_op jit(solution)/shard_map/ppermute | solution.py:200
  300.8 28.1 %collective-permute-start.18 = (bf16[16,96,384]{2,1,0:T(8,128)(2,1)}, bf16[16,96,384]{2,1,0:T(8,128)(2,1)}, u32[]{:S(2)}, u32[]{:S(2)}) collective-permute-start(bf16[16,96,384]{2,1,0:T(8,128)(2,1)} %get-tuple-element.203.refs_24_.refs_27_), channel_id=1, source_target_pairs={{0,16},{16,0},{1,17},{17,1},{2,18},{18,2},{3,19},{19,3},{4,20},{20... | collective-permute-start | bytes 3538952 | tf_op jit(solution)/shard_map/ppermute | solution.py:200
  333.1 22.2 %collective-permute-start.22 = (bf16[1,2,48,768]{3,2,1,0:T(8,128)(2,1)}, bf16[1,2,48,768]{3,2,1,0:T(8,128)(2,1)}, u32[]{:S(2)}, u32[]{:S(2)}) collective-permute-start(bf16[1,2,48,768]{3,2,1,0:T(8,128)(2,1)} %get-tuple-element.222.refs_15_), channel_id=1, source_target_pairs={{0,1},{1,0},{2,3},{3,2},{4,5},{5,4},{6,7},{7,6},{8,9},{9,8},{10,11... | collective-permute-start | bytes 442376 | tf_op jit(solution)/shard_map/ppermute | solution.py:200
  333.1 16.8 %collective-permute-start.19 = (bf16[2,2,48,768]{3,2,1,0:T(8,128)(2,1)}, bf16[2,2,48,768]{3,2,1,0:T(8,128)(2,1)S(1)}, u32[]{:S(2)}, u32[]{:S(2)}) collective-permute-start(bf16[2,2,48,768]{3,2,1,0:T(8,128)(2,1)} %get-tuple-element.210.refs_17_), channel_id=1, source_target_pairs={{0,8},{1,9},{2,10},{3,11},{4,12},{5,13},{6,14},{7,15},{8,0},{9,1},... | collective-permute-start | bytes 884744 | tf_op jit(solution)/shard_map/ppermute | solution.py:200
  353.9 13.4 %collective-permute-start.26 = (bf16[1,360,384]{2,1,0:T(8,128)(2,1)}, bf16[1,360,384]{2,1,0:T(8,128)(2,1)S(1)}, u32[]{:S(2)}, u32[]{:S(2)}) collective-permute-start(bf16[1,360,384]{2,1,0:T(8,128)(2,1)} %get-tuple-element.204.refs_25_), channel_id=1, source_target_pairs={{0,2},{1,3},{2,0},{3,1},{4,6},{5,7},{6,4},{7,5},{8,10},{9,11},{10,... | collective-permute-start | bytes 829448 | tf_op jit(solution)/shard_map/ppermute | solution.py:200
  355.0 15.6 %collective-permute-start.24 = (bf16[8,96,384]{2,1,0:T(8,128)(2,1)S(1)}, bf16[8,96,384]{2,1,0:T(8,128)(2,1)}, u32[]{:S(2)}, u32[]{:S(2)}) collective-permute-start(bf16[8,96,384]{2,1,0:T(8,128)(2,1)S(1)} %copy-done.16), channel_id=1, source_target_pairs={{0,4},{1,5},{2,6},{3,7},{4,0},{5,1},{6,2},{7,3},{8,12},{9,13},{10,... | collective-permute-start | bytes 1769480 | tf_op jit(solution)/shard_map/ppermute | solution.py:200
  355.0 15.5 %collective-permute-start.25 = (bf16[16,304,384]{2,1,0:T(8,128)(2,1)}, bf16[16,304,384]{2,1,0:T(8,128)(2,1)}, u32[]{:S(2)}, u32[]{:S(2)}) collective-permute-start(bf16[16,304,384]{2,1,0:T(8,128)(2,1)} %conditions.1.refs_4_.refs_6_), channel_id=1, source_target_pairs={{0,1},{1,0},{2,3},{3,2},{4,5},{5,4},{6,7},{7,6},{8,9},{9,8},{10,11... | collective-permute-start | bytes 11206664 | tf_op jit(solution)/shard_map/ppermute | solution.py:200
  375.5 22.4 %collective-permute-start.29 = (bf16[1,360,384]{2,1,0:T(8,128)(2,1)}, bf16[1,360,384]{2,1,0:T(8,128)(2,1)}, u32[]{:S(2)}, u32[]{:S(2)}) collective-permute-start(bf16[1,360,384]{2,1,0:T(8,128)(2,1)} %get-tuple-element.233.refs_16_.refs_10_.refs_13_), channel_id=1, source_target_pairs={{0,16},{16,0},{1,17},{17,1},{2,18},{18,2},{3,19},{19,3},{4,20},{20... | collective-permute-start | bytes 829448 | tf_op jit(solution)/shard_map/ppermute | solution.py:200
  377.0 20.9 %collective-permute-start.27 = (bf16[4,96,384]{2,1,0:T(8,128)(2,1)}, bf16[4,96,384]{2,1,0:T(8,128)(2,1)}, u32[]{:S(2)}, u32[]{:S(2)}) collective-permute-start(bf16[4,96,384]{2,1,0:T(8,128)(2,1)} %get-tuple-element.229.refs_12_), channel_id=1, source_target_pairs={{0,8},{1,9},{2,10},{3,11},{4,12},{5,13},{6,14},{7,15},{8,0},{9,1},... | collective-permute-start | bytes 884744 | tf_op jit(solution)/shard_map/ppermute | solution.py:200
  378.4 21.9 %collective-permute-start.28 = (bf16[4,304,384]{2,1,0:T(8,128)(2,1)}, bf16[4,304,384]{2,1,0:T(8,128)(2,1)S(1)}, u32[]{:S(2)}, u32[]{:S(2)}) collective-permute-start(bf16[4,304,384]{2,1,0:T(8,128)(2,1)} %get-tuple-element.231.refs_14_.refs_17_), channel_id=1, source_target_pairs={{0,2},{1,3},{2,0},{3,1},{4,6},{5,7},{6,4},{7,5},{8,10},{9,11},{10,... | collective-permute-start | bytes 2801672 | tf_op jit(solution)/shard_map/ppermute | solution.py:200
  408.1 13.1 %collective-permute-start.39 = (f32[16,128]{1,0:T(8,128)}, f32[16,128]{1,0:T(8,128)S(1)}, u32[]{:S(2)}, u32[]{:S(2)}) collective-permute-start(f32[16,128]{1,0:T(8,128)} %get-tuple-element.246), channel_id=1, source_target_pairs={{0,17},{1,16},{2,19},{3,18},{4,21},{5,20},{6,23},{7,22},{8,25},{9,... | collective-permute-start | bytes 24584 | tf_op jit(solution)/shard_map/ppermute | solution.py:1112
  408.1 13.1 %collective-permute-start.38 = (f32[16,128]{1,0:T(8,128)}, f32[16,128]{1,0:T(8,128)S(1)}, u32[]{:S(2)}, u32[]{:S(2)}) collective-permute-start(f32[16,128]{1,0:T(8,128)} %get-tuple-element.246), channel_id=1, source_target_pairs={{0,1},{1,0},{2,3},{3,2},{4,5},{5,4},{6,7},{7,6},{8,9},{9,8},{10,11... | collective-permute-start | bytes 24584 | tf_op jit(solution)/shard_map/ppermute | solution.py:1112
  424.7 14.2 %collective-permute-start.34 = (bf16[96,384]{1,0:T(8,128)(2,1)S(1)}, bf16[96,384]{1,0:T(8,128)(2,1)S(1)}, u32[]{:S(2)}, u32[]{:S(2)}) collective-permute-start(bf16[96,384]{1,0:T(8,128)(2,1)S(1)} %bitcast.40), channel_id=1, source_target_pairs={{0,17},{1,16},{2,19},{3,18},{4,21},{5,20},{6,23},{7,22},{8,25},{9,... | collective-permute-start | bytes 221192 | tf_op jit(solution)/shard_map/ppermute | solution.py:1145
  (42 other events, 338.1 us)
Sparse Core Ops, SparseCore 0:
  21.5 101.6 all-gather.2

commit v5 on v4

--- a/solution.py
+++ b/solution.py
@@ -193,7 +193,7 @@
             at += rows * count
         return found
 
-    def run(self, array, after="sum"):
+    def run(self, array, after="sum", sent=None):
         last = self.counts["sample"].bit_length() - 1
 
         def exchange(array, axis, bit):
@@ -210,7 +210,11 @@
 
         zero = lambda place: 0
         parts, size = [(array, zero, False)], array.shape[0]
-        for axis, bit in self.order:
+        order = self.order
+        if sent is not None:
+            parts.append((exchange(sent, *order[0]), zero, False))
+            order = order[1:]
+        for axis, bit in order:
             at = bit if axis == "sample" else last
             size = size // 2
             if len(parts) == 1 and (axis, bit) == ("sample", 0):
@@ -590,7 +594,7 @@
 
 def attention_kernel(
     halving, head_dim, place, q_ref, k_ref, v_ref, g_ref, qt_ref, kt_ref, vt_ref, gt_ref, bias_ref,
-    mixed_ref, dq_ref, dkt_ref, dvt_ref, db_ref, kz, vz, plow, dslow, dsum,
+    mixed_ref, dq_ref, dkt_ref, dvt_ref, sent_ref, kept_ref, kz, vz, plow, dslow, dsum, dlow,
 ):
     h = pl.program_id(0)
     samples, length, wide = q_ref.shape
@@ -631,10 +635,14 @@
         if s < samples - 1:
             dsum[...] = total
         else:
-            for p, (dest, _) in enumerate(halving.places()):
-                for c in range(2):
-                    at = (dest + c) * share
-                    db_ref[2 * p + c, 0] = total[at : at + share].astype(BF16)
+            dlow[...] = total.astype(dlow.dtype)
+            bit = halving.order[0][1]
+            slabs = halving.places()[: sent_ref.shape[0] // 2]
+            for ref, value in ((sent_ref, 1 - place[bit]), (kept_ref, place[bit])):
+                for p, (dest, _) in enumerate(slabs):
+                    for c in range(2):
+                        at = (dest + c) * share + value * (share << bit)
+                        ref[2 * p + c, 0] = dlow[pl.ds(pl.multiple_of(at, 16 if share % 16 == 0 else 8), share), :].astype(BF16)
         dq_ref[s] += dot(grad_low, k_ref[s] * mask) * scale
         dvt_ref[s] = dot(gt_ref[s], plow[s % 2]).astype(BF16)
         dkt_ref[s] = (dot(qt_ref[s], dslow[s % 2]) * scale).astype(BF16)
@@ -649,7 +657,8 @@
     bias_in = pl.BlockSpec(
         (parts, 1, share, length), lambda h, core: (0, core[0] * (heads // 2) + chunk * CHUNK_HEADS + h, 0, 0)
     )
-    bias_out = pl.BlockSpec((parts, 1, share, length), lambda h, core: (0, h, 0, 0))
+    bias_out = pl.BlockSpec((parts // 2, 1, share, length), lambda h, core: (0, h, 0, 0))
+    aligned = share % 16 == 0
     held = pl.BlockSpec((samples, length, wide), lambda h, core: (0, 0, 0))
     return call(
         "attention",
@@ -658,13 +667,14 @@
         [(a, nat) for a in nats] + [(a, turn) for a in turned] + [(bias, bias_in)],
         [((samples, length, wide), F32, held)] * 2
         + [((samples, CHUNK_HEADS * head_dim, length), BF16, turn_out)] * 2
-        + [((parts, CHUNK_HEADS, share, length), BF16, bias_out)],
+        + [((parts // 2, CHUNK_HEADS, share, length), BF16, bias_out)] * 2,
         [
             pltpu.VMEM((samples, wide, length), BF16),
             pltpu.VMEM((samples, wide, length), BF16),
             pltpu.VMEM((2, length, length), BF16),
             pltpu.VMEM((2, length, length), BF16),
             pltpu.VMEM((length, length), F32),
+            pltpu.VMEM((length, length), BF16 if aligned else F32),
         ],
         deps,
         order,
@@ -1065,13 +1075,13 @@
     mixeds, dqs, dkts, dvts, bias_sums = [], [], [], [], []
     deps = advance(order, early)
     for chunk in range(chunks):
-        mixed, dq, dkt, dvt, db = attention_call(chunk, nats, turned, bias, head_dim, chip_x, deps, order)
+        mixed, dq, dkt, dvt, sent, kept = attention_call(chunk, nats, turned, bias, head_dim, chip_x, deps, order)
         mixeds.append(mixed)
         dqs.append(dq)
         dkts.append(dkt)
         dvts.append(dvt)
-        bias_sums.append(Running(chip_x.run(db, "swap")))
         deps = advance(order, *bias_sums, *([early] if chunk % 2 else []))
+        bias_sums.append(Running(chip_x.run(kept, "swap", sent)))
 
     joined, joined_sent, q_bias_grad = mixed_call(
         gate, gated_grad, mixeds, dqs, dkts, dvts, deps, order
@@ -1080,12 +1090,12 @@
     qkvg_sum = Running(
         chip_y.run(qkvg_call(first, joined, joined_sent, chip_y, [], order), "cores")
     )
-    deps = advance(order, *bias_sums, qkvg_sum, early)
+    deps = advance(order, *bias_sums, qkvg_sum)
     block_out, acts_grad, projected, zero_low, cond_b_zero, zero_b_zero, out_grad = outputs_call(
         acts, cotangent, partial, acts_part, zero_gate, factor, [joined, joined_got],
         out_w, qkvg_w, deps, order,
     )
-    deps = advance(order, *bias_sums, qkvg_sum)
+    deps = advance(order, *bias_sums, qkvg_sum, early)
     rest, rest_shapes = conditions_call(
         cond, conditioning(0), zero(0)[0], zero_low, projected, cond_gate, cond_norm, out_grad,
         [gain_one, cond_b_zero, cond_b_one, zero_b_zero, zero_b_one, q_bias_grad], along_x, deps, order,

time: 458 us -> 449 us (0.980)
  waiting for transfers between devices: 47.6 us -> 41.3 us
    ppermute x30, waiting for transfers between devices: 37.8 us -> 28.9 us  [exchange(): lax.ppermute(array, axis, [(i, i ^ 1 << bit) for i in range(self.counts[a...]
    pallas_call x26 -> x25, Pallas kernels: 342 us -> 339 us  [call(): pl.pallas_call(run, grid_spec=pltpu.PrefetchScalarGridSpec(num_scalar_pre...]
  transfers between devices with their start and end apart: 45 -> 45, of which waited for: 14 -> 12; matrix products, arithmetic and copies ran while one was open for 1% -> 1% of each run, Pallas kernels for 67% -> 70%
where the time goes in v5:
time: 449 us; the launch traced here: 445 us
  Pallas kernels  339 us (76%)
  waiting for transfers between devices  41.3 us (9%)
  starting transfers between devices  37.4 us (8%)
  between operations  15.4 us (3%)
  local copies, waits for them, and re-layouts  10.6 us (2%)
    pallas_call x25, Pallas kernels, call(): pl.pallas_call(run, grid_spec=pltpu.PrefetchScalarGridSpec(num_scalar_pre...  339 us
    ppermute x30, starting transfers between devices, exchange(): lax.ppermute(array, axis, [(i, i ^ 1 << bit) for i in range(self.counts[a...  28.9 us
    ppermute x30, waiting for transfers between devices, exchange(): lax.ppermute(array, axis, [(i, i ^ 1 << bit) for i in range(self.counts[a...  28.9 us
  transfers between devices with their start and end apart: 45, of which 12 were waited for; matrix products, arithmetic and copies ran while one was open for 1% of the time, Pallas kernels for 70%

profile of v5, /device:TPU:0, one launch (start us, length us, event | category | flops | bytes accessed | tf_op | source)
XLA Modules:
  0.0 445.3 jit_solution(15959300979185364336)
XLA Ops:
  8.4 13.0 %pair_forward.1 = bf16[16,48,768]{2,1,0:T(8,128)(2,1)} custom-call(s32[5]{0:T(128)} %broadcast_1_place_ref.2.place_ref, bf16[48,768,128]{2,1,0:T(8,128)(2,1)} %bitcast.49, bf16[1,128]{1,0:T(2,128)(2,1)} %bitcast.63, bf16[16,128]{1,0:T(8,128)(2,1)} %bitcast.42, s32[1,768]{1,0:T(1,128)} %refs_3_.2, s32[1]{0:T(128)S(6)} %copy.40.refs_4_), custom_call_target="tpu_custom_call" | custom-call | flops 99999997952 | bytes 1000000 | tf_op jit(solution)/shard_map/pair_forward/pallas_call | solution.py:81
  23.9 57.3 %transition.1 = (f32[2,768,768]{2,1,0:T(8,128)}, f32[2,768,768]{2,1,0:T(8,128)}, f32[768,384]{1,0:T(8,128)}, f32[768,384]{1,0:T(8,128)}, bf16[32,360,384]{2,1,0:...) custom-call(s32[5]{0:T(128)} %stack.23.place_ref, bf16[2,768,768]{2,1,0:T(8,128)(2,1)} %bitcast.53, ...), custom_call_target="tpu_custom_call" | custom-call | flops 99999997952 | bytes 1000000 | tf_op jit(solution)/shard_map/transition/pallas_call | solution.py:81
  83.0 27.9 %inputs.1 = (bf16[4,768,768]{2,1,0:T(8,128)(2,1)}, f32[4,768,384]{2,1,0:T(8,128)}, f32[4,768,384]{2,1,0:T(8,128)}, bf16[4,4,768,128]{3,2,1,0:T(8,128)(2,1)}, bf1...) custom-call(s32[5]{0:T(128)} %stack.23.place_ref, ...), custom_call_target="tpu_custom_call" | custom-call | flops 99999997952 | bytes 1000000 | tf_op jit(solution)/shard_map/inputs/pallas_call | solution.py:81
  110.9 7.0 %combine.11 = (bf16[8,360,384]{2,1,0:T(8,128)(2,1)}, bf16[8,360,384]{2,1,0:T(8,128)(2,1)}) custom-call(s32[5]{0:T(128)} %stack.23.place_ref, bf16[32,360,384]{2,1,0:T(8,128)(2,1)} %get-tuple-element.141.refs_16_.refs_0_.refs_2_, bf16[32,360,384]{2,1,0:T(8,128)(2,1)} %collective-permute-done.2.refs_1_.refs_3_, ...), custom_call_target="tpu_custom_call" | custom-call | flops 99999997952 | bytes 1000000 | tf_op jit(solution)/shard_map/combine/pallas_call | solution.py:81
  120.2 3.0 all-gather.3.cloned.1.call-done
  123.2 23.8 %attention.4 = (f32[4,768,128]{2,1,0:T(8,128)}, f32[4,768,128]{2,1,0:T(8,128)}, bf16[4,96,768]{2,1,0:T(8,128)(2,1)}, bf16[4,96,768]{2,1,0:T(8,128)(2,1)}, bf16[8...) custom-call(s32[5]{0:T(128)} %stack.23.place_ref, bf16[4,4,768,128]{3,2,1,0:T(8,128)(2,1)} %get-tuple-element.146.refs_0_, ...), custom_call_target="tpu_custom_call" | custom-call | flops 16999999488 | bytes 1000000 | tf_op jit(solution)/shard_map/attention/pallas_call | solution.py:81
  148.4 23.9 %attention.5 = (f32[4,768,128]{2,1,0:T(8,128)}, f32[4,768,128]{2,1,0:T(8,128)}, bf16[4,96,768]{2,1,0:T(8,128)(2,1)}, bf16[4,96,768]{2,1,0:T(8,128)(2,1)}, bf16[8...) custom-call(s32[5]{0:T(128)} %stack.23.place_ref, bf16[4,4,768,128]{3,2,1,0:T(8,128)(2,1)} %get-tuple-element.146.refs_0_, ...), custom_call_target="tpu_custom_call" | custom-call | flops 16999999488 | bytes 1000000 | tf_op jit(solution)/shard_map/attention/pallas_call | solution.py:81
  173.2 2.6 collective-permute-done.3.refs_1_.refs_3_
  175.8 5.5 %combine.12 = (bf16[4,2,48,768]{3,2,1,0:T(8,128)(2,1)}, bf16[4,2,48,768]{3,2,1,0:T(8,128)(2,1)}, bf16[4,360,384]{2,1,0:T(8,128)(2,1)}, bf16[4,360,384]{2,1,0:T(8,128)(2,1)}) custom-call(s32[5]{0:T(128)} %stack.23.place_ref, bf16[8,2,48,768]{3,2,1,0:T(8,128)(2,1)} %get-tuple-element.160.refs_0_.refs_2_, ...), custom_call_target="tpu_custom_call" | custom-call | flops 99999997952 | bytes 1000000 | tf_op jit(solution)/shard_map/combine/pallas_call | solution.py:81
  183.3 24.1 %attention.6 = (f32[4,768,128]{2,1,0:T(8,128)}, f32[4,768,128]{2,1,0:T(8,128)}, bf16[4,96,768]{2,1,0:T(8,128)(2,1)}, bf16[4,96,768]{2,1,0:T(8,128)(2,1)}, bf16[8...) custom-call(s32[5]{0:T(128)} %stack.23.place_ref, bf16[4,4,768,128]{3,2,1,0:T(8,128)(2,1)} %get-tuple-element.146.refs_0_, ...), custom_call_target="tpu_custom_call" | custom-call | flops 16999999488 | bytes 1000000 | tf_op jit(solution)/shard_map/attention/pallas_call | solution.py:81
  210.1 3.9 combine.13
  216.6 24.2 %attention.7 = (f32[4,768,128]{2,1,0:T(8,128)}, f32[4,768,128]{2,1,0:T(8,128)}, bf16[4,96,768]{2,1,0:T(8,128)(2,1)}, bf16[4,96,768]{2,1,0:T(8,128)(2,1)}, bf16[8...) custom-call(s32[5]{0:T(128)} %stack.23.place_ref, bf16[4,4,768,128]{3,2,1,0:T(8,128)(2,1)} %get-tuple-element.146.refs_0_, ...), custom_call_target="tpu_custom_call" | custom-call | flops 16999999488 | bytes 1000000 | tf_op jit(solution)/shard_map/attention/pallas_call | solution.py:81
  243.8 5.3 %combine.14 = (bf16[1,2,48,768]{3,2,1,0:T(8,128)(2,1)}, bf16[1,2,48,768]{3,2,1,0:T(8,128)(2,1)}, bf16[2,2,48,768]{3,2,1,0:T(8,128)(2,1)}, bf16[2,2,48,768]{3,2,1...) custom-call(s32[5]{0:T(128)} %stack.23.place_ref, ...), custom_call_target="tpu_custom_call" | custom-call | flops 99999997952 | bytes 1000000 | tf_op jit(solution)/shard_map/combine/pallas_call | solution.py:81
  249.3 2.8 collective-permute-start.18
  252.2 15.3 %mixed.1 = (bf16[2,768,1920]{2,1,0:T(8,128)(2,1)}, bf16[2,768,1920]{2,1,0:T(8,128)(2,1)}, f32[1,384]{1,0:T(1,128)}) custom-call(s32[5]{0:T(128)} %stack.23.place_ref, f32[4,768,384]{2,1,0:T(8,128)} %get-tuple-element.144.refs_0_, f32[4,768,384]{2,1,0:T(8,128)} %get-tuple-element.145.refs_1_, f32[4,768,128]{2,1,0:T(8,128)} %get-tuple-element.157.refs_2_, ...), custom_call_target="tpu_custom_call" | custom-call | flops 99999997952 | bytes 1000000 | tf_op jit(solution)/shard_map/mixed/pallas_call | solution.py:81
  267.6 14.5 %qkvg_grad.1.refs_12_.refs_13_.refs_8_.refs_10_ = bf16[32,96,384]{2,1,0:T(8,128)(2,1)} custom-call(s32[5]{0:T(128)} %stack.23.place_ref, bf16[4,768,768]{2,1,0:T(8,128)(2,1)} %get-tuple-element.154.refs_4_.refs_0_, bf16[2,768,1920]{2,1,0:T(8,128)(2,1)} %get-tuple-element.196.refs_1_.refs_2_.refs_5_.refs_6_, ...), custom_call_target="tpu_custom_call" | custom-call | flops 99999997952 | bytes 1000000 | tf_op jit(solution)/shard_map/qkvg_grad/pallas_call | solution.py:81
  282.1 5.1 %combine.15 = (bf16[1,2,48,768]{3,2,1,0:T(8,128)(2,1)}, bf16[1,2,48,768]{3,2,1,0:T(8,128)(2,1)}, bf16[2,2,48,768]{3,2,1,0:T(8,128)(2,1)}, bf16[2,2,48,768]{3,2,1...) custom-call(s32[5]{0:T(128)} %stack.23.place_ref, ...), custom_call_target="tpu_custom_call" | custom-call | flops 99999997952 | bytes 1000000 | tf_op jit(solution)/shard_map/combine/pallas_call | solution.py:81
  293.4 25.5 %outputs.1 = (bf16[2,768,768]{2,1,0:T(8,128)(2,1)}, bf16[2,768,768]{2,1,0:T(8,128)(2,1)}, bf16[768,1536]{1,0:T(8,128)(2,1)}, bf16[768,768]{1,0:T(8,128)(2,1)}, f...) custom-call(s32[5]{0:T(128)} %stack.23.place_ref, bf16[2,768,768]{2,1,0:T(8,128)(2,1)} %bitcast.55, ...), custom_call_target="tpu_custom_call" | custom-call | flops 99999997952 | bytes 1000000 | tf_op jit(solution)/shard_map/outputs/pallas_call | solution.py:81
  320.3 4.8 %combine.16 = (bf16[1,2,48,768]{3,2,1,0:T(8,128)(2,1)}, bf16[1,2,48,768]{3,2,1,0:T(8,128)(2,1)}, bf16[2,2,48,768]{3,2,1,0:T(8,128)(2,1)}, bf16[2,2,48,768]{3,2,1...) custom-call(s32[5]{0:T(128)} %stack.23.place_ref, ...), custom_call_target="tpu_custom_call" | custom-call | flops 99999997952 | bytes 1000000 | tf_op jit(solution)/shard_map/combine/pallas_call | solution.py:81
  325.8 10.3 %conditions.1.refs_4_.refs_6_ = bf16[16,304,384]{2,1,0:T(8,128)(2,1)} custom-call(s32[5]{0:T(128)} %stack.23.place_ref, bf16[768,384]{1,0:T(8,128)(2,1)} %bitcast.62, f32[1,768]{1,0:T(1,128)} %get-tuple-element.263.refs_3_.refs_5_.refs_1_, bf16[384,3072]{1,0:T(8,128)(2,1)} %refs_2_.1, bf16[384,1536]{1,0:T(8,128)(2,1)} %refs_3_.3, ...), custom_call_target="tpu_custom_call" | custom-call | flops 99999997952 | bytes 1000000 | tf_op jit(solution)/shard_map/conditions/pallas_call | solution.py:81
  336.1 5.9 %collective-permute-done.19.refs_1_.refs_3_ = bf16[2,2,48,768]{3,2,1,0:T(8,128)(2,1)S(1)} collective-permute-done((bf16[2,2,48,768]{3,2,1,0:T(8,128)(2,1)}, bf16[2,2,48,768]{3,2,1,0:T(8,128)(2,1)S(1)}, u32[]{:S(2)}, u32[]{:S(2)}) %collective-permute-start.19) | collective-permute-done | bytes 294944 | tf_op jit(solution)/shard_map/ppermute | solution.py:200
  347.5 11.9 %pair_backward.2 = (f32[48,768,128]{2,1,0:T(8,128)}, f32[16,128]{1,0:T(8,128)}) custom-call(s32[5]{0:T(128)} %stack.23.place_ref, bf16[48,768,128]{2,1,0:T(8,128)(2,1)} %bitcast.50, f32[1,128]{1,0:T(1,128)} %slice.34.refs_1_.refs_10_, bf16[16,128]{1,0:T(8,128)(2,1)} %maximum_select_fusion.refs_2_, bf16[2,48,768]{2,1,0:T(8,128)(2,1)} %bitcast.69, ...), custom_call_target="tpu_custom_call" | custom-call | flops 99999997952 | bytes 1000000 | tf_op jit(solution)/shard_map/pair_backward/pallas_call | solution.py:81
  359.5 3.3 collective-permute-done.24.refs_1_.refs_3_
  362.8 4.9 %combine.18 = (bf16[4,96,384]{2,1,0:T(8,128)(2,1)}, bf16[4,96,384]{2,1,0:T(8,128)(2,1)}, bf16[4,304,384]{2,1,0:T(8,128)(2,1)}, bf16[4,304,384]{2,1,0:T(8,128)(2,1)}, bf16[1,360,384]{2,1,0:T(8,128)(2,1)}) custom-call(s32[5]{0:T(128)} %stack.23.place_ref, bf16[8,96,384]{2,1,0:T(8,128)(2,1)} %get-tuple-element.224.refs_20_.refs_0_.refs_2_, ...), custom_call_target="tpu_custom_call" | custom-call | flops 99999997952 | bytes 1000000 | tf_op jit(solution)/shard_map/combine/pallas_call | solution.py:81
  370.1 18.3 %pair_backward.3 = (f32[48,768,128]{2,1,0:T(8,128)}, f32[16,128]{1,0:T(8,128)}) custom-call(s32[5]{0:T(128)} %stack.23.place_ref, bf16[48,768,128]{2,1,0:T(8,128)(2,1)} %bitcast.51, f32[1,128]{1,0:T(1,128)} %slice.34.refs_1_.refs_10_, bf16[16,128]{1,0:T(8,128)(2,1)} %maximum_select_fusion.refs_2_, ...), custom_call_target="tpu_custom_call", output_to_operand_aliasing={{0}: (12, {})} | custom-call | flops 99999997952 | bytes 1000000 | tf_op jit(solution)/shard_map/pair_backward/pallas_call | solution.py:81
  388.4 3.2 collective-permute-done.28.refs_7_.refs_9_
  392.6 4.2 combine.19
  400.7 2.8 collective-permute-done.30.refs_1_.refs_3_
  403.6 4.2 collective-permute-done.31.refs_5_.refs_7_
  416.8 5.5 %collective-permute-done.35.refs_1_ = bf16[1,304,384]{2,1,0:T(8,128)(2,1)S(1)} collective-permute-done((bf16[1,304,384]{2,1,0:T(8,128)(2,1)S(1)}, bf16[1,304,384]{2,1,0:T(8,128)(2,1)S(1)}, u32[]{:S(2)}, u32[]{:S(2)}) %collective-permute-start.35) | collective-permute-done | bytes 233504 | tf_op jit(solution)/shard_map/ppermute | solution.py:200
  425.1 4.5 %collective-permute-done.43 = f32[16,128]{1,0:T(8,128)S(1)} collective-permute-done((f32[16,128]{1,0:T(8,128)S(1)}, f32[16,128]{1,0:T(8,128)S(1)}, u32[]{:S(2)}, u32[]{:S(2)}) %collective-permute-start.43) | collective-permute-done | bytes 8224 | tf_op jit(solution)/shard_map/ppermute | solution.py:1122
  433.4 4.9 %results.1 = (f32[48,384]{1,0:T(8,128)}, f32[24,3072]{1,0:T(8,128)}, f32[24,1536]{1,0:T(8,128)}, f32[48,3072]{1,0:T(8,128)}, f32[48,768]{1,0:T(8,128)}, /*index=...) custom-call(s32[5]{0:T(128)} %stack.23.place_ref, ...), custom_call_target="tpu_custom_call" | custom-call | flops 99999997952 | bytes 1000000 | tf_op jit(solution)/shard_map/results/pallas_call | solution.py:81
  (157 shorter events, 56.5 us)
Async XLA Ops:
  7.2 116.0 %all-gather.3.cloned.1.call-start = ((), (), s32[]{:S(2)}) async-start(), calls=%async_computation | async-start | bytes 20054016 | tf_op jit(solution)/shard_map/all_gather | solution.py:1030
  21.4 61.6 %collective-permute-start = (bf16[2,768,768]{2,1,0:T(8,128)(2,1)}, bf16[2,768,768]{2,1,0:T(8,128)(2,1)}, u32[]{:S(2)}, u32[]{:S(2)}) collective-permute-start(bf16[2,768,768]{2,1,0:T(8,128)(2,1)} %bitcast.52), channel_id=1, source_target_pairs={{0,1},{1,0},{2,3},{3,2},{4,5},{5,4},{6,7},{7,6},{8,9},{9,8},{10,11... | collective-permute-start | bytes 7077896 | tf_op jit(solution)/shard_map/ppermute | solution.py:1025
  21.9 61.0 %collective-permute-start.1 = (bf16[2,768,768]{2,1,0:T(8,128)(2,1)}, bf16[2,768,768]{2,1,0:T(8,128)(2,1)}, u32[]{:S(2)}, u32[]{:S(2)}) collective-permute-start(bf16[2,768,768]{2,1,0:T(8,128)(2,1)} %bitcast.56), channel_id=1, source_target_pairs={{0,1},{1,0},{2,3},{3,2},{4,5},{5,4},{6,7},{7,6},{8,9},{9,8},{10,11... | collective-permute-start | bytes 7077896 | tf_op jit(solution)/shard_map/ppermute | solution.py:1025
  81.2 29.6 %collective-permute-start.2 = (bf16[32,360,384]{2,1,0:T(8,128)(2,1)}, bf16[32,360,384]{2,1,0:T(8,128)(2,1)}, u32[]{:S(2)}, u32[]{:S(2)}) collective-permute-start(bf16[32,360,384]{2,1,0:T(8,128)(2,1)} %get-tuple-element.141.refs_16_.refs_0_.refs_2_), channel_id=1, source_target_pairs={{0,1},{1,0},{2,3},{3,2},{4,5},{5,4},{6,7},{7,6},{8,9},{9,8},{10,11... | collective-permute-start | bytes 26542088 | tf_op jit(solution)/shard_map/ppermute | solution.py:200
  117.9 55.3 %collective-permute-start.4 = (bf16[8,360,384]{2,1,0:T(8,128)(2,1)}, bf16[8,360,384]{2,1,0:T(8,128)(2,1)}, u32[]{:S(2)}, u32[]{:S(2)}) collective-permute-start(bf16[8,360,384]{2,1,0:T(8,128)(2,1)} %get-tuple-element.155.refs_9_.refs_11_), channel_id=1, source_target_pairs={{0,16},{16,0},{1,17},{17,1},{2,18},{18,2},{3,19},{19,3},{4,20},{20... | collective-permute-start | bytes 6635528 | tf_op jit(solution)/shard_map/ppermute | solution.py:200
  147.1 28.7 %collective-permute-start.3 = (bf16[8,2,48,768]{3,2,1,0:T(8,128)(2,1)}, bf16[8,2,48,768]{3,2,1,0:T(8,128)(2,1)}, u32[]{:S(2)}, u32[]{:S(2)}) collective-permute-start(bf16[8,2,48,768]{3,2,1,0:T(8,128)(2,1)} %get-tuple-element.158.refs_9_), channel_id=1, source_target_pairs={{0,2},{1,3},{2,0},{3,1},{4,6},{5,7},{6,4},{7,5},{8,10},{9,11},{10,... | collective-permute-start | bytes 3538952 | tf_op jit(solution)/shard_map/ppermute | solution.py:200
  172.3 36.9 %collective-permute-start.6 = (bf16[8,2,48,768]{3,2,1,0:T(8,128)(2,1)}, bf16[8,2,48,768]{3,2,1,0:T(8,128)(2,1)}, u32[]{:S(2)}, u32[]{:S(2)}) collective-permute-start(bf16[8,2,48,768]{3,2,1,0:T(8,128)(2,1)} %get-tuple-element.161.refs_8_), channel_id=1, source_target_pairs={{0,2},{1,3},{2,0},{3,1},{4,6},{5,7},{6,4},{7,5},{8,10},{9,11},{10,... | collective-permute-start | bytes 3538952 | tf_op jit(solution)/shard_map/ppermute | solution.py:200
  181.3 27.9 %collective-permute-start.5 = (bf16[4,2,48,768]{3,2,1,0:T(8,128)(2,1)}, bf16[4,2,48,768]{3,2,1,0:T(8,128)(2,1)S(1)}, u32[]{:S(2)}, u32[]{:S(2)}) collective-permute-start(bf16[4,2,48,768]{3,2,1,0:T(8,128)(2,1)} %get-tuple-element.162.refs_9_), channel_id=1, source_target_pairs={{0,4},{1,5},{2,6},{3,7},{4,0},{5,1},{6,2},{7,3},{8,12},{9,13},{10,... | collective-permute-start | bytes 1769480 | tf_op jit(solution)/shard_map/ppermute | solution.py:200
  182.8 60.1 %collective-permute-start.10 = (bf16[4,360,384]{2,1,0:T(8,128)(2,1)}, bf16[4,360,384]{2,1,0:T(8,128)(2,1)}, u32[]{:S(2)}, u32[]{:S(2)}) collective-permute-start(bf16[4,360,384]{2,1,0:T(8,128)(2,1)} %get-tuple-element.164.refs_11_.refs_13_), channel_id=1, source_target_pairs={{0,4},{1,5},{2,6},{3,7},{4,0},{5,1},{6,2},{7,3},{8,12},{9,13},{10,... | collective-permute-start | bytes 3317768 | tf_op jit(solution)/shard_map/ppermute | solution.py:200
  207.4 35.6 %collective-permute-start.9 = (bf16[8,2,48,768]{3,2,1,0:T(8,128)(2,1)}, bf16[8,2,48,768]{3,2,1,0:T(8,128)(2,1)}, u32[]{:S(2)}, u32[]{:S(2)}) collective-permute-start(bf16[8,2,48,768]{3,2,1,0:T(8,128)(2,1)} %get-tuple-element.168.refs_8_), channel_id=1, source_target_pairs={{0,2},{1,3},{2,0},{3,1},{4,6},{5,7},{6,4},{7,5},{8,10},{9,11},{10,... | collective-permute-start | bytes 3538952 | tf_op jit(solution)/shard_map/ppermute | solution.py:200
  214.0 28.9 %collective-permute-start.7 = (bf16[2,2,48,768]{3,2,1,0:T(8,128)(2,1)}, bf16[2,2,48,768]{3,2,1,0:T(8,128)(2,1)S(1)}, u32[]{:S(2)}, u32[]{:S(2)}) collective-permute-start(bf16[2,2,48,768]{3,2,1,0:T(8,128)(2,1)} %get-tuple-element.169.refs_9_), channel_id=1, source_target_pairs={{0,8},{1,9},{2,10},{3,11},{4,12},{5,13},{6,14},{7,15},{8,0},{9,1},... | collective-permute-start | bytes 884744 | tf_op jit(solution)/shard_map/ppermute | solution.py:200
  216.4 26.5 %collective-permute-start.8 = (bf16[4,2,48,768]{3,2,1,0:T(8,128)(2,1)}, bf16[4,2,48,768]{3,2,1,0:T(8,128)(2,1)S(1)}, u32[]{:S(2)}, u32[]{:S(2)}) collective-permute-start(bf16[4,2,48,768]{3,2,1,0:T(8,128)(2,1)} %get-tuple-element.171.refs_11_.refs_13_), channel_id=1, source_target_pairs={{0,4},{1,5},{2,6},{3,7},{4,0},{5,1},{6,2},{7,3},{8,12},{9,13},{10,... | collective-permute-start | bytes 1769480 | tf_op jit(solution)/shard_map/ppermute | solution.py:200
  240.9 41.2 %collective-permute-start.14 = (bf16[8,2,48,768]{3,2,1,0:T(8,128)(2,1)}, bf16[8,2,48,768]{3,2,1,0:T(8,128)(2,1)}, u32[]{:S(2)}, u32[]{:S(2)}) collective-permute-start(bf16[8,2,48,768]{3,2,1,0:T(8,128)(2,1)} %get-tuple-element.187.refs_16_), channel_id=1, source_target_pairs={{0,2},{1,3},{2,0},{3,1},{4,6},{5,7},{6,4},{7,5},{8,10},{9,11},{10,... | collective-permute-start | bytes 3538952 | tf_op jit(solution)/shard_map/ppermute | solution.py:200
  249.1 98.1 %collective-permute-start.20 = (bf16[1,2,48,768]{3,2,1,0:T(8,128)(2,1)}, bf16[1,2,48,768]{3,2,1,0:T(8,128)(2,1)}, u32[]{:S(2)}, u32[]{:S(2)}) collective-permute-start(bf16[1,2,48,768]{3,2,1,0:T(8,128)(2,1)} %get-tuple-element.188.refs_18_), channel_id=1, source_target_pairs={{0,1},{1,0},{2,3},{3,2},{4,5},{5,4},{6,7},{7,6},{8,9},{9,8},{10,11... | collective-permute-start | bytes 442376 | tf_op jit(solution)/shard_map/ppermute | solution.py:200
  249.1 32.9 %collective-permute-start.12 = (bf16[2,2,48,768]{3,2,1,0:T(8,128)(2,1)}, bf16[2,2,48,768]{3,2,1,0:T(8,128)(2,1)}, u32[]{:S(2)}, u32[]{:S(2)}) collective-permute-start(bf16[2,2,48,768]{3,2,1,0:T(8,128)(2,1)} %get-tuple-element.190.refs_20_), channel_id=1, source_target_pairs={{0,8},{1,9},{2,10},{3,11},{4,12},{5,13},{6,14},{7,15},{8,0},{9,1},... | collective-permute-start | bytes 884744 | tf_op jit(solution)/shard_map/ppermute | solution.py:200
  249.3 69.6 %collective-permute-start.18 = (bf16[2,360,384]{2,1,0:T(8,128)(2,1)}, bf16[2,360,384]{2,1,0:T(8,128)(2,1)}, u32[]{:S(2)}, u32[]{:S(2)}) collective-permute-start(bf16[2,360,384]{2,1,0:T(8,128)(2,1)} %get-tuple-element.194.refs_24_), channel_id=1, source_target_pairs={{0,8},{1,9},{2,10},{3,11},{4,12},{5,13},{6,14},{7,15},{8,0},{9,1},... | collective-permute-start | bytes 1658888 | tf_op jit(solution)/shard_map/ppermute | solution.py:200
  252.1 29.9 %collective-permute-start.13 = (bf16[4,2,48,768]{3,2,1,0:T(8,128)(2,1)}, bf16[4,2,48,768]{3,2,1,0:T(8,128)(2,1)}, u32[]{:S(2)}, u32[]{:S(2)}) collective-permute-start(bf16[4,2,48,768]{3,2,1,0:T(8,128)(2,1)} %get-tuple-element.192.refs_22_.refs_26_), channel_id=1, source_target_pairs={{0,4},{1,5},{2,6},{3,7},{4,0},{5,1},{6,2},{7,3},{8,12},{9,13},{10,... | collective-permute-start | bytes 1769480 | tf_op jit(solution)/shard_map/ppermute | solution.py:200
  287.1 31.9 %collective-permute-start.15 = (bf16[2,2,48,768]{3,2,1,0:T(8,128)(2,1)}, bf16[2,2,48,768]{3,2,1,0:T(8,128)(2,1)S(1)}, u32[]{:S(2)}, u32[]{:S(2)}) collective-permute-start(bf16[2,2,48,768]{3,2,1,0:T(8,128)(2,1)} %get-tuple-element.201.refs_20_), channel_id=1, source_target_pairs={{0,8},{1,9},{2,10},{3,11},{4,12},{5,13},{6,14},{7,15},{8,0},{9,1},... | collective-permute-start | bytes 884744 | tf_op jit(solution)/shard_map/ppermute | solution.py:200
  289.5 29.6 %collective-permute-start.16 = (bf16[4,2,48,768]{3,2,1,0:T(8,128)(2,1)}, bf16[4,2,48,768]{3,2,1,0:T(8,128)(2,1)S(1)}, u32[]{:S(2)}, u32[]{:S(2)}) collective-permute-start(bf16[4,2,48,768]{3,2,1,0:T(8,128)(2,1)} %get-tuple-element.203.refs_22_), channel_id=1, source_target_pairs={{0,4},{1,5},{2,6},{3,7},{4,0},{5,1},{6,2},{7,3},{8,12},{9,13},{10,... | collective-permute-start | bytes 1769480 | tf_op jit(solution)/shard_map/ppermute | solution.py:200
  292.0 28.3 %collective-permute-start.17 = (bf16[16,96,384]{2,1,0:T(8,128)(2,1)}, bf16[16,96,384]{2,1,0:T(8,128)(2,1)}, u32[]{:S(2)}, u32[]{:S(2)}) collective-permute-start(bf16[16,96,384]{2,1,0:T(8,128)(2,1)} %get-tuple-element.205.refs_24_.refs_25_), channel_id=1, source_target_pairs={{0,16},{16,0},{1,17},{17,1},{2,18},{18,2},{3,19},{19,3},{4,20},{20... | collective-permute-start | bytes 3538952 | tf_op jit(solution)/shard_map/ppermute | solution.py:200
  318.9 28.3 %collective-permute-start.21 = (bf16[1,2,48,768]{3,2,1,0:T(8,128)(2,1)}, bf16[1,2,48,768]{3,2,1,0:T(8,128)(2,1)}, u32[]{:S(2)}, u32[]{:S(2)}) collective-permute-start(bf16[1,2,48,768]{3,2,1,0:T(8,128)(2,1)} %get-tuple-element.199.refs_18_), channel_id=1, source_target_pairs={{0,1},{1,0},{2,3},{3,2},{4,5},{5,4},{6,7},{7,6},{8,9},{9,8},{10,11... | collective-permute-start | bytes 442376 | tf_op jit(solution)/shard_map/ppermute | solution.py:200
  325.1 22.4 %collective-permute-start.22 = (bf16[1,2,48,768]{3,2,1,0:T(8,128)(2,1)}, bf16[1,2,48,768]{3,2,1,0:T(8,128)(2,1)}, u32[]{:S(2)}, u32[]{:S(2)}) collective-permute-start(bf16[1,2,48,768]{3,2,1,0:T(8,128)(2,1)} %get-tuple-element.222.refs_15_), channel_id=1, source_target_pairs={{0,1},{1,0},{2,3},{3,2},{4,5},{5,4},{6,7},{7,6},{8,9},{9,8},{10,11... | collective-permute-start | bytes 442376 | tf_op jit(solution)/shard_map/ppermute | solution.py:200
  325.2 16.7 %collective-permute-start.19 = (bf16[2,2,48,768]{3,2,1,0:T(8,128)(2,1)}, bf16[2,2,48,768]{3,2,1,0:T(8,128)(2,1)S(1)}, u32[]{:S(2)}, u32[]{:S(2)}) collective-permute-start(bf16[2,2,48,768]{3,2,1,0:T(8,128)(2,1)} %get-tuple-element.210.refs_17_), channel_id=1, source_target_pairs={{0,8},{1,9},{2,10},{3,11},{4,12},{5,13},{6,14},{7,15},{8,0},{9,1},... | collective-permute-start | bytes 884744 | tf_op jit(solution)/shard_map/ppermute | solution.py:200
  345.8 13.6 %collective-permute-start.26 = (bf16[1,360,384]{2,1,0:T(8,128)(2,1)}, bf16[1,360,384]{2,1,0:T(8,128)(2,1)S(1)}, u32[]{:S(2)}, u32[]{:S(2)}) collective-permute-start(bf16[1,360,384]{2,1,0:T(8,128)(2,1)} %get-tuple-element.225.refs_21_), channel_id=1, source_target_pairs={{0,2},{1,3},{2,0},{3,1},{4,6},{5,7},{6,4},{7,5},{8,10},{9,11},{10,... | collective-permute-start | bytes 829448 | tf_op jit(solution)/shard_map/ppermute | solution.py:200
  347.2 15.5 %collective-permute-start.24 = (bf16[8,96,384]{2,1,0:T(8,128)(2,1)S(1)}, bf16[8,96,384]{2,1,0:T(8,128)(2,1)}, u32[]{:S(2)}, u32[]{:S(2)}) collective-permute-start(bf16[8,96,384]{2,1,0:T(8,128)(2,1)S(1)} %copy-done.16), channel_id=1, source_target_pairs={{0,4},{1,5},{2,6},{3,7},{4,0},{5,1},{6,2},{7,3},{8,12},{9,13},{10,... | collective-permute-start | bytes 1769480 | tf_op jit(solution)/shard_map/ppermute | solution.py:200
  347.3 15.5 %collective-permute-start.25 = (bf16[16,304,384]{2,1,0:T(8,128)(2,1)}, bf16[16,304,384]{2,1,0:T(8,128)(2,1)}, u32[]{:S(2)}, u32[]{:S(2)}) collective-permute-start(bf16[16,304,384]{2,1,0:T(8,128)(2,1)} %conditions.1.refs_4_.refs_6_), channel_id=1, source_target_pairs={{0,1},{1,0},{2,3},{3,2},{4,5},{5,4},{6,7},{7,6},{8,9},{9,8},{10,11... | collective-permute-start | bytes 11206664 | tf_op jit(solution)/shard_map/ppermute | solution.py:200
  367.7 20.7 %collective-permute-start.29 = (bf16[1,360,384]{2,1,0:T(8,128)(2,1)}, bf16[1,360,384]{2,1,0:T(8,128)(2,1)}, u32[]{:S(2)}, u32[]{:S(2)}) collective-permute-start(bf16[1,360,384]{2,1,0:T(8,128)(2,1)} %get-tuple-element.235.refs_16_.refs_10_.refs_13_), channel_id=1, source_target_pairs={{0,16},{16,0},{1,17},{17,1},{2,18},{18,2},{3,19},{19,3},{4,20},{20... | collective-permute-start | bytes 829448 | tf_op jit(solution)/shard_map/ppermute | solution.py:200
  369.1 19.2 %collective-permute-start.27 = (bf16[4,96,384]{2,1,0:T(8,128)(2,1)}, bf16[4,96,384]{2,1,0:T(8,128)(2,1)}, u32[]{:S(2)}, u32[]{:S(2)}) collective-permute-start(bf16[4,96,384]{2,1,0:T(8,128)(2,1)} %get-tuple-element.231.refs_12_), channel_id=1, source_target_pairs={{0,8},{1,9},{2,10},{3,11},{4,12},{5,13},{6,14},{7,15},{8,0},{9,1},... | collective-permute-start | bytes 884744 | tf_op jit(solution)/shard_map/ppermute | solution.py:200
  369.7 21.9 %collective-permute-start.28 = (bf16[4,304,384]{2,1,0:T(8,128)(2,1)}, bf16[4,304,384]{2,1,0:T(8,128)(2,1)S(1)}, u32[]{:S(2)}, u32[]{:S(2)}) collective-permute-start(bf16[4,304,384]{2,1,0:T(8,128)(2,1)} %get-tuple-element.233.refs_14_.refs_17_), channel_id=1, source_target_pairs={{0,2},{1,3},{2,0},{3,1},{4,6},{5,7},{6,4},{7,5},{8,10},{9,11},{10,... | collective-permute-start | bytes 2801672 | tf_op jit(solution)/shard_map/ppermute | solution.py:200
  398.6 14.6 %collective-permute-start.39 = (f32[16,128]{1,0:T(8,128)}, f32[16,128]{1,0:T(8,128)S(1)}, u32[]{:S(2)}, u32[]{:S(2)}) collective-permute-start(f32[16,128]{1,0:T(8,128)} %get-tuple-element.248), channel_id=1, source_target_pairs={{0,17},{1,16},{2,19},{3,18},{4,21},{5,20},{6,23},{7,22},{8,25},{9,... | collective-permute-start | bytes 24584 | tf_op jit(solution)/shard_map/ppermute | solution.py:1122
  398.6 14.6 %collective-permute-start.38 = (f32[16,128]{1,0:T(8,128)}, f32[16,128]{1,0:T(8,128)S(1)}, u32[]{:S(2)}, u32[]{:S(2)}) collective-permute-start(f32[16,128]{1,0:T(8,128)} %get-tuple-element.248), channel_id=1, source_target_pairs={{0,1},{1,0},{2,3},{3,2},{4,5},{5,4},{6,7},{7,6},{8,9},{9,8},{10,11... | collective-permute-start | bytes 24584 | tf_op jit(solution)/shard_map/ppermute | solution.py:1122
  399.3 14.0 %collective-permute-start.37 = (f32[16,128]{1,0:T(8,128)}, f32[16,128]{1,0:T(8,128)S(1)}, u32[]{:S(2)}, u32[]{:S(2)}) collective-permute-start(f32[16,128]{1,0:T(8,128)} %get-tuple-element.248), channel_id=1, source_target_pairs={{0,16},{1,17},{2,18},{3,19},{4,20},{5,21},{6,22},{7,23},{8,24},{9,... | collective-permute-start | bytes 24584 | tf_op jit(solution)/shard_map/ppermute | solution.py:1122
  (42 other events, 338.2 us)
Sparse Core Ops, SparseCore 0:
  21.5 101.6 all-gather.2

commit v6 on v5

--- a/solution.py
+++ b/solution.py
@@ -17,7 +17,7 @@
 LONG, SHORT = 10**11, 17 * 10**9
 TOKENS = 128
 HIDDEN = 768
-VMEM_LIMIT = 63 * 2**20
+VMEM_LIMIT = 64 * 2**20 - 2**17
 
 
 def dot(left, right, left_dim=1, right_dim=0):
@@ -308,17 +308,23 @@
     )[0]
 
 
-def pair_backward_kernel(chunks, place, pair_ref, gain_ref, weight_ref, *refs):
+def pair_backward_kernel(chunks, first, place, pair_ref, gain_ref, weight_ref, *refs):
     grad_refs, (out_ref, weight_grad_ref, grads) = refs[:chunks], refs[-3:]
     gain = gain_ref[...]
     channels = pair_ref.shape[2]
     average = jnp.full((channels, channels), 1.0 / channels, BF16)
     clear(pl.program_id(0), weight_grad_ref)
-    head = 0
-    for ref in grad_refs:
-        for h in range(ref.shape[0]):
-            grads[:, head, :] = ref[h].astype(F32)
-            head += 1
+    step = pl.program_id(0)
+    rows = pair_ref.shape[0]
+
+    @pl.when(step == 0)
+    def _():
+        head = 0
+        for ref in grad_refs:
+            for h in range(ref.shape[0]):
+                grads[:, head, :] = ref[h, first : first + grads.shape[0]].astype(F32)
+                head += 1
+
     scaled = weight_ref[...].astype(F32) * gain
     means = jnp.broadcast_to(jnp.mean(scaled, axis=-1, keepdims=True), scaled.shape)
     full = jnp.concatenate([scaled, means], axis=1)
@@ -330,7 +336,7 @@
         center = values.astype(F32) - dot(values, average)
         inverse = lax.rsqrt(jnp.mean(center * center, axis=-1, keepdims=True) + EPS)
         normed = center * inverse
-        grad = grads[i].astype(BF16)
+        grad = grads[step * rows + i].astype(BF16)
         weight_grad_ref[...] += dot(grad, (normed * gain).astype(BF16))
         both = dot(jnp.concatenate([grad, grad], axis=0), parts, 0, 0)
         grad_normed = both[:, :channels]
@@ -347,24 +353,24 @@
         weight_grad_ref[...] = jnp.concatenate([total[half:], total[:half]], axis=0)
 
 
-def pair_backward(first, count, block, out, pair, grads, gain, weight_t, deps, order):
+def pair_backward(first, count, out, pair, grads, gain, weight_t, deps, order):
     rows, length, channels = pair.shape
     heads = weight_t.shape[0]
-    blocked = pl.BlockSpec((block, length, channels), lambda t, place: (first + t, 0, 0))
-    ins = [(pair, blocked), (gain, spec(gain.shape)), (weight_t, spec(weight_t.shape))] + [
-        (g, pl.BlockSpec((g.shape[0], block, length), lambda t, place: (0, first + t, 0))) for g in grads
-    ]
+    block = 8
+    blocked = pl.BlockSpec((block, length, channels), lambda t, place: (first // block + t, 0, 0))
+    ins = [(pair, blocked), (gain, spec(gain.shape)), (weight_t, spec(weight_t.shape))]
+    ins += [(g, spec(g.shape)) for g in grads]
     aliases = {}
     if out is not None:
         aliases = {1 + len(ins): 0}
         ins.append((out, pl.BlockSpec(memory_space=pl.ANY)))
     return call(
         "pair_backward",
-        functools.partial(pair_backward_kernel, len(grads)),
-        count,
+        functools.partial(pair_backward_kernel, len(grads), first),
+        count // block,
         ins,
         [(pair.shape, F32, blocked), ((heads, channels), F32, spec((heads, channels)))],
-        [pltpu.VMEM((block, heads, length), F32)],
+        [pltpu.VMEM((count, heads, length), F32)],
         deps,
         order,
         LONG,
@@ -643,7 +649,7 @@
                     for c in range(2):
                         at = (dest + c) * share + value * (share << bit)
                         ref[2 * p + c, 0] = dlow[pl.ds(pl.multiple_of(at, 16 if share % 16 == 0 else 8), share), :].astype(BF16)
-        dq_ref[s] += dot(grad_low, k_ref[s] * mask) * scale
+        dq_ref[s] += (dot(grad_low, k_ref[s] * mask) * scale).astype(BF16)
         dvt_ref[s] = dot(gt_ref[s], plow[s % 2]).astype(BF16)
         dkt_ref[s] = (dot(qt_ref[s], dslow[s % 2]) * scale).astype(BF16)
 
@@ -665,7 +671,7 @@
         functools.partial(attention_kernel, halving, head_dim),
         CHUNK_HEADS,
         [(a, nat) for a in nats] + [(a, turn) for a in turned] + [(bias, bias_in)],
-        [((samples, length, wide), F32, held)] * 2
+        [((samples, length, wide), F32, held), ((samples, length, wide), BF16, held)]
         + [((samples, CHUNK_HEADS * head_dim, length), BF16, turn_out)] * 2
         + [((parts // 2, CHUNK_HEADS, share, length), BF16, bias_out)] * 2,
         [
@@ -704,9 +710,9 @@
     gate = gate_ref[...]
     gated = (gate * mixed).astype(BF16)
     grad_queries = join(dq_refs)
-    q_bias_out[...] += column_sum(grad_queries)
+    q_bias_out[...] += column_sum(grad_queries.astype(F32))
     grad_gate = gated_grad_ref[...] * mixed * slope(gate)
-    parts = [gated, grad_queries.astype(BF16), turn(dkt_refs), turn(dvt_refs), grad_gate.astype(BF16)]
+    parts = [gated, grad_queries, turn(dkt_refs), turn(dvt_refs), grad_gate.astype(BF16)]
     for i in range(2):
         here = slice(i * own_samples, (i + 1) * own_samples)
         for j, part in enumerate(parts):
@@ -1107,12 +1113,12 @@
     block = 16 if share % 16 == 0 else share
     turned_wt = jnp.where(core == 0, pair_wt, jnp.roll(pair_wt, heads // 2, axis=0))
     grads = [b.result[0] for b in bias_sums] + [b.result[1] for b in bias_sums]
-    grad_pair, part = pair_backward(0, 1, block, None, pair, grads, rows["pair"], turned_wt, [], order)
+    grad_pair, part = pair_backward(0, block, None, pair, grads, rows["pair"], turned_wt, [], order)
     pair_parts = [part]
     if share > block:
         deps = advance(order, qkvg_sum, rest, early)
         grad_pair, part = pair_backward(
-            1, share // block - 1, block, grad_pair, pair, grads, rows["pair"], turned_wt, deps, order
+            block, share - block, grad_pair, pair, grads, rows["pair"], turned_wt, deps, order
         )
         pair_parts.append(part)
     struct_bits = struct_count.bit_length() - 1

time: 449 us -> 444 us (0.989)
  no operation moved by 1% of the time
where the time goes in v6:
time: 444 us; the launch traced here: 441 us
  Pallas kernels  335 us (75%)
  waiting for transfers between devices  43 us (10%)
  starting transfers between devices  38.6 us (9%)
  between operations  15.3 us (3%)
  local copies, waits for them, and re-layouts  7.27 us (2%)
    pallas_call x25, Pallas kernels, call(): pl.pallas_call(run, grid_spec=pltpu.PrefetchScalarGridSpec(num_scalar_pre...  335 us
    ppermute x30, waiting for transfers between devices, exchange(): lax.ppermute(array, axis, [(i, i ^ 1 << bit) for i in range(self.counts[a...  31.6 us
    ppermute x30, starting transfers between devices, exchange(): lax.ppermute(array, axis, [(i, i ^ 1 << bit) for i in range(self.counts[a...  30.1 us
  transfers between devices with their start and end apart: 45, of which 12 were waited for; matrix products, arithmetic and copies ran while one was open for 1% of the time, Pallas kernels for 70%

profile of v6, /device:TPU:0, one launch (start us, length us, event | category | flops | bytes accessed | tf_op | source)
XLA Modules:
  0.0 440.6 jit_solution(3731551382372163292)
XLA Ops:
  8.4 12.9 %pair_forward.1 = bf16[16,48,768]{2,1,0:T(8,128)(2,1)} custom-call(s32[5]{0:T(128)} %broadcast_1_place_ref.2.place_ref, bf16[48,768,128]{2,1,0:T(8,128)(2,1)} %bitcast.49, bf16[1,128]{1,0:T(2,128)(2,1)} %bitcast.63, bf16[16,128]{1,0:T(8,128)(2,1)} %bitcast.42, s32[1,768]{1,0:T(1,128)} %refs_3_.2, s32[1]{0:T(128)S(6)} %copy.40.refs_4_), custom_call_target="tpu_custom_call" | custom-call | flops 99999997952 | bytes 1000000 | tf_op jit(solution)/shard_map/pair_forward/pallas_call | solution.py:81
  23.9 57.4 %transition.1 = (f32[2,768,768]{2,1,0:T(8,128)}, f32[2,768,768]{2,1,0:T(8,128)}, f32[768,384]{1,0:T(8,128)}, f32[768,384]{1,0:T(8,128)}, bf16[32,360,384]{2,1,0:...) custom-call(s32[5]{0:T(128)} %stack.23.place_ref, bf16[2,768,768]{2,1,0:T(8,128)(2,1)} %bitcast.53, ...), custom_call_target="tpu_custom_call" | custom-call | flops 99999997952 | bytes 1000000 | tf_op jit(solution)/shard_map/transition/pallas_call | solution.py:81
  82.9 27.9 %inputs.1 = (bf16[4,768,768]{2,1,0:T(8,128)(2,1)}, f32[4,768,384]{2,1,0:T(8,128)}, f32[4,768,384]{2,1,0:T(8,128)}, bf16[4,4,768,128]{3,2,1,0:T(8,128)(2,1)}, bf1...) custom-call(s32[5]{0:T(128)} %stack.23.place_ref, ...), custom_call_target="tpu_custom_call" | custom-call | flops 99999997952 | bytes 1000000 | tf_op jit(solution)/shard_map/inputs/pallas_call | solution.py:81
  110.8 7.0 %combine.11 = (bf16[8,360,384]{2,1,0:T(8,128)(2,1)}, bf16[8,360,384]{2,1,0:T(8,128)(2,1)}) custom-call(s32[5]{0:T(128)} %stack.23.place_ref, bf16[32,360,384]{2,1,0:T(8,128)(2,1)} %get-tuple-element.141.refs_16_.refs_0_.refs_2_, bf16[32,360,384]{2,1,0:T(8,128)(2,1)} %collective-permute-done.2.refs_1_.refs_3_, ...), custom_call_target="tpu_custom_call" | custom-call | flops 99999997952 | bytes 1000000 | tf_op jit(solution)/shard_map/combine/pallas_call | solution.py:81
  120.2 2.9 all-gather.3.cloned.1.call-done
  123.2 23.6 %attention.4 = (f32[4,768,128]{2,1,0:T(8,128)}, bf16[4,768,128]{2,1,0:T(8,128)(2,1)}, bf16[4,96,768]{2,1,0:T(8,128)(2,1)}, bf16[4,96,768]{2,1,0:T(8,128)(2,1)}, ...) custom-call(s32[5]{0:T(128)} %stack.23.place_ref, bf16[4,4,768,128]{3,2,1,0:T(8,128)(2,1)} %get-tuple-element.146.refs_0_, ...), custom_call_target="tpu_custom_call" | custom-call | flops 16999999488 | bytes 1000000 | tf_op jit(solution)/shard_map/attention/pallas_call | solution.py:81
  148.1 23.8 %attention.5 = (f32[4,768,128]{2,1,0:T(8,128)}, bf16[4,768,128]{2,1,0:T(8,128)(2,1)}, bf16[4,96,768]{2,1,0:T(8,128)(2,1)}, bf16[4,96,768]{2,1,0:T(8,128)(2,1)}, ...) custom-call(s32[5]{0:T(128)} %stack.23.place_ref, bf16[4,4,768,128]{3,2,1,0:T(8,128)(2,1)} %get-tuple-element.146.refs_0_, ...), custom_call_target="tpu_custom_call" | custom-call | flops 16999999488 | bytes 1000000 | tf_op jit(solution)/shard_map/attention/pallas_call | solution.py:81
  172.7 3.0 collective-permute-done.3.refs_1_.refs_3_
  175.7 5.5 %combine.12 = (bf16[4,2,48,768]{3,2,1,0:T(8,128)(2,1)}, bf16[4,2,48,768]{3,2,1,0:T(8,128)(2,1)}, bf16[4,360,384]{2,1,0:T(8,128)(2,1)}, bf16[4,360,384]{2,1,0:T(8,128)(2,1)}) custom-call(s32[5]{0:T(128)} %stack.23.place_ref, bf16[8,2,48,768]{3,2,1,0:T(8,128)(2,1)} %get-tuple-element.160.refs_0_.refs_2_, ...), custom_call_target="tpu_custom_call" | custom-call | flops 99999997952 | bytes 1000000 | tf_op jit(solution)/shard_map/combine/pallas_call | solution.py:81
  183.2 23.8 %attention.6 = (f32[4,768,128]{2,1,0:T(8,128)}, bf16[4,768,128]{2,1,0:T(8,128)(2,1)}, bf16[4,96,768]{2,1,0:T(8,128)(2,1)}, bf16[4,96,768]{2,1,0:T(8,128)(2,1)}, ...) custom-call(s32[5]{0:T(128)} %stack.23.place_ref, bf16[4,4,768,128]{3,2,1,0:T(8,128)(2,1)} %get-tuple-element.146.refs_0_, ...), custom_call_target="tpu_custom_call" | custom-call | flops 16999999488 | bytes 1000000 | tf_op jit(solution)/shard_map/attention/pallas_call | solution.py:81
  208.7 3.9 combine.13
  215.2 24.1 %attention.7 = (f32[4,768,128]{2,1,0:T(8,128)}, bf16[4,768,128]{2,1,0:T(8,128)(2,1)}, bf16[4,96,768]{2,1,0:T(8,128)(2,1)}, bf16[4,96,768]{2,1,0:T(8,128)(2,1)}, ...) custom-call(s32[5]{0:T(128)} %stack.23.place_ref, bf16[4,4,768,128]{3,2,1,0:T(8,128)(2,1)} %get-tuple-element.146.refs_0_, ...), custom_call_target="tpu_custom_call" | custom-call | flops 16999999488 | bytes 1000000 | tf_op jit(solution)/shard_map/attention/pallas_call | solution.py:81
  241.4 5.3 %combine.14 = (bf16[1,2,48,768]{3,2,1,0:T(8,128)(2,1)}, bf16[1,2,48,768]{3,2,1,0:T(8,128)(2,1)}, bf16[2,2,48,768]{3,2,1,0:T(8,128)(2,1)}, bf16[2,2,48,768]{3,2,1...) custom-call(s32[5]{0:T(128)} %stack.23.place_ref, ...), custom_call_target="tpu_custom_call" | custom-call | flops 99999997952 | bytes 1000000 | tf_op jit(solution)/shard_map/combine/pallas_call | solution.py:81
  247.0 2.7 collective-permute-start.18
  250.0 14.4 %mixed.1 = (bf16[2,768,1920]{2,1,0:T(8,128)(2,1)}, bf16[2,768,1920]{2,1,0:T(8,128)(2,1)}, f32[1,384]{1,0:T(1,128)}) custom-call(s32[5]{0:T(128)} %stack.23.place_ref, f32[4,768,384]{2,1,0:T(8,128)} %get-tuple-element.144.refs_0_, f32[4,768,384]{2,1,0:T(8,128)} %get-tuple-element.145.refs_1_, f32[4,768,128]{2,1,0:T(8,128)} %get-tuple-element.157.refs_2_, ...), custom_call_target="tpu_custom_call" | custom-call | flops 99999997952 | bytes 1000000 | tf_op jit(solution)/shard_map/mixed/pallas_call | solution.py:81
  264.3 14.4 %qkvg_grad.1.refs_12_.refs_13_.refs_8_.refs_10_ = bf16[32,96,384]{2,1,0:T(8,128)(2,1)} custom-call(s32[5]{0:T(128)} %stack.23.place_ref, bf16[4,768,768]{2,1,0:T(8,128)(2,1)} %get-tuple-element.154.refs_4_.refs_0_, bf16[2,768,1920]{2,1,0:T(8,128)(2,1)} %get-tuple-element.196.refs_1_.refs_2_.refs_5_.refs_6_, ...), custom_call_target="tpu_custom_call" | custom-call | flops 99999997952 | bytes 1000000 | tf_op jit(solution)/shard_map/qkvg_grad/pallas_call | solution.py:81
  278.8 5.1 %combine.15 = (bf16[1,2,48,768]{3,2,1,0:T(8,128)(2,1)}, bf16[1,2,48,768]{3,2,1,0:T(8,128)(2,1)}, bf16[2,2,48,768]{3,2,1,0:T(8,128)(2,1)}, bf16[2,2,48,768]{3,2,1...) custom-call(s32[5]{0:T(128)} %stack.23.place_ref, ...), custom_call_target="tpu_custom_call" | custom-call | flops 99999997952 | bytes 1000000 | tf_op jit(solution)/shard_map/combine/pallas_call | solution.py:81
  283.8 3.4 collective-permute-start.15
  290.2 25.4 %outputs.1 = (bf16[2,768,768]{2,1,0:T(8,128)(2,1)}, bf16[2,768,768]{2,1,0:T(8,128)(2,1)}, bf16[768,1536]{1,0:T(8,128)(2,1)}, bf16[768,768]{1,0:T(8,128)(2,1)}, f...) custom-call(s32[5]{0:T(128)} %stack.23.place_ref, bf16[2,768,768]{2,1,0:T(8,128)(2,1)} %bitcast.55, ...), custom_call_target="tpu_custom_call" | custom-call | flops 99999997952 | bytes 1000000 | tf_op jit(solution)/shard_map/outputs/pallas_call | solution.py:81
  317.0 4.8 %combine.16 = (bf16[1,2,48,768]{3,2,1,0:T(8,128)(2,1)}, bf16[1,2,48,768]{3,2,1,0:T(8,128)(2,1)}, bf16[2,2,48,768]{3,2,1,0:T(8,128)(2,1)}, bf16[2,2,48,768]{3,2,1...) custom-call(s32[5]{0:T(128)} %stack.23.place_ref, ...), custom_call_target="tpu_custom_call" | custom-call | flops 99999997952 | bytes 1000000 | tf_op jit(solution)/shard_map/combine/pallas_call | solution.py:81
  322.5 10.3 %conditions.1.refs_4_.refs_6_ = bf16[16,304,384]{2,1,0:T(8,128)(2,1)} custom-call(s32[5]{0:T(128)} %stack.23.place_ref, bf16[768,384]{1,0:T(8,128)(2,1)} %bitcast.62, f32[1,768]{1,0:T(1,128)} %get-tuple-element.263.refs_3_.refs_5_.refs_1_, bf16[384,3072]{1,0:T(8,128)(2,1)} %refs_2_.1, bf16[384,1536]{1,0:T(8,128)(2,1)} %refs_3_.3, ...), custom_call_target="tpu_custom_call" | custom-call | flops 99999997952 | bytes 1000000 | tf_op jit(solution)/shard_map/conditions/pallas_call | solution.py:81
  332.8 5.9 %collective-permute-done.19.refs_1_.refs_3_ = bf16[2,2,48,768]{3,2,1,0:T(8,128)(2,1)} collective-permute-done((bf16[2,2,48,768]{3,2,1,0:T(8,128)(2,1)}, bf16[2,2,48,768]{3,2,1,0:T(8,128)(2,1)}, u32[]{:S(2)}, u32[]{:S(2)}) %collective-permute-start.19) | collective-permute-done | bytes 294944 | tf_op jit(solution)/shard_map/ppermute | solution.py:200
  343.5 10.8 %pair_backward.2 = (f32[48,768,128]{2,1,0:T(8,128)}, f32[16,128]{1,0:T(8,128)}) custom-call(s32[5]{0:T(128)} %stack.23.place_ref, bf16[48,768,128]{2,1,0:T(8,128)(2,1)} %bitcast.50, f32[1,128]{1,0:T(1,128)} %slice.34.refs_1_.refs_10_, bf16[16,128]{1,0:T(8,128)(2,1)} %maximum_select_fusion.refs_2_, bf16[2,48,768]{2,1,0:T(8,128)(2,1)} %bitcast.69, ...), custom_call_target="tpu_custom_call" | custom-call | flops 99999997952 | bytes 1000000 | tf_op jit(solution)/shard_map/pair_backward/pallas_call | solution.py:81
  354.3 4.7 %collective-permute-done.24.refs_1_.refs_3_ = bf16[8,96,384]{2,1,0:T(8,128)(2,1)} collective-permute-done((bf16[8,96,384]{2,1,0:T(8,128)(2,1)}, bf16[8,96,384]{2,1,0:T(8,128)(2,1)}, u32[]{:S(2)}, u32[]{:S(2)}) %collective-permute-start.24) | collective-permute-done | bytes 589856 | tf_op jit(solution)/shard_map/ppermute | solution.py:200
  358.9 4.9 %combine.18 = (bf16[4,96,384]{2,1,0:T(8,128)(2,1)}, bf16[4,96,384]{2,1,0:T(8,128)(2,1)}, bf16[4,304,384]{2,1,0:T(8,128)(2,1)}, bf16[4,304,384]{2,1,0:T(8,128)(2,1)}, bf16[1,360,384]{2,1,0:T(8,128)(2,1)}) custom-call(s32[5]{0:T(128)} %stack.23.place_ref, bf16[8,96,384]{2,1,0:T(8,128)(2,1)} %get-tuple-element.224.refs_20_.refs_0_.refs_2_, ...), custom_call_target="tpu_custom_call" | custom-call | flops 99999997952 | bytes 1000000 | tf_op jit(solution)/shard_map/combine/pallas_call | solution.py:81
  366.4 17.2 %pair_backward.3 = (f32[48,768,128]{2,1,0:T(8,128)}, f32[16,128]{1,0:T(8,128)}) custom-call(s32[5]{0:T(128)} %stack.23.place_ref, bf16[48,768,128]{2,1,0:T(8,128)(2,1)} %bitcast.51, f32[1,128]{1,0:T(1,128)} %slice.34.refs_1_.refs_10_, bf16[16,128]{1,0:T(8,128)(2,1)} %maximum_select_fusion.refs_2_, ...), custom_call_target="tpu_custom_call", output_to_operand_aliasing={{0}: (12, {})} | custom-call | flops 99999997952 | bytes 1000000 | tf_op jit(solution)/shard_map/pair_backward/pallas_call | solution.py:81
  383.5 4.3 collective-permute-done.28.refs_7_.refs_9_
  387.9 4.2 combine.19
  398.8 4.2 collective-permute-done.31.refs_5_.refs_7_
  412.1 5.4 %collective-permute-done.35.refs_1_ = bf16[1,304,384]{2,1,0:T(8,128)(2,1)S(1)} collective-permute-done((bf16[1,304,384]{2,1,0:T(8,128)(2,1)S(1)}, bf16[1,304,384]{2,1,0:T(8,128)(2,1)S(1)}, u32[]{:S(2)}, u32[]{:S(2)}) %collective-permute-start.35) | collective-permute-done | bytes 233504 | tf_op jit(solution)/shard_map/ppermute | solution.py:200
  420.4 4.5 %collective-permute-done.43 = f32[16,128]{1,0:T(8,128)S(1)} collective-permute-done((f32[16,128]{1,0:T(8,128)S(1)}, f32[16,128]{1,0:T(8,128)S(1)}, u32[]{:S(2)}, u32[]{:S(2)}) %collective-permute-start.43) | collective-permute-done | bytes 8224 | tf_op jit(solution)/shard_map/ppermute | solution.py:1128
  428.6 4.9 %results.1 = (f32[48,384]{1,0:T(8,128)}, f32[24,3072]{1,0:T(8,128)}, f32[24,1536]{1,0:T(8,128)}, f32[48,3072]{1,0:T(8,128)}, f32[48,768]{1,0:T(8,128)}, /*index=...) custom-call(s32[5]{0:T(128)} %stack.23.place_ref, ...), custom_call_target="tpu_custom_call" | custom-call | flops 99999997952 | bytes 1000000 | tf_op jit(solution)/shard_map/results/pallas_call | solution.py:81
  (139 shorter events, 52.9 us)
Async XLA Ops:
  7.2 116.0 %all-gather.3.cloned.1.call-start = ((), (), s32[]{:S(2)}) async-start(), calls=%async_computation | async-start | bytes 20054016 | tf_op jit(solution)/shard_map/all_gather | solution.py:1036
  21.4 61.5 %collective-permute-start = (bf16[2,768,768]{2,1,0:T(8,128)(2,1)}, bf16[2,768,768]{2,1,0:T(8,128)(2,1)}, u32[]{:S(2)}, u32[]{:S(2)}) collective-permute-start(bf16[2,768,768]{2,1,0:T(8,128)(2,1)} %bitcast.52), channel_id=1, source_target_pairs={{0,1},{1,0},{2,3},{3,2},{4,5},{5,4},{6,7},{7,6},{8,9},{9,8},{10,11... | collective-permute-start | bytes 7077896 | tf_op jit(solution)/shard_map/ppermute | solution.py:1031
  21.9 61.0 %collective-permute-start.1 = (bf16[2,768,768]{2,1,0:T(8,128)(2,1)}, bf16[2,768,768]{2,1,0:T(8,128)(2,1)}, u32[]{:S(2)}, u32[]{:S(2)}) collective-permute-start(bf16[2,768,768]{2,1,0:T(8,128)(2,1)} %bitcast.56), channel_id=1, source_target_pairs={{0,1},{1,0},{2,3},{3,2},{4,5},{5,4},{6,7},{7,6},{8,9},{9,8},{10,11... | collective-permute-start | bytes 7077896 | tf_op jit(solution)/shard_map/ppermute | solution.py:1031
  81.3 29.5 %collective-permute-start.2 = (bf16[32,360,384]{2,1,0:T(8,128)(2,1)}, bf16[32,360,384]{2,1,0:T(8,128)(2,1)}, u32[]{:S(2)}, u32[]{:S(2)}) collective-permute-start(bf16[32,360,384]{2,1,0:T(8,128)(2,1)} %get-tuple-element.141.refs_16_.refs_0_.refs_2_), channel_id=1, source_target_pairs={{0,1},{1,0},{2,3},{3,2},{4,5},{5,4},{6,7},{7,6},{8,9},{9,8},{10,11... | collective-permute-start | bytes 26542088 | tf_op jit(solution)/shard_map/ppermute | solution.py:200
  117.8 54.9 %collective-permute-start.4 = (bf16[8,360,384]{2,1,0:T(8,128)(2,1)}, bf16[8,360,384]{2,1,0:T(8,128)(2,1)}, u32[]{:S(2)}, u32[]{:S(2)}) collective-permute-start(bf16[8,360,384]{2,1,0:T(8,128)(2,1)} %get-tuple-element.155.refs_9_.refs_11_), channel_id=1, source_target_pairs={{0,16},{16,0},{1,17},{17,1},{2,18},{18,2},{3,19},{19,3},{4,20},{20... | collective-permute-start | bytes 6635528 | tf_op jit(solution)/shard_map/ppermute | solution.py:200
  146.8 28.9 %collective-permute-start.3 = (bf16[8,2,48,768]{3,2,1,0:T(8,128)(2,1)}, bf16[8,2,48,768]{3,2,1,0:T(8,128)(2,1)}, u32[]{:S(2)}, u32[]{:S(2)}) collective-permute-start(bf16[8,2,48,768]{3,2,1,0:T(8,128)(2,1)} %get-tuple-element.158.refs_9_), channel_id=1, source_target_pairs={{0,2},{1,3},{2,0},{3,1},{4,6},{5,7},{6,4},{7,5},{8,10},{9,11},{10,... | collective-permute-start | bytes 3538952 | tf_op jit(solution)/shard_map/ppermute | solution.py:200
  171.9 36.8 %collective-permute-start.6 = (bf16[8,2,48,768]{3,2,1,0:T(8,128)(2,1)}, bf16[8,2,48,768]{3,2,1,0:T(8,128)(2,1)}, u32[]{:S(2)}, u32[]{:S(2)}) collective-permute-start(bf16[8,2,48,768]{3,2,1,0:T(8,128)(2,1)} %get-tuple-element.161.refs_8_), channel_id=1, source_target_pairs={{0,2},{1,3},{2,0},{3,1},{4,6},{5,7},{6,4},{7,5},{8,10},{9,11},{10,... | collective-permute-start | bytes 3538952 | tf_op jit(solution)/shard_map/ppermute | solution.py:200
  181.2 27.4 %collective-permute-start.5 = (bf16[4,2,48,768]{3,2,1,0:T(8,128)(2,1)}, bf16[4,2,48,768]{3,2,1,0:T(8,128)(2,1)}, u32[]{:S(2)}, u32[]{:S(2)}) collective-permute-start(bf16[4,2,48,768]{3,2,1,0:T(8,128)(2,1)} %get-tuple-element.162.refs_9_), channel_id=1, source_target_pairs={{0,4},{1,5},{2,6},{3,7},{4,0},{5,1},{6,2},{7,3},{8,12},{9,13},{10,... | collective-permute-start | bytes 1769480 | tf_op jit(solution)/shard_map/ppermute | solution.py:200
  182.7 58.7 %collective-permute-start.10 = (bf16[4,360,384]{2,1,0:T(8,128)(2,1)}, bf16[4,360,384]{2,1,0:T(8,128)(2,1)}, u32[]{:S(2)}, u32[]{:S(2)}) collective-permute-start(bf16[4,360,384]{2,1,0:T(8,128)(2,1)} %get-tuple-element.164.refs_11_.refs_13_), channel_id=1, source_target_pairs={{0,4},{1,5},{2,6},{3,7},{4,0},{5,1},{6,2},{7,3},{8,12},{9,13},{10,... | collective-permute-start | bytes 3317768 | tf_op jit(solution)/shard_map/ppermute | solution.py:200
  207.0 34.3 %collective-permute-start.9 = (bf16[8,2,48,768]{3,2,1,0:T(8,128)(2,1)}, bf16[8,2,48,768]{3,2,1,0:T(8,128)(2,1)}, u32[]{:S(2)}, u32[]{:S(2)}) collective-permute-start(bf16[8,2,48,768]{3,2,1,0:T(8,128)(2,1)} %get-tuple-element.168.refs_8_), channel_id=1, source_target_pairs={{0,2},{1,3},{2,0},{3,1},{4,6},{5,7},{6,4},{7,5},{8,10},{9,11},{10,... | collective-permute-start | bytes 3538952 | tf_op jit(solution)/shard_map/ppermute | solution.py:200
  212.6 28.8 %collective-permute-start.7 = (bf16[2,2,48,768]{3,2,1,0:T(8,128)(2,1)}, bf16[2,2,48,768]{3,2,1,0:T(8,128)(2,1)}, u32[]{:S(2)}, u32[]{:S(2)}) collective-permute-start(bf16[2,2,48,768]{3,2,1,0:T(8,128)(2,1)} %get-tuple-element.169.refs_9_), channel_id=1, source_target_pairs={{0,8},{1,9},{2,10},{3,11},{4,12},{5,13},{6,14},{7,15},{8,0},{9,1},... | collective-permute-start | bytes 884744 | tf_op jit(solution)/shard_map/ppermute | solution.py:200
  215.0 26.4 %collective-permute-start.8 = (bf16[4,2,48,768]{3,2,1,0:T(8,128)(2,1)}, bf16[4,2,48,768]{3,2,1,0:T(8,128)(2,1)}, u32[]{:S(2)}, u32[]{:S(2)}) collective-permute-start(bf16[4,2,48,768]{3,2,1,0:T(8,128)(2,1)} %get-tuple-element.171.refs_11_.refs_13_), channel_id=1, source_target_pairs={{0,4},{1,5},{2,6},{3,7},{4,0},{5,1},{6,2},{7,3},{8,12},{9,13},{10,... | collective-permute-start | bytes 1769480 | tf_op jit(solution)/shard_map/ppermute | solution.py:200
  239.3 39.4 %collective-permute-start.14 = (bf16[8,2,48,768]{3,2,1,0:T(8,128)(2,1)}, bf16[8,2,48,768]{3,2,1,0:T(8,128)(2,1)}, u32[]{:S(2)}, u32[]{:S(2)}) collective-permute-start(bf16[8,2,48,768]{3,2,1,0:T(8,128)(2,1)} %get-tuple-element.187.refs_16_), channel_id=1, source_target_pairs={{0,2},{1,3},{2,0},{3,1},{4,6},{5,7},{6,4},{7,5},{8,10},{9,11},{10,... | collective-permute-start | bytes 3538952 | tf_op jit(solution)/shard_map/ppermute | solution.py:200
  246.7 96.5 %collective-permute-start.20 = (bf16[1,2,48,768]{3,2,1,0:T(8,128)(2,1)}, bf16[1,2,48,768]{3,2,1,0:T(8,128)(2,1)}, u32[]{:S(2)}, u32[]{:S(2)}) collective-permute-start(bf16[1,2,48,768]{3,2,1,0:T(8,128)(2,1)} %get-tuple-element.188.refs_18_), channel_id=1, source_target_pairs={{0,1},{1,0},{2,3},{3,2},{4,5},{5,4},{6,7},{7,6},{8,9},{9,8},{10,11... | collective-permute-start | bytes 442376 | tf_op jit(solution)/shard_map/ppermute | solution.py:200
  246.7 32.0 %collective-permute-start.12 = (bf16[2,2,48,768]{3,2,1,0:T(8,128)(2,1)}, bf16[2,2,48,768]{3,2,1,0:T(8,128)(2,1)}, u32[]{:S(2)}, u32[]{:S(2)}) collective-permute-start(bf16[2,2,48,768]{3,2,1,0:T(8,128)(2,1)} %get-tuple-element.190.refs_20_), channel_id=1, source_target_pairs={{0,8},{1,9},{2,10},{3,11},{4,12},{5,13},{6,14},{7,15},{8,0},{9,1},... | collective-permute-start | bytes 884744 | tf_op jit(solution)/shard_map/ppermute | solution.py:200
  247.0 68.5 %collective-permute-start.18 = (bf16[2,360,384]{2,1,0:T(8,128)(2,1)}, bf16[2,360,384]{2,1,0:T(8,128)(2,1)}, u32[]{:S(2)}, u32[]{:S(2)}) collective-permute-start(bf16[2,360,384]{2,1,0:T(8,128)(2,1)} %get-tuple-element.194.refs_24_), channel_id=1, source_target_pairs={{0,8},{1,9},{2,10},{3,11},{4,12},{5,13},{6,14},{7,15},{8,0},{9,1},... | collective-permute-start | bytes 1658888 | tf_op jit(solution)/shard_map/ppermute | solution.py:200
  249.7 29.1 %collective-permute-start.13 = (bf16[4,2,48,768]{3,2,1,0:T(8,128)(2,1)}, bf16[4,2,48,768]{3,2,1,0:T(8,128)(2,1)}, u32[]{:S(2)}, u32[]{:S(2)}) collective-permute-start(bf16[4,2,48,768]{3,2,1,0:T(8,128)(2,1)} %get-tuple-element.192.refs_22_.refs_26_), channel_id=1, source_target_pairs={{0,4},{1,5},{2,6},{3,7},{4,0},{5,1},{6,2},{7,3},{8,12},{9,13},{10,... | collective-permute-start | bytes 1769480 | tf_op jit(solution)/shard_map/ppermute | solution.py:200
  283.8 31.8 %collective-permute-start.15 = (bf16[2,2,48,768]{3,2,1,0:T(8,128)(2,1)}, bf16[2,2,48,768]{3,2,1,0:T(8,128)(2,1)}, u32[]{:S(2)}, u32[]{:S(2)}) collective-permute-start(bf16[2,2,48,768]{3,2,1,0:T(8,128)(2,1)} %get-tuple-element.201.refs_20_), channel_id=1, source_target_pairs={{0,8},{1,9},{2,10},{3,11},{4,12},{5,13},{6,14},{7,15},{8,0},{9,1},... | collective-permute-start | bytes 884744 | tf_op jit(solution)/shard_map/ppermute | solution.py:200
  287.2 28.5 %collective-permute-start.16 = (bf16[4,2,48,768]{3,2,1,0:T(8,128)(2,1)}, bf16[4,2,48,768]{3,2,1,0:T(8,128)(2,1)}, u32[]{:S(2)}, u32[]{:S(2)}) collective-permute-start(bf16[4,2,48,768]{3,2,1,0:T(8,128)(2,1)} %get-tuple-element.203.refs_22_), channel_id=1, source_target_pairs={{0,4},{1,5},{2,6},{3,7},{4,0},{5,1},{6,2},{7,3},{8,12},{9,13},{10,... | collective-permute-start | bytes 1769480 | tf_op jit(solution)/shard_map/ppermute | solution.py:200
  288.7 28.3 %collective-permute-start.17 = (bf16[16,96,384]{2,1,0:T(8,128)(2,1)}, bf16[16,96,384]{2,1,0:T(8,128)(2,1)}, u32[]{:S(2)}, u32[]{:S(2)}) collective-permute-start(bf16[16,96,384]{2,1,0:T(8,128)(2,1)} %get-tuple-element.205.refs_24_.refs_25_), channel_id=1, source_target_pairs={{0,16},{16,0},{1,17},{17,1},{2,18},{18,2},{3,19},{19,3},{4,20},{20... | collective-permute-start | bytes 3538952 | tf_op jit(solution)/shard_map/ppermute | solution.py:200
  315.6 27.6 %collective-permute-start.21 = (bf16[1,2,48,768]{3,2,1,0:T(8,128)(2,1)}, bf16[1,2,48,768]{3,2,1,0:T(8,128)(2,1)}, u32[]{:S(2)}, u32[]{:S(2)}) collective-permute-start(bf16[1,2,48,768]{3,2,1,0:T(8,128)(2,1)} %get-tuple-element.199.refs_18_), channel_id=1, source_target_pairs={{0,1},{1,0},{2,3},{3,2},{4,5},{5,4},{6,7},{7,6},{8,9},{9,8},{10,11... | collective-permute-start | bytes 442376 | tf_op jit(solution)/shard_map/ppermute | solution.py:200
  321.8 21.7 %collective-permute-start.22 = (bf16[1,2,48,768]{3,2,1,0:T(8,128)(2,1)}, bf16[1,2,48,768]{3,2,1,0:T(8,128)(2,1)}, u32[]{:S(2)}, u32[]{:S(2)}) collective-permute-start(bf16[1,2,48,768]{3,2,1,0:T(8,128)(2,1)} %get-tuple-element.222.refs_15_), channel_id=1, source_target_pairs={{0,1},{1,0},{2,3},{3,2},{4,5},{5,4},{6,7},{7,6},{8,9},{9,8},{10,11... | collective-permute-start | bytes 442376 | tf_op jit(solution)/shard_map/ppermute | solution.py:200
  321.8 17.0 %collective-permute-start.19 = (bf16[2,2,48,768]{3,2,1,0:T(8,128)(2,1)}, bf16[2,2,48,768]{3,2,1,0:T(8,128)(2,1)}, u32[]{:S(2)}, u32[]{:S(2)}) collective-permute-start(bf16[2,2,48,768]{3,2,1,0:T(8,128)(2,1)} %get-tuple-element.210.refs_17_), channel_id=1, source_target_pairs={{0,8},{1,9},{2,10},{3,11},{4,12},{5,13},{6,14},{7,15},{8,0},{9,1},... | collective-permute-start | bytes 884744 | tf_op jit(solution)/shard_map/ppermute | solution.py:200
  343.2 15.7 %collective-permute-start.24 = (bf16[8,96,384]{2,1,0:T(8,128)(2,1)}, bf16[8,96,384]{2,1,0:T(8,128)(2,1)}, u32[]{:S(2)}, u32[]{:S(2)}) collective-permute-start(bf16[8,96,384]{2,1,0:T(8,128)(2,1)} %get-tuple-element.223.refs_19_.refs_23_), channel_id=1, source_target_pairs={{0,4},{1,5},{2,6},{3,7},{4,0},{5,1},{6,2},{7,3},{8,12},{9,13},{10,... | collective-permute-start | bytes 1769480 | tf_op jit(solution)/shard_map/ppermute | solution.py:200
  343.2 15.7 %collective-permute-start.25 = (bf16[16,304,384]{2,1,0:T(8,128)(2,1)}, bf16[16,304,384]{2,1,0:T(8,128)(2,1)}, u32[]{:S(2)}, u32[]{:S(2)}) collective-permute-start(bf16[16,304,384]{2,1,0:T(8,128)(2,1)} %conditions.1.refs_4_.refs_6_), channel_id=1, source_target_pairs={{0,1},{1,0},{2,3},{3,2},{4,5},{5,4},{6,7},{7,6},{8,9},{9,8},{10,11... | collective-permute-start | bytes 11206664 | tf_op jit(solution)/shard_map/ppermute | solution.py:200
  363.8 19.7 %collective-permute-start.29 = (bf16[1,360,384]{2,1,0:T(8,128)(2,1)}, bf16[1,360,384]{2,1,0:T(8,128)(2,1)}, u32[]{:S(2)}, u32[]{:S(2)}) collective-permute-start(bf16[1,360,384]{2,1,0:T(8,128)(2,1)} %get-tuple-element.235.refs_16_.refs_10_.refs_13_), channel_id=1, source_target_pairs={{0,16},{16,0},{1,17},{17,1},{2,18},{18,2},{3,19},{19,3},{4,20},{20... | collective-permute-start | bytes 829448 | tf_op jit(solution)/shard_map/ppermute | solution.py:200
  365.3 18.2 %collective-permute-start.27 = (bf16[4,96,384]{2,1,0:T(8,128)(2,1)}, bf16[4,96,384]{2,1,0:T(8,128)(2,1)}, u32[]{:S(2)}, u32[]{:S(2)}) collective-permute-start(bf16[4,96,384]{2,1,0:T(8,128)(2,1)} %get-tuple-element.231.refs_12_), channel_id=1, source_target_pairs={{0,8},{1,9},{2,10},{3,11},{4,12},{5,13},{6,14},{7,15},{8,0},{9,1},... | collective-permute-start | bytes 884744 | tf_op jit(solution)/shard_map/ppermute | solution.py:200
  365.9 22.0 %collective-permute-start.28 = (bf16[4,304,384]{2,1,0:T(8,128)(2,1)}, bf16[4,304,384]{2,1,0:T(8,128)(2,1)}, u32[]{:S(2)}, u32[]{:S(2)}) collective-permute-start(bf16[4,304,384]{2,1,0:T(8,128)(2,1)} %get-tuple-element.233.refs_14_.refs_17_), channel_id=1, source_target_pairs={{0,2},{1,3},{2,0},{3,1},{4,6},{5,7},{6,4},{7,5},{8,10},{9,11},{10,... | collective-permute-start | bytes 2801672 | tf_op jit(solution)/shard_map/ppermute | solution.py:200
  394.0 14.5 %collective-permute-start.39 = (f32[16,128]{1,0:T(8,128)}, f32[16,128]{1,0:T(8,128)S(1)}, u32[]{:S(2)}, u32[]{:S(2)}) collective-permute-start(f32[16,128]{1,0:T(8,128)} %get-tuple-element.248), channel_id=1, source_target_pairs={{0,17},{1,16},{2,19},{3,18},{4,21},{5,20},{6,23},{7,22},{8,25},{9,... | collective-permute-start | bytes 24584 | tf_op jit(solution)/shard_map/ppermute | solution.py:1128
  394.0 14.5 %collective-permute-start.38 = (f32[16,128]{1,0:T(8,128)}, f32[16,128]{1,0:T(8,128)S(1)}, u32[]{:S(2)}, u32[]{:S(2)}) collective-permute-start(f32[16,128]{1,0:T(8,128)} %get-tuple-element.248), channel_id=1, source_target_pairs={{0,1},{1,0},{2,3},{3,2},{4,5},{5,4},{6,7},{7,6},{8,9},{9,8},{10,11... | collective-permute-start | bytes 24584 | tf_op jit(solution)/shard_map/ppermute | solution.py:1128
  394.7 13.8 %collective-permute-start.37 = (f32[16,128]{1,0:T(8,128)}, f32[16,128]{1,0:T(8,128)S(1)}, u32[]{:S(2)}, u32[]{:S(2)}) collective-permute-start(f32[16,128]{1,0:T(8,128)} %get-tuple-element.248), channel_id=1, source_target_pairs={{0,16},{1,17},{2,18},{3,19},{4,20},{5,21},{6,22},{7,23},{8,24},{9,... | collective-permute-start | bytes 24584 | tf_op jit(solution)/shard_map/ppermute | solution.py:1128
  412.1 13.4 %collective-permute-start.34 = (bf16[96,384]{1,0:T(8,128)(2,1)S(1)}, bf16[96,384]{1,0:T(8,128)(2,1)S(1)}, u32[]{:S(2)}, u32[]{:S(2)}) collective-permute-start(bf16[96,384]{1,0:T(8,128)(2,1)S(1)} %bitcast.40), channel_id=1, source_target_pairs={{0,17},{1,16},{2,19},{3,18},{4,21},{5,20},{6,23},{7,22},{8,25},{9,... | collective-permute-start | bytes 221192 | tf_op jit(solution)/shard_map/ppermute | solution.py:1161
  (33 other events, 306.5 us)
Sparse Core Ops, SparseCore 0:
  21.5 101.6 all-gather.2

commit v7 on v6

--- a/solution.py
+++ b/solution.py
@@ -14,6 +14,7 @@
 CHUNK_HEADS = 2
 LANES = 128
 PIECE = 384
+LOG2E = 1.4426950408889634
 LONG, SHORT = 10**11, 17 * 10**9
 TOKENS = 128
 HIDDEN = 768
@@ -621,12 +622,12 @@
         vz[s, pl.ds(off, head_dim), :] = vt_ref[s]
     parts, _, share, _ = bias_ref.shape
     if share % 16 == 0:
-        bias = bias_ref[:, 0].reshape(length, length).astype(F32)
+        bias = bias_ref[:, 0].reshape(length, length).astype(F32) * LOG2E
     else:
-        bias = jnp.concatenate([bias_ref[p, 0].astype(F32) for p in range(parts)], axis=0)
+        bias = jnp.concatenate([bias_ref[p, 0].astype(F32) for p in range(parts)], axis=0) * LOG2E
     for s in range(samples):
-        x = dot(q_ref[s], kz[s]) * scale + bias
-        x = jnp.exp(x - jnp.max(x, axis=-1, keepdims=True))
+        x = dot(q_ref[s], kz[s]) * (scale * LOG2E) + bias
+        x = jnp.exp2(x - jnp.max(x, axis=-1, keepdims=True))
         probs = x * (1.0 / jnp.sum(x, axis=-1, keepdims=True))
         low = probs.astype(BF16)
         plow[s % 2] = low
@@ -1148,6 +1149,7 @@
         two = 1 << left.pop(0) if left else 0
         pair_sum = summed(pair_sum, one, two, one | two) if two else summed(pair_sum, one)
     chains = (qkvg_sum, rest, early)
+    advance(order, *chains)
     while any(r.result is None for r in chains):
         advance(order, *chains, near=True)
     mine_qkvg, sent = qkvg_sum.result

time: 444 us -> 447 us (level)
  no operation moved by 1% of the time
where the time goes in v7:
time: 447 us; the launch traced here: 443 us
  Pallas kernels  337 us (75%)
  waiting for transfers between devices  43.2 us (10%)
  starting transfers between devices  38.6 us (9%)
  between operations  15.3 us (3%)
  local copies, waits for them, and re-layouts  7.12 us (2%)
    pallas_call x25, Pallas kernels, call(): pl.pallas_call(run, grid_spec=pltpu.PrefetchScalarGridSpec(num_scalar_pre...  337 us
    ppermute x30, waiting for transfers between devices, exchange(): lax.ppermute(array, axis, [(i, i ^ 1 << bit) for i in range(self.counts[a...  31.8 us
    ppermute x30, starting transfers between devices, exchange(): lax.ppermute(array, axis, [(i, i ^ 1 << bit) for i in range(self.counts[a...  30.1 us
  transfers between devices with their start and end apart: 45, of which 12 were waited for; matrix products, arithmetic and copies ran while one was open for 1% of the time, Pallas kernels for 70%

profile of v7, /device:TPU:0, one launch (start us, length us, event | category | flops | bytes accessed | tf_op | source)
XLA Modules:
  0.0 442.8 jit_solution(16471042573649856283)
XLA Ops:
  8.4 13.0 %pair_forward.1 = bf16[16,48,768]{2,1,0:T(8,128)(2,1)} custom-call(s32[5]{0:T(128)} %broadcast_1_place_ref.2.place_ref, bf16[48,768,128]{2,1,0:T(8,128)(2,1)} %bitcast.45, bf16[1,128]{1,0:T(2,128)(2,1)} %bitcast.63, bf16[16,128]{1,0:T(8,128)(2,1)} %bitcast.38, s32[1,768]{1,0:T(1,128)} %refs_3_.2, s32[1]{0:T(128)S(6)} %copy.40.refs_4_), custom_call_target="tpu_custom_call" | custom-call | flops 99999997952 | bytes 1000000 | tf_op jit(solution)/shard_map/pair_forward/pallas_call | solution.py:82
  23.9 57.3 %transition.1 = (f32[2,768,768]{2,1,0:T(8,128)}, f32[2,768,768]{2,1,0:T(8,128)}, f32[768,384]{1,0:T(8,128)}, f32[768,384]{1,0:T(8,128)}, bf16[32,360,384]{2,1,0:...) custom-call(s32[5]{0:T(128)} %stack.23.place_ref, bf16[2,768,768]{2,1,0:T(8,128)(2,1)} %bitcast.49, ...), custom_call_target="tpu_custom_call" | custom-call | flops 99999997952 | bytes 1000000 | tf_op jit(solution)/shard_map/transition/pallas_call | solution.py:82
  82.8 27.9 %inputs.1 = (bf16[4,768,768]{2,1,0:T(8,128)(2,1)}, f32[4,768,384]{2,1,0:T(8,128)}, f32[4,768,384]{2,1,0:T(8,128)}, bf16[4,4,768,128]{3,2,1,0:T(8,128)(2,1)}, bf1...) custom-call(s32[5]{0:T(128)} %stack.23.place_ref, ...), custom_call_target="tpu_custom_call" | custom-call | flops 99999997952 | bytes 1000000 | tf_op jit(solution)/shard_map/inputs/pallas_call | solution.py:82
  110.8 7.0 %combine.11 = (bf16[8,360,384]{2,1,0:T(8,128)(2,1)}, bf16[8,360,384]{2,1,0:T(8,128)(2,1)}) custom-call(s32[5]{0:T(128)} %stack.23.place_ref, bf16[32,360,384]{2,1,0:T(8,128)(2,1)} %get-tuple-element.141.refs_16_.refs_0_.refs_2_, bf16[32,360,384]{2,1,0:T(8,128)(2,1)} %collective-permute-done.2.refs_1_.refs_3_, ...), custom_call_target="tpu_custom_call" | custom-call | flops 99999997952 | bytes 1000000 | tf_op jit(solution)/shard_map/combine/pallas_call | solution.py:82
  120.2 3.0 all-gather.3.cloned.1.call-done
  123.2 23.6 %attention.4 = (f32[4,768,128]{2,1,0:T(8,128)}, bf16[4,768,128]{2,1,0:T(8,128)(2,1)}, bf16[4,96,768]{2,1,0:T(8,128)(2,1)}, bf16[4,96,768]{2,1,0:T(8,128)(2,1)}, ...) custom-call(s32[5]{0:T(128)} %stack.23.place_ref, bf16[4,4,768,128]{3,2,1,0:T(8,128)(2,1)} %get-tuple-element.146.refs_0_, ...), custom_call_target="tpu_custom_call" | custom-call | flops 16999999488 | bytes 1000000 | tf_op jit(solution)/shard_map/attention/pallas_call | solution.py:82
  148.2 23.8 %attention.5 = (f32[4,768,128]{2,1,0:T(8,128)}, bf16[4,768,128]{2,1,0:T(8,128)(2,1)}, bf16[4,96,768]{2,1,0:T(8,128)(2,1)}, bf16[4,96,768]{2,1,0:T(8,128)(2,1)}, ...) custom-call(s32[5]{0:T(128)} %stack.23.place_ref, bf16[4,4,768,128]{3,2,1,0:T(8,128)(2,1)} %get-tuple-element.146.refs_0_, ...), custom_call_target="tpu_custom_call" | custom-call | flops 16999999488 | bytes 1000000 | tf_op jit(solution)/shard_map/attention/pallas_call | solution.py:82
  172.8 2.9 collective-permute-done.3.refs_1_.refs_3_
  175.7 5.5 %combine.12 = (bf16[4,2,48,768]{3,2,1,0:T(8,128)(2,1)}, bf16[4,2,48,768]{3,2,1,0:T(8,128)(2,1)}, bf16[4,360,384]{2,1,0:T(8,128)(2,1)}, bf16[4,360,384]{2,1,0:T(8,128)(2,1)}) custom-call(s32[5]{0:T(128)} %stack.23.place_ref, bf16[8,2,48,768]{3,2,1,0:T(8,128)(2,1)} %get-tuple-element.160.refs_0_.refs_2_, ...), custom_call_target="tpu_custom_call" | custom-call | flops 99999997952 | bytes 1000000 | tf_op jit(solution)/shard_map/combine/pallas_call | solution.py:82
  183.2 23.8 %attention.6 = (f32[4,768,128]{2,1,0:T(8,128)}, bf16[4,768,128]{2,1,0:T(8,128)(2,1)}, bf16[4,96,768]{2,1,0:T(8,128)(2,1)}, bf16[4,96,768]{2,1,0:T(8,128)(2,1)}, ...) custom-call(s32[5]{0:T(128)} %stack.23.place_ref, bf16[4,4,768,128]{3,2,1,0:T(8,128)(2,1)} %get-tuple-element.146.refs_0_, ...), custom_call_target="tpu_custom_call" | custom-call | flops 16999999488 | bytes 1000000 | tf_op jit(solution)/shard_map/attention/pallas_call | solution.py:82
  208.7 3.9 combine.13
  215.3 24.1 %attention.7 = (f32[4,768,128]{2,1,0:T(8,128)}, bf16[4,768,128]{2,1,0:T(8,128)(2,1)}, bf16[4,96,768]{2,1,0:T(8,128)(2,1)}, bf16[4,96,768]{2,1,0:T(8,128)(2,1)}, ...) custom-call(s32[5]{0:T(128)} %stack.23.place_ref, bf16[4,4,768,128]{3,2,1,0:T(8,128)(2,1)} %get-tuple-element.146.refs_0_, ...), custom_call_target="tpu_custom_call" | custom-call | flops 16999999488 | bytes 1000000 | tf_op jit(solution)/shard_map/attention/pallas_call | solution.py:82
  241.4 5.3 %combine.14 = (bf16[1,2,48,768]{3,2,1,0:T(8,128)(2,1)}, bf16[1,2,48,768]{3,2,1,0:T(8,128)(2,1)}, bf16[2,2,48,768]{3,2,1,0:T(8,128)(2,1)}, bf16[2,2,48,768]{3,2,1...) custom-call(s32[5]{0:T(128)} %stack.23.place_ref, ...), custom_call_target="tpu_custom_call" | custom-call | flops 99999997952 | bytes 1000000 | tf_op jit(solution)/shard_map/combine/pallas_call | solution.py:82
  250.0 14.4 %mixed.1 = (bf16[2,768,1920]{2,1,0:T(8,128)(2,1)}, bf16[2,768,1920]{2,1,0:T(8,128)(2,1)}, f32[1,384]{1,0:T(1,128)}) custom-call(s32[5]{0:T(128)} %stack.23.place_ref, f32[4,768,384]{2,1,0:T(8,128)} %get-tuple-element.144.refs_0_, f32[4,768,384]{2,1,0:T(8,128)} %get-tuple-element.145.refs_1_, f32[4,768,128]{2,1,0:T(8,128)} %get-tuple-element.157.refs_2_, ...), custom_call_target="tpu_custom_call" | custom-call | flops 99999997952 | bytes 1000000 | tf_op jit(solution)/shard_map/mixed/pallas_call | solution.py:82
  264.3 14.4 %qkvg_grad.1.refs_12_.refs_13_.refs_8_.refs_10_ = bf16[32,96,384]{2,1,0:T(8,128)(2,1)} custom-call(s32[5]{0:T(128)} %stack.23.place_ref, bf16[4,768,768]{2,1,0:T(8,128)(2,1)} %get-tuple-element.154.refs_4_.refs_0_, bf16[2,768,1920]{2,1,0:T(8,128)(2,1)} %get-tuple-element.196.refs_1_.refs_2_.refs_5_.refs_6_, ...), custom_call_target="tpu_custom_call" | custom-call | flops 99999997952 | bytes 1000000 | tf_op jit(solution)/shard_map/qkvg_grad/pallas_call | solution.py:82
  278.8 5.0 %combine.15 = (bf16[1,2,48,768]{3,2,1,0:T(8,128)(2,1)}, bf16[1,2,48,768]{3,2,1,0:T(8,128)(2,1)}, bf16[2,2,48,768]{3,2,1,0:T(8,128)(2,1)}, bf16[2,2,48,768]{3,2,1...) custom-call(s32[5]{0:T(128)} %stack.23.place_ref, ...), custom_call_target="tpu_custom_call" | custom-call | flops 99999997952 | bytes 1000000 | tf_op jit(solution)/shard_map/combine/pallas_call | solution.py:82
  283.8 3.3 collective-permute-start.15
  290.1 25.4 %outputs.1 = (bf16[2,768,768]{2,1,0:T(8,128)(2,1)}, bf16[2,768,768]{2,1,0:T(8,128)(2,1)}, bf16[768,1536]{1,0:T(8,128)(2,1)}, bf16[768,768]{1,0:T(8,128)(2,1)}, f...) custom-call(s32[5]{0:T(128)} %stack.23.place_ref, bf16[2,768,768]{2,1,0:T(8,128)(2,1)} %bitcast.51, ...), custom_call_target="tpu_custom_call" | custom-call | flops 99999997952 | bytes 1000000 | tf_op jit(solution)/shard_map/outputs/pallas_call | solution.py:82
  317.0 4.8 %combine.16 = (bf16[1,2,48,768]{3,2,1,0:T(8,128)(2,1)}, bf16[1,2,48,768]{3,2,1,0:T(8,128)(2,1)}, bf16[2,2,48,768]{3,2,1,0:T(8,128)(2,1)}, bf16[2,2,48,768]{3,2,1...) custom-call(s32[5]{0:T(128)} %stack.23.place_ref, ...), custom_call_target="tpu_custom_call" | custom-call | flops 99999997952 | bytes 1000000 | tf_op jit(solution)/shard_map/combine/pallas_call | solution.py:82
  322.6 10.3 %conditions.1.refs_4_.refs_6_ = bf16[16,304,384]{2,1,0:T(8,128)(2,1)} custom-call(s32[5]{0:T(128)} %stack.23.place_ref, bf16[768,384]{1,0:T(8,128)(2,1)} %bitcast.58, f32[1,768]{1,0:T(1,128)} %get-tuple-element.263.refs_3_.refs_5_.refs_1_, bf16[384,3072]{1,0:T(8,128)(2,1)} %refs_2_.1, bf16[384,1536]{1,0:T(8,128)(2,1)} %refs_3_.3, ...), custom_call_target="tpu_custom_call" | custom-call | flops 99999997952 | bytes 1000000 | tf_op jit(solution)/shard_map/conditions/pallas_call | solution.py:82
  332.9 5.9 %collective-permute-done.19.refs_1_.refs_3_ = bf16[2,2,48,768]{3,2,1,0:T(8,128)(2,1)} collective-permute-done((bf16[2,2,48,768]{3,2,1,0:T(8,128)(2,1)}, bf16[2,2,48,768]{3,2,1,0:T(8,128)(2,1)}, u32[]{:S(2)}, u32[]{:S(2)}) %collective-permute-start.19) | collective-permute-done | bytes 294944 | tf_op jit(solution)/shard_map/ppermute | solution.py:201
  343.5 10.8 %pair_backward.2 = (f32[48,768,128]{2,1,0:T(8,128)}, f32[16,128]{1,0:T(8,128)}) custom-call(s32[5]{0:T(128)} %stack.23.place_ref, bf16[48,768,128]{2,1,0:T(8,128)(2,1)} %bitcast.46, f32[1,128]{1,0:T(1,128)} %slice.34.refs_1_.refs_10_, bf16[16,128]{1,0:T(8,128)(2,1)} %maximum_select_fusion.refs_2_, bf16[2,48,768]{2,1,0:T(8,128)(2,1)} %bitcast.69, ...), custom_call_target="tpu_custom_call" | custom-call | flops 99999997952 | bytes 1000000 | tf_op jit(solution)/shard_map/pair_backward/pallas_call | solution.py:82
  354.2 4.7 %collective-permute-done.24.refs_1_.refs_3_ = bf16[8,96,384]{2,1,0:T(8,128)(2,1)} collective-permute-done((bf16[8,96,384]{2,1,0:T(8,128)(2,1)}, bf16[8,96,384]{2,1,0:T(8,128)(2,1)}, u32[]{:S(2)}, u32[]{:S(2)}) %collective-permute-start.24) | collective-permute-done | bytes 589856 | tf_op jit(solution)/shard_map/ppermute | solution.py:201
  358.9 4.9 %combine.18 = (bf16[4,96,384]{2,1,0:T(8,128)(2,1)}, bf16[4,96,384]{2,1,0:T(8,128)(2,1)}, bf16[4,304,384]{2,1,0:T(8,128)(2,1)}, bf16[4,304,384]{2,1,0:T(8,128)(2,1)}, bf16[1,360,384]{2,1,0:T(8,128)(2,1)}) custom-call(s32[5]{0:T(128)} %stack.23.place_ref, bf16[8,96,384]{2,1,0:T(8,128)(2,1)} %get-tuple-element.224.refs_20_.refs_0_.refs_2_, ...), custom_call_target="tpu_custom_call" | custom-call | flops 99999997952 | bytes 1000000 | tf_op jit(solution)/shard_map/combine/pallas_call | solution.py:82
  366.4 17.2 %pair_backward.3 = (f32[48,768,128]{2,1,0:T(8,128)}, f32[16,128]{1,0:T(8,128)}) custom-call(s32[5]{0:T(128)} %stack.23.place_ref, bf16[48,768,128]{2,1,0:T(8,128)(2,1)} %bitcast.47, f32[1,128]{1,0:T(1,128)} %slice.34.refs_1_.refs_10_, bf16[16,128]{1,0:T(8,128)(2,1)} %maximum_select_fusion.refs_2_, ...), custom_call_target="tpu_custom_call", output_to_operand_aliasing={{0}: (12, {})} | custom-call | flops 99999997952 | bytes 1000000 | tf_op jit(solution)/shard_map/pair_backward/pallas_call | solution.py:82
  383.6 4.3 collective-permute-done.28.refs_7_.refs_9_
  387.9 4.0 combine.19
  398.7 4.2 collective-permute-done.31.refs_5_.refs_7_
  403.7 3.0 combine.20
  412.0 5.7 %collective-permute-done.35.refs_1_ = bf16[1,304,384]{2,1,0:T(8,128)(2,1)S(1)} collective-permute-done((bf16[1,304,384]{2,1,0:T(8,128)(2,1)}, bf16[1,304,384]{2,1,0:T(8,128)(2,1)S(1)}, u32[]{:S(2)}, u32[]{:S(2)}) %collective-permute-start.35) | collective-permute-done | bytes 233504 | tf_op jit(solution)/shard_map/ppermute | solution.py:201
  422.6 4.5 %collective-permute-done.43 = f32[16,128]{1,0:T(8,128)S(1)} collective-permute-done((f32[16,128]{1,0:T(8,128)S(1)}, f32[16,128]{1,0:T(8,128)S(1)}, u32[]{:S(2)}, u32[]{:S(2)}) %collective-permute-start.43) | collective-permute-done | bytes 8224 | tf_op jit(solution)/shard_map/ppermute | solution.py:1129
  430.8 4.9 %results.1 = (f32[48,384]{1,0:T(8,128)}, f32[24,3072]{1,0:T(8,128)}, f32[24,1536]{1,0:T(8,128)}, f32[48,3072]{1,0:T(8,128)}, f32[48,768]{1,0:T(8,128)}, /*index=...) custom-call(s32[5]{0:T(128)} %stack.23.place_ref, ...), custom_call_target="tpu_custom_call" | custom-call | flops 99999997952 | bytes 1000000 | tf_op jit(solution)/shard_map/results/pallas_call | solution.py:82
  (141 shorter events, 54.7 us)
Async XLA Ops:
  7.2 116.0 %all-gather.3.cloned.1.call-start = ((), (), s32[]{:S(2)}) async-start(), calls=%async_computation | async-start | bytes 20054016 | tf_op jit(solution)/shard_map/all_gather | solution.py:1037
  21.4 61.5 %collective-permute-start = (bf16[2,768,768]{2,1,0:T(8,128)(2,1)}, bf16[2,768,768]{2,1,0:T(8,128)(2,1)}, u32[]{:S(2)}, u32[]{:S(2)}) collective-permute-start(bf16[2,768,768]{2,1,0:T(8,128)(2,1)} %bitcast.48), channel_id=1, source_target_pairs={{0,1},{1,0},{2,3},{3,2},{4,5},{5,4},{6,7},{7,6},{8,9},{9,8},{10,11... | collective-permute-start | bytes 7077896 | tf_op jit(solution)/shard_map/ppermute | solution.py:1032
  21.9 60.9 %collective-permute-start.1 = (bf16[2,768,768]{2,1,0:T(8,128)(2,1)}, bf16[2,768,768]{2,1,0:T(8,128)(2,1)}, u32[]{:S(2)}, u32[]{:S(2)}) collective-permute-start(bf16[2,768,768]{2,1,0:T(8,128)(2,1)} %bitcast.52), channel_id=1, source_target_pairs={{0,1},{1,0},{2,3},{3,2},{4,5},{5,4},{6,7},{7,6},{8,9},{9,8},{10,11... | collective-permute-start | bytes 7077896 | tf_op jit(solution)/shard_map/ppermute | solution.py:1032
  81.2 29.5 %collective-permute-start.2 = (bf16[32,360,384]{2,1,0:T(8,128)(2,1)}, bf16[32,360,384]{2,1,0:T(8,128)(2,1)}, u32[]{:S(2)}, u32[]{:S(2)}) collective-permute-start(bf16[32,360,384]{2,1,0:T(8,128)(2,1)} %get-tuple-element.141.refs_16_.refs_0_.refs_2_), channel_id=1, source_target_pairs={{0,1},{1,0},{2,3},{3,2},{4,5},{5,4},{6,7},{7,6},{8,9},{9,8},{10,11... | collective-permute-start | bytes 26542088 | tf_op jit(solution)/shard_map/ppermute | solution.py:201
  117.8 55.1 %collective-permute-start.4 = (bf16[8,360,384]{2,1,0:T(8,128)(2,1)}, bf16[8,360,384]{2,1,0:T(8,128)(2,1)}, u32[]{:S(2)}, u32[]{:S(2)}) collective-permute-start(bf16[8,360,384]{2,1,0:T(8,128)(2,1)} %get-tuple-element.155.refs_9_.refs_11_), channel_id=1, source_target_pairs={{0,16},{16,0},{1,17},{17,1},{2,18},{18,2},{3,19},{19,3},{4,20},{20... | collective-permute-start | bytes 6635528 | tf_op jit(solution)/shard_map/ppermute | solution.py:201
  146.8 28.9 %collective-permute-start.3 = (bf16[8,2,48,768]{3,2,1,0:T(8,128)(2,1)}, bf16[8,2,48,768]{3,2,1,0:T(8,128)(2,1)}, u32[]{:S(2)}, u32[]{:S(2)}) collective-permute-start(bf16[8,2,48,768]{3,2,1,0:T(8,128)(2,1)} %get-tuple-element.158.refs_9_), channel_id=1, source_target_pairs={{0,2},{1,3},{2,0},{3,1},{4,6},{5,7},{6,4},{7,5},{8,10},{9,11},{10,... | collective-permute-start | bytes 3538952 | tf_op jit(solution)/shard_map/ppermute | solution.py:201
  172.0 36.7 %collective-permute-start.6 = (bf16[8,2,48,768]{3,2,1,0:T(8,128)(2,1)}, bf16[8,2,48,768]{3,2,1,0:T(8,128)(2,1)}, u32[]{:S(2)}, u32[]{:S(2)}) collective-permute-start(bf16[8,2,48,768]{3,2,1,0:T(8,128)(2,1)} %get-tuple-element.161.refs_8_), channel_id=1, source_target_pairs={{0,2},{1,3},{2,0},{3,1},{4,6},{5,7},{6,4},{7,5},{8,10},{9,11},{10,... | collective-permute-start | bytes 3538952 | tf_op jit(solution)/shard_map/ppermute | solution.py:201
  181.2 27.5 %collective-permute-start.5 = (bf16[4,2,48,768]{3,2,1,0:T(8,128)(2,1)}, bf16[4,2,48,768]{3,2,1,0:T(8,128)(2,1)}, u32[]{:S(2)}, u32[]{:S(2)}) collective-permute-start(bf16[4,2,48,768]{3,2,1,0:T(8,128)(2,1)} %get-tuple-element.162.refs_9_), channel_id=1, source_target_pairs={{0,4},{1,5},{2,6},{3,7},{4,0},{5,1},{6,2},{7,3},{8,12},{9,13},{10,... | collective-permute-start | bytes 1769480 | tf_op jit(solution)/shard_map/ppermute | solution.py:201
  182.7 58.7 %collective-permute-start.10 = (bf16[4,360,384]{2,1,0:T(8,128)(2,1)}, bf16[4,360,384]{2,1,0:T(8,128)(2,1)}, u32[]{:S(2)}, u32[]{:S(2)}) collective-permute-start(bf16[4,360,384]{2,1,0:T(8,128)(2,1)} %get-tuple-element.164.refs_11_.refs_13_), channel_id=1, source_target_pairs={{0,4},{1,5},{2,6},{3,7},{4,0},{5,1},{6,2},{7,3},{8,12},{9,13},{10,... | collective-permute-start | bytes 3317768 | tf_op jit(solution)/shard_map/ppermute | solution.py:201
  207.1 34.3 %collective-permute-start.9 = (bf16[8,2,48,768]{3,2,1,0:T(8,128)(2,1)}, bf16[8,2,48,768]{3,2,1,0:T(8,128)(2,1)}, u32[]{:S(2)}, u32[]{:S(2)}) collective-permute-start(bf16[8,2,48,768]{3,2,1,0:T(8,128)(2,1)} %get-tuple-element.168.refs_8_), channel_id=1, source_target_pairs={{0,2},{1,3},{2,0},{3,1},{4,6},{5,7},{6,4},{7,5},{8,10},{9,11},{10,... | collective-permute-start | bytes 3538952 | tf_op jit(solution)/shard_map/ppermute | solution.py:201
  212.6 28.7 %collective-permute-start.7 = (bf16[2,2,48,768]{3,2,1,0:T(8,128)(2,1)}, bf16[2,2,48,768]{3,2,1,0:T(8,128)(2,1)}, u32[]{:S(2)}, u32[]{:S(2)}) collective-permute-start(bf16[2,2,48,768]{3,2,1,0:T(8,128)(2,1)} %get-tuple-element.169.refs_9_), channel_id=1, source_target_pairs={{0,8},{1,9},{2,10},{3,11},{4,12},{5,13},{6,14},{7,15},{8,0},{9,1},... | collective-permute-start | bytes 884744 | tf_op jit(solution)/shard_map/ppermute | solution.py:201
  215.0 26.3 %collective-permute-start.8 = (bf16[4,2,48,768]{3,2,1,0:T(8,128)(2,1)}, bf16[4,2,48,768]{3,2,1,0:T(8,128)(2,1)}, u32[]{:S(2)}, u32[]{:S(2)}) collective-permute-start(bf16[4,2,48,768]{3,2,1,0:T(8,128)(2,1)} %get-tuple-element.171.refs_11_.refs_13_), channel_id=1, source_target_pairs={{0,4},{1,5},{2,6},{3,7},{4,0},{5,1},{6,2},{7,3},{8,12},{9,13},{10,... | collective-permute-start | bytes 1769480 | tf_op jit(solution)/shard_map/ppermute | solution.py:201
  239.3 39.4 %collective-permute-start.14 = (bf16[8,2,48,768]{3,2,1,0:T(8,128)(2,1)}, bf16[8,2,48,768]{3,2,1,0:T(8,128)(2,1)}, u32[]{:S(2)}, u32[]{:S(2)}) collective-permute-start(bf16[8,2,48,768]{3,2,1,0:T(8,128)(2,1)} %get-tuple-element.187.refs_16_), channel_id=1, source_target_pairs={{0,2},{1,3},{2,0},{3,1},{4,6},{5,7},{6,4},{7,5},{8,10},{9,11},{10,... | collective-permute-start | bytes 3538952 | tf_op jit(solution)/shard_map/ppermute | solution.py:201
  246.7 96.5 %collective-permute-start.20 = (bf16[1,2,48,768]{3,2,1,0:T(8,128)(2,1)}, bf16[1,2,48,768]{3,2,1,0:T(8,128)(2,1)}, u32[]{:S(2)}, u32[]{:S(2)}) collective-permute-start(bf16[1,2,48,768]{3,2,1,0:T(8,128)(2,1)} %get-tuple-element.188.refs_18_), channel_id=1, source_target_pairs={{0,1},{1,0},{2,3},{3,2},{4,5},{5,4},{6,7},{7,6},{8,9},{9,8},{10,11... | collective-permute-start | bytes 442376 | tf_op jit(solution)/shard_map/ppermute | solution.py:201
  246.7 32.0 %collective-permute-start.12 = (bf16[2,2,48,768]{3,2,1,0:T(8,128)(2,1)}, bf16[2,2,48,768]{3,2,1,0:T(8,128)(2,1)}, u32[]{:S(2)}, u32[]{:S(2)}) collective-permute-start(bf16[2,2,48,768]{3,2,1,0:T(8,128)(2,1)} %get-tuple-element.190.refs_20_), channel_id=1, source_target_pairs={{0,8},{1,9},{2,10},{3,11},{4,12},{5,13},{6,14},{7,15},{8,0},{9,1},... | collective-permute-start | bytes 884744 | tf_op jit(solution)/shard_map/ppermute | solution.py:201
  247.0 68.5 %collective-permute-start.18 = (bf16[2,360,384]{2,1,0:T(8,128)(2,1)}, bf16[2,360,384]{2,1,0:T(8,128)(2,1)}, u32[]{:S(2)}, u32[]{:S(2)}) collective-permute-start(bf16[2,360,384]{2,1,0:T(8,128)(2,1)} %get-tuple-element.194.refs_24_), channel_id=1, source_target_pairs={{0,8},{1,9},{2,10},{3,11},{4,12},{5,13},{6,14},{7,15},{8,0},{9,1},... | collective-permute-start | bytes 1658888 | tf_op jit(solution)/shard_map/ppermute | solution.py:201
  249.7 29.1 %collective-permute-start.13 = (bf16[4,2,48,768]{3,2,1,0:T(8,128)(2,1)}, bf16[4,2,48,768]{3,2,1,0:T(8,128)(2,1)}, u32[]{:S(2)}, u32[]{:S(2)}) collective-permute-start(bf16[4,2,48,768]{3,2,1,0:T(8,128)(2,1)} %get-tuple-element.192.refs_22_.refs_26_), channel_id=1, source_target_pairs={{0,4},{1,5},{2,6},{3,7},{4,0},{5,1},{6,2},{7,3},{8,12},{9,13},{10,... | collective-permute-start | bytes 1769480 | tf_op jit(solution)/shard_map/ppermute | solution.py:201
  283.8 31.8 %collective-permute-start.15 = (bf16[2,2,48,768]{3,2,1,0:T(8,128)(2,1)}, bf16[2,2,48,768]{3,2,1,0:T(8,128)(2,1)}, u32[]{:S(2)}, u32[]{:S(2)}) collective-permute-start(bf16[2,2,48,768]{3,2,1,0:T(8,128)(2,1)} %get-tuple-element.201.refs_20_), channel_id=1, source_target_pairs={{0,8},{1,9},{2,10},{3,11},{4,12},{5,13},{6,14},{7,15},{8,0},{9,1},... | collective-permute-start | bytes 884744 | tf_op jit(solution)/shard_map/ppermute | solution.py:201
  287.2 28.5 %collective-permute-start.16 = (bf16[4,2,48,768]{3,2,1,0:T(8,128)(2,1)}, bf16[4,2,48,768]{3,2,1,0:T(8,128)(2,1)}, u32[]{:S(2)}, u32[]{:S(2)}) collective-permute-start(bf16[4,2,48,768]{3,2,1,0:T(8,128)(2,1)} %get-tuple-element.203.refs_22_), channel_id=1, source_target_pairs={{0,4},{1,5},{2,6},{3,7},{4,0},{5,1},{6,2},{7,3},{8,12},{9,13},{10,... | collective-permute-start | bytes 1769480 | tf_op jit(solution)/shard_map/ppermute | solution.py:201
  288.7 28.3 %collective-permute-start.17 = (bf16[16,96,384]{2,1,0:T(8,128)(2,1)}, bf16[16,96,384]{2,1,0:T(8,128)(2,1)}, u32[]{:S(2)}, u32[]{:S(2)}) collective-permute-start(bf16[16,96,384]{2,1,0:T(8,128)(2,1)} %get-tuple-element.205.refs_24_.refs_25_), channel_id=1, source_target_pairs={{0,16},{16,0},{1,17},{17,1},{2,18},{18,2},{3,19},{19,3},{4,20},{20... | collective-permute-start | bytes 3538952 | tf_op jit(solution)/shard_map/ppermute | solution.py:201
  315.5 27.7 %collective-permute-start.21 = (bf16[1,2,48,768]{3,2,1,0:T(8,128)(2,1)}, bf16[1,2,48,768]{3,2,1,0:T(8,128)(2,1)}, u32[]{:S(2)}, u32[]{:S(2)}) collective-permute-start(bf16[1,2,48,768]{3,2,1,0:T(8,128)(2,1)} %get-tuple-element.199.refs_18_), channel_id=1, source_target_pairs={{0,1},{1,0},{2,3},{3,2},{4,5},{5,4},{6,7},{7,6},{8,9},{9,8},{10,11... | collective-permute-start | bytes 442376 | tf_op jit(solution)/shard_map/ppermute | solution.py:201
  321.7 21.7 %collective-permute-start.22 = (bf16[1,2,48,768]{3,2,1,0:T(8,128)(2,1)}, bf16[1,2,48,768]{3,2,1,0:T(8,128)(2,1)}, u32[]{:S(2)}, u32[]{:S(2)}) collective-permute-start(bf16[1,2,48,768]{3,2,1,0:T(8,128)(2,1)} %get-tuple-element.222.refs_15_), channel_id=1, source_target_pairs={{0,1},{1,0},{2,3},{3,2},{4,5},{5,4},{6,7},{7,6},{8,9},{9,8},{10,11... | collective-permute-start | bytes 442376 | tf_op jit(solution)/shard_map/ppermute | solution.py:201
  321.8 17.0 %collective-permute-start.19 = (bf16[2,2,48,768]{3,2,1,0:T(8,128)(2,1)}, bf16[2,2,48,768]{3,2,1,0:T(8,128)(2,1)}, u32[]{:S(2)}, u32[]{:S(2)}) collective-permute-start(bf16[2,2,48,768]{3,2,1,0:T(8,128)(2,1)} %get-tuple-element.210.refs_17_), channel_id=1, source_target_pairs={{0,8},{1,9},{2,10},{3,11},{4,12},{5,13},{6,14},{7,15},{8,0},{9,1},... | collective-permute-start | bytes 884744 | tf_op jit(solution)/shard_map/ppermute | solution.py:201
  343.2 15.7 %collective-permute-start.24 = (bf16[8,96,384]{2,1,0:T(8,128)(2,1)}, bf16[8,96,384]{2,1,0:T(8,128)(2,1)}, u32[]{:S(2)}, u32[]{:S(2)}) collective-permute-start(bf16[8,96,384]{2,1,0:T(8,128)(2,1)} %get-tuple-element.223.refs_19_.refs_23_), channel_id=1, source_target_pairs={{0,4},{1,5},{2,6},{3,7},{4,0},{5,1},{6,2},{7,3},{8,12},{9,13},{10,... | collective-permute-start | bytes 1769480 | tf_op jit(solution)/shard_map/ppermute | solution.py:201
  343.2 15.7 %collective-permute-start.25 = (bf16[16,304,384]{2,1,0:T(8,128)(2,1)}, bf16[16,304,384]{2,1,0:T(8,128)(2,1)}, u32[]{:S(2)}, u32[]{:S(2)}) collective-permute-start(bf16[16,304,384]{2,1,0:T(8,128)(2,1)} %conditions.1.refs_4_.refs_6_), channel_id=1, source_target_pairs={{0,1},{1,0},{2,3},{3,2},{4,5},{5,4},{6,7},{7,6},{8,9},{9,8},{10,11... | collective-permute-start | bytes 11206664 | tf_op jit(solution)/shard_map/ppermute | solution.py:201
  363.8 19.7 %collective-permute-start.29 = (bf16[1,360,384]{2,1,0:T(8,128)(2,1)}, bf16[1,360,384]{2,1,0:T(8,128)(2,1)}, u32[]{:S(2)}, u32[]{:S(2)}) collective-permute-start(bf16[1,360,384]{2,1,0:T(8,128)(2,1)} %get-tuple-element.235.refs_16_.refs_10_.refs_13_), channel_id=1, source_target_pairs={{0,16},{16,0},{1,17},{17,1},{2,18},{18,2},{3,19},{19,3},{4,20},{20... | collective-permute-start | bytes 829448 | tf_op jit(solution)/shard_map/ppermute | solution.py:201
  365.3 18.3 %collective-permute-start.27 = (bf16[4,96,384]{2,1,0:T(8,128)(2,1)}, bf16[4,96,384]{2,1,0:T(8,128)(2,1)}, u32[]{:S(2)}, u32[]{:S(2)}) collective-permute-start(bf16[4,96,384]{2,1,0:T(8,128)(2,1)} %get-tuple-element.231.refs_12_), channel_id=1, source_target_pairs={{0,8},{1,9},{2,10},{3,11},{4,12},{5,13},{6,14},{7,15},{8,0},{9,1},... | collective-permute-start | bytes 884744 | tf_op jit(solution)/shard_map/ppermute | solution.py:201
  365.9 22.0 %collective-permute-start.28 = (bf16[4,304,384]{2,1,0:T(8,128)(2,1)}, bf16[4,304,384]{2,1,0:T(8,128)(2,1)}, u32[]{:S(2)}, u32[]{:S(2)}) collective-permute-start(bf16[4,304,384]{2,1,0:T(8,128)(2,1)} %get-tuple-element.233.refs_14_.refs_17_), channel_id=1, source_target_pairs={{0,2},{1,3},{2,0},{3,1},{4,6},{5,7},{6,4},{7,5},{8,10},{9,11},{10,... | collective-permute-start | bytes 2801672 | tf_op jit(solution)/shard_map/ppermute | solution.py:201
  393.9 14.5 %collective-permute-start.39 = (f32[16,128]{1,0:T(8,128)}, f32[16,128]{1,0:T(8,128)S(1)}, u32[]{:S(2)}, u32[]{:S(2)}) collective-permute-start(f32[16,128]{1,0:T(8,128)} %get-tuple-element.248), channel_id=1, source_target_pairs={{0,17},{1,16},{2,19},{3,18},{4,21},{5,20},{6,23},{7,22},{8,25},{9,... | collective-permute-start | bytes 24584 | tf_op jit(solution)/shard_map/ppermute | solution.py:1129
  393.9 14.5 %collective-permute-start.38 = (f32[16,128]{1,0:T(8,128)}, f32[16,128]{1,0:T(8,128)S(1)}, u32[]{:S(2)}, u32[]{:S(2)}) collective-permute-start(f32[16,128]{1,0:T(8,128)} %get-tuple-element.248), channel_id=1, source_target_pairs={{0,1},{1,0},{2,3},{3,2},{4,5},{5,4},{6,7},{7,6},{8,9},{9,8},{10,11... | collective-permute-start | bytes 24584 | tf_op jit(solution)/shard_map/ppermute | solution.py:1129
  394.6 13.8 %collective-permute-start.37 = (f32[16,128]{1,0:T(8,128)}, f32[16,128]{1,0:T(8,128)S(1)}, u32[]{:S(2)}, u32[]{:S(2)}) collective-permute-start(f32[16,128]{1,0:T(8,128)} %get-tuple-element.248), channel_id=1, source_target_pairs={{0,16},{1,17},{2,18},{3,19},{4,20},{5,21},{6,22},{7,23},{8,24},{9,... | collective-permute-start | bytes 24584 | tf_op jit(solution)/shard_map/ppermute | solution.py:1129
  412.0 15.7 %collective-permute-start.34 = (bf16[96,384]{1,0:T(8,128)(2,1)}, bf16[96,384]{1,0:T(8,128)(2,1)S(1)}, u32[]{:S(2)}, u32[]{:S(2)}) collective-permute-start(bf16[96,384]{1,0:T(8,128)(2,1)} %bitcast.61), channel_id=1, source_target_pairs={{0,17},{1,16},{2,19},{3,18},{4,21},{5,20},{6,23},{7,22},{8,25},{9,... | collective-permute-start | bytes 221192 | tf_op jit(solution)/shard_map/ppermute | solution.py:1163
  (34 other events, 309.6 us)
Sparse Core Ops, SparseCore 0:
  21.5 101.6 all-gather.2
